TPU v7x, 32 devices: a whole 2x2x4 slice. The times are simulated.
32 devices in a mesh: section: 4 (over z), tower: 2 (over x), lane: 4 (over y, core).
Axes of the slice: x: 2, y: 2, z: 4, core: 2. Of those that a mesh axis runs over, the one named last changes fastest.
Arguments:
- in_flight: bfloat16 [4, 2, 64, 3072], P('section', 'tower', 'lane'), may hold values from -6 to 6
- fresh_batches: bfloat16 [4, 2, 64, 3072], P(None, 'tower', 'lane'), may hold values from -6 to 6
- offsets: int32 [4], P('lane'), may hold values from 0 to 3, as said below
- norm_gain: float32 [4, 2, 3072], P('section', 'tower'), may hold values from 0.5 to 3
- w_query: bfloat16 [4, 2, 3072, 2048], P('section', 'tower', None, 'lane'), may hold values from -0.109375 to 0.109375
- w_keyval: bfloat16 [4, 2, 2, 3072, 2048], P('section', 'tower', None, None, 'lane'), may hold values from -0.109375 to 0.109375
- w_out: bfloat16 [4, 2, 2048, 3072], P('section', 'tower', 'lane'), may hold values from -0.125 to 0.125
Outputs:
- states: bfloat16 [2, 4, 2, 64, 3072], P(None, 'section', 'tower', 'lane')
Inputs may be any that keep to these rules, and one draw needn't show every extreme that they name: offsets is a permutation of 0 to 3.
All inputs are finite; a program needn't handle non-finite values.
Results may differ from a plain program's by a relative error of at most 0.017.
Values may be sent and summed in bfloat16 or wider, within the bound.
No kernel may reach another device: no remote copies, remote signals or barrier semaphores. Data moves between devices by JAX's collectives and lax.ppermute only.
A program may use at most 64 MiB of HBM per device.

v0:
```python
import jax
import jax.numpy as jnp
from jax import lax
from jax.sharding import PartitionSpec as P

HEAD_DIM = 128


epsilon = 1e-06


def from_partner(value, axis, distance):
    mask = 2**distance
    pairs = [(source, source ^ mask) for source in range(lax.axis_size(axis))]
    return lax.ppermute(value, axis, pairs)


def shifted(value, axis, steps):
    count = lax.axis_size(axis)
    leading, last = (max(0, -steps), min(count, count - steps))
    return lax.ppermute(value, axis, [(source, source + steps) for source in range(leading, last)])


def one_tick(state, norm_w, wq_local, wkv_local, wo_local):
    tok_rows = state.shape[0]
    wide = state.astype(jnp.float32)
    normed = (
        wide * lax.rsqrt(jnp.mean(wide * wide, -1, keepdims=True) + epsilon) * norm_w[None, :]
    ).astype(jnp.bfloat16)
    partner = from_partner(normed, "tower", 0)
    own_all, partner_all = (
        lax.all_gather(normed, "lane", axis=0, tiled=True),
        lax.all_gather(partner, "lane", axis=0, tiled=True),
    )
    all_rows = own_all.shape[0]
    clips = all_rows // tok_rows
    head_cols = wq_local.shape[1]
    heads_here = head_cols // HEAD_DIM
    query = jnp.dot(own_all, wq_local, preferred_element_type=jnp.float32).astype(jnp.bfloat16)
    keyval = jnp.einsum(
        "rd,cdh->crh", partner_all, wkv_local, preferred_element_type=jnp.float32
    ).astype(jnp.bfloat16)
    shaped = (clips, tok_rows, heads_here, HEAD_DIM)
    scores = jnp.einsum(
        "lqhe,lkhe->lhqk",
        query.reshape(shaped),
        keyval[0].reshape(shaped),
        preferred_element_type=jnp.float32,
    ) / jnp.sqrt(jnp.float32(HEAD_DIM))
    attn_weights = jax.nn.softmax(scores, axis=-1).astype(jnp.bfloat16)
    mixed = jnp.einsum(
        "lhqk,lkhe->lqhe",
        attn_weights,
        keyval[1].reshape(shaped),
        preferred_element_type=jnp.float32,
    ).astype(jnp.bfloat16)
    mixed = mixed.reshape(all_rows, head_cols)
    head_total = lax.psum_scatter(
        jnp.dot(mixed, wo_local, preferred_element_type=jnp.float32),
        "lane",
        scatter_dimension=0,
        tiled=True,
    )
    return (wide + head_total).astype(jnp.bfloat16)


def shards(in_flight, fresh_batches, offsets, norm_gain, w_query, w_keyval, w_out):
    norm_w = norm_gain[0, 0]
    wq_local = w_query[0, 0]
    wkv_local = w_keyval[0, 0]
    wo_local = w_out[0, 0]
    first = one_tick(in_flight[0, 0], norm_w, wq_local, wkv_local, wo_local)
    handed = shifted(first, "section", 1)
    picked = lax.dynamic_index_in_dim(fresh_batches[:, 0], offsets[0], 0, keepdims=False)
    section_pos = lax.axis_index("section")
    second_in = jnp.where(section_pos == 0, picked, handed)
    second = one_tick(second_in, norm_w, wq_local, wkv_local, wo_local)
    return jnp.stack([first, second])[:, None, None]


def solution(mesh):
    placed = (
        P("section", "tower", "lane", None),
        P(None, "tower", "lane", None),
        P("lane"),
        P("section", "tower", None),
        P("section", "tower", None, "lane"),
        P("section", "tower", None, None, "lane"),
        P("section", "tower", "lane", None),
    )
    return jax.shard_map(
        shards,
        mesh=mesh,
        in_specs=placed,
        out_specs=P(None, "section", "tower", "lane", None),
        check_vma=False,
    )
```

profile of v0, /device:TPU:0, one launch (start us, length us, event | category | flops | bytes accessed | tf_op | source)
XLA Modules:
  0.0 126.5 jit_solution(12566158612452588096)
XLA Ops:
  6.5 0.0 copy-start
  6.5 0.0 reduce-scatter.3.cloned.1.call-start
  6.5 1.2 fusion.44
  7.7 1.0 fusion.46
  8.7 3.0 %collective-permute-start = (bf16[16,3072]{1,0:T(8,128)(2,1)S(1)}, bf16[16,3072]{1,0:T(8,128)(2,1)S(1)}, u32[]{:S(2)}, u32[]{:S(2)}) collective-permute-start(bf16[16,3072]{1,0:T(8,128)(2,1)S(1)} %fusion.46), channel_id=1, source_target_pairs={{0,4},{4,0},{1,5},{5,1},{2,6},{6,2},{3,7},{7,3},{8,12},{12,8},{9,1... | collective-permute-start | bytes 294920 | tf_op jit(solution)/shard_map/ppermute | solution.py:15
  11.7 6.5 %all_gather.13 = bf16[64,3072]{1,0:T(8,128)(2,1)S(1)} all-gather(bf16[16,3072]{1,0:T(8,128)(2,1)S(1)} %fusion.46), channel_id=1, replica_groups=mesh['section'=4,'tower'=2,'lane'=4] {'lane'}, dimensions={0}, use_global_device_ids=true | all-gather | bytes 491520 | tf_op jit(solution)/shard_map/all_gather | solution.py:32
  18.2 2.5 %fusion.30 = bf16[64,512]{1,0:T(8,128)(2,1)S(1)} fusion(bf16[64,3072]{1,0:T(8,128)(2,1)S(1)} %all_gather.13, bf16[1,1,3072,512]{3,2,1,0:T(8,128)(2,1)} %param.11), kind=kOutput, calls=%fused_computation.24 | convolution fusion | flops 201359360 | bytes 3604480 | tf_op jit(solution)/shard_map/dot_general | solution.py:39
  20.8 0.0 collective-permute-done
  20.8 6.6 %all_gather.12 = bf16[64,3072]{1,0:T(8,128)(2,1)S(1)} all-gather(bf16[16,3072]{1,0:T(8,128)(2,1)S(1)} %collective-permute-done), channel_id=1, replica_groups=mesh['section'=4,'tower'=2,'lane'=4] {'lane'}, dimensions={0}, use_global_device_ids=true | all-gather | bytes 491520 | tf_op jit(solution)/shard_map/all_gather | solution.py:33
  27.4 4.0 %fusion.25 = bf16[2,64,512]{2,1,0:T(8,128)(2,1)S(1)} fusion(bf16[1,1,2,3072,512]{4,3,2,1,0:T(8,128)(2,1)} %param.12, bf16[64,3072]{1,0:T(8,128)(2,1)S(1)} %all_gather.12), kind=kOutput, calls=%fused_computation.19 | convolution fusion | flops 402718720 | bytes 6815744 | tf_op jit(solution)/shard_map/rd,cdh->crh/dot_general | solution.py:40
  31.4 0.0 copy-start.1
  31.4 0.2 fusion.75
  31.6 0.8 convolution_multiply_fusion.1
  32.4 0.0 copy-start.3
  32.4 1.2 fusion.36
  33.7 0.0 copy-done
  33.7 1.5 %fusion.8 = f32[64,3072]{1,0:T(8,128)} fusion(bf16[1,1,512,3072]{3,2,1,0:T(8,128)(2,1)S(1)} %copy-done, bf16[8,8,4,128]{3,2,1,0:T(4,128)(2,1)S(1)} %bitcast.76), kind=kOutput, calls=%fused_computation.8 | convolution fusion | flops 201326592 | bytes 3997696 | tf_op jit(solution)/shard_map/dot_general | solution.py:59
  35.3 0.0 reduce-scatter.3.cloned.1.call-update
  35.3 0.0 reduce-scatter.5.cloned.1.call-start
  35.3 23.4 %reduce-scatter.3.cloned.1.call-done = f32[16,3072]{1,0:T(8,128)} async-done(((f32[64,3072]{1,0:T(8,128)}), f32[16,3072]{1,0:T(8,128)}) %reduce-scatter.3.cloned.1.call-update) | async-done | bytes 196624 | tf_op jit(solution)/shard_map/reduce_scatter | solution.py:58
  58.7 0.0 copy-done.1
  58.7 0.9 fusion.47
  59.7 3.4 %collective-permute-start.1 = (bf16[16,3072]{1,0:T(8,128)(2,1)S(1)}, bf16[16,3072]{1,0:T(8,128)(2,1)S(1)}, u32[]{:S(2)}, u32[]{:S(2)}) collective-permute-start(bf16[16,3072]{1,0:T(8,128)(2,1)S(1)} %fusion.47), channel_id=1, source_target_pairs={{0,8},{8,16},{16,24},{1,9},{9,17},{17,25},{2,10},{10,18},{18,26},{... | collective-permute-start | bytes 294920 | tf_op jit(solution)/shard_map/ppermute | solution.py:21
  63.7 1.5 %collective-permute-done.1 = bf16[16,3072]{1,0:T(8,128)(2,1)S(1)} collective-permute-done((bf16[16,3072]{1,0:T(8,128)(2,1)S(1)}, bf16[16,3072]{1,0:T(8,128)(2,1)S(1)}, u32[]{:S(2)}, u32[]{:S(2)}) %collective-permute-start.1) | collective-permute-done | bytes 98336 | tf_op jit(solution)/shard_map/ppermute | solution.py:21
  65.3 1.0 fusion.40
  66.3 0.0 copy-done.3
  66.3 0.1 fusion.42
  66.4 1.5 %collective-permute-start.2 = (bf16[16,3072]{1,0:T(8,128)(2,1)S(1)}, bf16[16,3072]{1,0:T(8,128)(2,1)}, u32[]{:S(2)}, u32[]{:S(2)}) collective-permute-start(bf16[16,3072]{1,0:T(8,128)(2,1)S(1)} %fusion.42), channel_id=1, source_target_pairs={{0,4},{4,0},{1,5},{5,1},{2,6},{6,2},{3,7},{7,3},{8,12},{12,8},{9,1... | collective-permute-start | bytes 294920 | tf_op jit(solution)/shard_map/ppermute | solution.py:15
  67.9 6.1 %all_gather.15 = bf16[64,3072]{1,0:T(8,128)(2,1)S(1)} all-gather(bf16[16,3072]{1,0:T(8,128)(2,1)S(1)} %fusion.42), channel_id=1, replica_groups=mesh['section'=4,'tower'=2,'lane'=4] {'lane'}, dimensions={0}, use_global_device_ids=true | all-gather | bytes 491520 | tf_op jit(solution)/shard_map/all_gather | solution.py:32
  74.1 2.5 %fusion.33 = bf16[64,512]{1,0:T(8,128)(2,1)S(1)} fusion(bf16[64,3072]{1,0:T(8,128)(2,1)S(1)} %all_gather.15, bf16[1,1,3072,512]{3,2,1,0:T(8,128)(2,1)} %param.11), kind=kOutput, calls=%fused_computation.25 | convolution fusion | flops 201359360 | bytes 3604480 | tf_op jit(solution)/shard_map/dot_general | solution.py:39
  76.6 0.7 reshape.39
  77.3 0.0 collective-permute-done.2
  77.3 6.8 %all_gather.14 = bf16[64,3072]{1,0:T(8,128)(2,1)S(1)} all-gather(bf16[16,3072]{1,0:T(8,128)(2,1)} %collective-permute-done.2), channel_id=1, replica_groups=mesh['section'=4,'tower'=2,'lane'=4] {'lane'}, dimensions={0}, use_global_device_ids=true | all-gather | bytes 491520 | tf_op jit(solution)/shard_map/all_gather | solution.py:33
  84.1 0.0 copy-start.2
  84.1 4.0 %fusion.22 = bf16[2,64,512]{2,1,0:T(8,128)(2,1)S(1)} fusion(bf16[1,1,2,3072,512]{4,3,2,1,0:T(8,128)(2,1)} %param.12, bf16[64,3072]{1,0:T(8,128)(2,1)S(1)} %all_gather.14), kind=kOutput, calls=%fused_computation.18 | convolution fusion | flops 402718720 | bytes 6815744 | tf_op jit(solution)/shard_map/rd,cdh->crh/dot_general | solution.py:40
  88.1 0.6 reshape_squeeze.15
  88.7 0.0 copy-done.2
  88.7 1.0 fusion.80
  89.8 1.7 %convolution_multiply_fusion = f32[4,4,16,16]{2,3,1,0:T(8,128)} fusion(bf16[4,16,4,128]{3,2,1,0:T(4,128)(2,1)} %reshape_squeeze.15, bf16[4,16,4,128]{3,2,1,0:T(4,128)(2,1)S(1)} %copy-done.2), kind=kOutput, calls=%fused_computation.22 | convolution fusion | flops 1052672 | bytes 147456 | tf_op jit(solution)/shard_map/lqhe,lkhe->lhqk/dot_general | solution.py:44
  91.4 1.2 fusion.37
  92.7 1.5 %fusion.6 = f32[64,3072]{1,0:T(8,128)} fusion(bf16[1,1,512,3072]{3,2,1,0:T(8,128)(2,1)S(1)} %copy-done, bf16[8,8,4,128]{3,2,1,0:T(4,128)(2,1)S(1)} %bitcast.77), kind=kOutput, calls=%fused_computation.6 | convolution fusion | flops 201326592 | bytes 3997696 | tf_op jit(solution)/shard_map/dot_general | solution.py:59
  94.2 0.0 reduce-scatter.5.cloned.1.call-update
  94.3 23.8 %reduce-scatter.5.cloned.1.call-done = f32[16,3072]{1,0:T(8,128)} async-done(((f32[64,3072]{1,0:T(8,128)}), f32[16,3072]{1,0:T(8,128)}) %reduce-scatter.5.cloned.1.call-update) | async-done | bytes 196624 | tf_op jit(solution)/shard_map/reduce_scatter | solution.py:58
  118.0 0.9 fusion.48
  119.0 0.7 maximum_bitcast_fusion
  (10 shorter events, 0.2 us)
Async XLA Ops:
  6.5 27.2 %copy-start = (bf16[1,1,512,3072]{3,2,1,0:T(8,128)(2,1)S(1)}, bf16[1,1,512,3072]{3,2,1,0:T(8,128)(2,1)}, u32[]{:S(2)}) copy-start(bf16[1,1,512,3072]{3,2,1,0:T(8,128)(2,1)} %param.13) | copy-start | bytes 9437188
  6.5 52.2 %reduce-scatter.3.cloned.1.call-start = ((), (), s32[]{:S(2)}) async-start(), calls=%async_computation.2 | async-start | bytes 983040 | tf_op jit(solution)/shard_map/reduce_scatter | solution.py:58
  8.7 12.1 %collective-permute-start = (bf16[16,3072]{1,0:T(8,128)(2,1)S(1)}, bf16[16,3072]{1,0:T(8,128)(2,1)S(1)}, u32[]{:S(2)}, u32[]{:S(2)}) collective-permute-start(bf16[16,3072]{1,0:T(8,128)(2,1)S(1)} %fusion.46), channel_id=1, source_target_pairs={{0,4},{4,0},{1,5},{5,1},{2,6},{6,2},{3,7},{7,3},{8,12},{12,8},{9,1... | collective-permute-start | bytes 294920 | tf_op jit(solution)/shard_map/ppermute | solution.py:15
  31.4 27.3 %copy-start.1 = (bf16[1,1,16,3072]{3,2,1,0:T(8,128)(2,1)S(1)}, bf16[1,1,16,3072]{3,2,1,0:T(8,128)(2,1)}, u32[]{:S(2)}) copy-start(bf16[1,1,16,3072]{3,2,1,0:T(8,128)(2,1)} %param.7) | copy-start | bytes 294916
  32.4 33.9 %copy-start.3 = (f32[1,1,3072]{2,1,0:T(1,128)S(1)}, f32[1,1,3072]{2,1,0:T(1,128)}, u32[]{:S(2)}) copy-start(f32[1,1,3072]{2,1,0:T(1,128)} %param.10) | copy-start | bytes 36868
  35.3 82.7 %reduce-scatter.5.cloned.1.call-start = ((), (), s32[]{:S(2)}) async-start(), calls=%async_computation.3 | async-start | bytes 983040 | tf_op jit(solution)/shard_map/reduce_scatter | solution.py:58
  59.7 5.6 %collective-permute-start.1 = (bf16[16,3072]{1,0:T(8,128)(2,1)S(1)}, bf16[16,3072]{1,0:T(8,128)(2,1)S(1)}, u32[]{:S(2)}, u32[]{:S(2)}) collective-permute-start(bf16[16,3072]{1,0:T(8,128)(2,1)S(1)} %fusion.47), channel_id=1, source_target_pairs={{0,8},{8,16},{16,24},{1,9},{9,17},{17,25},{2,10},{10,18},{18,26},{... | collective-permute-start | bytes 294920 | tf_op jit(solution)/shard_map/ppermute | solution.py:21
  66.4 10.9 %collective-permute-start.2 = (bf16[16,3072]{1,0:T(8,128)(2,1)S(1)}, bf16[16,3072]{1,0:T(8,128)(2,1)}, u32[]{:S(2)}, u32[]{:S(2)}) collective-permute-start(bf16[16,3072]{1,0:T(8,128)(2,1)S(1)} %fusion.42), channel_id=1, source_target_pairs={{0,4},{4,0},{1,5},{5,1},{2,6},{6,2},{3,7},{7,3},{8,12},{12,8},{9,1... | collective-permute-start | bytes 294920 | tf_op jit(solution)/shard_map/ppermute | solution.py:15
  84.1 4.7 %copy-start.2 = (bf16[4,16,4,128]{3,2,1,0:T(4,128)(2,1)S(1)}, bf16[4,16,4,128]{3,2,1,0:T(4,128)(2,1)}, u32[]{:S(2)}) copy-start(bf16[4,16,4,128]{3,2,1,0:T(4,128)(2,1)} %reshape.39) | copy-start | bytes 196612
Sparse Core Ops, SparseCore 0:
  35.4 23.2 reduce-scatter.2
  94.4 23.5 reduce-scatter.4
where the time goes:
time: 127 us
  waiting for transfers between devices  48.7 us (38%)
  blocking collectives  26 us (20%)
  matrix products  22.3 us (18%)
  between operations  14.2 us (11%)
  starting transfers between devices  7.98 us (6%)
  other arithmetic  5.9 us (5%)
  local copies, waits for them, and re-layouts  1.49 us (1%)
    reduce_scatter x2, waiting for transfers between devices, one_tick(): lax.psum_scatter(jnp.dot(mixed, wo_local, preferred_element_type=jnp.floa...  47.1 us
    all_gather x2, blocking collectives, one_tick(): lax.all_gather(partner, 'lane', axis=0, tiled=True)  13.4 us
    all_gather x2, blocking collectives, one_tick(): lax.all_gather(normed, 'lane', axis=0, tiled=True)  12.6 us
    dot_general x2, matrix products, one_tick(): jnp.einsum('rd,cdh->crh', partner_all, wkv_local, preferred_element_type=...  7.94 us
    dot_general x2, matrix products, one_tick(): jnp.dot(own_all, wq_local, preferred_element_type=jnp.float32)  5.08 us
    ppermute x2, starting transfers between devices, from_partner(): return lax.ppermute(value, axis, pairs)  4.53 us
    ppermute x1, starting transfers between devices, shifted(): lax.ppermute(value, axis, [(source, source + steps) for source in range(l...  3.4 us
    dot_general x2, matrix products, one_tick(): jnp.dot(mixed, wo_local, preferred_element_type=jnp.float32)  3.08 us
  transfers between devices with their start and end apart: 5, of which 3 were waited for; matrix products, arithmetic and copies ran while one was open for 5% of the time, Pallas kernels for 0%

commit v1 on v0

v1 whole, which is shorter than its diff:
```python
import functools

import jax
import jax.numpy as jnp
from jax import lax
from jax.experimental import pallas as pl
from jax.experimental.pallas import tpu as pltpu
from jax.sharding import PartitionSpec as P

HEAD_DIM = 128
EPSILON = 1e-06
BOTH = ("tower", "lane")


def swapped(value, mask):
    count = lax.axis_size(BOTH)
    return lax.ppermute(value, BOTH, [(i, i ^ mask) for i in range(count)])


def handed_on(value):
    count = lax.axis_size("section")
    even = [(s, s ^ 1) for s in range(count) if s ^ 1 < count]
    odd = [(s, t) for s in range(1, count) for t in [((s - 1) ^ 1) + 1] if t < count]
    from_even = lax.ppermute(value, "section", even)
    from_odd = lax.ppermute(value, "section", odd) if odd else from_even
    return jnp.where(lax.axis_index("section") % 2 == 1, from_even, from_odd)


def normalized(state, gain):
    wide = state.astype(jnp.float32)
    scale = lax.rsqrt(jnp.mean(wide * wide, -1, keepdims=True) + EPSILON)
    return (wide * scale * gain[None, :]).astype(jnp.bfloat16)


def layer_kernel(tok, mine_ref, theirs_ref, wq_ref, wkv_ref, wo_ref, keep_ref, send_ref):
    half = keep_ref.shape[0]
    rows = 2 * half
    own = jnp.concatenate([mine_ref[:half], theirs_ref[:half]], 0)
    partner = jnp.concatenate([mine_ref[half:], theirs_ref[half:]], 0)

    def project(left, right):
        return jnp.dot(left, right, preferred_element_type=jnp.float32).astype(jnp.bfloat16)

    query = project(own, wq_ref[...])
    keys = project(partner, wkv_ref[0])
    values = project(partner, wkv_ref[1])
    row_clip = lax.broadcasted_iota(jnp.int32, (rows, rows), 0) // tok
    col_clip = lax.broadcasted_iota(jnp.int32, (rows, rows), 1) // tok
    same_clip = row_clip == col_clip
    mixed = []
    for start in range(0, query.shape[1], HEAD_DIM):
        head = slice(start, start + HEAD_DIM)
        scores = lax.dot_general(
            query[:, head], keys[:, head], (((1,), (1,)), ((), ())), preferred_element_type=jnp.float32
        ) * (HEAD_DIM**-0.5)
        scores = jnp.where(same_clip, scores, -jnp.inf)
        weights = jnp.exp(scores - jnp.max(scores, -1, keepdims=True))
        weights = weights / jnp.sum(weights, -1, keepdims=True)
        mixed.append(project(weights.astype(jnp.bfloat16), values[:, head]))
    part = jnp.dot(jnp.concatenate(mixed, 1), wo_ref[...], preferred_element_type=jnp.float32)
    keep_ref[...] = part[:half]
    send_ref[...] = part[half:].astype(jnp.bfloat16)


def layer_part(mine, theirs, wq, wkv, wo, tok):
    half, width = mine.shape[0] // 2, mine.shape[1]
    return pl.pallas_call(
        functools.partial(layer_kernel, tok),
        out_shape=(
            jax.ShapeDtypeStruct((half, width), jnp.float32),
            jax.ShapeDtypeStruct((half, width), jnp.bfloat16),
        ),
        in_specs=[pl.BlockSpec(memory_space=pltpu.VMEM)] * 5,
        out_specs=(pl.BlockSpec(memory_space=pltpu.VMEM),) * 2,
        compiler_params=pltpu.CompilerParams(vmem_limit_bytes=32 << 20),
    )(mine, theirs, wq, wkv, wo)


def one_tick(state, gain, wq, wkv, wo):
    tok = state.shape[0]
    lanes = lax.axis_size("lane")
    normed = normalized(state, gain)
    distances = [tower * lanes + 2 * k for tower in range(2) for k in range(lanes // 2)]
    mine = jnp.concatenate([swapped(normed, d) if d else normed for d in distances], 0)
    theirs = swapped(mine, 1)
    keep, send = layer_part(mine, theirs, wq, wkv, wo, tok)
    total = keep + swapped(send, 1).astype(jnp.float32)
    result = state.astype(jnp.float32) + total[:tok]
    for k in range(1, lanes // 2):
        share = total[k * tok : (k + 1) * tok].astype(jnp.bfloat16)
        result = result + swapped(share, 2 * k).astype(jnp.float32)
    return result.astype(jnp.bfloat16)


def shards(in_flight, fresh_batches, offsets, norm_gain, w_query, w_keyval, w_out):
    gain = norm_gain[0, 0]
    weights = (w_query[0, 0], w_keyval[0, 0], w_out[0, 0])
    picked = lax.dynamic_index_in_dim(fresh_batches[:, 0], offsets[0], 0, keepdims=False)
    first = one_tick(in_flight[0, 0], gain, *weights)
    second_in = jnp.where(lax.axis_index("section") == 0, picked, handed_on(first))
    second = one_tick(second_in, gain, *weights)
    return jnp.stack([first, second])[:, None, None]


def solution(mesh):
    placed = (
        P("section", "tower", "lane", None),
        P(None, "tower", "lane", None),
        P("lane"),
        P("section", "tower", None),
        P("section", "tower", None, "lane"),
        P("section", "tower", None, None, "lane"),
        P("section", "tower", "lane", None),
    )
    return jax.shard_map(
        shards,
        mesh=mesh,
        in_specs=placed,
        out_specs=P(None, "section", "tower", "lane", None),
        check_vma=False,
    )
```

time: 127 us -> 63.1 us (0.50)
  blocking collectives: 26 us -> 0 us
  waiting for transfers between devices: 48.7 us -> 24 us
  matrix products: 22.3 us -> 0 us
  between operations: 14.2 us -> 0.77 us
  local copies, waits for them, and re-layouts: 1.49 us -> 11.3 us
  starting transfers between devices: 7.98 us -> 16.2 us
  Pallas kernels: 0 us -> 6.49 us
  other arithmetic: 5.9 us -> 4.07 us
    reduce_scatter x2 -> x0, waiting for transfers between devices: 47.1 us -> none  [one_tick(): lax.psum_scatter(jnp.dot(mixed, wo_local, preferred_element_type=jnp.floa...]
    all_gather x4 -> x0, blocking collectives: 26 us -> none  [the longest x2 13.4 us: one_tick(): lax.all_gather(partner, 'lane', axis=0, tiled=True)]
    ppermute x3 -> x14, waiting for transfers between devices: 1.54 us -> 24 us  [the longest x12 22 us: swapped(): return lax.ppermute(value, BOTH, [(i, i ^ mask) for i in range(count)])]
    dot_general x10 -> x0, matrix products: 21 us -> none  [the longest x2 7.94 us: one_tick(): jnp.einsum('rd,cdh->crh', partner_all, wkv_local, preferred_element_type=...]
    unnamed x8 -> x16, local copies, waits for them, and re-layouts: 0.02 us -> 11.2 us
    ppermute x3 -> x14, starting transfers between devices: 7.93 us -> 16.2 us  [the longest x12 11 us: swapped(): return lax.ppermute(value, BOTH, [(i, i ^ mask) for i in range(count)])]
    pallas_call x0 -> x2, Pallas kernels: none -> 6.49 us  [layer_part(): pl.pallas_call(functools.partial(layer_kernel, tok), out_shape=(jax.Shape...]
  transfers between devices with their start and end apart: 5 -> 14, of which waited for: 3 -> 12; matrix products, arithmetic and copies ran while one was open for 5% -> 0% of each run, Pallas kernels for 0% -> 0%
where the time goes in v1:
time: 63.1 us; the launch traced here: 62.7 us
  waiting for transfers between devices  24 us (38%)
  starting transfers between devices  16.2 us (26%)
  local copies, waits for them, and re-layouts  11.3 us (18%)
  Pallas kernels  6.49 us (10%)
  other arithmetic  4.07 us (6%)
  between operations  0.77 us (1%)
    ppermute x12, waiting for transfers between devices, swapped(): return lax.ppermute(value, BOTH, [(i, i ^ mask) for i in range(count)])  22 us
    unnamed x16, local copies, waits for them, and re-layouts  11.2 us
    ppermute x12, starting transfers between devices, swapped(): return lax.ppermute(value, BOTH, [(i, i ^ mask) for i in range(count)])  11 us
    pallas_call x2, Pallas kernels, layer_part(): pl.pallas_call(functools.partial(layer_kernel, tok), out_shape=(jax.Shape...  6.49 us
    ppermute x1, starting transfers between devices, handed_on(): from_even = lax.ppermute(value, 'section', even)  4.56 us
    reduce_sum x2, other arithmetic, normalized(): scale = lax.rsqrt(jnp.mean(wide * wide, -1, keepdims=True) + EPSILON)  2.08 us
    ppermute x1, waiting for transfers between devices, handed_on(): from_even = lax.ppermute(value, 'section', even)  1.93 us
  transfers between devices with their start and end apart: 14, of which 12 were waited for; matrix products, arithmetic and copies ran while one was open for 0% of the time, Pallas kernels for 0%

profile of v1, /device:TPU:0, one launch (start us, length us, event | category | flops | bytes accessed | tf_op | source)
XLA Modules:
  0.0 62.7 jit_solution(5525160248371998089)
XLA Ops:
  0.0 1.0 %fusion.5 = f32[16]{0:T(128)S(1)} fusion(bf16[1,1,16,3072]{3,2,1,0:T(8,128)(2,1)} %param.7), kind=kLoop, calls=%fused_computation.15 | loop fusion | flops 147440 | bytes 98368 | tf_op jit(solution)/shard_map/reduce_sum | solution.py:31
  1.0 1.0 %fusion.7 = bf16[16,3072]{1,0:T(8,128)(2,1)S(1)} fusion(bf16[1,1,16,3072]{3,2,1,0:T(8,128)(2,1)} %param.7, f32[3072]{0:T(1024)} %bitcast.30, f32[16]{0:T(128)S(1)} %add_rsqrt_fusion.1), kind=kLoop, calls=%fused_computation.17 | loop fusion | flops 196608 | bytes 208960 | tf_op jit(solution)/shard_map/convert_element_type | solution.py:32
  2.0 4.0 %collective-permute-start.2 = (bf16[16,3072]{1,0:T(8,128)(2,1)S(1)}, bf16[16,3072]{1,0:T(8,128)(2,1)S(1)}, u32[]{:S(2)}, u32[]{:S(2)}) collective-permute-start(bf16[16,3072]{1,0:T(8,128)(2,1)S(1)} %fusion.7), channel_id=1, source_target_pairs={{0,6},{1,7},{2,4},{3,5},{4,2},{5,3},{6,0},{7,1},{8,14},{9,15},{10,... | collective-permute-start | bytes 294920 | tf_op jit(solution)/shard_map/ppermute | solution.py:17
  6.0 0.5 collective-permute-start.1
  6.5 0.1 collective-permute-start
  6.6 2.9 %collective-permute-done.2 = bf16[16,3072]{1,0:T(8,128)(2,1)S(1)} collective-permute-done((bf16[16,3072]{1,0:T(8,128)(2,1)S(1)}, bf16[16,3072]{1,0:T(8,128)(2,1)S(1)}, u32[]{:S(2)}, u32[]{:S(2)}) %collective-permute-start.2) | collective-permute-done | bytes 98336 | tf_op jit(solution)/shard_map/ppermute | solution.py:17
  9.6 1.7 %collective-permute-done.1 = bf16[16,3072]{1,0:T(8,128)(2,1)S(1)} collective-permute-done((bf16[16,3072]{1,0:T(8,128)(2,1)S(1)}, bf16[16,3072]{1,0:T(8,128)(2,1)S(1)}, u32[]{:S(2)}, u32[]{:S(2)}) %collective-permute-start.1) | collective-permute-done | bytes 98336 | tf_op jit(solution)/shard_map/ppermute | solution.py:17
  11.2 0.0 collective-permute-done
  11.3 0.1 collective-permute-start.3
  11.3 1.7 %collective-permute-done.3.theirs_ref = bf16[64,3072]{1,0:T(8,128)(2,1)S(1)} collective-permute-done((bf16[64,3072]{1,0:T(8,128)(2,1)S(1)}, bf16[64,3072]{1,0:T(8,128)(2,1)S(1)}, u32[]{:S(2)}, u32[]{:S(2)}) %collective-permute-start.3) | collective-permute-done | bytes 393248 | tf_op jit(solution)/shard_map/ppermute | solution.py:17
  13.0 0.0 copy-start
  13.1 2.8 %copy-done = bf16[1,1,2,3072,512]{4,3,2,1,0:T(8,128)(2,1)S(1)} copy-done((bf16[1,1,2,3072,512]{4,3,2,1,0:T(8,128)(2,1)S(1)}, bf16[1,1,2,3072,512]{4,3,2,1,0:T(8,128)(2,1)}, u32[]{:S(2)}) %copy-start) | copy-done | bytes 6291480
  15.8 0.0 copy-start.2
  15.8 1.9 %copy-done.2 = bf16[1,1,3072,512]{3,2,1,0:T(8,128)(2,1)S(1)} copy-done((bf16[1,1,3072,512]{3,2,1,0:T(8,128)(2,1)S(1)}, bf16[1,1,3072,512]{3,2,1,0:T(8,128)(2,1)}, u32[]{:S(2)}) %copy-start.2) | copy-done | bytes 3145752
  17.7 0.0 copy-start.4
  17.7 1.9 %copy-done.4 = bf16[1,1,512,3072]{3,2,1,0:T(8,128)(2,1)S(1)} copy-done((bf16[1,1,512,3072]{3,2,1,0:T(8,128)(2,1)S(1)}, bf16[1,1,512,3072]{3,2,1,0:T(8,128)(2,1)}, u32[]{:S(2)}) %copy-start.4) | copy-done | bytes 3145752
  19.6 0.0 copy-start.6
  19.6 0.0 copy-start.7
  19.6 0.0 copy-start.3
  19.6 3.2 %shard_map.73 = (f32[32,3072]{1,0:T(8,128)S(1)}, bf16[32,3072]{1,0:T(8,128)(2,1)S(1)}) custom-call(bf16[64,3072]{1,0:T(8,128)(2,1)S(1)} %pad_maximum_fusion.mine_ref, bf16[64,3072]{1,0:T(8,128)(2,1)S(1)} %collective-permute-done.3.theirs_ref, bf16[3072,512]{1,0:T(8,128)(2,1)S(1)} %bitcast.25, bf16[2,3072,512]{2,1,0:T(8,128)(2,1)S(1)} %bitcast.23, ...), custom_call_target="tpu_custom_call" | custom-call | tf_op jit(solution)/shard_map/pallas_call | solution.py:67
  22.9 0.2 collective-permute-start.4
  23.1 1.3 %collective-permute-done.4 = bf16[32,3072]{1,0:T(8,128)(2,1)S(1)} collective-permute-done((bf16[32,3072]{1,0:T(8,128)(2,1)S(1)}, bf16[32,3072]{1,0:T(8,128)(2,1)S(1)}, u32[]{:S(2)}, u32[]{:S(2)}) %collective-permute-start.4) | collective-permute-done | bytes 196640 | tf_op jit(solution)/shard_map/ppermute | solution.py:17
  24.4 1.4 %collective-permute-start.5 = (bf16[16,3072]{1,0:T(8,128)(2,1)S(1)}, bf16[16,3072]{1,0:T(8,128)(2,1)S(1)}, u32[]{:S(2)}, u32[]{:S(2)}) collective-permute-start(bf16[16,3072]{1,0:T(8,128)(2,1)S(1)} %slice.29), channel_id=1, source_target_pairs={{0,2},{1,3},{2,0},{3,1},{4,6},{5,7},{6,4},{7,5},{8,10},{9,11},{10,... | collective-permute-start | bytes 294920 | tf_op jit(solution)/shard_map/ppermute | solution.py:17
  25.9 3.5 %collective-permute-done.5 = bf16[16,3072]{1,0:T(8,128)(2,1)S(1)} collective-permute-done((bf16[16,3072]{1,0:T(8,128)(2,1)S(1)}, bf16[16,3072]{1,0:T(8,128)(2,1)S(1)}, u32[]{:S(2)}, u32[]{:S(2)}) %collective-permute-start.5) | collective-permute-done | bytes 98336 | tf_op jit(solution)/shard_map/ppermute | solution.py:17
  29.3 0.0 copy-done.6
  29.4 0.7 %collective-permute-start.7 = (bf16[16,3072]{1,0:T(8,128)(2,1)S(1)}, bf16[16,3072]{1,0:T(8,128)(2,1)S(1)}, u32[]{:S(2)}, u32[]{:S(2)}) collective-permute-start(bf16[16,3072]{1,0:T(8,128)(2,1)S(1)} %fusion.9), channel_id=1, source_target_pairs={{8,16},{16,8},{9,17},{17,9},{10,18},{18,10},{11,19},{19,11},{12,20... | collective-permute-start | bytes 294920 | tf_op jit(solution)/shard_map/ppermute | solution.py:25
  30.1 4.6 %collective-permute-start.6 = (bf16[16,3072]{1,0:T(8,128)(2,1)S(1)}, bf16[16,3072]{1,0:T(8,128)(2,1)S(1)}, u32[]{:S(2)}, u32[]{:S(2)}) collective-permute-start(bf16[16,3072]{1,0:T(8,128)(2,1)S(1)} %fusion.9), channel_id=1, source_target_pairs={{0,8},{8,0},{16,24},{24,16},{1,9},{9,1},{17,25},{25,17},{2,10},{10... | collective-permute-start | bytes 294920 | tf_op jit(solution)/shard_map/ppermute | solution.py:24
  35.3 0.0 collective-permute-done.7
  35.3 1.9 %collective-permute-done.6 = bf16[16,3072]{1,0:T(8,128)(2,1)S(1)} collective-permute-done((bf16[16,3072]{1,0:T(8,128)(2,1)S(1)}, bf16[16,3072]{1,0:T(8,128)(2,1)S(1)}, u32[]{:S(2)}, u32[]{:S(2)}) %collective-permute-start.6) | collective-permute-done | bytes 98336 | tf_op jit(solution)/shard_map/ppermute | solution.py:24
  37.2 1.1 %fusion = (f32[16]{0:T(128)S(1)}, bf16[16,3072]{1,0:T(8,128)(2,1)S(1)}) fusion(bf16[16,3072]{1,0:T(8,128)(2,1)S(1)} %collective-permute-done.6, bf16[16,3072]{1,0:T(8,128)(2,1)S(1)} %collective-permute-done.7, pred[]{:T(512)S(6)} %eq.9, bf16[4,1,16,3072]{3,2,1,0:T(8,128)(2,1)} %param.8, s32[]{:T(128)S(6)} %select_n.26, pred[]{:T(512)S(6)} %eq.8), kind=kLoop, calls=%fused_computation.10 | loop fusion | flops 245744 | bytes 393286 | tf_op jit(solution)/shard_map/reduce_sum | solution.py:31
  38.3 0.0 copy-done.7
  38.3 0.1 fusion.2
  38.4 2.3 %collective-permute-start.10 = (bf16[16,3072]{1,0:T(8,128)(2,1)S(1)}, bf16[16,3072]{1,0:T(8,128)(2,1)S(1)}, u32[]{:S(2)}, u32[]{:S(2)}) collective-permute-start(bf16[16,3072]{1,0:T(8,128)(2,1)S(1)} %fusion.2), channel_id=1, source_target_pairs={{0,6},{1,7},{2,4},{3,5},{4,2},{5,3},{6,0},{7,1},{8,14},{9,15},{10,... | collective-permute-start | bytes 294920 | tf_op jit(solution)/shard_map/ppermute | solution.py:17
  40.7 0.5 collective-permute-start.9
  41.2 0.7 %collective-permute-start.8 = (bf16[16,3072]{1,0:T(8,128)(2,1)S(1)}, bf16[16,3072]{1,0:T(8,128)(2,1)S(1)}, u32[]{:S(2)}, u32[]{:S(2)}) collective-permute-start(bf16[16,3072]{1,0:T(8,128)(2,1)S(1)} %fusion.2), channel_id=1, source_target_pairs={{0,2},{1,3},{2,0},{3,1},{4,6},{5,7},{6,4},{7,5},{8,10},{9,11},{10,... | collective-permute-start | bytes 294920 | tf_op jit(solution)/shard_map/ppermute | solution.py:17
  41.9 2.0 %collective-permute-done.10 = bf16[16,3072]{1,0:T(8,128)(2,1)S(1)} collective-permute-done((bf16[16,3072]{1,0:T(8,128)(2,1)S(1)}, bf16[16,3072]{1,0:T(8,128)(2,1)S(1)}, u32[]{:S(2)}, u32[]{:S(2)}) %collective-permute-start.10) | collective-permute-done | bytes 98336 | tf_op jit(solution)/shard_map/ppermute | solution.py:17
  44.0 1.3 %collective-permute-done.9 = bf16[16,3072]{1,0:T(8,128)(2,1)S(1)} collective-permute-done((bf16[16,3072]{1,0:T(8,128)(2,1)S(1)}, bf16[16,3072]{1,0:T(8,128)(2,1)S(1)}, u32[]{:S(2)}, u32[]{:S(2)}) %collective-permute-start.9) | collective-permute-done | bytes 98336 | tf_op jit(solution)/shard_map/ppermute | solution.py:17
  45.3 0.5 collective-permute-done.8
  45.8 0.1 collective-permute-start.11
  45.9 1.7 %collective-permute-done.11.theirs_ref = bf16[64,3072]{1,0:T(8,128)(2,1)S(1)} collective-permute-done((bf16[64,3072]{1,0:T(8,128)(2,1)S(1)}, bf16[64,3072]{1,0:T(8,128)(2,1)S(1)}, u32[]{:S(2)}, u32[]{:S(2)}) %collective-permute-start.11) | collective-permute-done | bytes 393248 | tf_op jit(solution)/shard_map/ppermute | solution.py:17
  47.6 0.0 copy-done.3
  47.6 0.0 copy-start.1
  47.6 2.8 %copy-done.1 = bf16[1,1,2,3072,512]{4,3,2,1,0:T(8,128)(2,1)S(1)} copy-done((bf16[1,1,2,3072,512]{4,3,2,1,0:T(8,128)(2,1)S(1)}, bf16[1,1,2,3072,512]{4,3,2,1,0:T(8,128)(2,1)}, u32[]{:S(2)}) %copy-start.1) | copy-done | bytes 6291480
  50.4 0.0 copy-start.5
  50.4 1.9 %copy-done.5 = bf16[1,1,512,3072]{3,2,1,0:T(8,128)(2,1)S(1)} copy-done((bf16[1,1,512,3072]{3,2,1,0:T(8,128)(2,1)S(1)}, bf16[1,1,512,3072]{3,2,1,0:T(8,128)(2,1)}, u32[]{:S(2)}) %copy-start.5) | copy-done | bytes 3145752
  52.3 3.2 %shard_map.74 = (f32[32,3072]{1,0:T(8,128)S(1)}, bf16[32,3072]{1,0:T(8,128)(2,1)S(1)}) custom-call(bf16[64,3072]{1,0:T(8,128)(2,1)S(1)} %pad_maximum_fusion.1.mine_ref, bf16[64,3072]{1,0:T(8,128)(2,1)S(1)} %collective-permute-done.11.theirs_ref, bf16[3072,512]{1,0:T(8,128)(2,1)S(1)} %bitcast.26, bf16[2,3072,512]{2,1,0:T(8,128)(2,1)S(1)} %bitcast.24, ...), custom_call_target="tpu_custom_call" | custom-call | tf_op jit(solution)/shard_map/pallas_call | solution.py:67
  55.5 0.2 collective-permute-start.12
  55.7 1.3 %collective-permute-done.12 = bf16[32,3072]{1,0:T(8,128)(2,1)S(1)} collective-permute-done((bf16[32,3072]{1,0:T(8,128)(2,1)S(1)}, bf16[32,3072]{1,0:T(8,128)(2,1)S(1)}, u32[]{:S(2)}, u32[]{:S(2)}) %collective-permute-start.12) | collective-permute-done | bytes 196640 | tf_op jit(solution)/shard_map/ppermute | solution.py:17
  57.1 0.8 %collective-permute-start.13 = (bf16[16,3072]{1,0:T(8,128)(2,1)S(1)}, bf16[16,3072]{1,0:T(8,128)(2,1)S(1)}, u32[]{:S(2)}, u32[]{:S(2)}) collective-permute-start(bf16[16,3072]{1,0:T(8,128)(2,1)S(1)} %slice.28), channel_id=1, source_target_pairs={{0,2},{1,3},{2,0},{3,1},{4,6},{5,7},{6,4},{7,5},{8,10},{9,11},{10,... | collective-permute-start | bytes 294920 | tf_op jit(solution)/shard_map/ppermute | solution.py:17
  57.9 4.1 %collective-permute-done.13 = bf16[16,3072]{1,0:T(8,128)(2,1)S(1)} collective-permute-done((bf16[16,3072]{1,0:T(8,128)(2,1)S(1)}, bf16[16,3072]{1,0:T(8,128)(2,1)S(1)}, u32[]{:S(2)}, u32[]{:S(2)}) %collective-permute-start.13) | collective-permute-done | bytes 98336 | tf_op jit(solution)/shard_map/ppermute | solution.py:17
  62.1 0.7 %maximum_bitcast_fusion = bf16[2,1,1,16,3072]{4,3,2,1,0:T(8,128)(2,1)} fusion(bf16[1,16,3072]{2,1,0:T(8,128)(2,1)S(1)} %fusion.10, bf16[1,16,3072]{2,1,0:T(8,128)(2,1)S(1)} %bitcast.29), kind=kLoop, calls=%fused_computation.22 | loop fusion | flops 98304 | bytes 393216 | tf_op jit(solution)/shard_map/broadcast_in_dim | solution.py:102
  (10 shorter events, 0.2 us)
Async XLA Ops:
  2.0 7.5 %collective-permute-start.2 = (bf16[16,3072]{1,0:T(8,128)(2,1)S(1)}, bf16[16,3072]{1,0:T(8,128)(2,1)S(1)}, u32[]{:S(2)}, u32[]{:S(2)}) collective-permute-start(bf16[16,3072]{1,0:T(8,128)(2,1)S(1)} %fusion.7), channel_id=1, source_target_pairs={{0,6},{1,7},{2,4},{3,5},{4,2},{5,3},{6,0},{7,1},{8,14},{9,15},{10,... | collective-permute-start | bytes 294920 | tf_op jit(solution)/shard_map/ppermute | solution.py:17
  6.0 5.2 %collective-permute-start.1 = (bf16[16,3072]{1,0:T(8,128)(2,1)S(1)}, bf16[16,3072]{1,0:T(8,128)(2,1)S(1)}, u32[]{:S(2)}, u32[]{:S(2)}) collective-permute-start(bf16[16,3072]{1,0:T(8,128)(2,1)S(1)} %fusion.7), channel_id=1, source_target_pairs={{0,4},{1,5},{2,6},{3,7},{4,0},{5,1},{6,2},{7,3},{8,12},{9,13},{10,... | collective-permute-start | bytes 294920 | tf_op jit(solution)/shard_map/ppermute | solution.py:17
  6.5 4.7 %collective-permute-start = (bf16[16,3072]{1,0:T(8,128)(2,1)S(1)}, bf16[16,3072]{1,0:T(8,128)(2,1)S(1)}, u32[]{:S(2)}, u32[]{:S(2)}) collective-permute-start(bf16[16,3072]{1,0:T(8,128)(2,1)S(1)} %fusion.7), channel_id=1, source_target_pairs={{0,2},{1,3},{2,0},{3,1},{4,6},{5,7},{6,4},{7,5},{8,10},{9,11},{10,... | collective-permute-start | bytes 294920 | tf_op jit(solution)/shard_map/ppermute | solution.py:17
  11.3 1.8 %collective-permute-start.3 = (bf16[64,3072]{1,0:T(8,128)(2,1)S(1)}, bf16[64,3072]{1,0:T(8,128)(2,1)S(1)}, u32[]{:S(2)}, u32[]{:S(2)}) collective-permute-start(bf16[64,3072]{1,0:T(8,128)(2,1)S(1)} %pad_maximum_fusion.mine_ref), channel_id=1, source_target_pairs={{0,1},{1,0},{2,3},{3,2},{4,5},{5,4},{6,7},{7,6},{8,9},{9,8},{10,11... | collective-permute-start | bytes 1179656 | tf_op jit(solution)/shard_map/ppermute | solution.py:17
  13.0 2.8 %copy-start = (bf16[1,1,2,3072,512]{4,3,2,1,0:T(8,128)(2,1)S(1)}, bf16[1,1,2,3072,512]{4,3,2,1,0:T(8,128)(2,1)}, u32[]{:S(2)}) copy-start(bf16[1,1,2,3072,512]{4,3,2,1,0:T(8,128)(2,1)} %param.12) | copy-start | bytes 18874372
  15.8 1.9 %copy-start.2 = (bf16[1,1,3072,512]{3,2,1,0:T(8,128)(2,1)S(1)}, bf16[1,1,3072,512]{3,2,1,0:T(8,128)(2,1)}, u32[]{:S(2)}) copy-start(bf16[1,1,3072,512]{3,2,1,0:T(8,128)(2,1)} %param.11) | copy-start | bytes 9437188
  17.7 1.9 %copy-start.4 = (bf16[1,1,512,3072]{3,2,1,0:T(8,128)(2,1)S(1)}, bf16[1,1,512,3072]{3,2,1,0:T(8,128)(2,1)}, u32[]{:S(2)}) copy-start(bf16[1,1,512,3072]{3,2,1,0:T(8,128)(2,1)} %param.13) | copy-start | bytes 9437188
  19.6 9.7 %copy-start.6 = (bf16[1,1,16,3072]{3,2,1,0:T(8,128)(2,1)S(1)}, bf16[1,1,16,3072]{3,2,1,0:T(8,128)(2,1)}, u32[]{:S(2)}) copy-start(bf16[1,1,16,3072]{3,2,1,0:T(8,128)(2,1)} %param.7) | copy-start | bytes 294916
  19.6 18.7 %copy-start.7 = (f32[1,1,3072]{2,1,0:T(1,128)S(1)}, f32[1,1,3072]{2,1,0:T(1,128)}, u32[]{:S(2)}) copy-start(f32[1,1,3072]{2,1,0:T(1,128)} %param.10) | copy-start | bytes 36868
  19.6 28.0 %copy-start.3 = (bf16[1,1,3072,512]{3,2,1,0:T(8,128)(2,1)S(1)}, bf16[1,1,3072,512]{3,2,1,0:T(8,128)(2,1)}, u32[]{:S(2)}) copy-start(bf16[1,1,3072,512]{3,2,1,0:T(8,128)(2,1)} %param.11) | copy-start | bytes 9437188
  22.9 1.5 %collective-permute-start.4 = (bf16[32,3072]{1,0:T(8,128)(2,1)S(1)}, bf16[32,3072]{1,0:T(8,128)(2,1)S(1)}, u32[]{:S(2)}, u32[]{:S(2)}) collective-permute-start(bf16[32,3072]{1,0:T(8,128)(2,1)S(1)} %get-tuple-element.10), channel_id=1, source_target_pairs={{0,1},{1,0},{2,3},{3,2},{4,5},{5,4},{6,7},{7,6},{8,9},{9,8},{10,11... | collective-permute-start | bytes 589832 | tf_op jit(solution)/shard_map/ppermute | solution.py:17
  24.4 4.9 %collective-permute-start.5 = (bf16[16,3072]{1,0:T(8,128)(2,1)S(1)}, bf16[16,3072]{1,0:T(8,128)(2,1)S(1)}, u32[]{:S(2)}, u32[]{:S(2)}) collective-permute-start(bf16[16,3072]{1,0:T(8,128)(2,1)S(1)} %slice.29), channel_id=1, source_target_pairs={{0,2},{1,3},{2,0},{3,1},{4,6},{5,7},{6,4},{7,5},{8,10},{9,11},{10,... | collective-permute-start | bytes 294920 | tf_op jit(solution)/shard_map/ppermute | solution.py:17
  29.4 5.9 %collective-permute-start.7 = (bf16[16,3072]{1,0:T(8,128)(2,1)S(1)}, bf16[16,3072]{1,0:T(8,128)(2,1)S(1)}, u32[]{:S(2)}, u32[]{:S(2)}) collective-permute-start(bf16[16,3072]{1,0:T(8,128)(2,1)S(1)} %fusion.9), channel_id=1, source_target_pairs={{8,16},{16,8},{9,17},{17,9},{10,18},{18,10},{11,19},{19,11},{12,20... | collective-permute-start | bytes 294920 | tf_op jit(solution)/shard_map/ppermute | solution.py:25
  30.1 7.2 %collective-permute-start.6 = (bf16[16,3072]{1,0:T(8,128)(2,1)S(1)}, bf16[16,3072]{1,0:T(8,128)(2,1)S(1)}, u32[]{:S(2)}, u32[]{:S(2)}) collective-permute-start(bf16[16,3072]{1,0:T(8,128)(2,1)S(1)} %fusion.9), channel_id=1, source_target_pairs={{0,8},{8,0},{16,24},{24,16},{1,9},{9,1},{17,25},{25,17},{2,10},{10... | collective-permute-start | bytes 294920 | tf_op jit(solution)/shard_map/ppermute | solution.py:24
  38.4 5.6 %collective-permute-start.10 = (bf16[16,3072]{1,0:T(8,128)(2,1)S(1)}, bf16[16,3072]{1,0:T(8,128)(2,1)S(1)}, u32[]{:S(2)}, u32[]{:S(2)}) collective-permute-start(bf16[16,3072]{1,0:T(8,128)(2,1)S(1)} %fusion.2), channel_id=1, source_target_pairs={{0,6},{1,7},{2,4},{3,5},{4,2},{5,3},{6,0},{7,1},{8,14},{9,15},{10,... | collective-permute-start | bytes 294920 | tf_op jit(solution)/shard_map/ppermute | solution.py:17
  40.7 4.6 %collective-permute-start.9 = (bf16[16,3072]{1,0:T(8,128)(2,1)S(1)}, bf16[16,3072]{1,0:T(8,128)(2,1)S(1)}, u32[]{:S(2)}, u32[]{:S(2)}) collective-permute-start(bf16[16,3072]{1,0:T(8,128)(2,1)S(1)} %fusion.2), channel_id=1, source_target_pairs={{0,4},{1,5},{2,6},{3,7},{4,0},{5,1},{6,2},{7,3},{8,12},{9,13},{10,... | collective-permute-start | bytes 294920 | tf_op jit(solution)/shard_map/ppermute | solution.py:17
  41.2 4.6 %collective-permute-start.8 = (bf16[16,3072]{1,0:T(8,128)(2,1)S(1)}, bf16[16,3072]{1,0:T(8,128)(2,1)S(1)}, u32[]{:S(2)}, u32[]{:S(2)}) collective-permute-start(bf16[16,3072]{1,0:T(8,128)(2,1)S(1)} %fusion.2), channel_id=1, source_target_pairs={{0,2},{1,3},{2,0},{3,1},{4,6},{5,7},{6,4},{7,5},{8,10},{9,11},{10,... | collective-permute-start | bytes 294920 | tf_op jit(solution)/shard_map/ppermute | solution.py:17
  45.8 1.8 %collective-permute-start.11 = (bf16[64,3072]{1,0:T(8,128)(2,1)S(1)}, bf16[64,3072]{1,0:T(8,128)(2,1)S(1)}, u32[]{:S(2)}, u32[]{:S(2)}) collective-permute-start(bf16[64,3072]{1,0:T(8,128)(2,1)S(1)} %pad_maximum_fusion.1.mine_ref), channel_id=1, source_target_pairs={{0,1},{1,0},{2,3},{3,2},{4,5},{5,4},{6,7},{7,6},{8,9},{9,8},{10,11... | collective-permute-start | bytes 1179656 | tf_op jit(solution)/shard_map/ppermute | solution.py:17
  47.6 2.8 %copy-start.1 = (bf16[1,1,2,3072,512]{4,3,2,1,0:T(8,128)(2,1)S(1)}, bf16[1,1,2,3072,512]{4,3,2,1,0:T(8,128)(2,1)}, u32[]{:S(2)}) copy-start(bf16[1,1,2,3072,512]{4,3,2,1,0:T(8,128)(2,1)} %param.12) | copy-start | bytes 18874372
  50.4 1.9 %copy-start.5 = (bf16[1,1,512,3072]{3,2,1,0:T(8,128)(2,1)S(1)}, bf16[1,1,512,3072]{3,2,1,0:T(8,128)(2,1)}, u32[]{:S(2)}) copy-start(bf16[1,1,512,3072]{3,2,1,0:T(8,128)(2,1)} %param.13) | copy-start | bytes 9437188
  55.5 1.5 %collective-permute-start.12 = (bf16[32,3072]{1,0:T(8,128)(2,1)S(1)}, bf16[32,3072]{1,0:T(8,128)(2,1)S(1)}, u32[]{:S(2)}, u32[]{:S(2)}) collective-permute-start(bf16[32,3072]{1,0:T(8,128)(2,1)S(1)} %get-tuple-element.12), channel_id=1, source_target_pairs={{0,1},{1,0},{2,3},{3,2},{4,5},{5,4},{6,7},{7,6},{8,9},{9,8},{10,11... | collective-permute-start | bytes 589832 | tf_op jit(solution)/shard_map/ppermute | solution.py:17
  57.1 4.9 %collective-permute-start.13 = (bf16[16,3072]{1,0:T(8,128)(2,1)S(1)}, bf16[16,3072]{1,0:T(8,128)(2,1)S(1)}, u32[]{:S(2)}, u32[]{:S(2)}) collective-permute-start(bf16[16,3072]{1,0:T(8,128)(2,1)S(1)} %slice.28), channel_id=1, source_target_pairs={{0,2},{1,3},{2,0},{3,1},{4,6},{5,7},{6,4},{7,5},{8,10},{9,11},{10,... | collective-permute-start | bytes 294920 | tf_op jit(solution)/shard_map/ppermute | solution.py:17

commit v2 on v1

--- a/solution.py
+++ b/solution.py
@@ -1,4 +1,5 @@
 import functools
+import math
 
 import jax
 import jax.numpy as jnp
@@ -29,7 +30,7 @@
 def normalized(state, gain):
     wide = state.astype(jnp.float32)
     scale = lax.rsqrt(jnp.mean(wide * wide, -1, keepdims=True) + EPSILON)
-    return (wide * scale * gain[None, :]).astype(jnp.bfloat16)
+    return (wide * scale * gain).astype(jnp.bfloat16)
 
 
 def layer_kernel(tok, mine_ref, theirs_ref, wq_ref, wkv_ref, wo_ref, keep_ref, send_ref):
@@ -72,18 +73,66 @@
         ),
         in_specs=[pl.BlockSpec(memory_space=pltpu.VMEM)] * 5,
         out_specs=(pl.BlockSpec(memory_space=pltpu.VMEM),) * 2,
-        compiler_params=pltpu.CompilerParams(vmem_limit_bytes=32 << 20),
+        compiler_params=pltpu.CompilerParams(vmem_limit_bytes=16 << 20),
     )(mine, theirs, wq, wkv, wo)
 
 
-def one_tick(state, gain, wq, wkv, wo):
+def entry_kernel(x_ref, gain_ref, normed_ref, x_out, gain_out):
+    normed_ref[...] = normalized(x_ref[...], gain_ref[0])
+    x_out[...] = x_ref[...]
+    gain_out[...] = gain_ref[...]
+
+
+def entry(state, gain):
+    return pl.pallas_call(
+        entry_kernel,
+        out_shape=(
+            pltpu.VMEM(state.shape, jnp.bfloat16),
+            pltpu.VMEM(state.shape, state.dtype),
+            pltpu.VMEM(gain.shape, gain.dtype),
+        ),
+        in_specs=[pl.BlockSpec(memory_space=pltpu.VMEM)] * 2,
+        out_specs=(pl.BlockSpec(memory_space=pltpu.VMEM),) * 3,
+        compiler_params=pltpu.CompilerParams(vmem_limit_bytes=16 << 20),
+    )(state, gain)
+
+
+def load_kernel(offset_ref, fresh_ref, wq_ref, wkv_ref, wo_ref, *outs_and_sem):
+    *outs, sems = outs_and_sem
+    copies = [(fresh_ref.at[offset_ref[0]], outs[0])]
+    for source, target in ((wq_ref, outs[1]), (wkv_ref.at[0], outs[2].at[0]), (wkv_ref.at[1], outs[2].at[1]), (wo_ref, outs[3])):
+        rows = source.shape[0] // 2
+        copies += [(source.at[pl.ds(i * rows, rows)], target.at[pl.ds(i * rows, rows)]) for i in range(2)]
+    started = [pltpu.make_async_copy(a, b, sems.at[i]) for i, (a, b) in enumerate(copies)]
+    for copy in started:
+        copy.start()
+    for copy in started:
+        copy.wait()
+
+
+def load(offsets, fresh, wq, wkv, wo):
+    moved = (fresh.shape[1:], wq.shape, wkv.shape, wo.shape)
+    size = 2 * sum(math.prod(shape) for shape in moved)
+    return pl.pallas_call(
+        load_kernel,
+        out_shape=tuple(pltpu.VMEM(shape, jnp.bfloat16) for shape in moved),
+        in_specs=[pl.BlockSpec(memory_space=pltpu.SMEM)] + [pl.BlockSpec(memory_space=pltpu.HBM)] * 4,
+        out_specs=(pl.BlockSpec(memory_space=pltpu.VMEM),) * 4,
+        scratch_shapes=[pltpu.SemaphoreType.DMA((9,))],
+        cost_estimate=pl.CostEstimate(flops=0, bytes_accessed=size, transcendentals=0),
+        compiler_params=pltpu.CompilerParams(vmem_limit_bytes=16 << 20),
+    )(offsets, *(pltpu.with_memory_space_constraint(a, pltpu.HBM) for a in (fresh, wq, wkv, wo)))
+
+
+def one_tick(state, normed, weights):
     tok = state.shape[0]
     lanes = lax.axis_size("lane")
-    normed = normalized(state, gain)
     distances = [tower * lanes + 2 * k for tower in range(2) for k in range(lanes // 2)]
-    mine = jnp.concatenate([swapped(normed, d) if d else normed for d in distances], 0)
+    blocks = {d: swapped(normed, d) if d else normed for d in reversed(distances)}
+    mine = jnp.concatenate([blocks[d] for d in distances], 0)
+    mine, weights = lax.optimization_barrier((mine, weights))
     theirs = swapped(mine, 1)
-    keep, send = layer_part(mine, theirs, wq, wkv, wo, tok)
+    keep, send = layer_part(mine, theirs, *weights, tok)
     total = keep + swapped(send, 1).astype(jnp.float32)
     result = state.astype(jnp.float32) + total[:tok]
     for k in range(1, lanes // 2):
@@ -93,12 +142,11 @@
 
 
 def shards(in_flight, fresh_batches, offsets, norm_gain, w_query, w_keyval, w_out):
-    gain = norm_gain[0, 0]
-    weights = (w_query[0, 0], w_keyval[0, 0], w_out[0, 0])
-    picked = lax.dynamic_index_in_dim(fresh_batches[:, 0], offsets[0], 0, keepdims=False)
-    first = one_tick(in_flight[0, 0], gain, *weights)
+    normed, state, gain = entry(in_flight[0, 0], norm_gain[0])
+    picked, *weights = load(offsets, fresh_batches[:, 0], w_query[0, 0], w_keyval[0, 0], w_out[0, 0])
+    first = one_tick(state, normed, weights)
     second_in = jnp.where(lax.axis_index("section") == 0, picked, handed_on(first))
-    second = one_tick(second_in, gain, *weights)
+    second = one_tick(second_in, normalized(second_in, gain[0]), weights)
     return jnp.stack([first, second])[:, None, None]
 
 

time: 63.1 us -> 55.7 us (0.88)
  the two profiles are of different devices: /device:TPU:0 before, /device:TPU:16 now
where the time goes in v2:
time: 55.7 us; the launch traced here: 55.4 us
  waiting for transfers between devices  22.4 us (40%)
  starting transfers between devices  13.4 us (24%)
  Pallas kernels  11.4 us (20%)
  local copies, waits for them, and re-layouts  6.31 us (11%)
  other arithmetic  1.19 us (2%)
  between operations  0.82 us (1%)
    ppermute x12, waiting for transfers between devices, swapped(): return lax.ppermute(value, BOTH, [(i, i ^ mask) for i in range(count)])  17.8 us
    ppermute x12, starting transfers between devices, swapped(): return lax.ppermute(value, BOTH, [(i, i ^ mask) for i in range(count)])  9.81 us
    pallas_call x2, Pallas kernels, layer_part(): pl.pallas_call(functools.partial(layer_kernel, tok), out_shape=(jax.Shape...  6.49 us
    unnamed x12, local copies, waits for them, and re-layouts  6.28 us
    pallas_call x1, Pallas kernels, load(): pl.pallas_call(load_kernel, out_shape=tuple((pltpu.VMEM(shape, jnp.bfloat...  4.76 us
    ppermute x1, waiting for transfers between devices, handed_on(): from_odd = lax.ppermute(value, 'section', odd) if odd else from_even  3.46 us
    ppermute x1, starting transfers between devices, handed_on(): from_odd = lax.ppermute(value, 'section', odd) if odd else from_even  1.91 us
    ppermute x1, starting transfers between devices, handed_on(): from_even = lax.ppermute(value, 'section', even)  1.64 us
  transfers between devices with their start and end apart: 14, of which 11 were waited for; matrix products, arithmetic and copies ran while one was open for 0% of the time, Pallas kernels for 9%

profile of v2, /device:TPU:16, one launch (start us, length us, event | category | flops | bytes accessed | tf_op | source)
XLA Modules:
  0.0 55.4 jit_solution(4228241091881523927)
XLA Ops:
  0.0 0.0 copy-start.4
  0.0 0.9 %copy-done.4 = bf16[1,1,16,3072]{3,2,1,0:T(8,128)(2,1)S(1)} copy-done((bf16[1,1,16,3072]{3,2,1,0:T(8,128)(2,1)S(1)}, bf16[1,1,16,3072]{3,2,1,0:T(8,128)(2,1)}, u32[]{:S(2)}) %copy-start.4) | copy-done | bytes 98328
  0.9 0.0 copy-start.5
  0.9 0.7 %copy-done.5 = f32[1,1,3072]{2,1,0:T(1,128)S(1)} copy-done((f32[1,1,3072]{2,1,0:T(1,128)S(1)}, f32[1,1,3072]{2,1,0:T(1,128)}, u32[]{:S(2)}) %copy-start.5) | copy-done | bytes 12312
  1.6 0.1 shard_map.73
  1.7 2.5 %collective-permute-start.2 = (bf16[16,3072]{1,0:T(8,128)(2,1)S(1)}, bf16[16,3072]{1,0:T(8,128)(2,1)S(1)}, u32[]{:S(2)}, u32[]{:S(2)}) collective-permute-start(bf16[16,3072]{1,0:T(8,128)(2,1)S(1)} %get-tuple-element.25), channel_id=1, source_target_pairs={{0,6},{1,7},{2,4},{3,5},{4,2},{5,3},{6,0},{7,1},{8,14},{9,15},{10,... | collective-permute-start | bytes 294920 | tf_op jit(solution)/shard_map/ppermute | solution.py:18
  4.3 0.5 collective-permute-start.1
  4.8 0.5 collective-permute-start
  5.9 4.8 %shard_map.74 = (bf16[16,3072]{1,0:T(8,128)(2,1)S(1)}, bf16[3072,512]{1,0:T(8,128)(2,1)S(1)}, bf16[2,3072,512]{2,1,0:T(8,128)(2,1)S(1)}, bf16[512,3072]{1,0:T(8,128)(2,1)S(1)}) custom-call(s32[1]{0:T(128)S(6)} %copy.9.offset_ref, bf16[4,16,3072]{2,1,0:T(8,128)(2,1)} %bitcast.20, bf16[3072,512]{1,0:T(8,128)(2,1)} %bitcast.18, bf16[2,3072,512]{2,1,0:T(8,128)(2,1)} %bitcast.17, ...), custom_call_target="tpu_custom_call" | custom-call | bytes 12681216 | tf_op jit(solution)/shard_map/pallas_call | solution.py:116
  10.7 0.0 copy-start
  10.7 0.0 copy-start.2
  10.7 0.0 collective-permute-done.2
  10.7 0.0 collective-permute-done.1
  10.8 0.0 collective-permute-done
  10.8 0.1 collective-permute-start.3
  10.9 1.7 %collective-permute-done.3.theirs_ref = bf16[64,3072]{1,0:T(8,128)(2,1)S(1)} collective-permute-done((bf16[64,3072]{1,0:T(8,128)(2,1)S(1)}, bf16[64,3072]{1,0:T(8,128)(2,1)S(1)}, u32[]{:S(2)}, u32[]{:S(2)}) %collective-permute-start.3) | collective-permute-done | bytes 393248 | tf_op jit(solution)/shard_map/ppermute | solution.py:18
  12.6 3.2 %shard_map.75 = (f32[32,3072]{1,0:T(8,128)S(1)}, bf16[32,3072]{1,0:T(8,128)(2,1)S(1)}) custom-call(bf16[64,3072]{1,0:T(8,128)(2,1)S(1)} %pad_maximum_fusion.mine_ref, bf16[64,3072]{1,0:T(8,128)(2,1)S(1)} %collective-permute-done.3.theirs_ref, bf16[3072,512]{1,0:T(8,128)(2,1)S(1)} %get-tuple-element.38.wq_ref, ...), custom_call_target="tpu_custom_call" | custom-call | tf_op jit(solution)/shard_map/pallas_call | solution.py:68
  15.8 0.0 copy-done
  15.8 0.0 copy-done.2
  15.9 0.2 collective-permute-start.4
  16.1 1.3 %collective-permute-done.4 = bf16[32,3072]{1,0:T(8,128)(2,1)S(1)} collective-permute-done((bf16[32,3072]{1,0:T(8,128)(2,1)S(1)}, bf16[32,3072]{1,0:T(8,128)(2,1)S(1)}, u32[]{:S(2)}, u32[]{:S(2)}) %collective-permute-start.4) | collective-permute-done | bytes 196640 | tf_op jit(solution)/shard_map/ppermute | solution.py:18
  17.4 1.6 %collective-permute-start.5 = (bf16[16,3072]{1,0:T(8,128)(2,1)S(1)}, bf16[16,3072]{1,0:T(8,128)(2,1)S(1)}, u32[]{:S(2)}, u32[]{:S(2)}) collective-permute-start(bf16[16,3072]{1,0:T(8,128)(2,1)S(1)} %slice.33), channel_id=1, source_target_pairs={{0,2},{1,3},{2,0},{3,1},{4,6},{5,7},{6,4},{7,5},{8,10},{9,11},{10,... | collective-permute-start | bytes 294920 | tf_op jit(solution)/shard_map/ppermute | solution.py:18
  19.0 3.3 %collective-permute-done.5 = bf16[16,3072]{1,0:T(8,128)(2,1)S(1)} collective-permute-done((bf16[16,3072]{1,0:T(8,128)(2,1)S(1)}, bf16[16,3072]{1,0:T(8,128)(2,1)S(1)}, u32[]{:S(2)}, u32[]{:S(2)}) %collective-permute-start.5) | collective-permute-done | bytes 98336 | tf_op jit(solution)/shard_map/ppermute | solution.py:18
  22.4 1.6 %collective-permute-start.6 = (bf16[16,3072]{1,0:T(8,128)(2,1)S(1)}, bf16[16,3072]{1,0:T(8,128)(2,1)S(1)}, u32[]{:S(2)}, u32[]{:S(2)}) collective-permute-start(bf16[16,3072]{1,0:T(8,128)(2,1)S(1)} %fusion.6), channel_id=1, source_target_pairs={{0,8},{8,0},{16,24},{24,16},{1,9},{9,1},{17,25},{25,17},{2,10},{10... | collective-permute-start | bytes 294920 | tf_op jit(solution)/shard_map/ppermute | solution.py:25
  24.0 1.9 %collective-permute-start.7 = (bf16[16,3072]{1,0:T(8,128)(2,1)S(1)}, bf16[16,3072]{1,0:T(8,128)(2,1)S(1)}, u32[]{:S(2)}, u32[]{:S(2)}) collective-permute-start(bf16[16,3072]{1,0:T(8,128)(2,1)S(1)} %fusion.6), channel_id=1, source_target_pairs={{8,16},{16,8},{9,17},{17,9},{10,18},{18,10},{11,19},{19,11},{12,20... | collective-permute-start | bytes 294920 | tf_op jit(solution)/shard_map/ppermute | solution.py:26
  26.0 1.1 %collective-permute-done.6 = bf16[16,3072]{1,0:T(8,128)(2,1)S(1)} collective-permute-done((bf16[16,3072]{1,0:T(8,128)(2,1)S(1)}, bf16[16,3072]{1,0:T(8,128)(2,1)S(1)}, u32[]{:S(2)}, u32[]{:S(2)}) %collective-permute-start.6) | collective-permute-done | bytes 98336 | tf_op jit(solution)/shard_map/ppermute | solution.py:25
  27.1 3.5 %collective-permute-done.7 = bf16[16,3072]{1,0:T(8,128)(2,1)S(1)} collective-permute-done((bf16[16,3072]{1,0:T(8,128)(2,1)S(1)}, bf16[16,3072]{1,0:T(8,128)(2,1)S(1)}, u32[]{:S(2)}, u32[]{:S(2)}) %collective-permute-start.7) | collective-permute-done | bytes 98336 | tf_op jit(solution)/shard_map/ppermute | solution.py:26
  30.5 0.2 fusion
  30.7 0.1 fusion.2
  30.8 2.5 %collective-permute-start.10 = (bf16[16,3072]{1,0:T(8,128)(2,1)S(1)}, bf16[16,3072]{1,0:T(8,128)(2,1)S(1)}, u32[]{:S(2)}, u32[]{:S(2)}) collective-permute-start(bf16[16,3072]{1,0:T(8,128)(2,1)S(1)} %fusion.2), channel_id=1, source_target_pairs={{0,6},{1,7},{2,4},{3,5},{4,2},{5,3},{6,0},{7,1},{8,14},{9,15},{10,... | collective-permute-start | bytes 294920 | tf_op jit(solution)/shard_map/ppermute | solution.py:18
  33.3 0.5 collective-permute-start.9
  33.8 0.5 collective-permute-start.8
  34.4 2.0 %collective-permute-done.10 = bf16[16,3072]{1,0:T(8,128)(2,1)S(1)} collective-permute-done((bf16[16,3072]{1,0:T(8,128)(2,1)S(1)}, bf16[16,3072]{1,0:T(8,128)(2,1)S(1)}, u32[]{:S(2)}, u32[]{:S(2)}) %collective-permute-start.10) | collective-permute-done | bytes 98336 | tf_op jit(solution)/shard_map/ppermute | solution.py:18
  36.4 1.5 %collective-permute-done.9 = bf16[16,3072]{1,0:T(8,128)(2,1)S(1)} collective-permute-done((bf16[16,3072]{1,0:T(8,128)(2,1)S(1)}, bf16[16,3072]{1,0:T(8,128)(2,1)S(1)}, u32[]{:S(2)}, u32[]{:S(2)}) %collective-permute-start.9) | collective-permute-done | bytes 98336 | tf_op jit(solution)/shard_map/ppermute | solution.py:18
  37.9 0.5 collective-permute-done.8
  38.5 0.1 collective-permute-start.11
  38.6 1.7 %collective-permute-done.11.theirs_ref = bf16[64,3072]{1,0:T(8,128)(2,1)S(1)} collective-permute-done((bf16[64,3072]{1,0:T(8,128)(2,1)S(1)}, bf16[64,3072]{1,0:T(8,128)(2,1)S(1)}, u32[]{:S(2)}, u32[]{:S(2)}) %collective-permute-start.11) | collective-permute-done | bytes 393248 | tf_op jit(solution)/shard_map/ppermute | solution.py:18
  40.3 0.0 copy-start.1
  40.3 2.8 %copy-done.1 = bf16[2,3072,512]{2,1,0:T(8,128)(2,1)S(1)} copy-done((bf16[2,3072,512]{2,1,0:T(8,128)(2,1)S(1)}, bf16[2,3072,512]{2,1,0:T(8,128)(2,1)}, u32[]{:S(2)}) %copy-start.1) | copy-done | bytes 6291480
  43.1 0.0 copy-start.3
  43.1 1.9 %copy-done.3 = bf16[512,3072]{1,0:T(8,128)(2,1)S(1)} copy-done((bf16[512,3072]{1,0:T(8,128)(2,1)S(1)}, bf16[512,3072]{1,0:T(8,128)(2,1)}, u32[]{:S(2)}) %copy-start.3) | copy-done | bytes 3145752
  45.0 3.2 %shard_map.76 = (f32[32,3072]{1,0:T(8,128)S(1)}, bf16[32,3072]{1,0:T(8,128)(2,1)S(1)}) custom-call(bf16[64,3072]{1,0:T(8,128)(2,1)S(1)} %pad_maximum_fusion.1.mine_ref, bf16[64,3072]{1,0:T(8,128)(2,1)S(1)} %collective-permute-done.11.theirs_ref, bf16[3072,512]{1,0:T(8,128)(2,1)S(1)} %get-tuple-element.38.wq_ref, bf16[2,3072,512]{2,1,0:T(8,128)(2,1)S(1)} %copy-done.1, ...), custom_call_target="tpu_custom_call" | custom-call | tf_op jit(solution)/shard_map/pallas_call | solution.py:68
  48.2 0.2 collective-permute-start.12
  48.4 1.3 %collective-permute-done.12 = bf16[32,3072]{1,0:T(8,128)(2,1)S(1)} collective-permute-done((bf16[32,3072]{1,0:T(8,128)(2,1)S(1)}, bf16[32,3072]{1,0:T(8,128)(2,1)S(1)}, u32[]{:S(2)}, u32[]{:S(2)}) %collective-permute-start.12) | collective-permute-done | bytes 196640 | tf_op jit(solution)/shard_map/ppermute | solution.py:18
  49.8 0.6 %collective-permute-start.13 = (bf16[16,3072]{1,0:T(8,128)(2,1)S(1)}, bf16[16,3072]{1,0:T(8,128)(2,1)S(1)}, u32[]{:S(2)}, u32[]{:S(2)}) collective-permute-start(bf16[16,3072]{1,0:T(8,128)(2,1)S(1)} %slice.32), channel_id=1, source_target_pairs={{0,2},{1,3},{2,0},{3,1},{4,6},{5,7},{6,4},{7,5},{8,10},{9,11},{10,... | collective-permute-start | bytes 294920 | tf_op jit(solution)/shard_map/ppermute | solution.py:18
  50.4 4.3 %collective-permute-done.13 = bf16[16,3072]{1,0:T(8,128)(2,1)S(1)} collective-permute-done((bf16[16,3072]{1,0:T(8,128)(2,1)S(1)}, bf16[16,3072]{1,0:T(8,128)(2,1)S(1)}, u32[]{:S(2)}, u32[]{:S(2)}) %collective-permute-start.13) | collective-permute-done | bytes 98336 | tf_op jit(solution)/shard_map/ppermute | solution.py:18
  54.7 0.7 %maximum_bitcast_fusion = bf16[2,1,1,16,3072]{4,3,2,1,0:T(8,128)(2,1)} fusion(bf16[1,16,3072]{2,1,0:T(8,128)(2,1)S(1)} %fusion.7, bf16[1,16,3072]{2,1,0:T(8,128)(2,1)S(1)} %bitcast.21), kind=kLoop, calls=%fused_computation.17 | loop fusion | flops 98304 | bytes 393216 | tf_op jit(solution)/shard_map/broadcast_in_dim | solution.py:150
  (9 shorter events, 0.3 us)
Async XLA Ops:
  0.0 0.9 %copy-start.4 = (bf16[1,1,16,3072]{3,2,1,0:T(8,128)(2,1)S(1)}, bf16[1,1,16,3072]{3,2,1,0:T(8,128)(2,1)}, u32[]{:S(2)}) copy-start(bf16[1,1,16,3072]{3,2,1,0:T(8,128)(2,1)} %param.7) | copy-start | bytes 294916
  0.9 0.7 %copy-start.5 = (f32[1,1,3072]{2,1,0:T(1,128)S(1)}, f32[1,1,3072]{2,1,0:T(1,128)}, u32[]{:S(2)}) copy-start(f32[1,1,3072]{2,1,0:T(1,128)} %param.10) | copy-start | bytes 36868
  1.7 9.0 %collective-permute-start.2 = (bf16[16,3072]{1,0:T(8,128)(2,1)S(1)}, bf16[16,3072]{1,0:T(8,128)(2,1)S(1)}, u32[]{:S(2)}, u32[]{:S(2)}) collective-permute-start(bf16[16,3072]{1,0:T(8,128)(2,1)S(1)} %get-tuple-element.25), channel_id=1, source_target_pairs={{0,6},{1,7},{2,4},{3,5},{4,2},{5,3},{6,0},{7,1},{8,14},{9,15},{10,... | collective-permute-start | bytes 294920 | tf_op jit(solution)/shard_map/ppermute | solution.py:18
  4.3 6.5 %collective-permute-start.1 = (bf16[16,3072]{1,0:T(8,128)(2,1)S(1)}, bf16[16,3072]{1,0:T(8,128)(2,1)S(1)}, u32[]{:S(2)}, u32[]{:S(2)}) collective-permute-start(bf16[16,3072]{1,0:T(8,128)(2,1)S(1)} %get-tuple-element.25), channel_id=1, source_target_pairs={{0,4},{1,5},{2,6},{3,7},{4,0},{5,1},{6,2},{7,3},{8,12},{9,13},{10,... | collective-permute-start | bytes 294920 | tf_op jit(solution)/shard_map/ppermute | solution.py:18
  4.8 6.0 %collective-permute-start = (bf16[16,3072]{1,0:T(8,128)(2,1)S(1)}, bf16[16,3072]{1,0:T(8,128)(2,1)S(1)}, u32[]{:S(2)}, u32[]{:S(2)}) collective-permute-start(bf16[16,3072]{1,0:T(8,128)(2,1)S(1)} %get-tuple-element.25), channel_id=1, source_target_pairs={{0,2},{1,3},{2,0},{3,1},{4,6},{5,7},{6,4},{7,5},{8,10},{9,11},{10,... | collective-permute-start | bytes 294920 | tf_op jit(solution)/shard_map/ppermute | solution.py:18
  10.7 5.1 %copy-start = (bf16[2,3072,512]{2,1,0:T(8,128)(2,1)}, bf16[2,3072,512]{2,1,0:T(8,128)(2,1)S(1)}, u32[]{:S(2)}) copy-start(bf16[2,3072,512]{2,1,0:T(8,128)(2,1)S(1)} %get-tuple-element.39.wkv_ref) | copy-start | bytes 18874372
  10.7 5.1 %copy-start.2 = (bf16[512,3072]{1,0:T(8,128)(2,1)}, bf16[512,3072]{1,0:T(8,128)(2,1)S(1)}, u32[]{:S(2)}) copy-start(bf16[512,3072]{1,0:T(8,128)(2,1)S(1)} %get-tuple-element.40.wo_ref) | copy-start | bytes 9437188
  10.8 1.8 %collective-permute-start.3 = (bf16[64,3072]{1,0:T(8,128)(2,1)S(1)}, bf16[64,3072]{1,0:T(8,128)(2,1)S(1)}, u32[]{:S(2)}, u32[]{:S(2)}) collective-permute-start(bf16[64,3072]{1,0:T(8,128)(2,1)S(1)} %pad_maximum_fusion.mine_ref), channel_id=1, source_target_pairs={{0,1},{1,0},{2,3},{3,2},{4,5},{5,4},{6,7},{7,6},{8,9},{9,8},{10,11... | collective-permute-start | bytes 1179656 | tf_op jit(solution)/shard_map/ppermute | solution.py:18
  15.9 1.5 %collective-permute-start.4 = (bf16[32,3072]{1,0:T(8,128)(2,1)S(1)}, bf16[32,3072]{1,0:T(8,128)(2,1)S(1)}, u32[]{:S(2)}, u32[]{:S(2)}) collective-permute-start(bf16[32,3072]{1,0:T(8,128)(2,1)S(1)} %get-tuple-element.34), channel_id=1, source_target_pairs={{0,1},{1,0},{2,3},{3,2},{4,5},{5,4},{6,7},{7,6},{8,9},{9,8},{10,11... | collective-permute-start | bytes 589832 | tf_op jit(solution)/shard_map/ppermute | solution.py:18
  17.4 4.9 %collective-permute-start.5 = (bf16[16,3072]{1,0:T(8,128)(2,1)S(1)}, bf16[16,3072]{1,0:T(8,128)(2,1)S(1)}, u32[]{:S(2)}, u32[]{:S(2)}) collective-permute-start(bf16[16,3072]{1,0:T(8,128)(2,1)S(1)} %slice.33), channel_id=1, source_target_pairs={{0,2},{1,3},{2,0},{3,1},{4,6},{5,7},{6,4},{7,5},{8,10},{9,11},{10,... | collective-permute-start | bytes 294920 | tf_op jit(solution)/shard_map/ppermute | solution.py:18
  22.4 4.7 %collective-permute-start.6 = (bf16[16,3072]{1,0:T(8,128)(2,1)S(1)}, bf16[16,3072]{1,0:T(8,128)(2,1)S(1)}, u32[]{:S(2)}, u32[]{:S(2)}) collective-permute-start(bf16[16,3072]{1,0:T(8,128)(2,1)S(1)} %fusion.6), channel_id=1, source_target_pairs={{0,8},{8,0},{16,24},{24,16},{1,9},{9,1},{17,25},{25,17},{2,10},{10... | collective-permute-start | bytes 294920 | tf_op jit(solution)/shard_map/ppermute | solution.py:25
  24.0 6.5 %collective-permute-start.7 = (bf16[16,3072]{1,0:T(8,128)(2,1)S(1)}, bf16[16,3072]{1,0:T(8,128)(2,1)S(1)}, u32[]{:S(2)}, u32[]{:S(2)}) collective-permute-start(bf16[16,3072]{1,0:T(8,128)(2,1)S(1)} %fusion.6), channel_id=1, source_target_pairs={{8,16},{16,8},{9,17},{17,9},{10,18},{18,10},{11,19},{19,11},{12,20... | collective-permute-start | bytes 294920 | tf_op jit(solution)/shard_map/ppermute | solution.py:26
  30.8 5.6 %collective-permute-start.10 = (bf16[16,3072]{1,0:T(8,128)(2,1)S(1)}, bf16[16,3072]{1,0:T(8,128)(2,1)S(1)}, u32[]{:S(2)}, u32[]{:S(2)}) collective-permute-start(bf16[16,3072]{1,0:T(8,128)(2,1)S(1)} %fusion.2), channel_id=1, source_target_pairs={{0,6},{1,7},{2,4},{3,5},{4,2},{5,3},{6,0},{7,1},{8,14},{9,15},{10,... | collective-permute-start | bytes 294920 | tf_op jit(solution)/shard_map/ppermute | solution.py:18
  33.3 4.6 %collective-permute-start.9 = (bf16[16,3072]{1,0:T(8,128)(2,1)S(1)}, bf16[16,3072]{1,0:T(8,128)(2,1)S(1)}, u32[]{:S(2)}, u32[]{:S(2)}) collective-permute-start(bf16[16,3072]{1,0:T(8,128)(2,1)S(1)} %fusion.2), channel_id=1, source_target_pairs={{0,4},{1,5},{2,6},{3,7},{4,0},{5,1},{6,2},{7,3},{8,12},{9,13},{10,... | collective-permute-start | bytes 294920 | tf_op jit(solution)/shard_map/ppermute | solution.py:18
  33.8 4.6 %collective-permute-start.8 = (bf16[16,3072]{1,0:T(8,128)(2,1)S(1)}, bf16[16,3072]{1,0:T(8,128)(2,1)S(1)}, u32[]{:S(2)}, u32[]{:S(2)}) collective-permute-start(bf16[16,3072]{1,0:T(8,128)(2,1)S(1)} %fusion.2), channel_id=1, source_target_pairs={{0,2},{1,3},{2,0},{3,1},{4,6},{5,7},{6,4},{7,5},{8,10},{9,11},{10,... | collective-permute-start | bytes 294920 | tf_op jit(solution)/shard_map/ppermute | solution.py:18
  38.5 1.8 %collective-permute-start.11 = (bf16[64,3072]{1,0:T(8,128)(2,1)S(1)}, bf16[64,3072]{1,0:T(8,128)(2,1)S(1)}, u32[]{:S(2)}, u32[]{:S(2)}) collective-permute-start(bf16[64,3072]{1,0:T(8,128)(2,1)S(1)} %pad_maximum_fusion.1.mine_ref), channel_id=1, source_target_pairs={{0,1},{1,0},{2,3},{3,2},{4,5},{5,4},{6,7},{7,6},{8,9},{9,8},{10,11... | collective-permute-start | bytes 1179656 | tf_op jit(solution)/shard_map/ppermute | solution.py:18
  40.3 2.8 %copy-start.1 = (bf16[2,3072,512]{2,1,0:T(8,128)(2,1)S(1)}, bf16[2,3072,512]{2,1,0:T(8,128)(2,1)}, u32[]{:S(2)}) copy-start(bf16[2,3072,512]{2,1,0:T(8,128)(2,1)} %copy-done) | copy-start | bytes 18874372
  43.1 1.9 %copy-start.3 = (bf16[512,3072]{1,0:T(8,128)(2,1)S(1)}, bf16[512,3072]{1,0:T(8,128)(2,1)}, u32[]{:S(2)}) copy-start(bf16[512,3072]{1,0:T(8,128)(2,1)} %copy-done.2) | copy-start | bytes 9437188
  48.2 1.5 %collective-permute-start.12 = (bf16[32,3072]{1,0:T(8,128)(2,1)S(1)}, bf16[32,3072]{1,0:T(8,128)(2,1)S(1)}, u32[]{:S(2)}, u32[]{:S(2)}) collective-permute-start(bf16[32,3072]{1,0:T(8,128)(2,1)S(1)} %get-tuple-element.42), channel_id=1, source_target_pairs={{0,1},{1,0},{2,3},{3,2},{4,5},{5,4},{6,7},{7,6},{8,9},{9,8},{10,11... | collective-permute-start | bytes 589832 | tf_op jit(solution)/shard_map/ppermute | solution.py:18
  49.8 4.9 %collective-permute-start.13 = (bf16[16,3072]{1,0:T(8,128)(2,1)S(1)}, bf16[16,3072]{1,0:T(8,128)(2,1)S(1)}, u32[]{:S(2)}, u32[]{:S(2)}) collective-permute-start(bf16[16,3072]{1,0:T(8,128)(2,1)S(1)} %slice.32), channel_id=1, source_target_pairs={{0,2},{1,3},{2,0},{3,1},{4,6},{5,7},{6,4},{7,5},{8,10},{9,11},{10,... | collective-permute-start | bytes 294920 | tf_op jit(solution)/shard_map/ppermute | solution.py:18

commit v3 on v1

v3 whole, which is shorter than its diff:
```python
import functools

import jax
import jax.numpy as jnp
from jax import lax
from jax.experimental import pallas as pl
from jax.experimental.pallas import tpu as pltpu
from jax.sharding import PartitionSpec as P

HEAD_DIM = 128
EPSILON = 1e-06
BOTH = ("tower", "lane")
PIECES = 4


def swapped(value, mask):
    count = lax.axis_size(BOTH)
    return lax.ppermute(value, BOTH, [(i, i ^ mask) for i in range(count)])


def handed_on(value):
    count = lax.axis_size("section")
    return lax.ppermute(value, "section", [(s, s + 1) for s in range(count - 1)])


def in_hbm(*arrays):
    return [pltpu.with_memory_space_constraint(a, pltpu.HBM) for a in arrays]


def normalized(state, gain):
    wide = state.astype(jnp.float32)
    scale = lax.rsqrt(jnp.mean(wide * wide, -1, keepdims=True) + EPSILON)
    return (wide * scale * gain).astype(jnp.bfloat16)


def layer_kernel(tok, mine_ref, theirs_ref, wq_ref, wkv_ref, wo_ref, keep_ref, send_ref):
    half, depth = keep_ref.shape
    rows = 2 * half
    own = jnp.concatenate([mine_ref[:half], theirs_ref[:half]], 0)
    partner = jnp.concatenate([mine_ref[half:], theirs_ref[half:]], 0)

    def project(left, right):
        return jnp.dot(left, right, preferred_element_type=jnp.float32).astype(jnp.bfloat16)

    query = project(own, wq_ref[...])
    keys = project(partner, wkv_ref[:depth])
    values = project(partner, wkv_ref[depth:])
    row_clip = lax.broadcasted_iota(jnp.int32, (rows, rows), 0) // tok
    col_clip = lax.broadcasted_iota(jnp.int32, (rows, rows), 1) // tok
    same_clip = row_clip == col_clip
    mixed = []
    for start in range(0, query.shape[1], HEAD_DIM):
        head = slice(start, start + HEAD_DIM)
        scores = lax.dot_general(
            query[:, head], keys[:, head], (((1,), (1,)), ((), ())), preferred_element_type=jnp.float32
        ) * (HEAD_DIM**-0.5)
        scores = jnp.where(same_clip, scores, -jnp.inf)
        weights = jnp.exp(scores - jnp.max(scores, -1, keepdims=True))
        weights = weights / jnp.sum(weights, -1, keepdims=True)
        mixed.append(project(weights.astype(jnp.bfloat16), values[:, head]))
    part = jnp.dot(jnp.concatenate(mixed, 1), wo_ref[...], preferred_element_type=jnp.float32)
    keep_ref[...] = part[:half]
    send_ref[...] = part[half:].astype(jnp.bfloat16)


def layer_part(mine, theirs, weights, tok):
    half, width = mine.shape[0] // 2, mine.shape[1]
    return pl.pallas_call(
        functools.partial(layer_kernel, tok),
        out_shape=(
            jax.ShapeDtypeStruct((half, width), jnp.float32),
            jax.ShapeDtypeStruct((half, width), jnp.bfloat16),
        ),
        in_specs=[pl.BlockSpec(memory_space=pltpu.VMEM)] * 5,
        out_specs=(pl.BlockSpec(memory_space=pltpu.VMEM),) * 2,
        compiler_params=pltpu.CompilerParams(vmem_limit_bytes=16 << 20),
    )(mine, theirs, *(pltpu.with_memory_space_constraint(w, pltpu.VMEM) for w in weights))


def entry_kernel(x_ref, gain_ref, normed_ref, x_out, gain_out, sems):
    copies = [
        pltpu.make_async_copy(x_ref, x_out, sems.at[0]),
        pltpu.make_async_copy(gain_ref, gain_out, sems.at[1]),
    ]
    for copy in copies:
        copy.start()
    for copy in copies:
        copy.wait()
    normed_ref[...] = normalized(x_out[...], gain_out[0])


def entry(state, gain):
    return pl.pallas_call(
        entry_kernel,
        out_shape=(
            pltpu.VMEM(state.shape, jnp.bfloat16),
            pltpu.VMEM(state.shape, state.dtype),
            pltpu.VMEM(gain.shape, gain.dtype),
        ),
        in_specs=[pl.BlockSpec(memory_space=pltpu.HBM)] * 2,
        out_specs=(pl.BlockSpec(memory_space=pltpu.VMEM),) * 3,
        scratch_shapes=[pltpu.SemaphoreType.DMA((2,))],
        compiler_params=pltpu.CompilerParams(vmem_limit_bytes=16 << 20),
    )(*in_hbm(state, gain))


def load_kernel(*refs):
    *refs, sems = refs
    count = len(refs) // 2
    copies = []
    for source, target in zip(refs[:count], refs[count:]):
        pieces = PIECES if source.shape[0] % (16 * PIECES) == 0 else 1
        rows = source.shape[0] // pieces
        for i in range(pieces):
            here = pl.ds(i * rows, rows)
            copies.append(pltpu.make_async_copy(source.at[here], target.at[here], sems.at[len(copies)]))
            copies[-1].start()
    for copy in copies:
        copy.wait()


def load(*arrays):
    return pl.pallas_call(
        load_kernel,
        out_shape=tuple(pltpu.VMEM(a.shape, a.dtype) for a in arrays),
        in_specs=[pl.BlockSpec(memory_space=pltpu.HBM)] * len(arrays),
        out_specs=(pl.BlockSpec(memory_space=pltpu.VMEM),) * len(arrays),
        scratch_shapes=[pltpu.SemaphoreType.DMA((PIECES * len(arrays),))],
        cost_estimate=pl.CostEstimate(
            flops=0, bytes_accessed=sum(a.size * a.dtype.itemsize for a in arrays), transcendentals=0
        ),
        compiler_params=pltpu.CompilerParams(vmem_limit_bytes=16 << 20),
    )(*in_hbm(*arrays))


def second_kernel(section_ref, offset_ref, handed_ref, fresh_ref, gain_ref, state_ref, normed_ref):
    tok = handed_ref.shape[0]
    picked = fresh_ref[pl.ds(pl.multiple_of(offset_ref[0] * tok, tok), tok)]
    state = jnp.where(section_ref[0] == 0, picked, handed_ref[...])
    state_ref[...] = state
    normed_ref[...] = normalized(state, gain_ref[0])


def second_entry(section, offsets, handed, fresh, gain):
    return pl.pallas_call(
        second_kernel,
        out_shape=(jax.ShapeDtypeStruct(handed.shape, handed.dtype),) * 2,
        in_specs=[pl.BlockSpec(memory_space=pltpu.SMEM)] * 2 + [pl.BlockSpec(memory_space=pltpu.VMEM)] * 3,
        out_specs=(pl.BlockSpec(memory_space=pltpu.VMEM),) * 2,
        compiler_params=pltpu.CompilerParams(vmem_limit_bytes=16 << 20),
    )(section, offsets, handed, fresh, gain)


def gathered(normed):
    lanes = lax.axis_size("lane")
    distances = [tower * lanes + 2 * k for tower in range(2) for k in range(lanes // 2)]
    blocks = {d: swapped(normed, d) if d else normed for d in distances}
    return jnp.concatenate([blocks[d] for d in distances], 0)


def reduced(state, keep, sent):
    tok = state.shape[0]
    total = keep + sent.astype(jnp.float32)
    result = state.astype(jnp.float32) + total[:tok]
    for k in range(1, lax.axis_size("lane") // 2):
        share = total[k * tok : (k + 1) * tok].astype(jnp.bfloat16)
        result = result + swapped(share, 2 * k).astype(jnp.float32)
    return result.astype(jnp.bfloat16)


def shards(in_flight, fresh_batches, offsets, norm_gain, w_query, w_keyval, w_out):
    normed, state, gain = entry(in_flight[0, 0], norm_gain[0])
    section = jnp.reshape(lax.axis_index("section"), (1,)).astype(jnp.int32)
    normed, section = lax.optimization_barrier((normed, section))
    wq, wkv = load(
        w_query[0, 0],
        w_keyval.reshape(-1, w_keyval.shape[-1]),
    )
    mine, wq, wkv = lax.optimization_barrier((gathered(normed), wq, wkv))
    wo, fresh = load(w_out[0, 0], fresh_batches.reshape(-1, fresh_batches.shape[-1]))
    weights = (wq, wkv, wo)
    keep, send = layer_part(mine, swapped(mine, 1), weights, state.shape[0])
    first = reduced(state, keep, swapped(send, 1))
    state, normed = second_entry(section, offsets, handed_on(first), fresh, gain)
    mine = gathered(normed)
    keep, send = layer_part(mine, swapped(mine, 1), weights, state.shape[0])
    second = reduced(state, keep, swapped(send, 1))
    return jnp.stack([first, second])[:, None, None]


def solution(mesh):
    placed = (
        P("section", "tower", "lane", None),
        P(None, "tower", "lane", None),
        P("lane"),
        P("section", "tower", None),
        P("section", "tower", None, "lane"),
        P("section", "tower", None, None, "lane"),
        P("section", "tower", "lane", None),
    )
    return jax.shard_map(
        shards,
        mesh=mesh,
        in_specs=placed,
        out_specs=P(None, "section", "tower", "lane", None),
        check_vma=False,
    )
```

time: 63.1 us -> 49.6 us (0.79)
  local copies, waits for them, and re-layouts: 11.3 us -> 0.06 us
  Pallas kernels: 6.49 us -> 13.5 us
  waiting for transfers between devices: 24 us -> 19.9 us
  other arithmetic: 4.07 us -> 0.89 us
  starting transfers between devices: 16.2 us -> 14.3 us
    unnamed x16 -> x3, local copies, waits for them, and re-layouts: 11.2 us -> 0.02 us
    pallas_call x0 -> x4, Pallas kernels: none -> 6.99 us  [the longest x2 5.81 us: load(): pl.pallas_call(load_kernel, out_shape=tuple((pltpu.VMEM(a.shape, a.dtype)...]
    ppermute x12, waiting for transfers between devices: 22 us -> 18.3 us  [swapped(): return lax.ppermute(value, BOTH, [(i, i ^ mask) for i in range(count)])]
    reduce_sum x2 -> x0, other arithmetic: 2.08 us -> none  [normalized(): scale = lax.rsqrt(jnp.mean(wide * wide, -1, keepdims=True) + EPSILON)]
    ppermute x2 -> x1, starting transfers between devices: 5.23 us -> 3.49 us  [handed_on(): lax.ppermute(value, 'section', [(s, s + 1) for s in range(count - 1)])]
    convert_element_type x3 -> x1, other arithmetic: 1.12 us -> 0.04 us  [reduced(): return result.astype(jnp.bfloat16)]
    ppermute x2 -> x1, waiting for transfers between devices: 1.93 us -> 1.54 us  [handed_on(): lax.ppermute(value, 'section', [(s, s + 1) for s in range(count - 1)])]
  transfers between devices with their start and end apart: 14 -> 13, of which waited for: 12 -> 9; matrix products, arithmetic and copies ran while one was open for 0% -> 0% of each run, Pallas kernels for 0% -> 12%
where the time goes in v3:
time: 49.6 us; the launch traced here: 49.4 us
  waiting for transfers between devices  19.9 us (40%)
  starting transfers between devices  14.3 us (29%)
  Pallas kernels  13.5 us (27%)
  other arithmetic  0.89 us (2%)
  between operations  0.78 us (2%)
    ppermute x12, waiting for transfers between devices, swapped(): return lax.ppermute(value, BOTH, [(i, i ^ mask) for i in range(count)])  18.3 us
    ppermute x12, starting transfers between devices, swapped(): return lax.ppermute(value, BOTH, [(i, i ^ mask) for i in range(count)])  10.8 us
    pallas_call x2, Pallas kernels, layer_part(): pl.pallas_call(functools.partial(layer_kernel, tok), out_shape=(jax.Shape...  6.49 us
    pallas_call x2, Pallas kernels, load(): pl.pallas_call(load_kernel, out_shape=tuple((pltpu.VMEM(a.shape, a.dtype)...  5.81 us
    ppermute x1, starting transfers between devices, handed_on(): lax.ppermute(value, 'section', [(s, s + 1) for s in range(count - 1)])  3.49 us
    ppermute x1, waiting for transfers between devices, handed_on(): lax.ppermute(value, 'section', [(s, s + 1) for s in range(count - 1)])  1.54 us
    pallas_call x1, Pallas kernels, entry(): pl.pallas_call(entry_kernel, out_shape=(pltpu.VMEM(state.shape, jnp.bfloa...  1.04 us
  transfers between devices with their start and end apart: 13, of which 9 were waited for; matrix products, arithmetic and copies ran while one was open for 0% of the time, Pallas kernels for 12%

profile of v3, /device:TPU:0, one launch (start us, length us, event | category | flops | bytes accessed | tf_op | source)
XLA Modules:
  0.0 49.4 jit_solution(3468882887310834361)
XLA Ops:
  0.0 1.0 %shard_map.73 = (bf16[16,3072]{1,0:T(8,128)(2,1)S(1)}, bf16[16,3072]{1,0:T(8,128)(2,1)S(1)}, f32[1,3072]{1,0:T(1,128)S(1)}) custom-call(bf16[16,3072]{1,0:T(8,128)(2,1)} %bitcast.19, f32[1,3072]{1,0:T(1,128)} %bitcast.20), custom_call_target="tpu_custom_call" | custom-call | tf_op jit(solution)/shard_map/pallas_call | solution.py:93
  1.1 3.0 %collective-permute-start = (bf16[16,3072]{1,0:T(8,128)(2,1)S(1)}, bf16[16,3072]{1,0:T(8,128)(2,1)S(1)}, u32[]{:S(2)}, u32[]{:S(2)}) collective-permute-start(bf16[16,3072]{1,0:T(8,128)(2,1)S(1)} %get-tuple-element.25), channel_id=1, source_target_pairs={{0,2},{1,3},{2,0},{3,1},{4,6},{5,7},{6,4},{7,5},{8,10},{9,11},{10,... | collective-permute-start | bytes 294920 | tf_op jit(solution)/shard_map/ppermute | solution.py:18
  4.1 1.5 %collective-permute-start.1 = (bf16[16,3072]{1,0:T(8,128)(2,1)S(1)}, bf16[16,3072]{1,0:T(8,128)(2,1)S(1)}, u32[]{:S(2)}, u32[]{:S(2)}) collective-permute-start(bf16[16,3072]{1,0:T(8,128)(2,1)S(1)} %get-tuple-element.25), channel_id=1, source_target_pairs={{0,4},{1,5},{2,6},{3,7},{4,0},{5,1},{6,2},{7,3},{8,12},{9,13},{10,... | collective-permute-start | bytes 294920 | tf_op jit(solution)/shard_map/ppermute | solution.py:18
  5.6 0.0 collective-permute-start.2
  5.6 3.8 %shard_map.74 = (bf16[3072,512]{1,0:T(8,128)(2,1)S(1)}, bf16[6144,512]{1,0:T(8,128)(2,1)S(1)}) custom-call(bf16[3072,512]{1,0:T(8,128)(2,1)} %bitcast.16, bf16[6144,512]{1,0:T(8,128)(2,1)} %bitcast.14), custom_call_target="tpu_custom_call" | custom-call | bytes 9437184 | tf_op jit(solution)/shard_map/pallas_call | solution.py:123
  9.4 0.0 collective-permute-done
  9.5 0.0 collective-permute-done.1
  9.5 1.6 %collective-permute-done.2 = bf16[16,3072]{1,0:T(8,128)(2,1)S(1)} collective-permute-done((bf16[16,3072]{1,0:T(8,128)(2,1)S(1)}, bf16[16,3072]{1,0:T(8,128)(2,1)S(1)}, u32[]{:S(2)}, u32[]{:S(2)}) %collective-permute-start.2) | collective-permute-done | bytes 98336 | tf_op jit(solution)/shard_map/ppermute | solution.py:18
  11.1 0.1 collective-permute-start.3
  11.2 2.0 %shard_map.75 = (bf16[512,3072]{1,0:T(8,128)(2,1)S(1)}, bf16[64,3072]{1,0:T(8,128)(2,1)S(1)}) custom-call(bf16[512,3072]{1,0:T(8,128)(2,1)} %bitcast.15, bf16[64,3072]{1,0:T(8,128)(2,1)} %bitcast.17), custom_call_target="tpu_custom_call" | custom-call | bytes 3538944 | tf_op jit(solution)/shard_map/pallas_call | solution.py:123
  13.2 0.0 collective-permute-done.3.theirs_ref
  13.2 3.2 %shard_map.76 = (f32[32,3072]{1,0:T(8,128)S(1)}, bf16[32,3072]{1,0:T(8,128)(2,1)S(1)}) custom-call(bf16[64,3072]{1,0:T(8,128)(2,1)S(1)} %pad_maximum_fusion.mine_ref, bf16[64,3072]{1,0:T(8,128)(2,1)S(1)} %collective-permute-done.3.theirs_ref, bf16[3072,512]{1,0:T(8,128)(2,1)S(1)} %get-tuple-element.29.wq_ref, ...), custom_call_target="tpu_custom_call" | custom-call | tf_op jit(solution)/shard_map/pallas_call | solution.py:68
  16.5 0.6 %collective-permute-start.4 = (bf16[32,3072]{1,0:T(8,128)(2,1)S(1)}, bf16[32,3072]{1,0:T(8,128)(2,1)S(1)}, u32[]{:S(2)}, u32[]{:S(2)}) collective-permute-start(bf16[32,3072]{1,0:T(8,128)(2,1)S(1)} %get-tuple-element.33), channel_id=1, source_target_pairs={{0,1},{1,0},{2,3},{3,2},{4,5},{5,4},{6,7},{7,6},{8,9},{9,8},{10,11... | collective-permute-start | bytes 589832 | tf_op jit(solution)/shard_map/ppermute | solution.py:18
  17.0 1.1 %collective-permute-done.4 = bf16[32,3072]{1,0:T(8,128)(2,1)S(1)} collective-permute-done((bf16[32,3072]{1,0:T(8,128)(2,1)S(1)}, bf16[32,3072]{1,0:T(8,128)(2,1)S(1)}, u32[]{:S(2)}, u32[]{:S(2)}) %collective-permute-start.4) | collective-permute-done | bytes 196640 | tf_op jit(solution)/shard_map/ppermute | solution.py:18
  18.2 1.0 %collective-permute-start.5 = (bf16[16,3072]{1,0:T(8,128)(2,1)S(1)}, bf16[16,3072]{1,0:T(8,128)(2,1)S(1)}, u32[]{:S(2)}, u32[]{:S(2)}) collective-permute-start(bf16[16,3072]{1,0:T(8,128)(2,1)S(1)} %slice.37), channel_id=1, source_target_pairs={{0,2},{1,3},{2,0},{3,1},{4,6},{5,7},{6,4},{7,5},{8,10},{9,11},{10,... | collective-permute-start | bytes 294920 | tf_op jit(solution)/shard_map/ppermute | solution.py:18
  19.2 4.1 %collective-permute-done.5 = bf16[16,3072]{1,0:T(8,128)(2,1)S(1)} collective-permute-done((bf16[16,3072]{1,0:T(8,128)(2,1)S(1)}, bf16[16,3072]{1,0:T(8,128)(2,1)S(1)}, u32[]{:S(2)}, u32[]{:S(2)}) %collective-permute-start.5) | collective-permute-done | bytes 98336 | tf_op jit(solution)/shard_map/ppermute | solution.py:18
  23.3 3.5 %collective-permute-start.6 = (bf16[16,3072]{1,0:T(8,128)(2,1)S(1)}, bf16[16,3072]{1,0:T(8,128)(2,1)S(1)}, u32[]{:S(2)}, u32[]{:S(2)}) collective-permute-start(bf16[16,3072]{1,0:T(8,128)(2,1)S(1)} %fusion.3), channel_id=1, source_target_pairs={{0,8},{8,16},{16,24},{1,9},{9,17},{17,25},{2,10},{10,18},{18,26},{... | collective-permute-start | bytes 294920 | tf_op jit(solution)/shard_map/ppermute | solution.py:23
  27.5 1.5 %collective-permute-done.6.handed_ref = bf16[16,3072]{1,0:T(8,128)(2,1)S(1)} collective-permute-done((bf16[16,3072]{1,0:T(8,128)(2,1)S(1)}, bf16[16,3072]{1,0:T(8,128)(2,1)S(1)}, u32[]{:S(2)}, u32[]{:S(2)}) %collective-permute-start.6) | collective-permute-done | bytes 98336 | tf_op jit(solution)/shard_map/ppermute | solution.py:23
  29.0 0.1 shard_map.77
  29.2 1.0 %collective-permute-start.7 = (bf16[16,3072]{1,0:T(8,128)(2,1)S(1)}, bf16[16,3072]{1,0:T(8,128)(2,1)S(1)}, u32[]{:S(2)}, u32[]{:S(2)}) collective-permute-start(bf16[16,3072]{1,0:T(8,128)(2,1)S(1)} %get-tuple-element.38), channel_id=1, source_target_pairs={{0,2},{1,3},{2,0},{3,1},{4,6},{5,7},{6,4},{7,5},{8,10},{9,11},{10,... | collective-permute-start | bytes 294920 | tf_op jit(solution)/shard_map/ppermute | solution.py:18
  30.2 1.4 %collective-permute-start.8 = (bf16[16,3072]{1,0:T(8,128)(2,1)S(1)}, bf16[16,3072]{1,0:T(8,128)(2,1)S(1)}, u32[]{:S(2)}, u32[]{:S(2)}) collective-permute-start(bf16[16,3072]{1,0:T(8,128)(2,1)S(1)} %get-tuple-element.38), channel_id=1, source_target_pairs={{0,4},{1,5},{2,6},{3,7},{4,0},{5,1},{6,2},{7,3},{8,12},{9,13},{10,... | collective-permute-start | bytes 294920 | tf_op jit(solution)/shard_map/ppermute | solution.py:18
  31.6 1.2 %collective-permute-start.9 = (bf16[16,3072]{1,0:T(8,128)(2,1)S(1)}, bf16[16,3072]{1,0:T(8,128)(2,1)S(1)}, u32[]{:S(2)}, u32[]{:S(2)}) collective-permute-start(bf16[16,3072]{1,0:T(8,128)(2,1)S(1)} %get-tuple-element.38), channel_id=1, source_target_pairs={{0,6},{1,7},{2,4},{3,5},{4,2},{5,3},{6,0},{7,1},{8,14},{9,15},{10,... | collective-permute-start | bytes 294920 | tf_op jit(solution)/shard_map/ppermute | solution.py:18
  32.8 2.1 %collective-permute-done.7 = bf16[16,3072]{1,0:T(8,128)(2,1)S(1)} collective-permute-done((bf16[16,3072]{1,0:T(8,128)(2,1)S(1)}, bf16[16,3072]{1,0:T(8,128)(2,1)S(1)}, u32[]{:S(2)}, u32[]{:S(2)}) %collective-permute-start.7) | collective-permute-done | bytes 98336 | tf_op jit(solution)/shard_map/ppermute | solution.py:18
  34.9 0.0 collective-permute-done.8
  34.9 2.2 %collective-permute-done.9 = bf16[16,3072]{1,0:T(8,128)(2,1)S(1)} collective-permute-done((bf16[16,3072]{1,0:T(8,128)(2,1)S(1)}, bf16[16,3072]{1,0:T(8,128)(2,1)S(1)}, u32[]{:S(2)}, u32[]{:S(2)}) %collective-permute-start.9) | collective-permute-done | bytes 98336 | tf_op jit(solution)/shard_map/ppermute | solution.py:18
  37.1 0.1 collective-permute-start.10
  37.2 1.7 %collective-permute-done.10.theirs_ref = bf16[64,3072]{1,0:T(8,128)(2,1)S(1)} collective-permute-done((bf16[64,3072]{1,0:T(8,128)(2,1)S(1)}, bf16[64,3072]{1,0:T(8,128)(2,1)S(1)}, u32[]{:S(2)}, u32[]{:S(2)}) %collective-permute-start.10) | collective-permute-done | bytes 393248 | tf_op jit(solution)/shard_map/ppermute | solution.py:18
  38.9 3.2 %shard_map.78 = (f32[32,3072]{1,0:T(8,128)S(1)}, bf16[32,3072]{1,0:T(8,128)(2,1)S(1)}) custom-call(bf16[64,3072]{1,0:T(8,128)(2,1)S(1)} %constant_dynamic-update-slice_fusion.mine_ref, bf16[64,3072]{1,0:T(8,128)(2,1)S(1)} %collective-permute-done.10.theirs_ref, bf16[3072,512]{1,0:T(8,128)(2,1)S(1)} %get-tuple-element.29.wq_ref, ...), custom_call_target="tpu_custom_call" | custom-call | tf_op jit(solution)/shard_map/pallas_call | solution.py:68
  42.2 0.2 collective-permute-start.11
  42.4 1.3 %collective-permute-done.11 = bf16[32,3072]{1,0:T(8,128)(2,1)S(1)} collective-permute-done((bf16[32,3072]{1,0:T(8,128)(2,1)S(1)}, bf16[32,3072]{1,0:T(8,128)(2,1)S(1)}, u32[]{:S(2)}, u32[]{:S(2)}) %collective-permute-start.11) | collective-permute-done | bytes 196640 | tf_op jit(solution)/shard_map/ppermute | solution.py:18
  43.7 0.7 %collective-permute-start.12 = (bf16[16,3072]{1,0:T(8,128)(2,1)S(1)}, bf16[16,3072]{1,0:T(8,128)(2,1)S(1)}, u32[]{:S(2)}, u32[]{:S(2)}) collective-permute-start(bf16[16,3072]{1,0:T(8,128)(2,1)S(1)} %slice.36), channel_id=1, source_target_pairs={{0,2},{1,3},{2,0},{3,1},{4,6},{5,7},{6,4},{7,5},{8,10},{9,11},{10,... | collective-permute-start | bytes 294920 | tf_op jit(solution)/shard_map/ppermute | solution.py:18
  44.5 4.2 %collective-permute-done.12 = bf16[16,3072]{1,0:T(8,128)(2,1)S(1)} collective-permute-done((bf16[16,3072]{1,0:T(8,128)(2,1)S(1)}, bf16[16,3072]{1,0:T(8,128)(2,1)S(1)}, u32[]{:S(2)}, u32[]{:S(2)}) %collective-permute-start.12) | collective-permute-done | bytes 98336 | tf_op jit(solution)/shard_map/ppermute | solution.py:18
  48.7 0.7 %maximum_bitcast_fusion = bf16[2,1,1,16,3072]{4,3,2,1,0:T(8,128)(2,1)} fusion(bf16[1,16,3072]{2,1,0:T(8,128)(2,1)S(1)} %fusion.4, bf16[1,16,3072]{2,1,0:T(8,128)(2,1)S(1)} %bitcast.18), kind=kLoop, calls=%fused_computation.11 | loop fusion | flops 98304 | bytes 393216 | tf_op jit(solution)/shard_map/broadcast_in_dim | solution.py:188
  (11 shorter events, 0.3 us)
Async XLA Ops:
  1.1 8.4 %collective-permute-start = (bf16[16,3072]{1,0:T(8,128)(2,1)S(1)}, bf16[16,3072]{1,0:T(8,128)(2,1)S(1)}, u32[]{:S(2)}, u32[]{:S(2)}) collective-permute-start(bf16[16,3072]{1,0:T(8,128)(2,1)S(1)} %get-tuple-element.25), channel_id=1, source_target_pairs={{0,2},{1,3},{2,0},{3,1},{4,6},{5,7},{6,4},{7,5},{8,10},{9,11},{10,... | collective-permute-start | bytes 294920 | tf_op jit(solution)/shard_map/ppermute | solution.py:18
  4.1 5.4 %collective-permute-start.1 = (bf16[16,3072]{1,0:T(8,128)(2,1)S(1)}, bf16[16,3072]{1,0:T(8,128)(2,1)S(1)}, u32[]{:S(2)}, u32[]{:S(2)}) collective-permute-start(bf16[16,3072]{1,0:T(8,128)(2,1)S(1)} %get-tuple-element.25), channel_id=1, source_target_pairs={{0,4},{1,5},{2,6},{3,7},{4,0},{5,1},{6,2},{7,3},{8,12},{9,13},{10,... | collective-permute-start | bytes 294920 | tf_op jit(solution)/shard_map/ppermute | solution.py:18
  5.6 5.5 %collective-permute-start.2 = (bf16[16,3072]{1,0:T(8,128)(2,1)S(1)}, bf16[16,3072]{1,0:T(8,128)(2,1)S(1)}, u32[]{:S(2)}, u32[]{:S(2)}) collective-permute-start(bf16[16,3072]{1,0:T(8,128)(2,1)S(1)} %get-tuple-element.25), channel_id=1, source_target_pairs={{0,6},{1,7},{2,4},{3,5},{4,2},{5,3},{6,0},{7,1},{8,14},{9,15},{10,... | collective-permute-start | bytes 294920 | tf_op jit(solution)/shard_map/ppermute | solution.py:18
  11.1 2.1 %collective-permute-start.3 = (bf16[64,3072]{1,0:T(8,128)(2,1)S(1)}, bf16[64,3072]{1,0:T(8,128)(2,1)S(1)}, u32[]{:S(2)}, u32[]{:S(2)}) collective-permute-start(bf16[64,3072]{1,0:T(8,128)(2,1)S(1)} %pad_maximum_fusion.mine_ref), channel_id=1, source_target_pairs={{0,1},{1,0},{2,3},{3,2},{4,5},{5,4},{6,7},{7,6},{8,9},{9,8},{10,11... | collective-permute-start | bytes 1179656 | tf_op jit(solution)/shard_map/ppermute | solution.py:18
  16.5 1.6 %collective-permute-start.4 = (bf16[32,3072]{1,0:T(8,128)(2,1)S(1)}, bf16[32,3072]{1,0:T(8,128)(2,1)S(1)}, u32[]{:S(2)}, u32[]{:S(2)}) collective-permute-start(bf16[32,3072]{1,0:T(8,128)(2,1)S(1)} %get-tuple-element.33), channel_id=1, source_target_pairs={{0,1},{1,0},{2,3},{3,2},{4,5},{5,4},{6,7},{7,6},{8,9},{9,8},{10,11... | collective-permute-start | bytes 589832 | tf_op jit(solution)/shard_map/ppermute | solution.py:18
  18.2 5.1 %collective-permute-start.5 = (bf16[16,3072]{1,0:T(8,128)(2,1)S(1)}, bf16[16,3072]{1,0:T(8,128)(2,1)S(1)}, u32[]{:S(2)}, u32[]{:S(2)}) collective-permute-start(bf16[16,3072]{1,0:T(8,128)(2,1)S(1)} %slice.37), channel_id=1, source_target_pairs={{0,2},{1,3},{2,0},{3,1},{4,6},{5,7},{6,4},{7,5},{8,10},{9,11},{10,... | collective-permute-start | bytes 294920 | tf_op jit(solution)/shard_map/ppermute | solution.py:18
  23.3 5.7 %collective-permute-start.6 = (bf16[16,3072]{1,0:T(8,128)(2,1)S(1)}, bf16[16,3072]{1,0:T(8,128)(2,1)S(1)}, u32[]{:S(2)}, u32[]{:S(2)}) collective-permute-start(bf16[16,3072]{1,0:T(8,128)(2,1)S(1)} %fusion.3), channel_id=1, source_target_pairs={{0,8},{8,16},{16,24},{1,9},{9,17},{17,25},{2,10},{10,18},{18,26},{... | collective-permute-start | bytes 294920 | tf_op jit(solution)/shard_map/ppermute | solution.py:23
  29.2 5.7 %collective-permute-start.7 = (bf16[16,3072]{1,0:T(8,128)(2,1)S(1)}, bf16[16,3072]{1,0:T(8,128)(2,1)S(1)}, u32[]{:S(2)}, u32[]{:S(2)}) collective-permute-start(bf16[16,3072]{1,0:T(8,128)(2,1)S(1)} %get-tuple-element.38), channel_id=1, source_target_pairs={{0,2},{1,3},{2,0},{3,1},{4,6},{5,7},{6,4},{7,5},{8,10},{9,11},{10,... | collective-permute-start | bytes 294920 | tf_op jit(solution)/shard_map/ppermute | solution.py:18
  30.2 4.8 %collective-permute-start.8 = (bf16[16,3072]{1,0:T(8,128)(2,1)S(1)}, bf16[16,3072]{1,0:T(8,128)(2,1)S(1)}, u32[]{:S(2)}, u32[]{:S(2)}) collective-permute-start(bf16[16,3072]{1,0:T(8,128)(2,1)S(1)} %get-tuple-element.38), channel_id=1, source_target_pairs={{0,4},{1,5},{2,6},{3,7},{4,0},{5,1},{6,2},{7,3},{8,12},{9,13},{10,... | collective-permute-start | bytes 294920 | tf_op jit(solution)/shard_map/ppermute | solution.py:18
  31.6 5.5 %collective-permute-start.9 = (bf16[16,3072]{1,0:T(8,128)(2,1)S(1)}, bf16[16,3072]{1,0:T(8,128)(2,1)S(1)}, u32[]{:S(2)}, u32[]{:S(2)}) collective-permute-start(bf16[16,3072]{1,0:T(8,128)(2,1)S(1)} %get-tuple-element.38), channel_id=1, source_target_pairs={{0,6},{1,7},{2,4},{3,5},{4,2},{5,3},{6,0},{7,1},{8,14},{9,15},{10,... | collective-permute-start | bytes 294920 | tf_op jit(solution)/shard_map/ppermute | solution.py:18
  37.1 1.8 %collective-permute-start.10 = (bf16[64,3072]{1,0:T(8,128)(2,1)S(1)}, bf16[64,3072]{1,0:T(8,128)(2,1)S(1)}, u32[]{:S(2)}, u32[]{:S(2)}) collective-permute-start(bf16[64,3072]{1,0:T(8,128)(2,1)S(1)} %constant_dynamic-update-slice_fusion.mine_ref), channel_id=1, source_target_pairs={{0,1},{1,0},{2,3},{3,2},{4,5},{5,4},{6,7},{7,6},{8,9},{9,8},{10,11... | collective-permute-start | bytes 1179656 | tf_op jit(solution)/shard_map/ppermute | solution.py:18
  42.2 1.5 %collective-permute-start.11 = (bf16[32,3072]{1,0:T(8,128)(2,1)S(1)}, bf16[32,3072]{1,0:T(8,128)(2,1)S(1)}, u32[]{:S(2)}, u32[]{:S(2)}) collective-permute-start(bf16[32,3072]{1,0:T(8,128)(2,1)S(1)} %get-tuple-element.40), channel_id=1, source_target_pairs={{0,1},{1,0},{2,3},{3,2},{4,5},{5,4},{6,7},{7,6},{8,9},{9,8},{10,11... | collective-permute-start | bytes 589832 | tf_op jit(solution)/shard_map/ppermute | solution.py:18
  43.7 4.9 %collective-permute-start.12 = (bf16[16,3072]{1,0:T(8,128)(2,1)S(1)}, bf16[16,3072]{1,0:T(8,128)(2,1)S(1)}, u32[]{:S(2)}, u32[]{:S(2)}) collective-permute-start(bf16[16,3072]{1,0:T(8,128)(2,1)S(1)} %slice.36), channel_id=1, source_target_pairs={{0,2},{1,3},{2,0},{3,1},{4,6},{5,7},{6,4},{7,5},{8,10},{9,11},{10,... | collective-permute-start | bytes 294920 | tf_op jit(solution)/shard_map/ppermute | solution.py:18

commit v4 on v3

--- a/solution.py
+++ b/solution.py
@@ -36,8 +36,8 @@
 def layer_kernel(tok, mine_ref, theirs_ref, wq_ref, wkv_ref, wo_ref, keep_ref, send_ref):
     half, depth = keep_ref.shape
     rows = 2 * half
-    own = jnp.concatenate([mine_ref[:half], theirs_ref[:half]], 0)
-    partner = jnp.concatenate([mine_ref[half:], theirs_ref[half:]], 0)
+    own = jnp.concatenate([mine_ref[half:], theirs_ref[half:]], 0)
+    partner = jnp.concatenate([mine_ref[:half], theirs_ref[:half]], 0)
 
     def project(left, right):
         return jnp.dot(left, right, preferred_element_type=jnp.float32).astype(jnp.bfloat16)
@@ -154,17 +154,16 @@
 def gathered(normed):
     lanes = lax.axis_size("lane")
     distances = [tower * lanes + 2 * k for tower in range(2) for k in range(lanes // 2)]
-    blocks = {d: swapped(normed, d) if d else normed for d in distances}
-    return jnp.concatenate([blocks[d] for d in distances], 0)
+    return jnp.concatenate([swapped(normed, d) if d else normed for d in reversed(distances)], 0)
 
 
 def reduced(state, keep, sent):
     tok = state.shape[0]
     total = keep + sent.astype(jnp.float32)
-    result = state.astype(jnp.float32) + total[:tok]
-    for k in range(1, lax.axis_size("lane") // 2):
-        share = total[k * tok : (k + 1) * tok].astype(jnp.bfloat16)
-        result = result + swapped(share, 2 * k).astype(jnp.float32)
+    blocks = list(reversed(jnp.split(total, keep.shape[0] // tok)))
+    result = state.astype(jnp.float32) + blocks[0]
+    for k in range(1, len(blocks)):
+        result = result + swapped(blocks[k].astype(jnp.bfloat16), 2 * k).astype(jnp.float32)
     return result.astype(jnp.bfloat16)
 
 

time: 49.6 us -> 48.3 us (0.974)
  waiting for transfers between devices: 19.9 us -> 18 us
  starting transfers between devices: 14.3 us -> 14.9 us
    ppermute x12, waiting for transfers between devices: 18.3 us -> 16.5 us  [swapped(): return lax.ppermute(value, BOTH, [(i, i ^ mask) for i in range(count)])]
    ppermute x12, starting transfers between devices: 10.8 us -> 11.3 us  [swapped(): return lax.ppermute(value, BOTH, [(i, i ^ mask) for i in range(count)])]
  transfers between devices with their start and end apart: 13 -> 13, of which waited for: 9 -> 10; matrix products, arithmetic and copies ran while one was open for 0% -> 0% of each run, Pallas kernels for 12% -> 12%
where the time goes in v4:
time: 48.3 us; the launch traced here: 48.1 us
  waiting for transfers between devices  18 us (37%)
  starting transfers between devices  14.9 us (31%)
  Pallas kernels  13.5 us (28%)
  other arithmetic  0.89 us (2%)
  between operations  0.78 us (2%)
    ppermute x12, waiting for transfers between devices, swapped(): return lax.ppermute(value, BOTH, [(i, i ^ mask) for i in range(count)])  16.5 us
    ppermute x12, starting transfers between devices, swapped(): return lax.ppermute(value, BOTH, [(i, i ^ mask) for i in range(count)])  11.3 us
    pallas_call x2, Pallas kernels, layer_part(): pl.pallas_call(functools.partial(layer_kernel, tok), out_shape=(jax.Shape...  6.49 us
    pallas_call x2, Pallas kernels, load(): pl.pallas_call(load_kernel, out_shape=tuple((pltpu.VMEM(a.shape, a.dtype)...  5.81 us
    ppermute x1, starting transfers between devices, handed_on(): lax.ppermute(value, 'section', [(s, s + 1) for s in range(count - 1)])  3.59 us
    ppermute x1, waiting for transfers between devices, handed_on(): lax.ppermute(value, 'section', [(s, s + 1) for s in range(count - 1)])  1.54 us
    pallas_call x1, Pallas kernels, entry(): pl.pallas_call(entry_kernel, out_shape=(pltpu.VMEM(state.shape, jnp.bfloa...  1.04 us
  transfers between devices with their start and end apart: 13, of which 10 were waited for; matrix products, arithmetic and copies ran while one was open for 0% of the time, Pallas kernels for 12%

profile of v4, /device:TPU:0, one launch (start us, length us, event | category | flops | bytes accessed | tf_op | source)
XLA Modules:
  0.0 48.1 jit_solution(13467040595869147383)
XLA Ops:
  0.0 1.0 %shard_map.73 = (bf16[16,3072]{1,0:T(8,128)(2,1)S(1)}, bf16[16,3072]{1,0:T(8,128)(2,1)S(1)}, f32[1,3072]{1,0:T(1,128)S(1)}) custom-call(bf16[16,3072]{1,0:T(8,128)(2,1)} %bitcast.19, f32[1,3072]{1,0:T(1,128)} %bitcast.20), custom_call_target="tpu_custom_call" | custom-call | tf_op jit(solution)/shard_map/pallas_call | solution.py:93
  1.1 4.0 %collective-permute-start = (bf16[16,3072]{1,0:T(8,128)(2,1)S(1)}, bf16[16,3072]{1,0:T(8,128)(2,1)S(1)}, u32[]{:S(2)}, u32[]{:S(2)}) collective-permute-start(bf16[16,3072]{1,0:T(8,128)(2,1)S(1)} %get-tuple-element.25), channel_id=1, source_target_pairs={{0,6},{1,7},{2,4},{3,5},{4,2},{5,3},{6,0},{7,1},{8,14},{9,15},{10,... | collective-permute-start | bytes 294920 | tf_op jit(solution)/shard_map/ppermute | solution.py:18
  5.0 0.5 %collective-permute-start.1 = (bf16[16,3072]{1,0:T(8,128)(2,1)S(1)}, bf16[16,3072]{1,0:T(8,128)(2,1)S(1)}, u32[]{:S(2)}, u32[]{:S(2)}) collective-permute-start(bf16[16,3072]{1,0:T(8,128)(2,1)S(1)} %get-tuple-element.25), channel_id=1, source_target_pairs={{0,4},{1,5},{2,6},{3,7},{4,0},{5,1},{6,2},{7,3},{8,12},{9,13},{10,... | collective-permute-start | bytes 294920 | tf_op jit(solution)/shard_map/ppermute | solution.py:18
  5.5 0.1 collective-permute-start.2
  5.7 3.8 %shard_map.74 = (bf16[3072,512]{1,0:T(8,128)(2,1)S(1)}, bf16[6144,512]{1,0:T(8,128)(2,1)S(1)}) custom-call(bf16[3072,512]{1,0:T(8,128)(2,1)} %bitcast.16, bf16[6144,512]{1,0:T(8,128)(2,1)} %bitcast.14), custom_call_target="tpu_custom_call" | custom-call | bytes 9437184 | tf_op jit(solution)/shard_map/pallas_call | solution.py:123
  9.5 0.0 collective-permute-done
  9.5 0.8 %collective-permute-done.1 = bf16[16,3072]{1,0:T(8,128)(2,1)S(1)} collective-permute-done((bf16[16,3072]{1,0:T(8,128)(2,1)S(1)}, bf16[16,3072]{1,0:T(8,128)(2,1)S(1)}, u32[]{:S(2)}, u32[]{:S(2)}) %collective-permute-start.1) | collective-permute-done | bytes 98336 | tf_op jit(solution)/shard_map/ppermute | solution.py:18
  10.2 0.0 collective-permute-done.2
  10.3 0.1 collective-permute-start.3
  10.4 2.0 %shard_map.75 = (bf16[512,3072]{1,0:T(8,128)(2,1)S(1)}, bf16[64,3072]{1,0:T(8,128)(2,1)S(1)}) custom-call(bf16[512,3072]{1,0:T(8,128)(2,1)} %bitcast.15, bf16[64,3072]{1,0:T(8,128)(2,1)} %bitcast.17), custom_call_target="tpu_custom_call" | custom-call | bytes 3538944 | tf_op jit(solution)/shard_map/pallas_call | solution.py:123
  12.4 0.0 collective-permute-done.3.theirs_ref
  12.4 3.2 %shard_map.76 = (f32[32,3072]{1,0:T(8,128)S(1)}, bf16[32,3072]{1,0:T(8,128)(2,1)S(1)}) custom-call(bf16[64,3072]{1,0:T(8,128)(2,1)S(1)} %pad_maximum_fusion.mine_ref, bf16[64,3072]{1,0:T(8,128)(2,1)S(1)} %collective-permute-done.3.theirs_ref, bf16[3072,512]{1,0:T(8,128)(2,1)S(1)} %get-tuple-element.29.wq_ref, ...), custom_call_target="tpu_custom_call" | custom-call | tf_op jit(solution)/shard_map/pallas_call | solution.py:68
  15.6 0.6 %collective-permute-start.4 = (bf16[32,3072]{1,0:T(8,128)(2,1)S(1)}, bf16[32,3072]{1,0:T(8,128)(2,1)S(1)}, u32[]{:S(2)}, u32[]{:S(2)}) collective-permute-start(bf16[32,3072]{1,0:T(8,128)(2,1)S(1)} %get-tuple-element.33), channel_id=1, source_target_pairs={{0,1},{1,0},{2,3},{3,2},{4,5},{5,4},{6,7},{7,6},{8,9},{9,8},{10,11... | collective-permute-start | bytes 589832 | tf_op jit(solution)/shard_map/ppermute | solution.py:18
  16.2 1.1 %collective-permute-done.4 = bf16[32,3072]{1,0:T(8,128)(2,1)S(1)} collective-permute-done((bf16[32,3072]{1,0:T(8,128)(2,1)S(1)}, bf16[32,3072]{1,0:T(8,128)(2,1)S(1)}, u32[]{:S(2)}, u32[]{:S(2)}) %collective-permute-start.4) | collective-permute-done | bytes 196640 | tf_op jit(solution)/shard_map/ppermute | solution.py:18
  17.3 1.5 %collective-permute-start.5 = (bf16[16,3072]{1,0:T(8,128)(2,1)S(1)}, bf16[16,3072]{1,0:T(8,128)(2,1)S(1)}, u32[]{:S(2)}, u32[]{:S(2)}) collective-permute-start(bf16[16,3072]{1,0:T(8,128)(2,1)S(1)} %split.37), channel_id=1, source_target_pairs={{0,2},{1,3},{2,0},{3,1},{4,6},{5,7},{6,4},{7,5},{8,10},{9,11},{10,... | collective-permute-start | bytes 294920 | tf_op jit(solution)/shard_map/ppermute | solution.py:18
  18.8 3.7 %collective-permute-done.5 = bf16[16,3072]{1,0:T(8,128)(2,1)S(1)} collective-permute-done((bf16[16,3072]{1,0:T(8,128)(2,1)S(1)}, bf16[16,3072]{1,0:T(8,128)(2,1)S(1)}, u32[]{:S(2)}, u32[]{:S(2)}) %collective-permute-start.5) | collective-permute-done | bytes 98336 | tf_op jit(solution)/shard_map/ppermute | solution.py:18
  22.5 3.6 %collective-permute-start.6 = (bf16[16,3072]{1,0:T(8,128)(2,1)S(1)}, bf16[16,3072]{1,0:T(8,128)(2,1)S(1)}, u32[]{:S(2)}, u32[]{:S(2)}) collective-permute-start(bf16[16,3072]{1,0:T(8,128)(2,1)S(1)} %fusion.3), channel_id=1, source_target_pairs={{0,8},{8,16},{16,24},{1,9},{9,17},{17,25},{2,10},{10,18},{18,26},{... | collective-permute-start | bytes 294920 | tf_op jit(solution)/shard_map/ppermute | solution.py:23
  26.7 1.5 %collective-permute-done.6.handed_ref = bf16[16,3072]{1,0:T(8,128)(2,1)S(1)} collective-permute-done((bf16[16,3072]{1,0:T(8,128)(2,1)S(1)}, bf16[16,3072]{1,0:T(8,128)(2,1)S(1)}, u32[]{:S(2)}, u32[]{:S(2)}) %collective-permute-start.6) | collective-permute-done | bytes 98336 | tf_op jit(solution)/shard_map/ppermute | solution.py:23
  28.3 0.1 shard_map.77
  28.4 2.3 %collective-permute-start.7 = (bf16[16,3072]{1,0:T(8,128)(2,1)S(1)}, bf16[16,3072]{1,0:T(8,128)(2,1)S(1)}, u32[]{:S(2)}, u32[]{:S(2)}) collective-permute-start(bf16[16,3072]{1,0:T(8,128)(2,1)S(1)} %get-tuple-element.38), channel_id=1, source_target_pairs={{0,6},{1,7},{2,4},{3,5},{4,2},{5,3},{6,0},{7,1},{8,14},{9,15},{10,... | collective-permute-start | bytes 294920 | tf_op jit(solution)/shard_map/ppermute | solution.py:18
  30.7 0.5 %collective-permute-start.8 = (bf16[16,3072]{1,0:T(8,128)(2,1)S(1)}, bf16[16,3072]{1,0:T(8,128)(2,1)S(1)}, u32[]{:S(2)}, u32[]{:S(2)}) collective-permute-start(bf16[16,3072]{1,0:T(8,128)(2,1)S(1)} %get-tuple-element.38), channel_id=1, source_target_pairs={{0,4},{1,5},{2,6},{3,7},{4,0},{5,1},{6,2},{7,3},{8,12},{9,13},{10,... | collective-permute-start | bytes 294920 | tf_op jit(solution)/shard_map/ppermute | solution.py:18
  31.2 0.7 %collective-permute-start.9 = (bf16[16,3072]{1,0:T(8,128)(2,1)S(1)}, bf16[16,3072]{1,0:T(8,128)(2,1)S(1)}, u32[]{:S(2)}, u32[]{:S(2)}) collective-permute-start(bf16[16,3072]{1,0:T(8,128)(2,1)S(1)} %get-tuple-element.38), channel_id=1, source_target_pairs={{0,2},{1,3},{2,0},{3,1},{4,6},{5,7},{6,4},{7,5},{8,10},{9,11},{10,... | collective-permute-start | bytes 294920 | tf_op jit(solution)/shard_map/ppermute | solution.py:18
  32.0 2.1 %collective-permute-done.7 = bf16[16,3072]{1,0:T(8,128)(2,1)S(1)} collective-permute-done((bf16[16,3072]{1,0:T(8,128)(2,1)S(1)}, bf16[16,3072]{1,0:T(8,128)(2,1)S(1)}, u32[]{:S(2)}, u32[]{:S(2)}) %collective-permute-start.7) | collective-permute-done | bytes 98336 | tf_op jit(solution)/shard_map/ppermute | solution.py:18
  34.1 1.2 %collective-permute-done.8 = bf16[16,3072]{1,0:T(8,128)(2,1)S(1)} collective-permute-done((bf16[16,3072]{1,0:T(8,128)(2,1)S(1)}, bf16[16,3072]{1,0:T(8,128)(2,1)S(1)}, u32[]{:S(2)}, u32[]{:S(2)}) %collective-permute-start.8) | collective-permute-done | bytes 98336 | tf_op jit(solution)/shard_map/ppermute | solution.py:18
  35.3 0.5 %collective-permute-done.9 = bf16[16,3072]{1,0:T(8,128)(2,1)S(1)} collective-permute-done((bf16[16,3072]{1,0:T(8,128)(2,1)S(1)}, bf16[16,3072]{1,0:T(8,128)(2,1)S(1)}, u32[]{:S(2)}, u32[]{:S(2)}) %collective-permute-start.9) | collective-permute-done | bytes 98336 | tf_op jit(solution)/shard_map/ppermute | solution.py:18
  35.9 0.1 collective-permute-start.10
  36.0 1.7 %collective-permute-done.10.theirs_ref = bf16[64,3072]{1,0:T(8,128)(2,1)S(1)} collective-permute-done((bf16[64,3072]{1,0:T(8,128)(2,1)S(1)}, bf16[64,3072]{1,0:T(8,128)(2,1)S(1)}, u32[]{:S(2)}, u32[]{:S(2)}) %collective-permute-start.10) | collective-permute-done | bytes 393248 | tf_op jit(solution)/shard_map/ppermute | solution.py:18
  37.7 3.2 %shard_map.78 = (f32[32,3072]{1,0:T(8,128)S(1)}, bf16[32,3072]{1,0:T(8,128)(2,1)S(1)}) custom-call(bf16[64,3072]{1,0:T(8,128)(2,1)S(1)} %constant_dynamic-update-slice_fusion.mine_ref, bf16[64,3072]{1,0:T(8,128)(2,1)S(1)} %collective-permute-done.10.theirs_ref, bf16[3072,512]{1,0:T(8,128)(2,1)S(1)} %get-tuple-element.29.wq_ref, ...), custom_call_target="tpu_custom_call" | custom-call | tf_op jit(solution)/shard_map/pallas_call | solution.py:68
  40.9 0.2 collective-permute-start.11
  41.1 1.3 %collective-permute-done.11 = bf16[32,3072]{1,0:T(8,128)(2,1)S(1)} collective-permute-done((bf16[32,3072]{1,0:T(8,128)(2,1)S(1)}, bf16[32,3072]{1,0:T(8,128)(2,1)S(1)}, u32[]{:S(2)}, u32[]{:S(2)}) %collective-permute-start.11) | collective-permute-done | bytes 196640 | tf_op jit(solution)/shard_map/ppermute | solution.py:18
  42.5 0.8 %collective-permute-start.12 = (bf16[16,3072]{1,0:T(8,128)(2,1)S(1)}, bf16[16,3072]{1,0:T(8,128)(2,1)S(1)}, u32[]{:S(2)}, u32[]{:S(2)}) collective-permute-start(bf16[16,3072]{1,0:T(8,128)(2,1)S(1)} %split.36), channel_id=1, source_target_pairs={{0,2},{1,3},{2,0},{3,1},{4,6},{5,7},{6,4},{7,5},{8,10},{9,11},{10,... | collective-permute-start | bytes 294920 | tf_op jit(solution)/shard_map/ppermute | solution.py:18
  43.3 4.1 %collective-permute-done.12 = bf16[16,3072]{1,0:T(8,128)(2,1)S(1)} collective-permute-done((bf16[16,3072]{1,0:T(8,128)(2,1)S(1)}, bf16[16,3072]{1,0:T(8,128)(2,1)S(1)}, u32[]{:S(2)}, u32[]{:S(2)}) %collective-permute-start.12) | collective-permute-done | bytes 98336 | tf_op jit(solution)/shard_map/ppermute | solution.py:18
  47.4 0.7 %maximum_bitcast_fusion = bf16[2,1,1,16,3072]{4,3,2,1,0:T(8,128)(2,1)} fusion(bf16[1,16,3072]{2,1,0:T(8,128)(2,1)S(1)} %fusion.4, bf16[1,16,3072]{2,1,0:T(8,128)(2,1)S(1)} %bitcast.18), kind=kLoop, calls=%fused_computation.11 | loop fusion | flops 98304 | bytes 393216 | tf_op jit(solution)/shard_map/broadcast_in_dim | solution.py:187
  (11 shorter events, 0.3 us)
Async XLA Ops:
  1.1 8.4 %collective-permute-start = (bf16[16,3072]{1,0:T(8,128)(2,1)S(1)}, bf16[16,3072]{1,0:T(8,128)(2,1)S(1)}, u32[]{:S(2)}, u32[]{:S(2)}) collective-permute-start(bf16[16,3072]{1,0:T(8,128)(2,1)S(1)} %get-tuple-element.25), channel_id=1, source_target_pairs={{0,6},{1,7},{2,4},{3,5},{4,2},{5,3},{6,0},{7,1},{8,14},{9,15},{10,... | collective-permute-start | bytes 294920 | tf_op jit(solution)/shard_map/ppermute | solution.py:18
  5.0 5.2 %collective-permute-start.1 = (bf16[16,3072]{1,0:T(8,128)(2,1)S(1)}, bf16[16,3072]{1,0:T(8,128)(2,1)S(1)}, u32[]{:S(2)}, u32[]{:S(2)}) collective-permute-start(bf16[16,3072]{1,0:T(8,128)(2,1)S(1)} %get-tuple-element.25), channel_id=1, source_target_pairs={{0,4},{1,5},{2,6},{3,7},{4,0},{5,1},{6,2},{7,3},{8,12},{9,13},{10,... | collective-permute-start | bytes 294920 | tf_op jit(solution)/shard_map/ppermute | solution.py:18
  5.5 4.7 %collective-permute-start.2 = (bf16[16,3072]{1,0:T(8,128)(2,1)S(1)}, bf16[16,3072]{1,0:T(8,128)(2,1)S(1)}, u32[]{:S(2)}, u32[]{:S(2)}) collective-permute-start(bf16[16,3072]{1,0:T(8,128)(2,1)S(1)} %get-tuple-element.25), channel_id=1, source_target_pairs={{0,2},{1,3},{2,0},{3,1},{4,6},{5,7},{6,4},{7,5},{8,10},{9,11},{10,... | collective-permute-start | bytes 294920 | tf_op jit(solution)/shard_map/ppermute | solution.py:18
  10.3 2.1 %collective-permute-start.3 = (bf16[64,3072]{1,0:T(8,128)(2,1)S(1)}, bf16[64,3072]{1,0:T(8,128)(2,1)S(1)}, u32[]{:S(2)}, u32[]{:S(2)}) collective-permute-start(bf16[64,3072]{1,0:T(8,128)(2,1)S(1)} %pad_maximum_fusion.mine_ref), channel_id=1, source_target_pairs={{0,1},{1,0},{2,3},{3,2},{4,5},{5,4},{6,7},{7,6},{8,9},{9,8},{10,11... | collective-permute-start | bytes 1179656 | tf_op jit(solution)/shard_map/ppermute | solution.py:18
  15.6 1.6 %collective-permute-start.4 = (bf16[32,3072]{1,0:T(8,128)(2,1)S(1)}, bf16[32,3072]{1,0:T(8,128)(2,1)S(1)}, u32[]{:S(2)}, u32[]{:S(2)}) collective-permute-start(bf16[32,3072]{1,0:T(8,128)(2,1)S(1)} %get-tuple-element.33), channel_id=1, source_target_pairs={{0,1},{1,0},{2,3},{3,2},{4,5},{5,4},{6,7},{7,6},{8,9},{9,8},{10,11... | collective-permute-start | bytes 589832 | tf_op jit(solution)/shard_map/ppermute | solution.py:18
  17.3 5.1 %collective-permute-start.5 = (bf16[16,3072]{1,0:T(8,128)(2,1)S(1)}, bf16[16,3072]{1,0:T(8,128)(2,1)S(1)}, u32[]{:S(2)}, u32[]{:S(2)}) collective-permute-start(bf16[16,3072]{1,0:T(8,128)(2,1)S(1)} %split.37), channel_id=1, source_target_pairs={{0,2},{1,3},{2,0},{3,1},{4,6},{5,7},{6,4},{7,5},{8,10},{9,11},{10,... | collective-permute-start | bytes 294920 | tf_op jit(solution)/shard_map/ppermute | solution.py:18
  22.5 5.8 %collective-permute-start.6 = (bf16[16,3072]{1,0:T(8,128)(2,1)S(1)}, bf16[16,3072]{1,0:T(8,128)(2,1)S(1)}, u32[]{:S(2)}, u32[]{:S(2)}) collective-permute-start(bf16[16,3072]{1,0:T(8,128)(2,1)S(1)} %fusion.3), channel_id=1, source_target_pairs={{0,8},{8,16},{16,24},{1,9},{9,17},{17,25},{2,10},{10,18},{18,26},{... | collective-permute-start | bytes 294920 | tf_op jit(solution)/shard_map/ppermute | solution.py:23
  28.4 5.6 %collective-permute-start.7 = (bf16[16,3072]{1,0:T(8,128)(2,1)S(1)}, bf16[16,3072]{1,0:T(8,128)(2,1)S(1)}, u32[]{:S(2)}, u32[]{:S(2)}) collective-permute-start(bf16[16,3072]{1,0:T(8,128)(2,1)S(1)} %get-tuple-element.38), channel_id=1, source_target_pairs={{0,6},{1,7},{2,4},{3,5},{4,2},{5,3},{6,0},{7,1},{8,14},{9,15},{10,... | collective-permute-start | bytes 294920 | tf_op jit(solution)/shard_map/ppermute | solution.py:18
  30.7 4.6 %collective-permute-start.8 = (bf16[16,3072]{1,0:T(8,128)(2,1)S(1)}, bf16[16,3072]{1,0:T(8,128)(2,1)S(1)}, u32[]{:S(2)}, u32[]{:S(2)}) collective-permute-start(bf16[16,3072]{1,0:T(8,128)(2,1)S(1)} %get-tuple-element.38), channel_id=1, source_target_pairs={{0,4},{1,5},{2,6},{3,7},{4,0},{5,1},{6,2},{7,3},{8,12},{9,13},{10,... | collective-permute-start | bytes 294920 | tf_op jit(solution)/shard_map/ppermute | solution.py:18
  31.2 4.6 %collective-permute-start.9 = (bf16[16,3072]{1,0:T(8,128)(2,1)S(1)}, bf16[16,3072]{1,0:T(8,128)(2,1)S(1)}, u32[]{:S(2)}, u32[]{:S(2)}) collective-permute-start(bf16[16,3072]{1,0:T(8,128)(2,1)S(1)} %get-tuple-element.38), channel_id=1, source_target_pairs={{0,2},{1,3},{2,0},{3,1},{4,6},{5,7},{6,4},{7,5},{8,10},{9,11},{10,... | collective-permute-start | bytes 294920 | tf_op jit(solution)/shard_map/ppermute | solution.py:18
  35.9 1.8 %collective-permute-start.10 = (bf16[64,3072]{1,0:T(8,128)(2,1)S(1)}, bf16[64,3072]{1,0:T(8,128)(2,1)S(1)}, u32[]{:S(2)}, u32[]{:S(2)}) collective-permute-start(bf16[64,3072]{1,0:T(8,128)(2,1)S(1)} %constant_dynamic-update-slice_fusion.mine_ref), channel_id=1, source_target_pairs={{0,1},{1,0},{2,3},{3,2},{4,5},{5,4},{6,7},{7,6},{8,9},{9,8},{10,11... | collective-permute-start | bytes 1179656 | tf_op jit(solution)/shard_map/ppermute | solution.py:18
  40.9 1.5 %collective-permute-start.11 = (bf16[32,3072]{1,0:T(8,128)(2,1)S(1)}, bf16[32,3072]{1,0:T(8,128)(2,1)S(1)}, u32[]{:S(2)}, u32[]{:S(2)}) collective-permute-start(bf16[32,3072]{1,0:T(8,128)(2,1)S(1)} %get-tuple-element.40), channel_id=1, source_target_pairs={{0,1},{1,0},{2,3},{3,2},{4,5},{5,4},{6,7},{7,6},{8,9},{9,8},{10,11... | collective-permute-start | bytes 589832 | tf_op jit(solution)/shard_map/ppermute | solution.py:18
  42.5 4.9 %collective-permute-start.12 = (bf16[16,3072]{1,0:T(8,128)(2,1)S(1)}, bf16[16,3072]{1,0:T(8,128)(2,1)S(1)}, u32[]{:S(2)}, u32[]{:S(2)}) collective-permute-start(bf16[16,3072]{1,0:T(8,128)(2,1)S(1)} %split.36), channel_id=1, source_target_pairs={{0,2},{1,3},{2,0},{3,1},{4,6},{5,7},{6,4},{7,5},{8,10},{9,11},{10,... | collective-permute-start | bytes 294920 | tf_op jit(solution)/shard_map/ppermute | solution.py:18

commit v5 on v4

v5 whole, which is shorter than its diff:
```python
import functools

import jax
import jax.numpy as jnp
from jax import lax
from jax.experimental import pallas as pl
from jax.experimental.pallas import tpu as pltpu
from jax.sharding import PartitionSpec as P

HEAD_DIM = 128
EPSILON = 1e-06
BOTH = ("tower", "lane")
PIECES = 4


def swapped(value, mask):
    count = lax.axis_size(BOTH)
    return lax.ppermute(value, BOTH, [(i, i ^ mask) for i in range(count)])


def climbed(value, hop):
    sections, lanes = lax.axis_size("section"), lax.axis_size("lane")
    results = []
    for climbs in range(2):
        pairs = []
        for s in range(sections):
            for lane in range(lanes):
                to, target = (s + 1, lane ^ hop) if lane % 2 == climbs else (s - 1, lane)
                if not 0 <= to < sections:
                    to, target = s, lane ^ 1
                pairs.append((s * lanes + lane, to * lanes + target))
        results.append(lax.ppermute(value, ("section", "lane"), pairs))
    return results


def in_hbm(*arrays):
    return [pltpu.with_memory_space_constraint(a, pltpu.HBM) for a in arrays]


def normalized(state, gain):
    wide = state.astype(jnp.float32)
    scale = lax.rsqrt(jnp.mean(wide * wide, -1, keepdims=True) + EPSILON)
    return (wide * scale * gain).astype(jnp.bfloat16)


def project(left, right):
    return jnp.dot(left, right, preferred_element_type=jnp.float32).astype(jnp.bfloat16)


def keyval_kernel(mine_ref, theirs_ref, wkv_ref, keys_ref, values_ref):
    depth = mine_ref.shape[1]
    partner = jnp.concatenate([mine_ref[...], theirs_ref[...]], 0)
    keys_ref[...] = project(partner, wkv_ref[:depth])
    values_ref[...] = project(partner, wkv_ref[depth:])


def attend_kernel(tok, mine_ref, theirs_ref, keys_ref, values_ref, wq_ref, wo_ref, keep_ref, send_ref):
    half = keep_ref.shape[0]
    rows = 2 * half
    query = project(jnp.concatenate([mine_ref[...], theirs_ref[...]], 0), wq_ref[...])
    row_clip = lax.broadcasted_iota(jnp.int32, (rows, rows), 0) // tok
    col_clip = lax.broadcasted_iota(jnp.int32, (rows, rows), 1) // tok
    same_clip = row_clip == col_clip
    mixed = []
    for start in range(0, query.shape[1], HEAD_DIM):
        head = slice(start, start + HEAD_DIM)
        scores = lax.dot_general(
            query[:, head], keys_ref[:, head], (((1,), (1,)), ((), ())), preferred_element_type=jnp.float32
        ) * (HEAD_DIM**-0.5)
        scores = jnp.where(same_clip, scores, -jnp.inf)
        weights = jnp.exp(scores - jnp.max(scores, -1, keepdims=True))
        weights = weights / jnp.sum(weights, -1, keepdims=True)
        mixed.append(project(weights.astype(jnp.bfloat16), values_ref[:, head]))
    part = jnp.dot(jnp.concatenate(mixed, 1), wo_ref[...], preferred_element_type=jnp.float32)
    keep_ref[...] = part[:half]
    send_ref[...] = part[half:].astype(jnp.bfloat16)


def in_vmem(*arrays):
    return [pltpu.with_memory_space_constraint(a, pltpu.VMEM) for a in arrays]


def on_chip(kernel, outs, *arrays, flops=0):
    size = sum(a.size * a.dtype.itemsize for a in arrays)
    return pl.pallas_call(
        kernel,
        out_shape=tuple(jax.ShapeDtypeStruct(shape, dtype) for shape, dtype in outs),
        in_specs=[pl.BlockSpec(memory_space=pltpu.VMEM)] * len(arrays),
        out_specs=(pl.BlockSpec(memory_space=pltpu.VMEM),) * len(outs),
        cost_estimate=pl.CostEstimate(flops=flops, bytes_accessed=size, transcendentals=0),
        compiler_params=pltpu.CompilerParams(vmem_limit_bytes=16 << 20),
    )(*arrays)


def layer_part(own, partner, weights, tok):
    wq, wkv, wo = weights[0], *in_vmem(weights[1]), weights[2]
    (half, width), head_cols = own.shape, wq.shape[1]
    partner_theirs = swapped(partner, 1)
    own_theirs = swapped(own, 1)
    pushed = 2 * 256 * width * head_cols
    keys, values = on_chip(
        keyval_kernel,
        [((2 * half, head_cols), jnp.bfloat16)] * 2,
        partner, partner_theirs, wkv,
        flops=2 * pushed,
    )
    return on_chip(
        functools.partial(attend_kernel, tok),
        [((half, width), jnp.float32), ((half, width), jnp.bfloat16)],
        own, own_theirs, keys, values, wq, wo,
        flops=3 * pushed,
    )


def sum_kernel(state_ref, keep_ref, sent_ref, own_ref, *out_refs):
    tok = state_ref.shape[0]
    total = keep_ref[...] + sent_ref[...].astype(jnp.float32)
    own_ref[...] = state_ref[...].astype(jnp.float32) + total[-tok:]
    for k, out_ref in enumerate(out_refs, 1):
        start = total.shape[0] - (k + 1) * tok
        out_ref[...] = total[start : start + tok].astype(jnp.bfloat16)


def entry_kernel(x_ref, gain_ref, normed_ref, x_out, gain_out, sems):
    copies = [
        pltpu.make_async_copy(x_ref, x_out, sems.at[0]),
        pltpu.make_async_copy(gain_ref, gain_out, sems.at[1]),
    ]
    for copy in copies:
        copy.start()
    for copy in copies:
        copy.wait()
    normed_ref[...] = normalized(x_out[...], gain_out[0])


def entry(state, gain):
    return pl.pallas_call(
        entry_kernel,
        out_shape=(
            pltpu.VMEM(state.shape, jnp.bfloat16),
            pltpu.VMEM(state.shape, state.dtype),
            pltpu.VMEM(gain.shape, gain.dtype),
        ),
        in_specs=[pl.BlockSpec(memory_space=pltpu.HBM)] * 2,
        out_specs=(pl.BlockSpec(memory_space=pltpu.VMEM),) * 3,
        scratch_shapes=[pltpu.SemaphoreType.DMA((2,))],
        compiler_params=pltpu.CompilerParams(vmem_limit_bytes=16 << 20),
    )(*in_hbm(state, gain))


def load_kernel(*refs):
    *refs, sems = refs
    count = len(refs) // 2
    copies = []
    for source, target in zip(refs[:count], refs[count:]):
        pieces = PIECES if source.shape[0] % (16 * PIECES) == 0 else 1
        rows = source.shape[0] // pieces
        for i in range(pieces):
            here = pl.ds(i * rows, rows)
            copies.append(pltpu.make_async_copy(source.at[here], target.at[here], sems.at[len(copies)]))
            copies[-1].start()
    for copy in copies:
        copy.wait()


def load(*arrays):
    return pl.pallas_call(
        load_kernel,
        out_shape=tuple(pltpu.VMEM(a.shape, a.dtype) for a in arrays),
        in_specs=[pl.BlockSpec(memory_space=pltpu.HBM)] * len(arrays),
        out_specs=(pl.BlockSpec(memory_space=pltpu.VMEM),) * len(arrays),
        scratch_shapes=[pltpu.SemaphoreType.DMA((PIECES * len(arrays),))],
        cost_estimate=pl.CostEstimate(
            flops=0, bytes_accessed=sum(a.size * a.dtype.itemsize for a in arrays), transcendentals=0
        ),
        compiler_params=pltpu.CompilerParams(vmem_limit_bytes=16 << 20),
    )(*in_hbm(*arrays))


def second_kernel(section_ref, lane_ref, offset_ref, fresh_ref, gain_ref, *refs):
    *handed_refs, state_ref, normed_ref = refs
    tok = state_ref.shape[0]
    even = lane_ref[0] % 2 == 0
    handed = 0.0
    for even_ref, odd_ref in zip(handed_refs[::2], handed_refs[1::2]):
        handed = handed + jnp.where(even, even_ref[...], odd_ref[...]).astype(jnp.float32)
    picked = fresh_ref[pl.ds(pl.multiple_of(offset_ref[0] * tok, tok), tok)]
    state = jnp.where(section_ref[0] == 0, picked, handed.astype(jnp.bfloat16))
    state_ref[...] = state
    normed_ref[...] = normalized(state, gain_ref[0])


def second_entry(section, lane, offsets, fresh, gain, handed):
    shape = handed[0].shape
    return pl.pallas_call(
        second_kernel,
        out_shape=(pltpu.VMEM(shape, jnp.bfloat16),) * 2,
        in_specs=[pl.BlockSpec(memory_space=pltpu.SMEM)] * 3
        + [pl.BlockSpec(memory_space=pltpu.VMEM)] * (2 + len(handed)),
        out_specs=(pl.BlockSpec(memory_space=pltpu.VMEM),) * 2,
        compiler_params=pltpu.CompilerParams(vmem_limit_bytes=16 << 20),
    )(section, lane, offsets, fresh, gain, *handed)


def gathered(normed):
    lanes = lax.axis_size("lane")
    towers = [[tower * lanes + 2 * k for k in reversed(range(lanes // 2))] for tower in range(2)]
    partner = [swapped(normed, d) for d in towers[1]]
    own = [swapped(normed, d) if d else normed for d in towers[0]]
    return jnp.concatenate(own, 0), jnp.concatenate(partner, 0)


def summed(state, keep, send):
    shape = state.shape
    outs = [(shape, jnp.float32)] + [(shape, jnp.bfloat16)] * (keep.shape[0] // shape[0] - 1)
    own, *others = on_chip(sum_kernel, outs, *in_vmem(state), keep, swapped(send, 1))
    return own, others


def completed(own, others):
    for k, other in enumerate(others, 1):
        own = own + swapped(other, 2 * k).astype(jnp.float32)
    return own.astype(jnp.bfloat16)


def index_of(axis):
    return jnp.reshape(lax.axis_index(axis), (1,)).astype(jnp.int32)


def shards(in_flight, fresh_batches, offsets, norm_gain, w_query, w_keyval, w_out):
    normed, state, gain = entry(in_flight[0, 0], norm_gain[0])
    tok = state.shape[0]
    normed, section, lane = lax.optimization_barrier((normed, index_of("section"), index_of("lane")))
    (wkv,) = load(w_keyval.reshape(-1, w_keyval.shape[-1]))
    own, partner, wkv = lax.optimization_barrier((*gathered(normed), wkv))
    wq, wo, fresh = w_query[0, 0], w_out[0, 0], fresh_batches.reshape(-1, fresh_batches.shape[-1])
    weights = (wq, wkv, wo)
    first_sum, others = summed(state, *layer_part(own, partner, weights, tok))
    sums = [first_sum.astype(jnp.bfloat16), *others]
    handed = [part for k in reversed(range(len(sums))) for part in climbed(sums[k], 2 * k)]
    state, normed = second_entry(section, lane, offsets, fresh, gain, handed)
    own, partner = gathered(normed)
    own, others = lax.optimization_barrier((own, others))
    keep, send, first_sum = lax.optimization_barrier((*layer_part(own, partner, weights, tok), first_sum))
    first = completed(first_sum, others)
    keep, send, first = lax.optimization_barrier((keep, send, first))
    second = completed(*summed(state, keep, send))
    return jnp.stack([first, second])[:, None, None]


def solution(mesh):
    placed = (
        P("section", "tower", "lane", None),
        P(None, "tower", "lane", None),
        P("lane"),
        P("section", "tower", None),
        P("section", "tower", None, "lane"),
        P("section", "tower", None, None, "lane"),
        P("section", "tower", "lane", None),
    )
    return jax.shard_map(
        shards,
        mesh=mesh,
        in_specs=placed,
        out_specs=P(None, "section", "tower", "lane", None),
        check_vma=False,
    )
```

time: 48.3 us -> 45.8 us (0.948)
  Pallas kernels: 13.5 us -> 11.1 us
  starting transfers between devices: 14.9 us -> 17 us
  waiting for transfers between devices: 18 us -> 16 us
    ppermute x12 -> x14, waiting for transfers between devices: 16.5 us -> 12 us  [swapped(): return lax.ppermute(value, BOTH, [(i, i ^ mask) for i in range(count)])]
    pallas_call x2 -> x1, Pallas kernels: 5.81 us -> 2.87 us  [load(): pl.pallas_call(load_kernel, out_shape=tuple((pltpu.VMEM(a.shape, a.dtype)...]
    ppermute x1 -> x4, waiting for transfers between devices: 1.54 us -> 3.95 us  [climbed(): results.append(lax.ppermute(value, ('section', 'lane'), pairs))]
    ppermute x1 -> x4, starting transfers between devices: 3.59 us -> 4.67 us  [climbed(): results.append(lax.ppermute(value, ('section', 'lane'), pairs))]
    ppermute x12 -> x14, starting transfers between devices: 11.3 us -> 12.3 us  [swapped(): return lax.ppermute(value, BOTH, [(i, i ^ mask) for i in range(count)])]
    pallas_call x3 -> x7, Pallas kernels: 6.62 us -> 7.16 us  [the longest x6 6.99 us: on_chip(): pl.pallas_call(kernel, out_shape=tuple((jax.ShapeDtypeStruct(shape, dtype...]
  transfers between devices with their start and end apart: 13 -> 18, of which waited for: 10 -> 12; matrix products, arithmetic and copies ran while one was open for 0% -> 0% of each run, Pallas kernels for 12% -> 16%
where the time goes in v5:
time: 45.8 us; the launch traced here: 45.7 us
  starting transfers between devices  17 us (37%)
  waiting for transfers between devices  16 us (35%)
  Pallas kernels  11.1 us (24%)
  between operations  0.85 us (2%)
  other arithmetic  0.79 us (2%)
    ppermute x14, starting transfers between devices, swapped(): return lax.ppermute(value, BOTH, [(i, i ^ mask) for i in range(count)])  12.3 us
    ppermute x14, waiting for transfers between devices, swapped(): return lax.ppermute(value, BOTH, [(i, i ^ mask) for i in range(count)])  12 us
    pallas_call x6, Pallas kernels, on_chip(): pl.pallas_call(kernel, out_shape=tuple((jax.ShapeDtypeStruct(shape, dtype...  6.99 us
    ppermute x4, starting transfers between devices, climbed(): results.append(lax.ppermute(value, ('section', 'lane'), pairs))  4.67 us
    ppermute x4, waiting for transfers between devices, climbed(): results.append(lax.ppermute(value, ('section', 'lane'), pairs))  3.95 us
    pallas_call x1, Pallas kernels, load(): pl.pallas_call(load_kernel, out_shape=tuple((pltpu.VMEM(a.shape, a.dtype)...  2.87 us
    pallas_call x1, Pallas kernels, entry(): pl.pallas_call(entry_kernel, out_shape=(pltpu.VMEM(state.shape, jnp.bfloa...  1.04 us
  transfers between devices with their start and end apart: 18, of which 12 were waited for; matrix products, arithmetic and copies ran while one was open for 0% of the time, Pallas kernels for 16%

profile of v5, /device:TPU:0, one launch (start us, length us, event | category | flops | bytes accessed | tf_op | source)
XLA Modules:
  0.0 45.7 jit_solution(12023740291038505908)
XLA Ops:
  0.0 1.0 %shard_map.73 = (bf16[16,3072]{1,0:T(8,128)(2,1)S(1)}, bf16[16,3072]{1,0:T(8,128)(2,1)S(1)}, f32[1,3072]{1,0:T(1,128)S(1)}) custom-call(bf16[16,3072]{1,0:T(8,128)(2,1)} %bitcast.22, f32[1,3072]{1,0:T(1,128)} %bitcast.23), custom_call_target="tpu_custom_call" | custom-call | tf_op jit(solution)/shard_map/pallas_call | solution.py:137
  1.1 3.0 %collective-permute-start = (bf16[16,3072]{1,0:T(8,128)(2,1)S(1)}, bf16[16,3072]{1,0:T(8,128)(2,1)S(1)}, u32[]{:S(2)}, u32[]{:S(2)}) collective-permute-start(bf16[16,3072]{1,0:T(8,128)(2,1)S(1)} %get-tuple-element.41), channel_id=1, source_target_pairs={{0,2},{1,3},{2,0},{3,1},{4,6},{5,7},{6,4},{7,5},{8,10},{9,11},{10,... | collective-permute-start | bytes 294920 | tf_op jit(solution)/shard_map/ppermute | solution.py:18
  4.1 1.4 %collective-permute-start.1 = (bf16[16,3072]{1,0:T(8,128)(2,1)S(1)}, bf16[16,3072]{1,0:T(8,128)(2,1)S(1)}, u32[]{:S(2)}, u32[]{:S(2)}) collective-permute-start(bf16[16,3072]{1,0:T(8,128)(2,1)S(1)} %get-tuple-element.41), channel_id=1, source_target_pairs={{0,6},{1,7},{2,4},{3,5},{4,2},{5,3},{6,0},{7,1},{8,14},{9,15},{10,... | collective-permute-start | bytes 294920 | tf_op jit(solution)/shard_map/ppermute | solution.py:18
  5.5 0.1 collective-permute-start.2
  5.6 2.9 %shard_map.74.wkv_ref = bf16[6144,512]{1,0:T(8,128)(2,1)S(1)} custom-call(bf16[6144,512]{1,0:T(8,128)(2,1)} %bitcast.20), custom_call_target="tpu_custom_call" | custom-call | bytes 6291456 | tf_op jit(solution)/shard_map/pallas_call | solution.py:167
  8.5 0.0 copy-start.1
  8.5 0.0 copy-start.2
  8.5 0.0 collective-permute-done
  8.6 1.9 %collective-permute-done.1 = bf16[16,3072]{1,0:T(8,128)(2,1)S(1)} collective-permute-done((bf16[16,3072]{1,0:T(8,128)(2,1)S(1)}, bf16[16,3072]{1,0:T(8,128)(2,1)S(1)}, u32[]{:S(2)}, u32[]{:S(2)}) %collective-permute-start.1) | collective-permute-done | bytes 98336 | tf_op jit(solution)/shard_map/ppermute | solution.py:18
  10.4 0.0 collective-permute-done.2
  10.5 0.1 collective-permute-start.4
  10.5 0.5 %collective-permute-start.3 = (bf16[32,3072]{1,0:T(8,128)(2,1)S(1)}, bf16[32,3072]{1,0:T(8,128)(2,1)S(1)}, u32[]{:S(2)}, u32[]{:S(2)}) collective-permute-start(bf16[32,3072]{1,0:T(8,128)(2,1)S(1)} %pad_maximum_fusion.mine_ref), channel_id=1, source_target_pairs={{0,1},{1,0},{2,3},{3,2},{4,5},{5,4},{6,7},{7,6},{8,9},{9,8},{10,11... | collective-permute-start | bytes 589832 | tf_op jit(solution)/shard_map/ppermute | solution.py:18
  11.0 0.9 %collective-permute-done.4.theirs_ref = bf16[32,3072]{1,0:T(8,128)(2,1)S(1)} collective-permute-done((bf16[32,3072]{1,0:T(8,128)(2,1)S(1)}, bf16[32,3072]{1,0:T(8,128)(2,1)S(1)}, u32[]{:S(2)}, u32[]{:S(2)}) %collective-permute-start.4) | collective-permute-done | bytes 196640 | tf_op jit(solution)/shard_map/ppermute | solution.py:18
  12.0 1.2 %shard_map.75 = (bf16[64,512]{1,0:T(8,128)(2,1)S(1)}, bf16[64,512]{1,0:T(8,128)(2,1)S(1)}) custom-call(bf16[32,3072]{1,0:T(8,128)(2,1)S(1)} %pad_maximum_fusion.1.mine_ref, bf16[32,3072]{1,0:T(8,128)(2,1)S(1)} %collective-permute-done.4.theirs_ref, bf16[6144,512]{1,0:T(8,128)(2,1)S(1)} %shard_map.74.wkv_ref), custom_call_target="tpu_custom_call" | custom-call | flops 1610612736 | bytes 6684672 | tf_op jit(solution)/shard_map/pallas_call | solution.py:85
  13.2 0.0 copy-start
  13.2 0.0 collective-permute-done.3.theirs_ref
  13.2 0.0 copy-done.1
  13.2 0.0 copy-done.2
  13.2 2.3 %shard_map.76 = (f32[32,3072]{1,0:T(8,128)S(1)}, bf16[32,3072]{1,0:T(8,128)(2,1)S(1)}) custom-call(bf16[32,3072]{1,0:T(8,128)(2,1)S(1)} %pad_maximum_fusion.mine_ref, bf16[32,3072]{1,0:T(8,128)(2,1)S(1)} %collective-permute-done.3.theirs_ref, bf16[64,512]{1,0:T(8,128)(2,1)S(1)} %get-tuple-element.45.keys_ref, ...), custom_call_target="tpu_custom_call" | custom-call | flops 2415919104 | bytes 6815744 | tf_op jit(solution)/shard_map/pallas_call | solution.py:85
  15.5 0.2 collective-permute-start.5
  15.7 1.3 %collective-permute-done.5.sent_ref = bf16[32,3072]{1,0:T(8,128)(2,1)S(1)} collective-permute-done((bf16[32,3072]{1,0:T(8,128)(2,1)S(1)}, bf16[32,3072]{1,0:T(8,128)(2,1)S(1)}, u32[]{:S(2)}, u32[]{:S(2)}) %collective-permute-start.5) | collective-permute-done | bytes 196640 | tf_op jit(solution)/shard_map/ppermute | solution.py:18
  17.0 0.1 shard_map.77
  17.1 1.7 %collective-permute-start.8 = (bf16[16,3072]{1,0:T(8,128)(2,1)S(1)}, bf16[16,3072]{1,0:T(8,128)(2,1)S(1)}, u32[]{:S(2)}, u32[]{:S(2)}) collective-permute-start(bf16[16,3072]{1,0:T(8,128)(2,1)S(1)} %convert_element_type.15), channel_id=1, source_target_pairs={{0,8},{1,0},{2,10},{3,2},{8,16},{9,1},{10,18},{11,3},{16,24},{17,9... | collective-permute-start | bytes 294920 | tf_op jit(solution)/shard_map/ppermute | solution.py:32
  18.7 0.0 collective-permute-start.9
  18.7 3.0 %collective-permute-start.6 = (bf16[16,3072]{1,0:T(8,128)(2,1)S(1)}, bf16[16,3072]{1,0:T(8,128)(2,1)S(1)}, u32[]{:S(2)}, u32[]{:S(2)}) collective-permute-start(bf16[16,3072]{1,0:T(8,128)(2,1)S(1)} %get-tuple-element.60), channel_id=1, source_target_pairs={{0,10},{1,0},{2,8},{3,2},{8,18},{9,1},{10,16},{11,3},{16,26},{17,9... | collective-permute-start | bytes 294920 | tf_op jit(solution)/shard_map/ppermute | solution.py:32
  21.7 0.0 collective-permute-start.7
  22.4 0.0 collective-permute-done.8.refs_2_
  22.4 1.0 %collective-permute-done.9.refs_3_ = bf16[16,3072]{1,0:T(8,128)(2,1)S(1)} collective-permute-done((bf16[16,3072]{1,0:T(8,128)(2,1)S(1)}, bf16[16,3072]{1,0:T(8,128)(2,1)S(1)}, u32[]{:S(2)}, u32[]{:S(2)}) %collective-permute-start.9) | collective-permute-done | bytes 98336 | tf_op jit(solution)/shard_map/ppermute | solution.py:32
  23.4 0.6 %collective-permute-done.6.refs_0_ = bf16[16,3072]{1,0:T(8,128)(2,1)S(1)} collective-permute-done((bf16[16,3072]{1,0:T(8,128)(2,1)S(1)}, bf16[16,3072]{1,0:T(8,128)(2,1)S(1)}, u32[]{:S(2)}, u32[]{:S(2)}) %collective-permute-start.6) | collective-permute-done | bytes 98336 | tf_op jit(solution)/shard_map/ppermute | solution.py:32
  23.9 2.4 %collective-permute-done.7.refs_1_ = bf16[16,3072]{1,0:T(8,128)(2,1)S(1)} collective-permute-done((bf16[16,3072]{1,0:T(8,128)(2,1)S(1)}, bf16[16,3072]{1,0:T(8,128)(2,1)S(1)}, u32[]{:S(2)}, u32[]{:S(2)}) %collective-permute-start.7) | collective-permute-done | bytes 98336 | tf_op jit(solution)/shard_map/ppermute | solution.py:32
  26.3 0.0 copy-done
  26.3 0.2 shard_map.78
  26.5 1.3 %collective-permute-start.12 = (bf16[16,3072]{1,0:T(8,128)(2,1)S(1)}, bf16[16,3072]{1,0:T(8,128)(2,1)S(1)}, u32[]{:S(2)}, u32[]{:S(2)}) collective-permute-start(bf16[16,3072]{1,0:T(8,128)(2,1)S(1)} %get-tuple-element.51), channel_id=1, source_target_pairs={{0,6},{1,7},{2,4},{3,5},{4,2},{5,3},{6,0},{7,1},{8,14},{9,15},{10,... | collective-permute-start | bytes 294920 | tf_op jit(solution)/shard_map/ppermute | solution.py:18
  27.9 0.7 %collective-permute-start.13 = (bf16[16,3072]{1,0:T(8,128)(2,1)S(1)}, bf16[16,3072]{1,0:T(8,128)(2,1)S(1)}, u32[]{:S(2)}, u32[]{:S(2)}) collective-permute-start(bf16[16,3072]{1,0:T(8,128)(2,1)S(1)} %get-tuple-element.51), channel_id=1, source_target_pairs={{0,4},{1,5},{2,6},{3,7},{4,0},{5,1},{6,2},{7,3},{8,12},{9,13},{10,... | collective-permute-start | bytes 294920 | tf_op jit(solution)/shard_map/ppermute | solution.py:18
  28.6 1.5 %collective-permute-start.10 = (bf16[16,3072]{1,0:T(8,128)(2,1)S(1)}, bf16[16,3072]{1,0:T(8,128)(2,1)S(1)}, u32[]{:S(2)}, u32[]{:S(2)}) collective-permute-start(bf16[16,3072]{1,0:T(8,128)(2,1)S(1)} %get-tuple-element.51), channel_id=1, source_target_pairs={{0,2},{1,3},{2,0},{3,1},{4,6},{5,7},{6,4},{7,5},{8,10},{9,11},{10,... | collective-permute-start | bytes 294920 | tf_op jit(solution)/shard_map/ppermute | solution.py:18
  30.1 2.0 %collective-permute-done.12 = bf16[16,3072]{1,0:T(8,128)(2,1)S(1)} collective-permute-done((bf16[16,3072]{1,0:T(8,128)(2,1)S(1)}, bf16[16,3072]{1,0:T(8,128)(2,1)S(1)}, u32[]{:S(2)}, u32[]{:S(2)}) %collective-permute-start.12) | collective-permute-done | bytes 98336 | tf_op jit(solution)/shard_map/ppermute | solution.py:18
  32.1 0.4 collective-permute-done.13
  32.5 0.1 collective-permute-start.14
  32.6 0.6 %collective-permute-done.10 = bf16[16,3072]{1,0:T(8,128)(2,1)S(1)} collective-permute-done((bf16[16,3072]{1,0:T(8,128)(2,1)S(1)}, bf16[16,3072]{1,0:T(8,128)(2,1)S(1)}, u32[]{:S(2)}, u32[]{:S(2)}) %collective-permute-start.10) | collective-permute-done | bytes 98336 | tf_op jit(solution)/shard_map/ppermute | solution.py:18
  33.2 0.1 collective-permute-start.11
  33.3 1.6 %collective-permute-start.15 = (bf16[16,3072]{1,0:T(8,128)(2,1)S(1)}, bf16[16,3072]{1,0:T(8,128)(2,1)S(1)}, u32[]{:S(2)}, u32[]{:S(2)}) collective-permute-start(bf16[16,3072]{1,0:T(8,128)(2,1)S(1)} %get-tuple-element.60), channel_id=1, source_target_pairs={{0,2},{1,3},{2,0},{3,1},{4,6},{5,7},{6,4},{7,5},{8,10},{9,11},{10,... | collective-permute-start | bytes 294920 | tf_op jit(solution)/shard_map/ppermute | solution.py:18
  34.9 0.0 collective-permute-done.14.theirs_ref
  34.9 1.2 %shard_map.79 = (bf16[64,512]{1,0:T(8,128)(2,1)S(1)}, bf16[64,512]{1,0:T(8,128)(2,1)S(1)}) custom-call(bf16[32,3072]{1,0:T(8,128)(2,1)S(1)} %constant_dynamic-update-slice_fusion.mine_ref, bf16[32,3072]{1,0:T(8,128)(2,1)S(1)} %collective-permute-done.14.theirs_ref, bf16[6144,512]{1,0:T(8,128)(2,1)S(1)} %shard_map.74.wkv_ref), custom_call_target="tpu_custom_call" | custom-call | flops 1610612736 | bytes 6684672 | tf_op jit(solution)/shard_map/pallas_call | solution.py:85
  36.1 0.0 collective-permute-done.11.theirs_ref
  36.1 2.3 %shard_map.80 = (f32[32,3072]{1,0:T(8,128)S(1)}, bf16[32,3072]{1,0:T(8,128)(2,1)S(1)}) custom-call(bf16[32,3072]{1,0:T(8,128)(2,1)S(1)} %pad_maximum_fusion.2.mine_ref, bf16[32,3072]{1,0:T(8,128)(2,1)S(1)} %collective-permute-done.11.theirs_ref, bf16[64,512]{1,0:T(8,128)(2,1)S(1)} %get-tuple-element.53.keys_ref, ...), custom_call_target="tpu_custom_call" | custom-call | flops 2415919104 | bytes 6815744 | tf_op jit(solution)/shard_map/pallas_call | solution.py:85
  38.3 0.2 collective-permute-done.15
  38.5 0.1 collective-permute-start.16
  38.6 1.4 %collective-permute-done.16.sent_ref = bf16[32,3072]{1,0:T(8,128)(2,1)S(1)} collective-permute-done((bf16[32,3072]{1,0:T(8,128)(2,1)S(1)}, bf16[32,3072]{1,0:T(8,128)(2,1)S(1)}, u32[]{:S(2)}, u32[]{:S(2)}) %collective-permute-start.16) | collective-permute-done | bytes 196640 | tf_op jit(solution)/shard_map/ppermute | solution.py:18
  40.1 1.6 %collective-permute-start.17 = (bf16[16,3072]{1,0:T(8,128)(2,1)S(1)}, bf16[16,3072]{1,0:T(8,128)(2,1)S(1)}, u32[]{:S(2)}, u32[]{:S(2)}) collective-permute-start(bf16[16,3072]{1,0:T(8,128)(2,1)S(1)} %get-tuple-element.66), channel_id=1, source_target_pairs={{0,2},{1,3},{2,0},{3,1},{4,6},{5,7},{6,4},{7,5},{8,10},{9,11},{10,... | collective-permute-start | bytes 294920 | tf_op jit(solution)/shard_map/ppermute | solution.py:18
  41.6 3.3 %collective-permute-done.17 = bf16[16,3072]{1,0:T(8,128)(2,1)S(1)} collective-permute-done((bf16[16,3072]{1,0:T(8,128)(2,1)S(1)}, bf16[16,3072]{1,0:T(8,128)(2,1)S(1)}, u32[]{:S(2)}, u32[]{:S(2)}) %collective-permute-start.17) | collective-permute-done | bytes 98336 | tf_op jit(solution)/shard_map/ppermute | solution.py:18
  45.0 0.7 %maximum_bitcast_fusion = bf16[2,1,1,16,3072]{4,3,2,1,0:T(8,128)(2,1)} fusion(bf16[1,16,3072]{2,1,0:T(8,128)(2,1)S(1)} %fusion, bf16[1,16,3072]{2,1,0:T(8,128)(2,1)S(1)} %bitcast.21), kind=kLoop, calls=%fused_computation.3 | loop fusion | flops 98304 | bytes 393216 | tf_op jit(solution)/shard_map/broadcast_in_dim | solution.py:248
  (9 shorter events, 0.2 us)
Async XLA Ops:
  1.1 7.5 %collective-permute-start = (bf16[16,3072]{1,0:T(8,128)(2,1)S(1)}, bf16[16,3072]{1,0:T(8,128)(2,1)S(1)}, u32[]{:S(2)}, u32[]{:S(2)}) collective-permute-start(bf16[16,3072]{1,0:T(8,128)(2,1)S(1)} %get-tuple-element.41), channel_id=1, source_target_pairs={{0,2},{1,3},{2,0},{3,1},{4,6},{5,7},{6,4},{7,5},{8,10},{9,11},{10,... | collective-permute-start | bytes 294920 | tf_op jit(solution)/shard_map/ppermute | solution.py:18
  4.1 6.4 %collective-permute-start.1 = (bf16[16,3072]{1,0:T(8,128)(2,1)S(1)}, bf16[16,3072]{1,0:T(8,128)(2,1)S(1)}, u32[]{:S(2)}, u32[]{:S(2)}) collective-permute-start(bf16[16,3072]{1,0:T(8,128)(2,1)S(1)} %get-tuple-element.41), channel_id=1, source_target_pairs={{0,6},{1,7},{2,4},{3,5},{4,2},{5,3},{6,0},{7,1},{8,14},{9,15},{10,... | collective-permute-start | bytes 294920 | tf_op jit(solution)/shard_map/ppermute | solution.py:18
  5.5 4.9 %collective-permute-start.2 = (bf16[16,3072]{1,0:T(8,128)(2,1)S(1)}, bf16[16,3072]{1,0:T(8,128)(2,1)S(1)}, u32[]{:S(2)}, u32[]{:S(2)}) collective-permute-start(bf16[16,3072]{1,0:T(8,128)(2,1)S(1)} %get-tuple-element.41), channel_id=1, source_target_pairs={{0,4},{1,5},{2,6},{3,7},{4,0},{5,1},{6,2},{7,3},{8,12},{9,13},{10,... | collective-permute-start | bytes 294920 | tf_op jit(solution)/shard_map/ppermute | solution.py:18
  8.5 4.7 %copy-start.1 = (bf16[1,1,3072,512]{3,2,1,0:T(8,128)(2,1)S(1)}, bf16[1,1,3072,512]{3,2,1,0:T(8,128)(2,1)}, u32[]{:S(2)}) copy-start(bf16[1,1,3072,512]{3,2,1,0:T(8,128)(2,1)} %param.11) | copy-start | bytes 9437188
  8.5 4.7 %copy-start.2 = (bf16[1,1,512,3072]{3,2,1,0:T(8,128)(2,1)S(1)}, bf16[1,1,512,3072]{3,2,1,0:T(8,128)(2,1)}, u32[]{:S(2)}) copy-start(bf16[1,1,512,3072]{3,2,1,0:T(8,128)(2,1)} %param.13) | copy-start | bytes 9437188
  10.5 1.5 %collective-permute-start.4 = (bf16[32,3072]{1,0:T(8,128)(2,1)S(1)}, bf16[32,3072]{1,0:T(8,128)(2,1)S(1)}, u32[]{:S(2)}, u32[]{:S(2)}) collective-permute-start(bf16[32,3072]{1,0:T(8,128)(2,1)S(1)} %pad_maximum_fusion.1.mine_ref), channel_id=1, source_target_pairs={{0,1},{1,0},{2,3},{3,2},{4,5},{5,4},{6,7},{7,6},{8,9},{9,8},{10,11... | collective-permute-start | bytes 589832 | tf_op jit(solution)/shard_map/ppermute | solution.py:18
  10.5 2.6 %collective-permute-start.3 = (bf16[32,3072]{1,0:T(8,128)(2,1)S(1)}, bf16[32,3072]{1,0:T(8,128)(2,1)S(1)}, u32[]{:S(2)}, u32[]{:S(2)}) collective-permute-start(bf16[32,3072]{1,0:T(8,128)(2,1)S(1)} %pad_maximum_fusion.mine_ref), channel_id=1, source_target_pairs={{0,1},{1,0},{2,3},{3,2},{4,5},{5,4},{6,7},{7,6},{8,9},{9,8},{10,11... | collective-permute-start | bytes 589832 | tf_op jit(solution)/shard_map/ppermute | solution.py:18
  13.2 13.2 %copy-start = (bf16[4,1,16,3072]{3,2,1,0:T(8,128)(2,1)S(1)}, bf16[4,1,16,3072]{3,2,1,0:T(8,128)(2,1)}, u32[]{:S(2)}) copy-start(bf16[4,1,16,3072]{3,2,1,0:T(8,128)(2,1)} %param.8) | copy-start | bytes 1179652
  15.5 1.5 %collective-permute-start.5 = (bf16[32,3072]{1,0:T(8,128)(2,1)S(1)}, bf16[32,3072]{1,0:T(8,128)(2,1)S(1)}, u32[]{:S(2)}, u32[]{:S(2)}) collective-permute-start(bf16[32,3072]{1,0:T(8,128)(2,1)S(1)} %get-tuple-element.48), channel_id=1, source_target_pairs={{0,1},{1,0},{2,3},{3,2},{4,5},{5,4},{6,7},{7,6},{8,9},{9,8},{10,11... | collective-permute-start | bytes 589832 | tf_op jit(solution)/shard_map/ppermute | solution.py:18
  17.1 5.3 %collective-permute-start.8 = (bf16[16,3072]{1,0:T(8,128)(2,1)S(1)}, bf16[16,3072]{1,0:T(8,128)(2,1)S(1)}, u32[]{:S(2)}, u32[]{:S(2)}) collective-permute-start(bf16[16,3072]{1,0:T(8,128)(2,1)S(1)} %convert_element_type.15), channel_id=1, source_target_pairs={{0,8},{1,0},{2,10},{3,2},{8,16},{9,1},{10,18},{11,3},{16,24},{17,9... | collective-permute-start | bytes 294920 | tf_op jit(solution)/shard_map/ppermute | solution.py:32
  18.7 4.6 %collective-permute-start.9 = (bf16[16,3072]{1,0:T(8,128)(2,1)S(1)}, bf16[16,3072]{1,0:T(8,128)(2,1)S(1)}, u32[]{:S(2)}, u32[]{:S(2)}) collective-permute-start(bf16[16,3072]{1,0:T(8,128)(2,1)S(1)} %convert_element_type.15), channel_id=1, source_target_pairs={{0,1},{1,9},{2,3},{3,11},{8,0},{9,17},{10,2},{11,19},{16,8},{17,25... | collective-permute-start | bytes 294920 | tf_op jit(solution)/shard_map/ppermute | solution.py:32
  18.7 5.2 %collective-permute-start.6 = (bf16[16,3072]{1,0:T(8,128)(2,1)S(1)}, bf16[16,3072]{1,0:T(8,128)(2,1)S(1)}, u32[]{:S(2)}, u32[]{:S(2)}) collective-permute-start(bf16[16,3072]{1,0:T(8,128)(2,1)S(1)} %get-tuple-element.60), channel_id=1, source_target_pairs={{0,10},{1,0},{2,8},{3,2},{8,18},{9,1},{10,16},{11,3},{16,26},{17,9... | collective-permute-start | bytes 294920 | tf_op jit(solution)/shard_map/ppermute | solution.py:32
  21.7 4.6 %collective-permute-start.7 = (bf16[16,3072]{1,0:T(8,128)(2,1)S(1)}, bf16[16,3072]{1,0:T(8,128)(2,1)S(1)}, u32[]{:S(2)}, u32[]{:S(2)}) collective-permute-start(bf16[16,3072]{1,0:T(8,128)(2,1)S(1)} %get-tuple-element.60), channel_id=1, source_target_pairs={{0,1},{1,11},{2,3},{3,9},{8,0},{9,19},{10,2},{11,17},{16,8},{17,27... | collective-permute-start | bytes 294920 | tf_op jit(solution)/shard_map/ppermute | solution.py:32
  26.5 5.6 %collective-permute-start.12 = (bf16[16,3072]{1,0:T(8,128)(2,1)S(1)}, bf16[16,3072]{1,0:T(8,128)(2,1)S(1)}, u32[]{:S(2)}, u32[]{:S(2)}) collective-permute-start(bf16[16,3072]{1,0:T(8,128)(2,1)S(1)} %get-tuple-element.51), channel_id=1, source_target_pairs={{0,6},{1,7},{2,4},{3,5},{4,2},{5,3},{6,0},{7,1},{8,14},{9,15},{10,... | collective-permute-start | bytes 294920 | tf_op jit(solution)/shard_map/ppermute | solution.py:18
  27.9 4.6 %collective-permute-start.13 = (bf16[16,3072]{1,0:T(8,128)(2,1)S(1)}, bf16[16,3072]{1,0:T(8,128)(2,1)S(1)}, u32[]{:S(2)}, u32[]{:S(2)}) collective-permute-start(bf16[16,3072]{1,0:T(8,128)(2,1)S(1)} %get-tuple-element.51), channel_id=1, source_target_pairs={{0,4},{1,5},{2,6},{3,7},{4,0},{5,1},{6,2},{7,3},{8,12},{9,13},{10,... | collective-permute-start | bytes 294920 | tf_op jit(solution)/shard_map/ppermute | solution.py:18
  28.6 4.6 %collective-permute-start.10 = (bf16[16,3072]{1,0:T(8,128)(2,1)S(1)}, bf16[16,3072]{1,0:T(8,128)(2,1)S(1)}, u32[]{:S(2)}, u32[]{:S(2)}) collective-permute-start(bf16[16,3072]{1,0:T(8,128)(2,1)S(1)} %get-tuple-element.51), channel_id=1, source_target_pairs={{0,2},{1,3},{2,0},{3,1},{4,6},{5,7},{6,4},{7,5},{8,10},{9,11},{10,... | collective-permute-start | bytes 294920 | tf_op jit(solution)/shard_map/ppermute | solution.py:18
  32.5 2.4 %collective-permute-start.14 = (bf16[32,3072]{1,0:T(8,128)(2,1)S(1)}, bf16[32,3072]{1,0:T(8,128)(2,1)S(1)}, u32[]{:S(2)}, u32[]{:S(2)}) collective-permute-start(bf16[32,3072]{1,0:T(8,128)(2,1)S(1)} %constant_dynamic-update-slice_fusion.mine_ref), channel_id=1, source_target_pairs={{0,1},{1,0},{2,3},{3,2},{4,5},{5,4},{6,7},{7,6},{8,9},{9,8},{10,11... | collective-permute-start | bytes 589832 | tf_op jit(solution)/shard_map/ppermute | solution.py:18
  33.2 2.9 %collective-permute-start.11 = (bf16[32,3072]{1,0:T(8,128)(2,1)S(1)}, bf16[32,3072]{1,0:T(8,128)(2,1)S(1)}, u32[]{:S(2)}, u32[]{:S(2)}) collective-permute-start(bf16[32,3072]{1,0:T(8,128)(2,1)S(1)} %pad_maximum_fusion.2.mine_ref), channel_id=1, source_target_pairs={{0,1},{1,0},{2,3},{3,2},{4,5},{5,4},{6,7},{7,6},{8,9},{9,8},{10,11... | collective-permute-start | bytes 589832 | tf_op jit(solution)/shard_map/ppermute | solution.py:18
  33.3 5.2 %collective-permute-start.15 = (bf16[16,3072]{1,0:T(8,128)(2,1)S(1)}, bf16[16,3072]{1,0:T(8,128)(2,1)S(1)}, u32[]{:S(2)}, u32[]{:S(2)}) collective-permute-start(bf16[16,3072]{1,0:T(8,128)(2,1)S(1)} %get-tuple-element.60), channel_id=1, source_target_pairs={{0,2},{1,3},{2,0},{3,1},{4,6},{5,7},{6,4},{7,5},{8,10},{9,11},{10,... | collective-permute-start | bytes 294920 | tf_op jit(solution)/shard_map/ppermute | solution.py:18
  38.5 1.5 %collective-permute-start.16 = (bf16[32,3072]{1,0:T(8,128)(2,1)S(1)}, bf16[32,3072]{1,0:T(8,128)(2,1)S(1)}, u32[]{:S(2)}, u32[]{:S(2)}) collective-permute-start(bf16[32,3072]{1,0:T(8,128)(2,1)S(1)} %get-tuple-element.64), channel_id=1, source_target_pairs={{0,1},{1,0},{2,3},{3,2},{4,5},{5,4},{6,7},{7,6},{8,9},{9,8},{10,11... | collective-permute-start | bytes 589832 | tf_op jit(solution)/shard_map/ppermute | solution.py:18
  40.1 4.9 %collective-permute-start.17 = (bf16[16,3072]{1,0:T(8,128)(2,1)S(1)}, bf16[16,3072]{1,0:T(8,128)(2,1)S(1)}, u32[]{:S(2)}, u32[]{:S(2)}) collective-permute-start(bf16[16,3072]{1,0:T(8,128)(2,1)S(1)} %get-tuple-element.66), channel_id=1, source_target_pairs={{0,2},{1,3},{2,0},{3,1},{4,6},{5,7},{6,4},{7,5},{8,10},{9,11},{10,... | collective-permute-start | bytes 294920 | tf_op jit(solution)/shard_map/ppermute | solution.py:18

commit v6 on v5

--- a/solution.py
+++ b/solution.py
@@ -18,19 +18,23 @@
     return lax.ppermute(value, BOTH, [(i, i ^ mask) for i in range(count)])
 
 
-def climbed(value, hop):
+def climbed(value, hop, climbs):
     sections, lanes = lax.axis_size("section"), lax.axis_size("lane")
-    results = []
-    for climbs in range(2):
-        pairs = []
-        for s in range(sections):
-            for lane in range(lanes):
-                to, target = (s + 1, lane ^ hop) if lane % 2 == climbs else (s - 1, lane)
-                if not 0 <= to < sections:
-                    to, target = s, lane ^ 1
-                pairs.append((s * lanes + lane, to * lanes + target))
-        results.append(lax.ppermute(value, ("section", "lane"), pairs))
-    return results
+    pairs = []
+    for s in range(sections):
+        for lane in range(lanes):
+            to, target = (s + 1, lane ^ hop) if lane % 2 == climbs else (s - 1, lane)
+            if not 0 <= to < sections:
+                to, target = s, lane ^ 1
+            pairs.append((s * lanes + lane, to * lanes + target))
+    return lax.ppermute(value, ("section", "lane"), pairs)
+
+
+def handed_on(own, others):
+    blocks = [climbed(own, 0, 0), climbed(own, 0, 1)]
+    for k, other in enumerate(others, 1):
+        blocks += [swapped(other, 2 * k), climbed(other, 2 * k, 1), climbed(other, 2 * k, 0)]
+    return jnp.concatenate(blocks, 0)
 
 
 def in_hbm(*arrays):
@@ -55,25 +59,34 @@
 
 
 def attend_kernel(tok, mine_ref, theirs_ref, keys_ref, values_ref, wq_ref, wo_ref, keep_ref, send_ref):
-    half = keep_ref.shape[0]
+    half, width = keep_ref.shape
     rows = 2 * half
     query = project(jnp.concatenate([mine_ref[...], theirs_ref[...]], 0), wq_ref[...])
     row_clip = lax.broadcasted_iota(jnp.int32, (rows, rows), 0) // tok
     col_clip = lax.broadcasted_iota(jnp.int32, (rows, rows), 1) // tok
     same_clip = row_clip == col_clip
-    mixed = []
-    for start in range(0, query.shape[1], HEAD_DIM):
-        head = slice(start, start + HEAD_DIM)
-        scores = lax.dot_general(
+    heads = [slice(start, start + HEAD_DIM) for start in range(0, query.shape[1], HEAD_DIM)]
+    scores = [
+        lax.dot_general(
             query[:, head], keys_ref[:, head], (((1,), (1,)), ((), ())), preferred_element_type=jnp.float32
-        ) * (HEAD_DIM**-0.5)
-        scores = jnp.where(same_clip, scores, -jnp.inf)
-        weights = jnp.exp(scores - jnp.max(scores, -1, keepdims=True))
-        weights = weights / jnp.sum(weights, -1, keepdims=True)
-        mixed.append(project(weights.astype(jnp.bfloat16), values_ref[:, head]))
-    part = jnp.dot(jnp.concatenate(mixed, 1), wo_ref[...], preferred_element_type=jnp.float32)
-    keep_ref[...] = part[:half]
-    send_ref[...] = part[half:].astype(jnp.bfloat16)
+        )
+        for head in heads
+    ]
+    scores = [jnp.where(same_clip, score * (HEAD_DIM**-0.5), -jnp.inf) for score in scores]
+    tops = [jnp.max(score, -1, keepdims=True) for score in scores]
+    weights = [jnp.exp(score - top).astype(jnp.bfloat16) for score, top in zip(scores, tops)]
+    ones = jnp.ones((rows, HEAD_DIM), jnp.bfloat16)
+    sums = [jnp.dot(weight, ones, preferred_element_type=jnp.float32) for weight in weights]
+    mixed = [
+        jnp.dot(weight, values_ref[:, head], preferred_element_type=jnp.float32)
+        for weight, head in zip(weights, heads)
+    ]
+    mixed = jnp.concatenate([(mix / total).astype(jnp.bfloat16) for mix, total in zip(mixed, sums)], 1)
+    for start in range(0, width, width // 4):
+        columns = slice(start, start + width // 4)
+        part = jnp.dot(mixed, wo_ref[:, columns], preferred_element_type=jnp.float32)
+        keep_ref[:, columns] = part[:half]
+        send_ref[:, columns] = part[half:].astype(jnp.bfloat16)
 
 
 def in_vmem(*arrays):
@@ -177,29 +190,34 @@
     )(*in_hbm(*arrays))
 
 
-def second_kernel(section_ref, lane_ref, offset_ref, fresh_ref, gain_ref, *refs):
-    *handed_refs, state_ref, normed_ref = refs
+def second_kernel(
+    section_ref, lane_ref, offset_ref, fresh_ref, gain_ref, own_ref, handed_ref, first_ref, state_ref, normed_ref
+):
     tok = state_ref.shape[0]
-    even = lane_ref[0] % 2 == 0
-    handed = 0.0
-    for even_ref, odd_ref in zip(handed_refs[::2], handed_refs[1::2]):
-        handed = handed + jnp.where(even, even_ref[...], odd_ref[...]).astype(jnp.float32)
+
+    def block(index):
+        return handed_ref[pl.ds(pl.multiple_of(index * tok, tok), tok)].astype(jnp.float32)
+
+    odd = lane_ref[0] % 2
+    first, handed = own_ref[...], block(odd)
+    for index in range(2, handed_ref.shape[0] // tok, 3):
+        first = first + block(index)
+        handed = handed + block(index + 2 - odd)
+    first_ref[...] = first.astype(jnp.bfloat16)
     picked = fresh_ref[pl.ds(pl.multiple_of(offset_ref[0] * tok, tok), tok)]
     state = jnp.where(section_ref[0] == 0, picked, handed.astype(jnp.bfloat16))
     state_ref[...] = state
     normed_ref[...] = normalized(state, gain_ref[0])
 
 
-def second_entry(section, lane, offsets, fresh, gain, handed):
-    shape = handed[0].shape
+def second_entry(section, lane, offsets, fresh, gain, own, handed):
     return pl.pallas_call(
         second_kernel,
-        out_shape=(pltpu.VMEM(shape, jnp.bfloat16),) * 2,
-        in_specs=[pl.BlockSpec(memory_space=pltpu.SMEM)] * 3
-        + [pl.BlockSpec(memory_space=pltpu.VMEM)] * (2 + len(handed)),
-        out_specs=(pl.BlockSpec(memory_space=pltpu.VMEM),) * 2,
-        compiler_params=pltpu.CompilerParams(vmem_limit_bytes=16 << 20),
-    )(section, lane, offsets, fresh, gain, *handed)
+        out_shape=(pltpu.VMEM(own.shape, jnp.bfloat16),) * 3,
+        in_specs=[pl.BlockSpec(memory_space=pltpu.SMEM)] * 3 + [pl.BlockSpec(memory_space=pltpu.VMEM)] * 4,
+        out_specs=(pl.BlockSpec(memory_space=pltpu.VMEM),) * 3,
+        compiler_params=pltpu.CompilerParams(vmem_limit_bytes=16 << 20),
+    )(section, lane, offsets, fresh, gain, own, handed)
 
 
 def gathered(normed):
@@ -232,19 +250,15 @@
     tok = state.shape[0]
     normed, section, lane = lax.optimization_barrier((normed, index_of("section"), index_of("lane")))
     (wkv,) = load(w_keyval.reshape(-1, w_keyval.shape[-1]))
-    own, partner, wkv = lax.optimization_barrier((*gathered(normed), wkv))
+    own, partner = gathered(normed)
+    partner, wkv = lax.optimization_barrier((partner, wkv))
     wq, wo, fresh = w_query[0, 0], w_out[0, 0], fresh_batches.reshape(-1, fresh_batches.shape[-1])
     weights = (wq, wkv, wo)
     first_sum, others = summed(state, *layer_part(own, partner, weights, tok))
-    sums = [first_sum.astype(jnp.bfloat16), *others]
-    handed = [part for k in reversed(range(len(sums))) for part in climbed(sums[k], 2 * k)]
-    state, normed = second_entry(section, lane, offsets, fresh, gain, handed)
+    handed = handed_on(first_sum.astype(jnp.bfloat16), others)
+    first, state, normed = second_entry(section, lane, offsets, fresh, gain, first_sum, handed)
     own, partner = gathered(normed)
-    own, others = lax.optimization_barrier((own, others))
-    keep, send, first_sum = lax.optimization_barrier((*layer_part(own, partner, weights, tok), first_sum))
-    first = completed(first_sum, others)
-    keep, send, first = lax.optimization_barrier((keep, send, first))
-    second = completed(*summed(state, keep, send))
+    second = completed(*summed(state, *layer_part(own, partner, weights, tok)))
     return jnp.stack([first, second])[:, None, None]
 
 

time: 45.8 us -> 44.5 us (0.972)
  starting transfers between devices: 17 us -> 15.7 us
  Pallas kernels: 11.1 us -> 9.82 us
  waiting for transfers between devices: 16 us -> 17 us
    ppermute x14, waiting for transfers between devices: 12 us -> 14.6 us  [swapped(): return lax.ppermute(value, BOTH, [(i, i ^ mask) for i in range(count)])]
    ppermute x4, waiting for transfers between devices: 3.95 us -> 2.47 us  [climbed(): return lax.ppermute(value, ('section', 'lane'), pairs)]
    pallas_call x6, Pallas kernels: 6.99 us -> 5.75 us  [on_chip(): pl.pallas_call(kernel, out_shape=tuple((jax.ShapeDtypeStruct(shape, dtype...]
    ppermute x14, starting transfers between devices: 12.3 us -> 11.1 us  [swapped(): return lax.ppermute(value, BOTH, [(i, i ^ mask) for i in range(count)])]
  transfers between devices with their start and end apart: 18 -> 18, of which waited for: 12 -> 12; matrix products, arithmetic and copies ran while one was open for 0% -> 0% of each run, Pallas kernels for 16% -> 12%
where the time goes in v6:
time: 44.5 us; the launch traced here: 44.3 us
  waiting for transfers between devices  17 us (38%)
  starting transfers between devices  15.7 us (35%)
  Pallas kernels  9.82 us (22%)
  between operations  0.9 us (2%)
  other arithmetic  0.74 us (2%)
    ppermute x14, waiting for transfers between devices, swapped(): return lax.ppermute(value, BOTH, [(i, i ^ mask) for i in range(count)])  14.6 us
    ppermute x14, starting transfers between devices, swapped(): return lax.ppermute(value, BOTH, [(i, i ^ mask) for i in range(count)])  11.1 us
    pallas_call x6, Pallas kernels, on_chip(): pl.pallas_call(kernel, out_shape=tuple((jax.ShapeDtypeStruct(shape, dtype...  5.75 us
    ppermute x4, starting transfers between devices, climbed(): return lax.ppermute(value, ('section', 'lane'), pairs)  4.6 us
    pallas_call x1, Pallas kernels, load(): pl.pallas_call(load_kernel, out_shape=tuple((pltpu.VMEM(a.shape, a.dtype)...  2.87 us
    ppermute x4, waiting for transfers between devices, climbed(): return lax.ppermute(value, ('section', 'lane'), pairs)  2.47 us
    pallas_call x1, Pallas kernels, entry(): pl.pallas_call(entry_kernel, out_shape=(pltpu.VMEM(state.shape, jnp.bfloa...  1.04 us
  transfers between devices with their start and end apart: 18, of which 12 were waited for; matrix products, arithmetic and copies ran while one was open for 0% of the time, Pallas kernels for 12%

profile of v6, /device:TPU:0, one launch (start us, length us, event | category | flops | bytes accessed | tf_op | source)
XLA Modules:
  0.0 44.3 jit_solution(5810694842214270264)
XLA Ops:
  0.0 1.0 %shard_map.73 = (bf16[16,3072]{1,0:T(8,128)(2,1)S(1)}, bf16[16,3072]{1,0:T(8,128)(2,1)S(1)}, f32[1,3072]{1,0:T(1,128)S(1)}) custom-call(bf16[16,3072]{1,0:T(8,128)(2,1)} %bitcast.22, f32[1,3072]{1,0:T(1,128)} %bitcast.23), custom_call_target="tpu_custom_call" | custom-call | tf_op jit(solution)/shard_map/pallas_call | solution.py:150
  1.1 4.0 %collective-permute-start.2 = (bf16[16,3072]{1,0:T(8,128)(2,1)S(1)}, bf16[16,3072]{1,0:T(8,128)(2,1)S(1)}, u32[]{:S(2)}, u32[]{:S(2)}) collective-permute-start(bf16[16,3072]{1,0:T(8,128)(2,1)S(1)} %get-tuple-element.33), channel_id=1, source_target_pairs={{0,6},{1,7},{2,4},{3,5},{4,2},{5,3},{6,0},{7,1},{8,14},{9,15},{10,... | collective-permute-start | bytes 294920 | tf_op jit(solution)/shard_map/ppermute | solution.py:18
  5.0 0.5 %collective-permute-start.3 = (bf16[16,3072]{1,0:T(8,128)(2,1)S(1)}, bf16[16,3072]{1,0:T(8,128)(2,1)S(1)}, u32[]{:S(2)}, u32[]{:S(2)}) collective-permute-start(bf16[16,3072]{1,0:T(8,128)(2,1)S(1)} %get-tuple-element.33), channel_id=1, source_target_pairs={{0,4},{1,5},{2,6},{3,7},{4,0},{5,1},{6,2},{7,3},{8,12},{9,13},{10,... | collective-permute-start | bytes 294920 | tf_op jit(solution)/shard_map/ppermute | solution.py:18
  5.5 0.1 collective-permute-start
  5.7 2.9 %shard_map.74.wkv_ref = bf16[6144,512]{1,0:T(8,128)(2,1)S(1)} custom-call(bf16[6144,512]{1,0:T(8,128)(2,1)} %bitcast.21), custom_call_target="tpu_custom_call" | custom-call | bytes 6291456 | tf_op jit(solution)/shard_map/pallas_call | solution.py:180
  8.5 0.0 copy-start.1
  8.5 0.0 copy-start.2
  8.6 0.0 collective-permute-done.2
  8.6 1.7 %collective-permute-done.3 = bf16[16,3072]{1,0:T(8,128)(2,1)S(1)} collective-permute-done((bf16[16,3072]{1,0:T(8,128)(2,1)S(1)}, bf16[16,3072]{1,0:T(8,128)(2,1)S(1)}, u32[]{:S(2)}, u32[]{:S(2)}) %collective-permute-start.3) | collective-permute-done | bytes 98336 | tf_op jit(solution)/shard_map/ppermute | solution.py:18
  10.3 0.1 collective-permute-start.4
  10.3 0.0 collective-permute-done
  10.4 0.5 %collective-permute-start.1 = (bf16[32,3072]{1,0:T(8,128)(2,1)S(1)}, bf16[32,3072]{1,0:T(8,128)(2,1)S(1)}, u32[]{:S(2)}, u32[]{:S(2)}) collective-permute-start(bf16[32,3072]{1,0:T(8,128)(2,1)S(1)} %constant_dynamic-update-slice_fusion.mine_ref), channel_id=1, source_target_pairs={{0,1},{1,0},{2,3},{3,2},{4,5},{5,4},{6,7},{7,6},{8,9},{9,8},{10,11... | collective-permute-start | bytes 589832 | tf_op jit(solution)/shard_map/ppermute | solution.py:18
  10.9 0.8 %collective-permute-done.4.theirs_ref = bf16[32,3072]{1,0:T(8,128)(2,1)S(1)} collective-permute-done((bf16[32,3072]{1,0:T(8,128)(2,1)S(1)}, bf16[32,3072]{1,0:T(8,128)(2,1)S(1)}, u32[]{:S(2)}, u32[]{:S(2)}) %collective-permute-start.4) | collective-permute-done | bytes 196640 | tf_op jit(solution)/shard_map/ppermute | solution.py:18
  11.8 1.2 %shard_map.75 = (bf16[64,512]{1,0:T(8,128)(2,1)S(1)}, bf16[64,512]{1,0:T(8,128)(2,1)S(1)}) custom-call(bf16[32,3072]{1,0:T(8,128)(2,1)S(1)} %pad_maximum_fusion.mine_ref, bf16[32,3072]{1,0:T(8,128)(2,1)S(1)} %collective-permute-done.4.theirs_ref, bf16[6144,512]{1,0:T(8,128)(2,1)S(1)} %shard_map.74.wkv_ref), custom_call_target="tpu_custom_call" | custom-call | flops 1610612736 | bytes 6684672 | tf_op jit(solution)/shard_map/pallas_call | solution.py:98
  13.0 0.0 copy-start
  13.0 0.0 collective-permute-done.1.theirs_ref
  13.0 0.0 copy-done.1
  13.0 0.0 copy-done.2
  13.0 1.6 %shard_map.76 = (f32[32,3072]{1,0:T(8,128)S(1)}, bf16[32,3072]{1,0:T(8,128)(2,1)S(1)}) custom-call(bf16[32,3072]{1,0:T(8,128)(2,1)S(1)} %constant_dynamic-update-slice_fusion.mine_ref, bf16[32,3072]{1,0:T(8,128)(2,1)S(1)} %collective-permute-done.1.theirs_ref, bf16[64,512]{1,0:T(8,128)(2,1)S(1)} %get-tuple-element.36.keys_ref, ...), custom_call_target="tpu_custom_call" | custom-call | flops 2415919104 | bytes 6815744 | tf_op jit(solution)/shard_map/pallas_call | solution.py:98
  14.7 0.2 collective-permute-start.5
  14.9 1.3 %collective-permute-done.5.sent_ref = bf16[32,3072]{1,0:T(8,128)(2,1)S(1)} collective-permute-done((bf16[32,3072]{1,0:T(8,128)(2,1)S(1)}, bf16[32,3072]{1,0:T(8,128)(2,1)S(1)}, u32[]{:S(2)}, u32[]{:S(2)}) %collective-permute-start.5) | collective-permute-done | bytes 196640 | tf_op jit(solution)/shard_map/ppermute | solution.py:18
  16.2 1.6 %collective-permute-start.6 = (bf16[16,3072]{1,0:T(8,128)(2,1)S(1)}, bf16[16,3072]{1,0:T(8,128)(2,1)S(1)}, u32[]{:S(2)}, u32[]{:S(2)}) collective-permute-start(bf16[16,3072]{1,0:T(8,128)(2,1)S(1)} %convert_element_type.9), channel_id=1, source_target_pairs={{0,8},{1,0},{2,10},{3,2},{8,16},{9,1},{10,18},{11,3},{16,24},{17,9... | collective-permute-start | bytes 294920 | tf_op jit(solution)/shard_map/ppermute | solution.py:30
  18.5 0.0 collective-permute-start.7
  18.5 0.6 %collective-permute-start.8 = (bf16[16,3072]{1,0:T(8,128)(2,1)S(1)}, bf16[16,3072]{1,0:T(8,128)(2,1)S(1)}, u32[]{:S(2)}, u32[]{:S(2)}) collective-permute-start(bf16[16,3072]{1,0:T(8,128)(2,1)S(1)} %get-tuple-element.41), channel_id=1, source_target_pairs={{0,2},{1,3},{2,0},{3,1},{4,6},{5,7},{6,4},{7,5},{8,10},{9,11},{10,... | collective-permute-start | bytes 294920 | tf_op jit(solution)/shard_map/ppermute | solution.py:18
  19.1 0.0 collective-permute-start.9
  19.1 3.0 %collective-permute-start.10 = (bf16[16,3072]{1,0:T(8,128)(2,1)S(1)}, bf16[16,3072]{1,0:T(8,128)(2,1)S(1)}, u32[]{:S(2)}, u32[]{:S(2)}) collective-permute-start(bf16[16,3072]{1,0:T(8,128)(2,1)S(1)} %get-tuple-element.41), channel_id=1, source_target_pairs={{0,10},{1,0},{2,8},{3,2},{8,18},{9,1},{10,16},{11,3},{16,26},{17,9... | collective-permute-start | bytes 294920 | tf_op jit(solution)/shard_map/ppermute | solution.py:30
  22.1 0.0 collective-permute-done.6
  22.1 1.0 %collective-permute-done.7 = bf16[16,3072]{1,0:T(8,128)(2,1)S(1)} collective-permute-done((bf16[16,3072]{1,0:T(8,128)(2,1)S(1)}, bf16[16,3072]{1,0:T(8,128)(2,1)S(1)}, u32[]{:S(2)}, u32[]{:S(2)}) %collective-permute-start.7) | collective-permute-done | bytes 98336 | tf_op jit(solution)/shard_map/ppermute | solution.py:30
  23.1 0.1 collective-permute-done.8
  23.2 1.4 %collective-permute-done.9 = bf16[16,3072]{1,0:T(8,128)(2,1)S(1)} collective-permute-done((bf16[16,3072]{1,0:T(8,128)(2,1)S(1)}, bf16[16,3072]{1,0:T(8,128)(2,1)S(1)}, u32[]{:S(2)}, u32[]{:S(2)}) %collective-permute-start.9) | collective-permute-done | bytes 98336 | tf_op jit(solution)/shard_map/ppermute | solution.py:30
  24.7 0.0 collective-permute-done.10
  24.7 0.0 copy-done
  24.7 0.2 shard_map.78
  24.9 2.5 %collective-permute-start.13 = (bf16[16,3072]{1,0:T(8,128)(2,1)S(1)}, bf16[16,3072]{1,0:T(8,128)(2,1)S(1)}, u32[]{:S(2)}, u32[]{:S(2)}) collective-permute-start(bf16[16,3072]{1,0:T(8,128)(2,1)S(1)} %get-tuple-element.44), channel_id=1, source_target_pairs={{0,6},{1,7},{2,4},{3,5},{4,2},{5,3},{6,0},{7,1},{8,14},{9,15},{10,... | collective-permute-start | bytes 294920 | tf_op jit(solution)/shard_map/ppermute | solution.py:18
  27.3 0.6 %collective-permute-start.14 = (bf16[16,3072]{1,0:T(8,128)(2,1)S(1)}, bf16[16,3072]{1,0:T(8,128)(2,1)S(1)}, u32[]{:S(2)}, u32[]{:S(2)}) collective-permute-start(bf16[16,3072]{1,0:T(8,128)(2,1)S(1)} %get-tuple-element.44), channel_id=1, source_target_pairs={{0,4},{1,5},{2,6},{3,7},{4,0},{5,1},{6,2},{7,3},{8,12},{9,13},{10,... | collective-permute-start | bytes 294920 | tf_op jit(solution)/shard_map/ppermute | solution.py:18
  28.0 0.5 %collective-permute-start.11 = (bf16[16,3072]{1,0:T(8,128)(2,1)S(1)}, bf16[16,3072]{1,0:T(8,128)(2,1)S(1)}, u32[]{:S(2)}, u32[]{:S(2)}) collective-permute-start(bf16[16,3072]{1,0:T(8,128)(2,1)S(1)} %get-tuple-element.44), channel_id=1, source_target_pairs={{0,2},{1,3},{2,0},{3,1},{4,6},{5,7},{6,4},{7,5},{8,10},{9,11},{10,... | collective-permute-start | bytes 294920 | tf_op jit(solution)/shard_map/ppermute | solution.py:18
  28.4 3.0 %collective-permute-done.13 = bf16[16,3072]{1,0:T(8,128)(2,1)S(1)} collective-permute-done((bf16[16,3072]{1,0:T(8,128)(2,1)S(1)}, bf16[16,3072]{1,0:T(8,128)(2,1)S(1)}, u32[]{:S(2)}, u32[]{:S(2)}) %collective-permute-start.13) | collective-permute-done | bytes 98336 | tf_op jit(solution)/shard_map/ppermute | solution.py:18
  31.5 1.3 %collective-permute-done.14 = bf16[16,3072]{1,0:T(8,128)(2,1)S(1)} collective-permute-done((bf16[16,3072]{1,0:T(8,128)(2,1)S(1)}, bf16[16,3072]{1,0:T(8,128)(2,1)S(1)}, u32[]{:S(2)}, u32[]{:S(2)}) %collective-permute-start.14) | collective-permute-done | bytes 98336 | tf_op jit(solution)/shard_map/ppermute | solution.py:18
  32.8 0.1 collective-permute-start.15
  32.9 0.1 collective-permute-done.11
  33.0 0.4 collective-permute-start.12
  33.5 0.8 %collective-permute-done.15.theirs_ref = bf16[32,3072]{1,0:T(8,128)(2,1)S(1)} collective-permute-done((bf16[32,3072]{1,0:T(8,128)(2,1)S(1)}, bf16[32,3072]{1,0:T(8,128)(2,1)S(1)}, u32[]{:S(2)}, u32[]{:S(2)}) %collective-permute-start.15) | collective-permute-done | bytes 196640 | tf_op jit(solution)/shard_map/ppermute | solution.py:18
  34.3 1.2 %shard_map.79 = (bf16[64,512]{1,0:T(8,128)(2,1)S(1)}, bf16[64,512]{1,0:T(8,128)(2,1)S(1)}) custom-call(bf16[32,3072]{1,0:T(8,128)(2,1)S(1)} %constant_dynamic-update-slice_fusion.9.mine_ref, bf16[32,3072]{1,0:T(8,128)(2,1)S(1)} %collective-permute-done.15.theirs_ref, bf16[6144,512]{1,0:T(8,128)(2,1)S(1)} %shard_map.74.wkv_ref), custom_call_target="tpu_custom_call" | custom-call | flops 1610612736 | bytes 6684672 | tf_op jit(solution)/shard_map/pallas_call | solution.py:98
  35.5 0.0 collective-permute-done.12.theirs_ref
  35.5 1.6 %shard_map.80 = (f32[32,3072]{1,0:T(8,128)S(1)}, bf16[32,3072]{1,0:T(8,128)(2,1)S(1)}) custom-call(bf16[32,3072]{1,0:T(8,128)(2,1)S(1)} %constant_dynamic-update-slice_fusion.7.mine_ref, bf16[32,3072]{1,0:T(8,128)(2,1)S(1)} %collective-permute-done.12.theirs_ref, bf16[64,512]{1,0:T(8,128)(2,1)S(1)} %get-tuple-element.45.keys_ref, ...), custom_call_target="tpu_custom_call" | custom-call | flops 2415919104 | bytes 6815744 | tf_op jit(solution)/shard_map/pallas_call | solution.py:98
  37.1 0.2 collective-permute-start.16
  37.3 1.3 %collective-permute-done.16.sent_ref = bf16[32,3072]{1,0:T(8,128)(2,1)S(1)} collective-permute-done((bf16[32,3072]{1,0:T(8,128)(2,1)S(1)}, bf16[32,3072]{1,0:T(8,128)(2,1)S(1)}, u32[]{:S(2)}, u32[]{:S(2)}) %collective-permute-start.16) | collective-permute-done | bytes 196640 | tf_op jit(solution)/shard_map/ppermute | solution.py:18
  38.7 0.9 %collective-permute-start.17 = (bf16[16,3072]{1,0:T(8,128)(2,1)S(1)}, bf16[16,3072]{1,0:T(8,128)(2,1)S(1)}, u32[]{:S(2)}, u32[]{:S(2)}) collective-permute-start(bf16[16,3072]{1,0:T(8,128)(2,1)S(1)} %get-tuple-element.50), channel_id=1, source_target_pairs={{0,2},{1,3},{2,0},{3,1},{4,6},{5,7},{6,4},{7,5},{8,10},{9,11},{10,... | collective-permute-start | bytes 294920 | tf_op jit(solution)/shard_map/ppermute | solution.py:18
  39.6 4.0 %collective-permute-done.17 = bf16[16,3072]{1,0:T(8,128)(2,1)S(1)} collective-permute-done((bf16[16,3072]{1,0:T(8,128)(2,1)S(1)}, bf16[16,3072]{1,0:T(8,128)(2,1)S(1)}, u32[]{:S(2)}, u32[]{:S(2)}) %collective-permute-start.17) | collective-permute-done | bytes 98336 | tf_op jit(solution)/shard_map/ppermute | solution.py:18
  43.6 0.7 %maximum_bitcast_fusion = bf16[2,1,1,16,3072]{4,3,2,1,0:T(8,128)(2,1)} fusion(bf16[1,16,3072]{2,1,0:T(8,128)(2,1)S(1)} %fusion, bf16[1,16,3072]{2,1,0:T(8,128)(2,1)S(1)} %bitcast.16), kind=kLoop, calls=%fused_computation.1 | loop fusion | flops 98304 | bytes 393216 | tf_op jit(solution)/shard_map/broadcast_in_dim | solution.py:262
  (16 shorter events, 0.2 us)
Async XLA Ops:
  1.1 7.5 %collective-permute-start.2 = (bf16[16,3072]{1,0:T(8,128)(2,1)S(1)}, bf16[16,3072]{1,0:T(8,128)(2,1)S(1)}, u32[]{:S(2)}, u32[]{:S(2)}) collective-permute-start(bf16[16,3072]{1,0:T(8,128)(2,1)S(1)} %get-tuple-element.33), channel_id=1, source_target_pairs={{0,6},{1,7},{2,4},{3,5},{4,2},{5,3},{6,0},{7,1},{8,14},{9,15},{10,... | collective-permute-start | bytes 294920 | tf_op jit(solution)/shard_map/ppermute | solution.py:18
  5.0 5.2 %collective-permute-start.3 = (bf16[16,3072]{1,0:T(8,128)(2,1)S(1)}, bf16[16,3072]{1,0:T(8,128)(2,1)S(1)}, u32[]{:S(2)}, u32[]{:S(2)}) collective-permute-start(bf16[16,3072]{1,0:T(8,128)(2,1)S(1)} %get-tuple-element.33), channel_id=1, source_target_pairs={{0,4},{1,5},{2,6},{3,7},{4,0},{5,1},{6,2},{7,3},{8,12},{9,13},{10,... | collective-permute-start | bytes 294920 | tf_op jit(solution)/shard_map/ppermute | solution.py:18
  5.5 4.8 %collective-permute-start = (bf16[16,3072]{1,0:T(8,128)(2,1)S(1)}, bf16[16,3072]{1,0:T(8,128)(2,1)S(1)}, u32[]{:S(2)}, u32[]{:S(2)}) collective-permute-start(bf16[16,3072]{1,0:T(8,128)(2,1)S(1)} %get-tuple-element.33), channel_id=1, source_target_pairs={{0,2},{1,3},{2,0},{3,1},{4,6},{5,7},{6,4},{7,5},{8,10},{9,11},{10,... | collective-permute-start | bytes 294920 | tf_op jit(solution)/shard_map/ppermute | solution.py:18
  8.5 4.5 %copy-start.1 = (bf16[1,1,3072,512]{3,2,1,0:T(8,128)(2,1)S(1)}, bf16[1,1,3072,512]{3,2,1,0:T(8,128)(2,1)}, u32[]{:S(2)}) copy-start(bf16[1,1,3072,512]{3,2,1,0:T(8,128)(2,1)} %param.11) | copy-start | bytes 9437188
  8.5 4.5 %copy-start.2 = (bf16[1,1,512,3072]{3,2,1,0:T(8,128)(2,1)S(1)}, bf16[1,1,512,3072]{3,2,1,0:T(8,128)(2,1)}, u32[]{:S(2)}) copy-start(bf16[1,1,512,3072]{3,2,1,0:T(8,128)(2,1)} %param.13) | copy-start | bytes 9437188
  10.3 1.5 %collective-permute-start.4 = (bf16[32,3072]{1,0:T(8,128)(2,1)S(1)}, bf16[32,3072]{1,0:T(8,128)(2,1)S(1)}, u32[]{:S(2)}, u32[]{:S(2)}) collective-permute-start(bf16[32,3072]{1,0:T(8,128)(2,1)S(1)} %pad_maximum_fusion.mine_ref), channel_id=1, source_target_pairs={{0,1},{1,0},{2,3},{3,2},{4,5},{5,4},{6,7},{7,6},{8,9},{9,8},{10,11... | collective-permute-start | bytes 589832 | tf_op jit(solution)/shard_map/ppermute | solution.py:18
  10.4 2.6 %collective-permute-start.1 = (bf16[32,3072]{1,0:T(8,128)(2,1)S(1)}, bf16[32,3072]{1,0:T(8,128)(2,1)S(1)}, u32[]{:S(2)}, u32[]{:S(2)}) collective-permute-start(bf16[32,3072]{1,0:T(8,128)(2,1)S(1)} %constant_dynamic-update-slice_fusion.mine_ref), channel_id=1, source_target_pairs={{0,1},{1,0},{2,3},{3,2},{4,5},{5,4},{6,7},{7,6},{8,9},{9,8},{10,11... | collective-permute-start | bytes 589832 | tf_op jit(solution)/shard_map/ppermute | solution.py:18
  13.0 11.7 %copy-start = (bf16[4,1,16,3072]{3,2,1,0:T(8,128)(2,1)S(1)}, bf16[4,1,16,3072]{3,2,1,0:T(8,128)(2,1)}, u32[]{:S(2)}) copy-start(bf16[4,1,16,3072]{3,2,1,0:T(8,128)(2,1)} %param.8) | copy-start | bytes 1179652
  14.7 1.5 %collective-permute-start.5 = (bf16[32,3072]{1,0:T(8,128)(2,1)S(1)}, bf16[32,3072]{1,0:T(8,128)(2,1)S(1)}, u32[]{:S(2)}, u32[]{:S(2)}) collective-permute-start(bf16[32,3072]{1,0:T(8,128)(2,1)S(1)} %get-tuple-element.39), channel_id=1, source_target_pairs={{0,1},{1,0},{2,3},{3,2},{4,5},{5,4},{6,7},{7,6},{8,9},{9,8},{10,11... | collective-permute-start | bytes 589832 | tf_op jit(solution)/shard_map/ppermute | solution.py:18
  16.2 5.8 %collective-permute-start.6 = (bf16[16,3072]{1,0:T(8,128)(2,1)S(1)}, bf16[16,3072]{1,0:T(8,128)(2,1)S(1)}, u32[]{:S(2)}, u32[]{:S(2)}) collective-permute-start(bf16[16,3072]{1,0:T(8,128)(2,1)S(1)} %convert_element_type.9), channel_id=1, source_target_pairs={{0,8},{1,0},{2,10},{3,2},{8,16},{9,1},{10,18},{11,3},{16,24},{17,9... | collective-permute-start | bytes 294920 | tf_op jit(solution)/shard_map/ppermute | solution.py:30
  18.5 4.6 %collective-permute-start.7 = (bf16[16,3072]{1,0:T(8,128)(2,1)S(1)}, bf16[16,3072]{1,0:T(8,128)(2,1)S(1)}, u32[]{:S(2)}, u32[]{:S(2)}) collective-permute-start(bf16[16,3072]{1,0:T(8,128)(2,1)S(1)} %convert_element_type.9), channel_id=1, source_target_pairs={{0,1},{1,9},{2,3},{3,11},{8,0},{9,17},{10,2},{11,19},{16,8},{17,25... | collective-permute-start | bytes 294920 | tf_op jit(solution)/shard_map/ppermute | solution.py:30
  18.5 4.7 %collective-permute-start.8 = (bf16[16,3072]{1,0:T(8,128)(2,1)S(1)}, bf16[16,3072]{1,0:T(8,128)(2,1)S(1)}, u32[]{:S(2)}, u32[]{:S(2)}) collective-permute-start(bf16[16,3072]{1,0:T(8,128)(2,1)S(1)} %get-tuple-element.41), channel_id=1, source_target_pairs={{0,2},{1,3},{2,0},{3,1},{4,6},{5,7},{6,4},{7,5},{8,10},{9,11},{10,... | collective-permute-start | bytes 294920 | tf_op jit(solution)/shard_map/ppermute | solution.py:18
  19.1 5.6 %collective-permute-start.9 = (bf16[16,3072]{1,0:T(8,128)(2,1)S(1)}, bf16[16,3072]{1,0:T(8,128)(2,1)S(1)}, u32[]{:S(2)}, u32[]{:S(2)}) collective-permute-start(bf16[16,3072]{1,0:T(8,128)(2,1)S(1)} %get-tuple-element.41), channel_id=1, source_target_pairs={{0,1},{1,11},{2,3},{3,9},{8,0},{9,19},{10,2},{11,17},{16,8},{17,27... | collective-permute-start | bytes 294920 | tf_op jit(solution)/shard_map/ppermute | solution.py:30
  19.1 5.6 %collective-permute-start.10 = (bf16[16,3072]{1,0:T(8,128)(2,1)S(1)}, bf16[16,3072]{1,0:T(8,128)(2,1)S(1)}, u32[]{:S(2)}, u32[]{:S(2)}) collective-permute-start(bf16[16,3072]{1,0:T(8,128)(2,1)S(1)} %get-tuple-element.41), channel_id=1, source_target_pairs={{0,10},{1,0},{2,8},{3,2},{8,18},{9,1},{10,16},{11,3},{16,26},{17,9... | collective-permute-start | bytes 294920 | tf_op jit(solution)/shard_map/ppermute | solution.py:30
  24.9 6.6 %collective-permute-start.13 = (bf16[16,3072]{1,0:T(8,128)(2,1)S(1)}, bf16[16,3072]{1,0:T(8,128)(2,1)S(1)}, u32[]{:S(2)}, u32[]{:S(2)}) collective-permute-start(bf16[16,3072]{1,0:T(8,128)(2,1)S(1)} %get-tuple-element.44), channel_id=1, source_target_pairs={{0,6},{1,7},{2,4},{3,5},{4,2},{5,3},{6,0},{7,1},{8,14},{9,15},{10,... | collective-permute-start | bytes 294920 | tf_op jit(solution)/shard_map/ppermute | solution.py:18
  27.3 5.4 %collective-permute-start.14 = (bf16[16,3072]{1,0:T(8,128)(2,1)S(1)}, bf16[16,3072]{1,0:T(8,128)(2,1)S(1)}, u32[]{:S(2)}, u32[]{:S(2)}) collective-permute-start(bf16[16,3072]{1,0:T(8,128)(2,1)S(1)} %get-tuple-element.44), channel_id=1, source_target_pairs={{0,4},{1,5},{2,6},{3,7},{4,0},{5,1},{6,2},{7,3},{8,12},{9,13},{10,... | collective-permute-start | bytes 294920 | tf_op jit(solution)/shard_map/ppermute | solution.py:18
  28.0 5.0 %collective-permute-start.11 = (bf16[16,3072]{1,0:T(8,128)(2,1)S(1)}, bf16[16,3072]{1,0:T(8,128)(2,1)S(1)}, u32[]{:S(2)}, u32[]{:S(2)}) collective-permute-start(bf16[16,3072]{1,0:T(8,128)(2,1)S(1)} %get-tuple-element.44), channel_id=1, source_target_pairs={{0,2},{1,3},{2,0},{3,1},{4,6},{5,7},{6,4},{7,5},{8,10},{9,11},{10,... | collective-permute-start | bytes 294920 | tf_op jit(solution)/shard_map/ppermute | solution.py:18
  32.8 1.5 %collective-permute-start.15 = (bf16[32,3072]{1,0:T(8,128)(2,1)S(1)}, bf16[32,3072]{1,0:T(8,128)(2,1)S(1)}, u32[]{:S(2)}, u32[]{:S(2)}) collective-permute-start(bf16[32,3072]{1,0:T(8,128)(2,1)S(1)} %constant_dynamic-update-slice_fusion.9.mine_ref), channel_id=1, source_target_pairs={{0,1},{1,0},{2,3},{3,2},{4,5},{5,4},{6,7},{7,6},{8,9},{9,8},{10,11... | collective-permute-start | bytes 589832 | tf_op jit(solution)/shard_map/ppermute | solution.py:18
  33.0 2.5 %collective-permute-start.12 = (bf16[32,3072]{1,0:T(8,128)(2,1)S(1)}, bf16[32,3072]{1,0:T(8,128)(2,1)S(1)}, u32[]{:S(2)}, u32[]{:S(2)}) collective-permute-start(bf16[32,3072]{1,0:T(8,128)(2,1)S(1)} %constant_dynamic-update-slice_fusion.7.mine_ref), channel_id=1, source_target_pairs={{0,1},{1,0},{2,3},{3,2},{4,5},{5,4},{6,7},{7,6},{8,9},{9,8},{10,11... | collective-permute-start | bytes 589832 | tf_op jit(solution)/shard_map/ppermute | solution.py:18
  37.1 1.5 %collective-permute-start.16 = (bf16[32,3072]{1,0:T(8,128)(2,1)S(1)}, bf16[32,3072]{1,0:T(8,128)(2,1)S(1)}, u32[]{:S(2)}, u32[]{:S(2)}) collective-permute-start(bf16[32,3072]{1,0:T(8,128)(2,1)S(1)} %get-tuple-element.48), channel_id=1, source_target_pairs={{0,1},{1,0},{2,3},{3,2},{4,5},{5,4},{6,7},{7,6},{8,9},{9,8},{10,11... | collective-permute-start | bytes 589832 | tf_op jit(solution)/shard_map/ppermute | solution.py:18
  38.7 4.9 %collective-permute-start.17 = (bf16[16,3072]{1,0:T(8,128)(2,1)S(1)}, bf16[16,3072]{1,0:T(8,128)(2,1)S(1)}, u32[]{:S(2)}, u32[]{:S(2)}) collective-permute-start(bf16[16,3072]{1,0:T(8,128)(2,1)S(1)} %get-tuple-element.50), channel_id=1, source_target_pairs={{0,2},{1,3},{2,0},{3,1},{4,6},{5,7},{6,4},{7,5},{8,10},{9,11},{10,... | collective-permute-start | bytes 294920 | tf_op jit(solution)/shard_map/ppermute | solution.py:18

commit v7 on v6

--- a/solution.py
+++ b/solution.py
@@ -51,24 +51,23 @@
     return jnp.dot(left, right, preferred_element_type=jnp.float32).astype(jnp.bfloat16)
 
 
-def keyval_kernel(mine_ref, theirs_ref, wkv_ref, keys_ref, values_ref):
-    depth = mine_ref.shape[1]
-    partner = jnp.concatenate([mine_ref[...], theirs_ref[...]], 0)
-    keys_ref[...] = project(partner, wkv_ref[:depth])
-    values_ref[...] = project(partner, wkv_ref[depth:])
-
-
-def attend_kernel(tok, mine_ref, theirs_ref, keys_ref, values_ref, wq_ref, wo_ref, keep_ref, send_ref):
+def query_kernel(mine_ref, theirs_ref, wq_ref, query_ref):
+    query_ref[...] = project(jnp.concatenate([mine_ref[...], theirs_ref[...]], 0), wq_ref[...])
+
+
+def attend_kernel(tok, mine_ref, theirs_ref, query_ref, wkv_ref, wo_ref, keep_ref, send_ref):
     half, width = keep_ref.shape
     rows = 2 * half
-    query = project(jnp.concatenate([mine_ref[...], theirs_ref[...]], 0), wq_ref[...])
+    partner = jnp.concatenate([mine_ref[...], theirs_ref[...]], 0)
+    keys = project(partner, wkv_ref[:width])
+    values = project(partner, wkv_ref[width:])
     row_clip = lax.broadcasted_iota(jnp.int32, (rows, rows), 0) // tok
     col_clip = lax.broadcasted_iota(jnp.int32, (rows, rows), 1) // tok
     same_clip = row_clip == col_clip
-    heads = [slice(start, start + HEAD_DIM) for start in range(0, query.shape[1], HEAD_DIM)]
+    heads = [slice(start, start + HEAD_DIM) for start in range(0, keys.shape[1], HEAD_DIM)]
     scores = [
         lax.dot_general(
-            query[:, head], keys_ref[:, head], (((1,), (1,)), ((), ())), preferred_element_type=jnp.float32
+            query_ref[:, head], keys[:, head], (((1,), (1,)), ((), ())), preferred_element_type=jnp.float32
         )
         for head in heads
     ]
@@ -78,7 +77,7 @@
     ones = jnp.ones((rows, HEAD_DIM), jnp.bfloat16)
     sums = [jnp.dot(weight, ones, preferred_element_type=jnp.float32) for weight in weights]
     mixed = [
-        jnp.dot(weight, values_ref[:, head], preferred_element_type=jnp.float32)
+        jnp.dot(weight, values[:, head], preferred_element_type=jnp.float32)
         for weight, head in zip(weights, heads)
     ]
     mixed = jnp.concatenate([(mix / total).astype(jnp.bfloat16) for mix, total in zip(mixed, sums)], 1)
@@ -108,30 +107,24 @@
 def layer_part(own, partner, weights, tok):
     wq, wkv, wo = weights[0], *in_vmem(weights[1]), weights[2]
     (half, width), head_cols = own.shape, wq.shape[1]
-    partner_theirs = swapped(partner, 1)
-    own_theirs = swapped(own, 1)
     pushed = 2 * 256 * width * head_cols
-    keys, values = on_chip(
-        keyval_kernel,
-        [((2 * half, head_cols), jnp.bfloat16)] * 2,
-        partner, partner_theirs, wkv,
-        flops=2 * pushed,
+    (query,) = on_chip(
+        query_kernel, [((2 * half, head_cols), jnp.bfloat16)], own, swapped(own, 1), wq, flops=pushed
     )
     return on_chip(
         functools.partial(attend_kernel, tok),
         [((half, width), jnp.float32), ((half, width), jnp.bfloat16)],
-        own, own_theirs, keys, values, wq, wo,
-        flops=3 * pushed,
+        partner, swapped(partner, 1), query, wkv, wo,
+        flops=4 * pushed,
     )
 
 
 def sum_kernel(state_ref, keep_ref, sent_ref, own_ref, *out_refs):
     tok = state_ref.shape[0]
     total = keep_ref[...] + sent_ref[...].astype(jnp.float32)
-    own_ref[...] = state_ref[...].astype(jnp.float32) + total[-tok:]
+    own_ref[...] = state_ref[...].astype(jnp.float32) + total[:tok]
     for k, out_ref in enumerate(out_refs, 1):
-        start = total.shape[0] - (k + 1) * tok
-        out_ref[...] = total[start : start + tok].astype(jnp.bfloat16)
+        out_ref[...] = total[k * tok : (k + 1) * tok].astype(jnp.bfloat16)
 
 
 def entry_kernel(x_ref, gain_ref, normed_ref, x_out, gain_out, sems):
@@ -222,7 +215,7 @@
 
 def gathered(normed):
     lanes = lax.axis_size("lane")
-    towers = [[tower * lanes + 2 * k for k in reversed(range(lanes // 2))] for tower in range(2)]
+    towers = [[tower * lanes + 2 * k for k in range(lanes // 2)] for tower in range(2)]
     partner = [swapped(normed, d) for d in towers[1]]
     own = [swapped(normed, d) if d else normed for d in towers[0]]
     return jnp.concatenate(own, 0), jnp.concatenate(partner, 0)

time: 44.5 us -> 44.4 us (level)
  transfers between devices with their start and end apart: 18 -> 18, of which waited for: 12 -> 13; matrix products, arithmetic and copies ran while one was open for 0% -> 0% of each run, Pallas kernels for 12% -> 10%
where the time goes in v7:
time: 44.4 us; the launch traced here: 44.2 us
  waiting for transfers between devices  17.4 us (39%)
  starting transfers between devices  15.3 us (34%)
  Pallas kernels  9.79 us (22%)
  between operations  0.88 us (2%)
  other arithmetic  0.74 us (2%)
    ppermute x14, waiting for transfers between devices, swapped(): return lax.ppermute(value, BOTH, [(i, i ^ mask) for i in range(count)])  14.9 us
    ppermute x14, starting transfers between devices, swapped(): return lax.ppermute(value, BOTH, [(i, i ^ mask) for i in range(count)])  11.1 us
    pallas_call x6, Pallas kernels, on_chip(): pl.pallas_call(kernel, out_shape=tuple((jax.ShapeDtypeStruct(shape, dtype...  5.57 us
    ppermute x4, starting transfers between devices, climbed(): return lax.ppermute(value, ('section', 'lane'), pairs)  4.19 us
    pallas_call x1, Pallas kernels, load(): pl.pallas_call(load_kernel, out_shape=tuple((pltpu.VMEM(a.shape, a.dtype)...  3.01 us
    ppermute x4, waiting for transfers between devices, climbed(): return lax.ppermute(value, ('section', 'lane'), pairs)  2.47 us
    pallas_call x1, Pallas kernels, entry(): pl.pallas_call(entry_kernel, out_shape=(pltpu.VMEM(state.shape, jnp.bfloa...  1.04 us
  transfers between devices with their start and end apart: 18, of which 13 were waited for; matrix products, arithmetic and copies ran while one was open for 0% of the time, Pallas kernels for 10%

profile of v7, /device:TPU:0, one launch (start us, length us, event | category | flops | bytes accessed | tf_op | source)
XLA Modules:
  0.0 44.2 jit_solution(9556320173678922122)
XLA Ops:
  0.0 1.0 %shard_map.73 = (bf16[16,3072]{1,0:T(8,128)(2,1)S(1)}, bf16[16,3072]{1,0:T(8,128)(2,1)S(1)}, f32[1,3072]{1,0:T(1,128)S(1)}) custom-call(bf16[16,3072]{1,0:T(8,128)(2,1)} %bitcast.22, f32[1,3072]{1,0:T(1,128)} %bitcast.23), custom_call_target="tpu_custom_call" | custom-call | tf_op jit(solution)/shard_map/pallas_call | solution.py:143
  1.1 3.0 %collective-permute-start.3 = (bf16[16,3072]{1,0:T(8,128)(2,1)S(1)}, bf16[16,3072]{1,0:T(8,128)(2,1)S(1)}, u32[]{:S(2)}, u32[]{:S(2)}) collective-permute-start(bf16[16,3072]{1,0:T(8,128)(2,1)S(1)} %get-tuple-element.29), channel_id=1, source_target_pairs={{0,2},{1,3},{2,0},{3,1},{4,6},{5,7},{6,4},{7,5},{8,10},{9,11},{10,... | collective-permute-start | bytes 294920 | tf_op jit(solution)/shard_map/ppermute | solution.py:18
  4.1 1.5 %collective-permute-start = (bf16[16,3072]{1,0:T(8,128)(2,1)S(1)}, bf16[16,3072]{1,0:T(8,128)(2,1)S(1)}, u32[]{:S(2)}, u32[]{:S(2)}) collective-permute-start(bf16[16,3072]{1,0:T(8,128)(2,1)S(1)} %get-tuple-element.29), channel_id=1, source_target_pairs={{0,4},{1,5},{2,6},{3,7},{4,0},{5,1},{6,2},{7,3},{8,12},{9,13},{10,... | collective-permute-start | bytes 294920 | tf_op jit(solution)/shard_map/ppermute | solution.py:18
  5.6 0.0 collective-permute-start.1
  5.6 0.0 copy-start
  5.6 0.0 copy-start.2
  5.7 3.0 %shard_map.74.wkv_ref = bf16[6144,512]{1,0:T(8,128)(2,1)S(1)} custom-call(bf16[6144,512]{1,0:T(8,128)(2,1)} %bitcast.21), custom_call_target="tpu_custom_call" | custom-call | bytes 6291456 | tf_op jit(solution)/shard_map/pallas_call | solution.py:173
  8.7 0.0 collective-permute-done.3
  8.7 0.1 collective-permute-start.4
  8.8 0.7 %collective-permute-done = bf16[16,3072]{1,0:T(8,128)(2,1)S(1)} collective-permute-done((bf16[16,3072]{1,0:T(8,128)(2,1)S(1)}, bf16[16,3072]{1,0:T(8,128)(2,1)S(1)}, u32[]{:S(2)}, u32[]{:S(2)}) %collective-permute-start) | collective-permute-done | bytes 98336 | tf_op jit(solution)/shard_map/ppermute | solution.py:18
  9.5 1.6 %collective-permute-done.1 = bf16[16,3072]{1,0:T(8,128)(2,1)S(1)} collective-permute-done((bf16[16,3072]{1,0:T(8,128)(2,1)S(1)}, bf16[16,3072]{1,0:T(8,128)(2,1)S(1)}, u32[]{:S(2)}, u32[]{:S(2)}) %collective-permute-start.1) | collective-permute-done | bytes 98336 | tf_op jit(solution)/shard_map/ppermute | solution.py:18
  11.1 0.1 collective-permute-start.2
  11.2 0.0 collective-permute-done.4.theirs_ref
  11.2 0.0 copy-done
  11.2 0.7 %shard_map.75.query_ref = bf16[64,512]{1,0:T(8,128)(2,1)S(1)} custom-call(bf16[32,3072]{1,0:T(8,128)(2,1)S(1)} %constant_dynamic-update-slice_fusion.mine_ref, bf16[32,3072]{1,0:T(8,128)(2,1)S(1)} %collective-permute-done.4.theirs_ref, bf16[3072,512]{1,0:T(8,128)(2,1)S(1)} %bitcast.15), custom_call_target="tpu_custom_call" | custom-call | flops 805306368 | bytes 3538944 | tf_op jit(solution)/shard_map/pallas_call | solution.py:97
  11.9 0.7 %collective-permute-done.2.theirs_ref = bf16[32,3072]{1,0:T(8,128)(2,1)S(1)} collective-permute-done((bf16[32,3072]{1,0:T(8,128)(2,1)S(1)}, bf16[32,3072]{1,0:T(8,128)(2,1)S(1)}, u32[]{:S(2)}, u32[]{:S(2)}) %collective-permute-start.2) | collective-permute-done | bytes 196640 | tf_op jit(solution)/shard_map/ppermute | solution.py:18
  12.6 0.0 copy-done.2
  12.6 0.0 copy-start.1
  12.6 2.1 %shard_map.76 = (f32[32,3072]{1,0:T(8,128)S(1)}, bf16[32,3072]{1,0:T(8,128)(2,1)S(1)}) custom-call(bf16[32,3072]{1,0:T(8,128)(2,1)S(1)} %pad_maximum_fusion.mine_ref, bf16[32,3072]{1,0:T(8,128)(2,1)S(1)} %collective-permute-done.2.theirs_ref, bf16[64,512]{1,0:T(8,128)(2,1)S(1)} %shard_map.75.query_ref, bf16[6144,512]{1,0:T(8,128)(2,1)S(1)} %shard_map.74.wkv_ref, ...), custom_call_target="tpu_custom_call" | custom-call | flops 3221225472 | bytes 9895936 | tf_op jit(solution)/shard_map/pallas_call | solution.py:97
  14.7 0.2 collective-permute-start.5
  14.9 1.3 %collective-permute-done.5.sent_ref = bf16[32,3072]{1,0:T(8,128)(2,1)S(1)} collective-permute-done((bf16[32,3072]{1,0:T(8,128)(2,1)S(1)}, bf16[32,3072]{1,0:T(8,128)(2,1)S(1)}, u32[]{:S(2)}, u32[]{:S(2)}) %collective-permute-start.5) | collective-permute-done | bytes 196640 | tf_op jit(solution)/shard_map/ppermute | solution.py:18
  16.3 1.6 %collective-permute-start.6 = (bf16[16,3072]{1,0:T(8,128)(2,1)S(1)}, bf16[16,3072]{1,0:T(8,128)(2,1)S(1)}, u32[]{:S(2)}, u32[]{:S(2)}) collective-permute-start(bf16[16,3072]{1,0:T(8,128)(2,1)S(1)} %convert_element_type.9), channel_id=1, source_target_pairs={{0,8},{1,0},{2,10},{3,2},{8,16},{9,1},{10,18},{11,3},{16,24},{17,9... | collective-permute-start | bytes 294920 | tf_op jit(solution)/shard_map/ppermute | solution.py:30
  18.5 0.0 collective-permute-start.7
  18.6 1.0 %collective-permute-start.8 = (bf16[16,3072]{1,0:T(8,128)(2,1)S(1)}, bf16[16,3072]{1,0:T(8,128)(2,1)S(1)}, u32[]{:S(2)}, u32[]{:S(2)}) collective-permute-start(bf16[16,3072]{1,0:T(8,128)(2,1)S(1)} %get-tuple-element.35), channel_id=1, source_target_pairs={{0,2},{1,3},{2,0},{3,1},{4,6},{5,7},{6,4},{7,5},{8,10},{9,11},{10,... | collective-permute-start | bytes 294920 | tf_op jit(solution)/shard_map/ppermute | solution.py:18
  19.6 0.0 collective-permute-start.9
  19.6 2.6 %collective-permute-start.10 = (bf16[16,3072]{1,0:T(8,128)(2,1)S(1)}, bf16[16,3072]{1,0:T(8,128)(2,1)S(1)}, u32[]{:S(2)}, u32[]{:S(2)}) collective-permute-start(bf16[16,3072]{1,0:T(8,128)(2,1)S(1)} %get-tuple-element.35), channel_id=1, source_target_pairs={{0,10},{1,0},{2,8},{3,2},{8,18},{9,1},{10,16},{11,3},{16,26},{17,9... | collective-permute-start | bytes 294920 | tf_op jit(solution)/shard_map/ppermute | solution.py:30
  22.1 0.0 collective-permute-done.6
  22.1 1.0 %collective-permute-done.7 = bf16[16,3072]{1,0:T(8,128)(2,1)S(1)} collective-permute-done((bf16[16,3072]{1,0:T(8,128)(2,1)S(1)}, bf16[16,3072]{1,0:T(8,128)(2,1)S(1)}, u32[]{:S(2)}, u32[]{:S(2)}) %collective-permute-start.7) | collective-permute-done | bytes 98336 | tf_op jit(solution)/shard_map/ppermute | solution.py:30
  23.2 0.1 collective-permute-done.8
  23.3 1.4 %collective-permute-done.9 = bf16[16,3072]{1,0:T(8,128)(2,1)S(1)} collective-permute-done((bf16[16,3072]{1,0:T(8,128)(2,1)S(1)}, bf16[16,3072]{1,0:T(8,128)(2,1)S(1)}, u32[]{:S(2)}, u32[]{:S(2)}) %collective-permute-start.9) | collective-permute-done | bytes 98336 | tf_op jit(solution)/shard_map/ppermute | solution.py:30
  24.7 0.0 collective-permute-done.10
  24.8 0.0 copy-done.1
  24.8 0.2 shard_map.78
  25.0 1.4 %collective-permute-start.14 = (bf16[16,3072]{1,0:T(8,128)(2,1)S(1)}, bf16[16,3072]{1,0:T(8,128)(2,1)S(1)}, u32[]{:S(2)}, u32[]{:S(2)}) collective-permute-start(bf16[16,3072]{1,0:T(8,128)(2,1)S(1)} %get-tuple-element.38), channel_id=1, source_target_pairs={{0,2},{1,3},{2,0},{3,1},{4,6},{5,7},{6,4},{7,5},{8,10},{9,11},{10,... | collective-permute-start | bytes 294920 | tf_op jit(solution)/shard_map/ppermute | solution.py:18
  26.4 1.0 %collective-permute-start.11 = (bf16[16,3072]{1,0:T(8,128)(2,1)S(1)}, bf16[16,3072]{1,0:T(8,128)(2,1)S(1)}, u32[]{:S(2)}, u32[]{:S(2)}) collective-permute-start(bf16[16,3072]{1,0:T(8,128)(2,1)S(1)} %get-tuple-element.38), channel_id=1, source_target_pairs={{0,4},{1,5},{2,6},{3,7},{4,0},{5,1},{6,2},{7,3},{8,12},{9,13},{10,... | collective-permute-start | bytes 294920 | tf_op jit(solution)/shard_map/ppermute | solution.py:18
  27.4 1.2 %collective-permute-start.12 = (bf16[16,3072]{1,0:T(8,128)(2,1)S(1)}, bf16[16,3072]{1,0:T(8,128)(2,1)S(1)}, u32[]{:S(2)}, u32[]{:S(2)}) collective-permute-start(bf16[16,3072]{1,0:T(8,128)(2,1)S(1)} %get-tuple-element.38), channel_id=1, source_target_pairs={{0,6},{1,7},{2,4},{3,5},{4,2},{5,3},{6,0},{7,1},{8,14},{9,15},{10,... | collective-permute-start | bytes 294920 | tf_op jit(solution)/shard_map/ppermute | solution.py:18
  28.6 1.5 %collective-permute-done.14 = bf16[16,3072]{1,0:T(8,128)(2,1)S(1)} collective-permute-done((bf16[16,3072]{1,0:T(8,128)(2,1)S(1)}, bf16[16,3072]{1,0:T(8,128)(2,1)S(1)}, u32[]{:S(2)}, u32[]{:S(2)}) %collective-permute-start.14) | collective-permute-done | bytes 98336 | tf_op jit(solution)/shard_map/ppermute | solution.py:18
  30.1 0.1 collective-permute-start.15
  30.2 1.6 %collective-permute-done.11 = bf16[16,3072]{1,0:T(8,128)(2,1)S(1)} collective-permute-done((bf16[16,3072]{1,0:T(8,128)(2,1)S(1)}, bf16[16,3072]{1,0:T(8,128)(2,1)S(1)}, u32[]{:S(2)}, u32[]{:S(2)}) %collective-permute-start.11) | collective-permute-done | bytes 98336 | tf_op jit(solution)/shard_map/ppermute | solution.py:18
  31.7 1.7 %collective-permute-done.12 = bf16[16,3072]{1,0:T(8,128)(2,1)S(1)} collective-permute-done((bf16[16,3072]{1,0:T(8,128)(2,1)S(1)}, bf16[16,3072]{1,0:T(8,128)(2,1)S(1)}, u32[]{:S(2)}, u32[]{:S(2)}) %collective-permute-start.12) | collective-permute-done | bytes 98336 | tf_op jit(solution)/shard_map/ppermute | solution.py:18
  33.4 0.1 collective-permute-start.13
  33.5 0.0 collective-permute-done.15.theirs_ref
  33.5 0.7 %shard_map.79.query_ref = bf16[64,512]{1,0:T(8,128)(2,1)S(1)} custom-call(bf16[32,3072]{1,0:T(8,128)(2,1)S(1)} %constant_dynamic-update-slice_fusion.9.mine_ref, bf16[32,3072]{1,0:T(8,128)(2,1)S(1)} %collective-permute-done.15.theirs_ref, bf16[3072,512]{1,0:T(8,128)(2,1)S(1)} %bitcast.16), custom_call_target="tpu_custom_call" | custom-call | flops 805306368 | bytes 3538944 | tf_op jit(solution)/shard_map/pallas_call | solution.py:97
  34.2 0.8 %collective-permute-done.13.theirs_ref = bf16[32,3072]{1,0:T(8,128)(2,1)S(1)} collective-permute-done((bf16[32,3072]{1,0:T(8,128)(2,1)S(1)}, bf16[32,3072]{1,0:T(8,128)(2,1)S(1)}, u32[]{:S(2)}, u32[]{:S(2)}) %collective-permute-start.13) | collective-permute-done | bytes 196640 | tf_op jit(solution)/shard_map/ppermute | solution.py:18
  34.9 2.1 %shard_map.80 = (f32[32,3072]{1,0:T(8,128)S(1)}, bf16[32,3072]{1,0:T(8,128)(2,1)S(1)}) custom-call(bf16[32,3072]{1,0:T(8,128)(2,1)S(1)} %constant_dynamic-update-slice_fusion.7.mine_ref, bf16[32,3072]{1,0:T(8,128)(2,1)S(1)} %collective-permute-done.13.theirs_ref, bf16[64,512]{1,0:T(8,128)(2,1)S(1)} %shard_map.79.query_ref, ...), custom_call_target="tpu_custom_call" | custom-call | flops 3221225472 | bytes 9895936 | tf_op jit(solution)/shard_map/pallas_call | solution.py:97
  37.0 0.2 collective-permute-start.16
  37.2 1.3 %collective-permute-done.16.sent_ref = bf16[32,3072]{1,0:T(8,128)(2,1)S(1)} collective-permute-done((bf16[32,3072]{1,0:T(8,128)(2,1)S(1)}, bf16[32,3072]{1,0:T(8,128)(2,1)S(1)}, u32[]{:S(2)}, u32[]{:S(2)}) %collective-permute-start.16) | collective-permute-done | bytes 196640 | tf_op jit(solution)/shard_map/ppermute | solution.py:18
  38.6 1.3 %collective-permute-start.17 = (bf16[16,3072]{1,0:T(8,128)(2,1)S(1)}, bf16[16,3072]{1,0:T(8,128)(2,1)S(1)}, u32[]{:S(2)}, u32[]{:S(2)}) collective-permute-start(bf16[16,3072]{1,0:T(8,128)(2,1)S(1)} %get-tuple-element.42), channel_id=1, source_target_pairs={{0,2},{1,3},{2,0},{3,1},{4,6},{5,7},{6,4},{7,5},{8,10},{9,11},{10,... | collective-permute-start | bytes 294920 | tf_op jit(solution)/shard_map/ppermute | solution.py:18
  39.9 3.6 %collective-permute-done.17 = bf16[16,3072]{1,0:T(8,128)(2,1)S(1)} collective-permute-done((bf16[16,3072]{1,0:T(8,128)(2,1)S(1)}, bf16[16,3072]{1,0:T(8,128)(2,1)S(1)}, u32[]{:S(2)}, u32[]{:S(2)}) %collective-permute-start.17) | collective-permute-done | bytes 98336 | tf_op jit(solution)/shard_map/ppermute | solution.py:18
  43.5 0.7 %maximum_bitcast_fusion = bf16[2,1,1,16,3072]{4,3,2,1,0:T(8,128)(2,1)} fusion(bf16[1,16,3072]{2,1,0:T(8,128)(2,1)S(1)} %fusion, bf16[1,16,3072]{2,1,0:T(8,128)(2,1)S(1)} %bitcast.18), kind=kLoop, calls=%fused_computation.1 | loop fusion | flops 98304 | bytes 393216 | tf_op jit(solution)/shard_map/broadcast_in_dim | solution.py:255
  (16 shorter events, 0.2 us)
Async XLA Ops:
  1.1 7.6 %collective-permute-start.3 = (bf16[16,3072]{1,0:T(8,128)(2,1)S(1)}, bf16[16,3072]{1,0:T(8,128)(2,1)S(1)}, u32[]{:S(2)}, u32[]{:S(2)}) collective-permute-start(bf16[16,3072]{1,0:T(8,128)(2,1)S(1)} %get-tuple-element.29), channel_id=1, source_target_pairs={{0,2},{1,3},{2,0},{3,1},{4,6},{5,7},{6,4},{7,5},{8,10},{9,11},{10,... | collective-permute-start | bytes 294920 | tf_op jit(solution)/shard_map/ppermute | solution.py:18
  4.1 5.4 %collective-permute-start = (bf16[16,3072]{1,0:T(8,128)(2,1)S(1)}, bf16[16,3072]{1,0:T(8,128)(2,1)S(1)}, u32[]{:S(2)}, u32[]{:S(2)}) collective-permute-start(bf16[16,3072]{1,0:T(8,128)(2,1)S(1)} %get-tuple-element.29), channel_id=1, source_target_pairs={{0,4},{1,5},{2,6},{3,7},{4,0},{5,1},{6,2},{7,3},{8,12},{9,13},{10,... | collective-permute-start | bytes 294920 | tf_op jit(solution)/shard_map/ppermute | solution.py:18
  5.6 5.5 %collective-permute-start.1 = (bf16[16,3072]{1,0:T(8,128)(2,1)S(1)}, bf16[16,3072]{1,0:T(8,128)(2,1)S(1)}, u32[]{:S(2)}, u32[]{:S(2)}) collective-permute-start(bf16[16,3072]{1,0:T(8,128)(2,1)S(1)} %get-tuple-element.29), channel_id=1, source_target_pairs={{0,6},{1,7},{2,4},{3,5},{4,2},{5,3},{6,0},{7,1},{8,14},{9,15},{10,... | collective-permute-start | bytes 294920 | tf_op jit(solution)/shard_map/ppermute | solution.py:18
  5.6 5.6 %copy-start = (bf16[1,1,3072,512]{3,2,1,0:T(8,128)(2,1)S(1)}, bf16[1,1,3072,512]{3,2,1,0:T(8,128)(2,1)}, u32[]{:S(2)}) copy-start(bf16[1,1,3072,512]{3,2,1,0:T(8,128)(2,1)} %param.11) | copy-start | bytes 9437188
  5.6 7.0 %copy-start.2 = (bf16[1,1,512,3072]{3,2,1,0:T(8,128)(2,1)S(1)}, bf16[1,1,512,3072]{3,2,1,0:T(8,128)(2,1)}, u32[]{:S(2)}) copy-start(bf16[1,1,512,3072]{3,2,1,0:T(8,128)(2,1)} %param.13) | copy-start | bytes 9437188
  8.7 2.5 %collective-permute-start.4 = (bf16[32,3072]{1,0:T(8,128)(2,1)S(1)}, bf16[32,3072]{1,0:T(8,128)(2,1)S(1)}, u32[]{:S(2)}, u32[]{:S(2)}) collective-permute-start(bf16[32,3072]{1,0:T(8,128)(2,1)S(1)} %constant_dynamic-update-slice_fusion.mine_ref), channel_id=1, source_target_pairs={{0,1},{1,0},{2,3},{3,2},{4,5},{5,4},{6,7},{7,6},{8,9},{9,8},{10,11... | collective-permute-start | bytes 589832 | tf_op jit(solution)/shard_map/ppermute | solution.py:18
  11.1 1.5 %collective-permute-start.2 = (bf16[32,3072]{1,0:T(8,128)(2,1)S(1)}, bf16[32,3072]{1,0:T(8,128)(2,1)S(1)}, u32[]{:S(2)}, u32[]{:S(2)}) collective-permute-start(bf16[32,3072]{1,0:T(8,128)(2,1)S(1)} %pad_maximum_fusion.mine_ref), channel_id=1, source_target_pairs={{0,1},{1,0},{2,3},{3,2},{4,5},{5,4},{6,7},{7,6},{8,9},{9,8},{10,11... | collective-permute-start | bytes 589832 | tf_op jit(solution)/shard_map/ppermute | solution.py:18
  12.6 12.2 %copy-start.1 = (bf16[4,1,16,3072]{3,2,1,0:T(8,128)(2,1)S(1)}, bf16[4,1,16,3072]{3,2,1,0:T(8,128)(2,1)}, u32[]{:S(2)}) copy-start(bf16[4,1,16,3072]{3,2,1,0:T(8,128)(2,1)} %param.8) | copy-start | bytes 1179652
  14.7 1.5 %collective-permute-start.5 = (bf16[32,3072]{1,0:T(8,128)(2,1)S(1)}, bf16[32,3072]{1,0:T(8,128)(2,1)S(1)}, u32[]{:S(2)}, u32[]{:S(2)}) collective-permute-start(bf16[32,3072]{1,0:T(8,128)(2,1)S(1)} %get-tuple-element.33), channel_id=1, source_target_pairs={{0,1},{1,0},{2,3},{3,2},{4,5},{5,4},{6,7},{7,6},{8,9},{9,8},{10,11... | collective-permute-start | bytes 589832 | tf_op jit(solution)/shard_map/ppermute | solution.py:18
  16.3 5.8 %collective-permute-start.6 = (bf16[16,3072]{1,0:T(8,128)(2,1)S(1)}, bf16[16,3072]{1,0:T(8,128)(2,1)S(1)}, u32[]{:S(2)}, u32[]{:S(2)}) collective-permute-start(bf16[16,3072]{1,0:T(8,128)(2,1)S(1)} %convert_element_type.9), channel_id=1, source_target_pairs={{0,8},{1,0},{2,10},{3,2},{8,16},{9,1},{10,18},{11,3},{16,24},{17,9... | collective-permute-start | bytes 294920 | tf_op jit(solution)/shard_map/ppermute | solution.py:30
  18.5 4.6 %collective-permute-start.7 = (bf16[16,3072]{1,0:T(8,128)(2,1)S(1)}, bf16[16,3072]{1,0:T(8,128)(2,1)S(1)}, u32[]{:S(2)}, u32[]{:S(2)}) collective-permute-start(bf16[16,3072]{1,0:T(8,128)(2,1)S(1)} %convert_element_type.9), channel_id=1, source_target_pairs={{0,1},{1,9},{2,3},{3,11},{8,0},{9,17},{10,2},{11,19},{16,8},{17,25... | collective-permute-start | bytes 294920 | tf_op jit(solution)/shard_map/ppermute | solution.py:30
  18.6 4.7 %collective-permute-start.8 = (bf16[16,3072]{1,0:T(8,128)(2,1)S(1)}, bf16[16,3072]{1,0:T(8,128)(2,1)S(1)}, u32[]{:S(2)}, u32[]{:S(2)}) collective-permute-start(bf16[16,3072]{1,0:T(8,128)(2,1)S(1)} %get-tuple-element.35), channel_id=1, source_target_pairs={{0,2},{1,3},{2,0},{3,1},{4,6},{5,7},{6,4},{7,5},{8,10},{9,11},{10,... | collective-permute-start | bytes 294920 | tf_op jit(solution)/shard_map/ppermute | solution.py:18
  19.6 5.2 %collective-permute-start.9 = (bf16[16,3072]{1,0:T(8,128)(2,1)S(1)}, bf16[16,3072]{1,0:T(8,128)(2,1)S(1)}, u32[]{:S(2)}, u32[]{:S(2)}) collective-permute-start(bf16[16,3072]{1,0:T(8,128)(2,1)S(1)} %get-tuple-element.35), channel_id=1, source_target_pairs={{0,1},{1,11},{2,3},{3,9},{8,0},{9,19},{10,2},{11,17},{16,8},{17,27... | collective-permute-start | bytes 294920 | tf_op jit(solution)/shard_map/ppermute | solution.py:30
  19.6 5.2 %collective-permute-start.10 = (bf16[16,3072]{1,0:T(8,128)(2,1)S(1)}, bf16[16,3072]{1,0:T(8,128)(2,1)S(1)}, u32[]{:S(2)}, u32[]{:S(2)}) collective-permute-start(bf16[16,3072]{1,0:T(8,128)(2,1)S(1)} %get-tuple-element.35), channel_id=1, source_target_pairs={{0,10},{1,0},{2,8},{3,2},{8,18},{9,1},{10,16},{11,3},{16,26},{17,9... | collective-permute-start | bytes 294920 | tf_op jit(solution)/shard_map/ppermute | solution.py:30
  25.0 5.1 %collective-permute-start.14 = (bf16[16,3072]{1,0:T(8,128)(2,1)S(1)}, bf16[16,3072]{1,0:T(8,128)(2,1)S(1)}, u32[]{:S(2)}, u32[]{:S(2)}) collective-permute-start(bf16[16,3072]{1,0:T(8,128)(2,1)S(1)} %get-tuple-element.38), channel_id=1, source_target_pairs={{0,2},{1,3},{2,0},{3,1},{4,6},{5,7},{6,4},{7,5},{8,10},{9,11},{10,... | collective-permute-start | bytes 294920 | tf_op jit(solution)/shard_map/ppermute | solution.py:18
  26.4 5.3 %collective-permute-start.11 = (bf16[16,3072]{1,0:T(8,128)(2,1)S(1)}, bf16[16,3072]{1,0:T(8,128)(2,1)S(1)}, u32[]{:S(2)}, u32[]{:S(2)}) collective-permute-start(bf16[16,3072]{1,0:T(8,128)(2,1)S(1)} %get-tuple-element.38), channel_id=1, source_target_pairs={{0,4},{1,5},{2,6},{3,7},{4,0},{5,1},{6,2},{7,3},{8,12},{9,13},{10,... | collective-permute-start | bytes 294920 | tf_op jit(solution)/shard_map/ppermute | solution.py:18
  27.4 6.0 %collective-permute-start.12 = (bf16[16,3072]{1,0:T(8,128)(2,1)S(1)}, bf16[16,3072]{1,0:T(8,128)(2,1)S(1)}, u32[]{:S(2)}, u32[]{:S(2)}) collective-permute-start(bf16[16,3072]{1,0:T(8,128)(2,1)S(1)} %get-tuple-element.38), channel_id=1, source_target_pairs={{0,6},{1,7},{2,4},{3,5},{4,2},{5,3},{6,0},{7,1},{8,14},{9,15},{10,... | collective-permute-start | bytes 294920 | tf_op jit(solution)/shard_map/ppermute | solution.py:18
  30.1 3.4 %collective-permute-start.15 = (bf16[32,3072]{1,0:T(8,128)(2,1)S(1)}, bf16[32,3072]{1,0:T(8,128)(2,1)S(1)}, u32[]{:S(2)}, u32[]{:S(2)}) collective-permute-start(bf16[32,3072]{1,0:T(8,128)(2,1)S(1)} %constant_dynamic-update-slice_fusion.9.mine_ref), channel_id=1, source_target_pairs={{0,1},{1,0},{2,3},{3,2},{4,5},{5,4},{6,7},{7,6},{8,9},{9,8},{10,11... | collective-permute-start | bytes 589832 | tf_op jit(solution)/shard_map/ppermute | solution.py:18
  33.4 1.5 %collective-permute-start.13 = (bf16[32,3072]{1,0:T(8,128)(2,1)S(1)}, bf16[32,3072]{1,0:T(8,128)(2,1)S(1)}, u32[]{:S(2)}, u32[]{:S(2)}) collective-permute-start(bf16[32,3072]{1,0:T(8,128)(2,1)S(1)} %constant_dynamic-update-slice_fusion.7.mine_ref), channel_id=1, source_target_pairs={{0,1},{1,0},{2,3},{3,2},{4,5},{5,4},{6,7},{7,6},{8,9},{9,8},{10,11... | collective-permute-start | bytes 589832 | tf_op jit(solution)/shard_map/ppermute | solution.py:18
  37.0 1.5 %collective-permute-start.16 = (bf16[32,3072]{1,0:T(8,128)(2,1)S(1)}, bf16[32,3072]{1,0:T(8,128)(2,1)S(1)}, u32[]{:S(2)}, u32[]{:S(2)}) collective-permute-start(bf16[32,3072]{1,0:T(8,128)(2,1)S(1)} %get-tuple-element.40), channel_id=1, source_target_pairs={{0,1},{1,0},{2,3},{3,2},{4,5},{5,4},{6,7},{7,6},{8,9},{9,8},{10,11... | collective-permute-start | bytes 589832 | tf_op jit(solution)/shard_map/ppermute | solution.py:18
  38.6 4.9 %collective-permute-start.17 = (bf16[16,3072]{1,0:T(8,128)(2,1)S(1)}, bf16[16,3072]{1,0:T(8,128)(2,1)S(1)}, u32[]{:S(2)}, u32[]{:S(2)}) collective-permute-start(bf16[16,3072]{1,0:T(8,128)(2,1)S(1)} %get-tuple-element.42), channel_id=1, source_target_pairs={{0,2},{1,3},{2,0},{3,1},{4,6},{5,7},{6,4},{7,5},{8,10},{9,11},{10,... | collective-permute-start | bytes 294920 | tf_op jit(solution)/shard_map/ppermute | solution.py:18

commit v8 on v7

--- a/solution.py
+++ b/solution.py
@@ -128,10 +128,11 @@
 
 
 def entry_kernel(x_ref, gain_ref, normed_ref, x_out, gain_out, sems):
-    copies = [
-        pltpu.make_async_copy(x_ref, x_out, sems.at[0]),
-        pltpu.make_async_copy(gain_ref, gain_out, sems.at[1]),
-    ]
+    width = x_ref.shape[1] // PIECES
+    copies = [pltpu.make_async_copy(gain_ref, gain_out, sems.at[PIECES])]
+    for i in range(PIECES):
+        here = (slice(None), pl.ds(i * width, width))
+        copies.append(pltpu.make_async_copy(x_ref.at[here], x_out.at[here], sems.at[i]))
     for copy in copies:
         copy.start()
     for copy in copies:
@@ -149,7 +150,7 @@
         ),
         in_specs=[pl.BlockSpec(memory_space=pltpu.HBM)] * 2,
         out_specs=(pl.BlockSpec(memory_space=pltpu.VMEM),) * 3,
-        scratch_shapes=[pltpu.SemaphoreType.DMA((2,))],
+        scratch_shapes=[pltpu.SemaphoreType.DMA((PIECES + 1,))],
         compiler_params=pltpu.CompilerParams(vmem_limit_bytes=16 << 20),
     )(*in_hbm(state, gain))
 

time: 44.4 us -> 44.4 us (level)
  no operation moved by 1% of the time
where the time goes in v8:
time: 44.4 us; the launch traced here: 44.2 us
  waiting for transfers between devices  17.4 us (39%)
  starting transfers between devices  15.3 us (34%)
  Pallas kernels  9.73 us (22%)
  between operations  0.88 us (2%)
  other arithmetic  0.74 us (2%)
    ppermute x14, waiting for transfers between devices, swapped(): return lax.ppermute(value, BOTH, [(i, i ^ mask) for i in range(count)])  14.9 us
    ppermute x14, starting transfers between devices, swapped(): return lax.ppermute(value, BOTH, [(i, i ^ mask) for i in range(count)])  11.1 us
    pallas_call x6, Pallas kernels, on_chip(): pl.pallas_call(kernel, out_shape=tuple((jax.ShapeDtypeStruct(shape, dtype...  5.57 us
    ppermute x4, starting transfers between devices, climbed(): return lax.ppermute(value, ('section', 'lane'), pairs)  4.18 us
    pallas_call x1, Pallas kernels, load(): pl.pallas_call(load_kernel, out_shape=tuple((pltpu.VMEM(a.shape, a.dtype)...  3.01 us
    ppermute x4, waiting for transfers between devices, climbed(): return lax.ppermute(value, ('section', 'lane'), pairs)  2.47 us
    pallas_call x1, Pallas kernels, entry(): pl.pallas_call(entry_kernel, out_shape=(pltpu.VMEM(state.shape, jnp.bfloa...  0.98 us
  transfers between devices with their start and end apart: 18, of which 13 were waited for; matrix products, arithmetic and copies ran while one was open for 0% of the time, Pallas kernels for 10%

profile of v8, /device:TPU:0, one launch (start us, length us, event | category | flops | bytes accessed | tf_op | source)
XLA Modules:
  0.0 44.2 jit_solution(7150017020118871431)
XLA Ops:
  0.0 1.0 %shard_map.73 = (bf16[16,3072]{1,0:T(8,128)(2,1)S(1)}, bf16[16,3072]{1,0:T(8,128)(2,1)S(1)}, f32[1,3072]{1,0:T(1,128)S(1)}) custom-call(bf16[16,3072]{1,0:T(8,128)(2,1)} %bitcast.22, f32[1,3072]{1,0:T(1,128)} %bitcast.23), custom_call_target="tpu_custom_call" | custom-call | tf_op jit(solution)/shard_map/pallas_call | solution.py:144
  1.0 3.0 %collective-permute-start.3 = (bf16[16,3072]{1,0:T(8,128)(2,1)S(1)}, bf16[16,3072]{1,0:T(8,128)(2,1)S(1)}, u32[]{:S(2)}, u32[]{:S(2)}) collective-permute-start(bf16[16,3072]{1,0:T(8,128)(2,1)S(1)} %get-tuple-element.29), channel_id=1, source_target_pairs={{0,2},{1,3},{2,0},{3,1},{4,6},{5,7},{6,4},{7,5},{8,10},{9,11},{10,... | collective-permute-start | bytes 294920 | tf_op jit(solution)/shard_map/ppermute | solution.py:18
  4.0 1.5 %collective-permute-start = (bf16[16,3072]{1,0:T(8,128)(2,1)S(1)}, bf16[16,3072]{1,0:T(8,128)(2,1)S(1)}, u32[]{:S(2)}, u32[]{:S(2)}) collective-permute-start(bf16[16,3072]{1,0:T(8,128)(2,1)S(1)} %get-tuple-element.29), channel_id=1, source_target_pairs={{0,4},{1,5},{2,6},{3,7},{4,0},{5,1},{6,2},{7,3},{8,12},{9,13},{10,... | collective-permute-start | bytes 294920 | tf_op jit(solution)/shard_map/ppermute | solution.py:18
  5.5 0.0 collective-permute-start.1
  5.6 0.0 copy-start
  5.6 0.0 copy-start.2
  5.6 3.0 %shard_map.74.wkv_ref = bf16[6144,512]{1,0:T(8,128)(2,1)S(1)} custom-call(bf16[6144,512]{1,0:T(8,128)(2,1)} %bitcast.21), custom_call_target="tpu_custom_call" | custom-call | bytes 6291456 | tf_op jit(solution)/shard_map/pallas_call | solution.py:174
  8.6 0.0 collective-permute-done.3
  8.6 0.1 collective-permute-start.4
  8.7 0.7 %collective-permute-done = bf16[16,3072]{1,0:T(8,128)(2,1)S(1)} collective-permute-done((bf16[16,3072]{1,0:T(8,128)(2,1)S(1)}, bf16[16,3072]{1,0:T(8,128)(2,1)S(1)}, u32[]{:S(2)}, u32[]{:S(2)}) %collective-permute-start) | collective-permute-done | bytes 98336 | tf_op jit(solution)/shard_map/ppermute | solution.py:18
  9.4 1.6 %collective-permute-done.1 = bf16[16,3072]{1,0:T(8,128)(2,1)S(1)} collective-permute-done((bf16[16,3072]{1,0:T(8,128)(2,1)S(1)}, bf16[16,3072]{1,0:T(8,128)(2,1)S(1)}, u32[]{:S(2)}, u32[]{:S(2)}) %collective-permute-start.1) | collective-permute-done | bytes 98336 | tf_op jit(solution)/shard_map/ppermute | solution.py:18
  11.0 0.1 collective-permute-start.2
  11.1 0.0 collective-permute-done.4.theirs_ref
  11.1 0.0 copy-done
  11.1 0.7 %shard_map.75.query_ref = bf16[64,512]{1,0:T(8,128)(2,1)S(1)} custom-call(bf16[32,3072]{1,0:T(8,128)(2,1)S(1)} %constant_dynamic-update-slice_fusion.mine_ref, bf16[32,3072]{1,0:T(8,128)(2,1)S(1)} %collective-permute-done.4.theirs_ref, bf16[3072,512]{1,0:T(8,128)(2,1)S(1)} %bitcast.15), custom_call_target="tpu_custom_call" | custom-call | flops 805306368 | bytes 3538944 | tf_op jit(solution)/shard_map/pallas_call | solution.py:97
  11.8 0.7 %collective-permute-done.2.theirs_ref = bf16[32,3072]{1,0:T(8,128)(2,1)S(1)} collective-permute-done((bf16[32,3072]{1,0:T(8,128)(2,1)S(1)}, bf16[32,3072]{1,0:T(8,128)(2,1)S(1)}, u32[]{:S(2)}, u32[]{:S(2)}) %collective-permute-start.2) | collective-permute-done | bytes 196640 | tf_op jit(solution)/shard_map/ppermute | solution.py:18
  12.6 0.0 copy-done.2
  12.6 0.0 copy-start.1
  12.6 2.1 %shard_map.76 = (f32[32,3072]{1,0:T(8,128)S(1)}, bf16[32,3072]{1,0:T(8,128)(2,1)S(1)}) custom-call(bf16[32,3072]{1,0:T(8,128)(2,1)S(1)} %pad_maximum_fusion.mine_ref, bf16[32,3072]{1,0:T(8,128)(2,1)S(1)} %collective-permute-done.2.theirs_ref, bf16[64,512]{1,0:T(8,128)(2,1)S(1)} %shard_map.75.query_ref, bf16[6144,512]{1,0:T(8,128)(2,1)S(1)} %shard_map.74.wkv_ref, ...), custom_call_target="tpu_custom_call" | custom-call | flops 3221225472 | bytes 9895936 | tf_op jit(solution)/shard_map/pallas_call | solution.py:97
  14.7 0.2 collective-permute-start.5
  14.9 1.3 %collective-permute-done.5.sent_ref = bf16[32,3072]{1,0:T(8,128)(2,1)S(1)} collective-permute-done((bf16[32,3072]{1,0:T(8,128)(2,1)S(1)}, bf16[32,3072]{1,0:T(8,128)(2,1)S(1)}, u32[]{:S(2)}, u32[]{:S(2)}) %collective-permute-start.5) | collective-permute-done | bytes 196640 | tf_op jit(solution)/shard_map/ppermute | solution.py:18
  16.2 1.6 %collective-permute-start.6 = (bf16[16,3072]{1,0:T(8,128)(2,1)S(1)}, bf16[16,3072]{1,0:T(8,128)(2,1)S(1)}, u32[]{:S(2)}, u32[]{:S(2)}) collective-permute-start(bf16[16,3072]{1,0:T(8,128)(2,1)S(1)} %convert_element_type.9), channel_id=1, source_target_pairs={{0,8},{1,0},{2,10},{3,2},{8,16},{9,1},{10,18},{11,3},{16,24},{17,9... | collective-permute-start | bytes 294920 | tf_op jit(solution)/shard_map/ppermute | solution.py:30
  18.5 0.0 collective-permute-start.7
  18.5 1.0 %collective-permute-start.8 = (bf16[16,3072]{1,0:T(8,128)(2,1)S(1)}, bf16[16,3072]{1,0:T(8,128)(2,1)S(1)}, u32[]{:S(2)}, u32[]{:S(2)}) collective-permute-start(bf16[16,3072]{1,0:T(8,128)(2,1)S(1)} %get-tuple-element.35), channel_id=1, source_target_pairs={{0,2},{1,3},{2,0},{3,1},{4,6},{5,7},{6,4},{7,5},{8,10},{9,11},{10,... | collective-permute-start | bytes 294920 | tf_op jit(solution)/shard_map/ppermute | solution.py:18
  19.5 0.0 collective-permute-start.9
  19.5 2.6 %collective-permute-start.10 = (bf16[16,3072]{1,0:T(8,128)(2,1)S(1)}, bf16[16,3072]{1,0:T(8,128)(2,1)S(1)}, u32[]{:S(2)}, u32[]{:S(2)}) collective-permute-start(bf16[16,3072]{1,0:T(8,128)(2,1)S(1)} %get-tuple-element.35), channel_id=1, source_target_pairs={{0,10},{1,0},{2,8},{3,2},{8,18},{9,1},{10,16},{11,3},{16,26},{17,9... | collective-permute-start | bytes 294920 | tf_op jit(solution)/shard_map/ppermute | solution.py:30
  22.1 0.0 collective-permute-done.6
  22.1 1.0 %collective-permute-done.7 = bf16[16,3072]{1,0:T(8,128)(2,1)S(1)} collective-permute-done((bf16[16,3072]{1,0:T(8,128)(2,1)S(1)}, bf16[16,3072]{1,0:T(8,128)(2,1)S(1)}, u32[]{:S(2)}, u32[]{:S(2)}) %collective-permute-start.7) | collective-permute-done | bytes 98336 | tf_op jit(solution)/shard_map/ppermute | solution.py:30
  23.1 0.1 collective-permute-done.8
  23.2 1.4 %collective-permute-done.9 = bf16[16,3072]{1,0:T(8,128)(2,1)S(1)} collective-permute-done((bf16[16,3072]{1,0:T(8,128)(2,1)S(1)}, bf16[16,3072]{1,0:T(8,128)(2,1)S(1)}, u32[]{:S(2)}, u32[]{:S(2)}) %collective-permute-start.9) | collective-permute-done | bytes 98336 | tf_op jit(solution)/shard_map/ppermute | solution.py:30
  24.7 0.0 collective-permute-done.10
  24.7 0.0 copy-done.1
  24.7 0.2 shard_map.78
  24.9 1.4 %collective-permute-start.14 = (bf16[16,3072]{1,0:T(8,128)(2,1)S(1)}, bf16[16,3072]{1,0:T(8,128)(2,1)S(1)}, u32[]{:S(2)}, u32[]{:S(2)}) collective-permute-start(bf16[16,3072]{1,0:T(8,128)(2,1)S(1)} %get-tuple-element.38), channel_id=1, source_target_pairs={{0,2},{1,3},{2,0},{3,1},{4,6},{5,7},{6,4},{7,5},{8,10},{9,11},{10,... | collective-permute-start | bytes 294920 | tf_op jit(solution)/shard_map/ppermute | solution.py:18
  26.3 1.0 %collective-permute-start.11 = (bf16[16,3072]{1,0:T(8,128)(2,1)S(1)}, bf16[16,3072]{1,0:T(8,128)(2,1)S(1)}, u32[]{:S(2)}, u32[]{:S(2)}) collective-permute-start(bf16[16,3072]{1,0:T(8,128)(2,1)S(1)} %get-tuple-element.38), channel_id=1, source_target_pairs={{0,4},{1,5},{2,6},{3,7},{4,0},{5,1},{6,2},{7,3},{8,12},{9,13},{10,... | collective-permute-start | bytes 294920 | tf_op jit(solution)/shard_map/ppermute | solution.py:18
  27.3 1.2 %collective-permute-start.12 = (bf16[16,3072]{1,0:T(8,128)(2,1)S(1)}, bf16[16,3072]{1,0:T(8,128)(2,1)S(1)}, u32[]{:S(2)}, u32[]{:S(2)}) collective-permute-start(bf16[16,3072]{1,0:T(8,128)(2,1)S(1)} %get-tuple-element.38), channel_id=1, source_target_pairs={{0,6},{1,7},{2,4},{3,5},{4,2},{5,3},{6,0},{7,1},{8,14},{9,15},{10,... | collective-permute-start | bytes 294920 | tf_op jit(solution)/shard_map/ppermute | solution.py:18
  28.5 1.5 %collective-permute-done.14 = bf16[16,3072]{1,0:T(8,128)(2,1)S(1)} collective-permute-done((bf16[16,3072]{1,0:T(8,128)(2,1)S(1)}, bf16[16,3072]{1,0:T(8,128)(2,1)S(1)}, u32[]{:S(2)}, u32[]{:S(2)}) %collective-permute-start.14) | collective-permute-done | bytes 98336 | tf_op jit(solution)/shard_map/ppermute | solution.py:18
  30.0 0.1 collective-permute-start.15
  30.1 1.6 %collective-permute-done.11 = bf16[16,3072]{1,0:T(8,128)(2,1)S(1)} collective-permute-done((bf16[16,3072]{1,0:T(8,128)(2,1)S(1)}, bf16[16,3072]{1,0:T(8,128)(2,1)S(1)}, u32[]{:S(2)}, u32[]{:S(2)}) %collective-permute-start.11) | collective-permute-done | bytes 98336 | tf_op jit(solution)/shard_map/ppermute | solution.py:18
  31.6 1.7 %collective-permute-done.12 = bf16[16,3072]{1,0:T(8,128)(2,1)S(1)} collective-permute-done((bf16[16,3072]{1,0:T(8,128)(2,1)S(1)}, bf16[16,3072]{1,0:T(8,128)(2,1)S(1)}, u32[]{:S(2)}, u32[]{:S(2)}) %collective-permute-start.12) | collective-permute-done | bytes 98336 | tf_op jit(solution)/shard_map/ppermute | solution.py:18
  33.4 0.1 collective-permute-start.13
  33.4 0.0 collective-permute-done.15.theirs_ref
  33.5 0.7 %shard_map.79.query_ref = bf16[64,512]{1,0:T(8,128)(2,1)S(1)} custom-call(bf16[32,3072]{1,0:T(8,128)(2,1)S(1)} %constant_dynamic-update-slice_fusion.9.mine_ref, bf16[32,3072]{1,0:T(8,128)(2,1)S(1)} %collective-permute-done.15.theirs_ref, bf16[3072,512]{1,0:T(8,128)(2,1)S(1)} %bitcast.16), custom_call_target="tpu_custom_call" | custom-call | flops 805306368 | bytes 3538944 | tf_op jit(solution)/shard_map/pallas_call | solution.py:97
  34.1 0.8 %collective-permute-done.13.theirs_ref = bf16[32,3072]{1,0:T(8,128)(2,1)S(1)} collective-permute-done((bf16[32,3072]{1,0:T(8,128)(2,1)S(1)}, bf16[32,3072]{1,0:T(8,128)(2,1)S(1)}, u32[]{:S(2)}, u32[]{:S(2)}) %collective-permute-start.13) | collective-permute-done | bytes 196640 | tf_op jit(solution)/shard_map/ppermute | solution.py:18
  34.9 2.1 %shard_map.80 = (f32[32,3072]{1,0:T(8,128)S(1)}, bf16[32,3072]{1,0:T(8,128)(2,1)S(1)}) custom-call(bf16[32,3072]{1,0:T(8,128)(2,1)S(1)} %constant_dynamic-update-slice_fusion.7.mine_ref, bf16[32,3072]{1,0:T(8,128)(2,1)S(1)} %collective-permute-done.13.theirs_ref, bf16[64,512]{1,0:T(8,128)(2,1)S(1)} %shard_map.79.query_ref, ...), custom_call_target="tpu_custom_call" | custom-call | flops 3221225472 | bytes 9895936 | tf_op jit(solution)/shard_map/pallas_call | solution.py:97
  37.0 0.2 collective-permute-start.16
  37.2 1.3 %collective-permute-done.16.sent_ref = bf16[32,3072]{1,0:T(8,128)(2,1)S(1)} collective-permute-done((bf16[32,3072]{1,0:T(8,128)(2,1)S(1)}, bf16[32,3072]{1,0:T(8,128)(2,1)S(1)}, u32[]{:S(2)}, u32[]{:S(2)}) %collective-permute-start.16) | collective-permute-done | bytes 196640 | tf_op jit(solution)/shard_map/ppermute | solution.py:18
  38.5 1.3 %collective-permute-start.17 = (bf16[16,3072]{1,0:T(8,128)(2,1)S(1)}, bf16[16,3072]{1,0:T(8,128)(2,1)S(1)}, u32[]{:S(2)}, u32[]{:S(2)}) collective-permute-start(bf16[16,3072]{1,0:T(8,128)(2,1)S(1)} %get-tuple-element.42), channel_id=1, source_target_pairs={{0,2},{1,3},{2,0},{3,1},{4,6},{5,7},{6,4},{7,5},{8,10},{9,11},{10,... | collective-permute-start | bytes 294920 | tf_op jit(solution)/shard_map/ppermute | solution.py:18
  39.8 3.6 %collective-permute-done.17 = bf16[16,3072]{1,0:T(8,128)(2,1)S(1)} collective-permute-done((bf16[16,3072]{1,0:T(8,128)(2,1)S(1)}, bf16[16,3072]{1,0:T(8,128)(2,1)S(1)}, u32[]{:S(2)}, u32[]{:S(2)}) %collective-permute-start.17) | collective-permute-done | bytes 98336 | tf_op jit(solution)/shard_map/ppermute | solution.py:18
  43.5 0.7 %maximum_bitcast_fusion = bf16[2,1,1,16,3072]{4,3,2,1,0:T(8,128)(2,1)} fusion(bf16[1,16,3072]{2,1,0:T(8,128)(2,1)S(1)} %fusion, bf16[1,16,3072]{2,1,0:T(8,128)(2,1)S(1)} %bitcast.18), kind=kLoop, calls=%fused_computation.1 | loop fusion | flops 98304 | bytes 393216 | tf_op jit(solution)/shard_map/broadcast_in_dim | solution.py:256
  (16 shorter events, 0.2 us)
Async XLA Ops:
  1.0 7.6 %collective-permute-start.3 = (bf16[16,3072]{1,0:T(8,128)(2,1)S(1)}, bf16[16,3072]{1,0:T(8,128)(2,1)S(1)}, u32[]{:S(2)}, u32[]{:S(2)}) collective-permute-start(bf16[16,3072]{1,0:T(8,128)(2,1)S(1)} %get-tuple-element.29), channel_id=1, source_target_pairs={{0,2},{1,3},{2,0},{3,1},{4,6},{5,7},{6,4},{7,5},{8,10},{9,11},{10,... | collective-permute-start | bytes 294920 | tf_op jit(solution)/shard_map/ppermute | solution.py:18
  4.0 5.4 %collective-permute-start = (bf16[16,3072]{1,0:T(8,128)(2,1)S(1)}, bf16[16,3072]{1,0:T(8,128)(2,1)S(1)}, u32[]{:S(2)}, u32[]{:S(2)}) collective-permute-start(bf16[16,3072]{1,0:T(8,128)(2,1)S(1)} %get-tuple-element.29), channel_id=1, source_target_pairs={{0,4},{1,5},{2,6},{3,7},{4,0},{5,1},{6,2},{7,3},{8,12},{9,13},{10,... | collective-permute-start | bytes 294920 | tf_op jit(solution)/shard_map/ppermute | solution.py:18
  5.5 5.5 %collective-permute-start.1 = (bf16[16,3072]{1,0:T(8,128)(2,1)S(1)}, bf16[16,3072]{1,0:T(8,128)(2,1)S(1)}, u32[]{:S(2)}, u32[]{:S(2)}) collective-permute-start(bf16[16,3072]{1,0:T(8,128)(2,1)S(1)} %get-tuple-element.29), channel_id=1, source_target_pairs={{0,6},{1,7},{2,4},{3,5},{4,2},{5,3},{6,0},{7,1},{8,14},{9,15},{10,... | collective-permute-start | bytes 294920 | tf_op jit(solution)/shard_map/ppermute | solution.py:18
  5.6 5.6 %copy-start = (bf16[1,1,3072,512]{3,2,1,0:T(8,128)(2,1)S(1)}, bf16[1,1,3072,512]{3,2,1,0:T(8,128)(2,1)}, u32[]{:S(2)}) copy-start(bf16[1,1,3072,512]{3,2,1,0:T(8,128)(2,1)} %param.11) | copy-start | bytes 9437188
  5.6 7.0 %copy-start.2 = (bf16[1,1,512,3072]{3,2,1,0:T(8,128)(2,1)S(1)}, bf16[1,1,512,3072]{3,2,1,0:T(8,128)(2,1)}, u32[]{:S(2)}) copy-start(bf16[1,1,512,3072]{3,2,1,0:T(8,128)(2,1)} %param.13) | copy-start | bytes 9437188
  8.6 2.5 %collective-permute-start.4 = (bf16[32,3072]{1,0:T(8,128)(2,1)S(1)}, bf16[32,3072]{1,0:T(8,128)(2,1)S(1)}, u32[]{:S(2)}, u32[]{:S(2)}) collective-permute-start(bf16[32,3072]{1,0:T(8,128)(2,1)S(1)} %constant_dynamic-update-slice_fusion.mine_ref), channel_id=1, source_target_pairs={{0,1},{1,0},{2,3},{3,2},{4,5},{5,4},{6,7},{7,6},{8,9},{9,8},{10,11... | collective-permute-start | bytes 589832 | tf_op jit(solution)/shard_map/ppermute | solution.py:18
  11.0 1.5 %collective-permute-start.2 = (bf16[32,3072]{1,0:T(8,128)(2,1)S(1)}, bf16[32,3072]{1,0:T(8,128)(2,1)S(1)}, u32[]{:S(2)}, u32[]{:S(2)}) collective-permute-start(bf16[32,3072]{1,0:T(8,128)(2,1)S(1)} %pad_maximum_fusion.mine_ref), channel_id=1, source_target_pairs={{0,1},{1,0},{2,3},{3,2},{4,5},{5,4},{6,7},{7,6},{8,9},{9,8},{10,11... | collective-permute-start | bytes 589832 | tf_op jit(solution)/shard_map/ppermute | solution.py:18
  12.6 12.1 %copy-start.1 = (bf16[4,1,16,3072]{3,2,1,0:T(8,128)(2,1)S(1)}, bf16[4,1,16,3072]{3,2,1,0:T(8,128)(2,1)}, u32[]{:S(2)}) copy-start(bf16[4,1,16,3072]{3,2,1,0:T(8,128)(2,1)} %param.8) | copy-start | bytes 1179652
  14.7 1.5 %collective-permute-start.5 = (bf16[32,3072]{1,0:T(8,128)(2,1)S(1)}, bf16[32,3072]{1,0:T(8,128)(2,1)S(1)}, u32[]{:S(2)}, u32[]{:S(2)}) collective-permute-start(bf16[32,3072]{1,0:T(8,128)(2,1)S(1)} %get-tuple-element.33), channel_id=1, source_target_pairs={{0,1},{1,0},{2,3},{3,2},{4,5},{5,4},{6,7},{7,6},{8,9},{9,8},{10,11... | collective-permute-start | bytes 589832 | tf_op jit(solution)/shard_map/ppermute | solution.py:18
  16.2 5.8 %collective-permute-start.6 = (bf16[16,3072]{1,0:T(8,128)(2,1)S(1)}, bf16[16,3072]{1,0:T(8,128)(2,1)S(1)}, u32[]{:S(2)}, u32[]{:S(2)}) collective-permute-start(bf16[16,3072]{1,0:T(8,128)(2,1)S(1)} %convert_element_type.9), channel_id=1, source_target_pairs={{0,8},{1,0},{2,10},{3,2},{8,16},{9,1},{10,18},{11,3},{16,24},{17,9... | collective-permute-start | bytes 294920 | tf_op jit(solution)/shard_map/ppermute | solution.py:30
  18.5 4.6 %collective-permute-start.7 = (bf16[16,3072]{1,0:T(8,128)(2,1)S(1)}, bf16[16,3072]{1,0:T(8,128)(2,1)S(1)}, u32[]{:S(2)}, u32[]{:S(2)}) collective-permute-start(bf16[16,3072]{1,0:T(8,128)(2,1)S(1)} %convert_element_type.9), channel_id=1, source_target_pairs={{0,1},{1,9},{2,3},{3,11},{8,0},{9,17},{10,2},{11,19},{16,8},{17,25... | collective-permute-start | bytes 294920 | tf_op jit(solution)/shard_map/ppermute | solution.py:30
  18.5 4.7 %collective-permute-start.8 = (bf16[16,3072]{1,0:T(8,128)(2,1)S(1)}, bf16[16,3072]{1,0:T(8,128)(2,1)S(1)}, u32[]{:S(2)}, u32[]{:S(2)}) collective-permute-start(bf16[16,3072]{1,0:T(8,128)(2,1)S(1)} %get-tuple-element.35), channel_id=1, source_target_pairs={{0,2},{1,3},{2,0},{3,1},{4,6},{5,7},{6,4},{7,5},{8,10},{9,11},{10,... | collective-permute-start | bytes 294920 | tf_op jit(solution)/shard_map/ppermute | solution.py:18
  19.5 5.2 %collective-permute-start.9 = (bf16[16,3072]{1,0:T(8,128)(2,1)S(1)}, bf16[16,3072]{1,0:T(8,128)(2,1)S(1)}, u32[]{:S(2)}, u32[]{:S(2)}) collective-permute-start(bf16[16,3072]{1,0:T(8,128)(2,1)S(1)} %get-tuple-element.35), channel_id=1, source_target_pairs={{0,1},{1,11},{2,3},{3,9},{8,0},{9,19},{10,2},{11,17},{16,8},{17,27... | collective-permute-start | bytes 294920 | tf_op jit(solution)/shard_map/ppermute | solution.py:30
  19.5 5.2 %collective-permute-start.10 = (bf16[16,3072]{1,0:T(8,128)(2,1)S(1)}, bf16[16,3072]{1,0:T(8,128)(2,1)S(1)}, u32[]{:S(2)}, u32[]{:S(2)}) collective-permute-start(bf16[16,3072]{1,0:T(8,128)(2,1)S(1)} %get-tuple-element.35), channel_id=1, source_target_pairs={{0,10},{1,0},{2,8},{3,2},{8,18},{9,1},{10,16},{11,3},{16,26},{17,9... | collective-permute-start | bytes 294920 | tf_op jit(solution)/shard_map/ppermute | solution.py:30
  24.9 5.1 %collective-permute-start.14 = (bf16[16,3072]{1,0:T(8,128)(2,1)S(1)}, bf16[16,3072]{1,0:T(8,128)(2,1)S(1)}, u32[]{:S(2)}, u32[]{:S(2)}) collective-permute-start(bf16[16,3072]{1,0:T(8,128)(2,1)S(1)} %get-tuple-element.38), channel_id=1, source_target_pairs={{0,2},{1,3},{2,0},{3,1},{4,6},{5,7},{6,4},{7,5},{8,10},{9,11},{10,... | collective-permute-start | bytes 294920 | tf_op jit(solution)/shard_map/ppermute | solution.py:18
  26.3 5.3 %collective-permute-start.11 = (bf16[16,3072]{1,0:T(8,128)(2,1)S(1)}, bf16[16,3072]{1,0:T(8,128)(2,1)S(1)}, u32[]{:S(2)}, u32[]{:S(2)}) collective-permute-start(bf16[16,3072]{1,0:T(8,128)(2,1)S(1)} %get-tuple-element.38), channel_id=1, source_target_pairs={{0,4},{1,5},{2,6},{3,7},{4,0},{5,1},{6,2},{7,3},{8,12},{9,13},{10,... | collective-permute-start | bytes 294920 | tf_op jit(solution)/shard_map/ppermute | solution.py:18
  27.3 6.0 %collective-permute-start.12 = (bf16[16,3072]{1,0:T(8,128)(2,1)S(1)}, bf16[16,3072]{1,0:T(8,128)(2,1)S(1)}, u32[]{:S(2)}, u32[]{:S(2)}) collective-permute-start(bf16[16,3072]{1,0:T(8,128)(2,1)S(1)} %get-tuple-element.38), channel_id=1, source_target_pairs={{0,6},{1,7},{2,4},{3,5},{4,2},{5,3},{6,0},{7,1},{8,14},{9,15},{10,... | collective-permute-start | bytes 294920 | tf_op jit(solution)/shard_map/ppermute | solution.py:18
  30.0 3.4 %collective-permute-start.15 = (bf16[32,3072]{1,0:T(8,128)(2,1)S(1)}, bf16[32,3072]{1,0:T(8,128)(2,1)S(1)}, u32[]{:S(2)}, u32[]{:S(2)}) collective-permute-start(bf16[32,3072]{1,0:T(8,128)(2,1)S(1)} %constant_dynamic-update-slice_fusion.9.mine_ref), channel_id=1, source_target_pairs={{0,1},{1,0},{2,3},{3,2},{4,5},{5,4},{6,7},{7,6},{8,9},{9,8},{10,11... | collective-permute-start | bytes 589832 | tf_op jit(solution)/shard_map/ppermute | solution.py:18
  33.4 1.5 %collective-permute-start.13 = (bf16[32,3072]{1,0:T(8,128)(2,1)S(1)}, bf16[32,3072]{1,0:T(8,128)(2,1)S(1)}, u32[]{:S(2)}, u32[]{:S(2)}) collective-permute-start(bf16[32,3072]{1,0:T(8,128)(2,1)S(1)} %constant_dynamic-update-slice_fusion.7.mine_ref), channel_id=1, source_target_pairs={{0,1},{1,0},{2,3},{3,2},{4,5},{5,4},{6,7},{7,6},{8,9},{9,8},{10,11... | collective-permute-start | bytes 589832 | tf_op jit(solution)/shard_map/ppermute | solution.py:18
  37.0 1.5 %collective-permute-start.16 = (bf16[32,3072]{1,0:T(8,128)(2,1)S(1)}, bf16[32,3072]{1,0:T(8,128)(2,1)S(1)}, u32[]{:S(2)}, u32[]{:S(2)}) collective-permute-start(bf16[32,3072]{1,0:T(8,128)(2,1)S(1)} %get-tuple-element.40), channel_id=1, source_target_pairs={{0,1},{1,0},{2,3},{3,2},{4,5},{5,4},{6,7},{7,6},{8,9},{9,8},{10,11... | collective-permute-start | bytes 589832 | tf_op jit(solution)/shard_map/ppermute | solution.py:18
  38.5 4.9 %collective-permute-start.17 = (bf16[16,3072]{1,0:T(8,128)(2,1)S(1)}, bf16[16,3072]{1,0:T(8,128)(2,1)S(1)}, u32[]{:S(2)}, u32[]{:S(2)}) collective-permute-start(bf16[16,3072]{1,0:T(8,128)(2,1)S(1)} %get-tuple-element.42), channel_id=1, source_target_pairs={{0,2},{1,3},{2,0},{3,1},{4,6},{5,7},{6,4},{7,5},{8,10},{9,11},{10,... | collective-permute-start | bytes 294920 | tf_op jit(solution)/shard_map/ppermute | solution.py:18

commit v9 on v6

--- a/solution.py
+++ b/solution.py
@@ -33,7 +33,7 @@
 def handed_on(own, others):
     blocks = [climbed(own, 0, 0), climbed(own, 0, 1)]
     for k, other in enumerate(others, 1):
-        blocks += [swapped(other, 2 * k), climbed(other, 2 * k, 1), climbed(other, 2 * k, 0)]
+        blocks += [climbed(other, 2 * k, 1), climbed(other, 2 * k, 0)]
     return jnp.concatenate(blocks, 0)
 
 
@@ -105,11 +105,13 @@
     )(*arrays)
 
 
-def layer_part(own, partner, weights, tok):
+def layer_part(own, partner, weights, tok, beside=()):
     wq, wkv, wo = weights[0], *in_vmem(weights[1]), weights[2]
     (half, width), head_cols = own.shape, wq.shape[1]
     partner_theirs = swapped(partner, 1)
     own_theirs = swapped(own, 1)
+    if beside:
+        partner_theirs, *beside = lax.optimization_barrier((partner_theirs, *beside))
     pushed = 2 * 256 * width * head_cols
     keys, values = on_chip(
         keyval_kernel,
@@ -117,12 +119,13 @@
         partner, partner_theirs, wkv,
         flops=2 * pushed,
     )
-    return on_chip(
+    keep, send = on_chip(
         functools.partial(attend_kernel, tok),
         [((half, width), jnp.float32), ((half, width), jnp.bfloat16)],
         own, own_theirs, keys, values, wq, wo,
         flops=3 * pushed,
     )
+    return keep, send, beside
 
 
 def sum_kernel(state_ref, keep_ref, sent_ref, own_ref, *out_refs):
@@ -135,10 +138,11 @@
 
 
 def entry_kernel(x_ref, gain_ref, normed_ref, x_out, gain_out, sems):
-    copies = [
-        pltpu.make_async_copy(x_ref, x_out, sems.at[0]),
-        pltpu.make_async_copy(gain_ref, gain_out, sems.at[1]),
-    ]
+    width = x_ref.shape[1] // PIECES
+    copies = [pltpu.make_async_copy(gain_ref, gain_out, sems.at[PIECES])]
+    for i in range(PIECES):
+        here = (slice(None), pl.ds(i * width, width))
+        copies.append(pltpu.make_async_copy(x_ref.at[here], x_out.at[here], sems.at[i]))
     for copy in copies:
         copy.start()
     for copy in copies:
@@ -156,7 +160,7 @@
         ),
         in_specs=[pl.BlockSpec(memory_space=pltpu.HBM)] * 2,
         out_specs=(pl.BlockSpec(memory_space=pltpu.VMEM),) * 3,
-        scratch_shapes=[pltpu.SemaphoreType.DMA((2,))],
+        scratch_shapes=[pltpu.SemaphoreType.DMA((PIECES + 1,))],
         compiler_params=pltpu.CompilerParams(vmem_limit_bytes=16 << 20),
     )(*in_hbm(state, gain))
 
@@ -190,34 +194,31 @@
     )(*in_hbm(*arrays))
 
 
-def second_kernel(
-    section_ref, lane_ref, offset_ref, fresh_ref, gain_ref, own_ref, handed_ref, first_ref, state_ref, normed_ref
-):
+def second_kernel(section_ref, lane_ref, offset_ref, fresh_ref, gain_ref, handed_ref, state_ref, normed_ref):
     tok = state_ref.shape[0]
 
     def block(index):
         return handed_ref[pl.ds(pl.multiple_of(index * tok, tok), tok)].astype(jnp.float32)
 
     odd = lane_ref[0] % 2
-    first, handed = own_ref[...], block(odd)
-    for index in range(2, handed_ref.shape[0] // tok, 3):
-        first = first + block(index)
-        handed = handed + block(index + 2 - odd)
-    first_ref[...] = first.astype(jnp.bfloat16)
+    handed = block(odd)
+    for index in range(2, handed_ref.shape[0] // tok, 2):
+        handed = handed + block(index + 1 - odd)
     picked = fresh_ref[pl.ds(pl.multiple_of(offset_ref[0] * tok, tok), tok)]
     state = jnp.where(section_ref[0] == 0, picked, handed.astype(jnp.bfloat16))
     state_ref[...] = state
     normed_ref[...] = normalized(state, gain_ref[0])
 
 
-def second_entry(section, lane, offsets, fresh, gain, own, handed):
+def second_entry(section, lane, offsets, fresh, gain, handed, tok):
+    shape = (tok, handed.shape[1])
     return pl.pallas_call(
         second_kernel,
-        out_shape=(pltpu.VMEM(own.shape, jnp.bfloat16),) * 3,
-        in_specs=[pl.BlockSpec(memory_space=pltpu.SMEM)] * 3 + [pl.BlockSpec(memory_space=pltpu.VMEM)] * 4,
-        out_specs=(pl.BlockSpec(memory_space=pltpu.VMEM),) * 3,
-        compiler_params=pltpu.CompilerParams(vmem_limit_bytes=16 << 20),
-    )(section, lane, offsets, fresh, gain, own, handed)
+        out_shape=(pltpu.VMEM(shape, jnp.bfloat16),) * 2,
+        in_specs=[pl.BlockSpec(memory_space=pltpu.SMEM)] * 3 + [pl.BlockSpec(memory_space=pltpu.VMEM)] * 3,
+        out_specs=(pl.BlockSpec(memory_space=pltpu.VMEM),) * 2,
+        compiler_params=pltpu.CompilerParams(vmem_limit_bytes=16 << 20),
+    )(section, lane, offsets, fresh, gain, handed)
 
 
 def gathered(normed):
@@ -254,11 +255,15 @@
     partner, wkv = lax.optimization_barrier((partner, wkv))
     wq, wo, fresh = w_query[0, 0], w_out[0, 0], fresh_batches.reshape(-1, fresh_batches.shape[-1])
     weights = (wq, wkv, wo)
-    first_sum, others = summed(state, *layer_part(own, partner, weights, tok))
+    first_sum, others = summed(state, *layer_part(own, partner, weights, tok)[:2])
     handed = handed_on(first_sum.astype(jnp.bfloat16), others)
-    first, state, normed = second_entry(section, lane, offsets, fresh, gain, first_sum, handed)
+    state, normed = second_entry(section, lane, offsets, fresh, gain, handed, tok)
+    normed, others = lax.optimization_barrier((normed, others))
     own, partner = gathered(normed)
-    second = completed(*summed(state, *layer_part(own, partner, weights, tok)))
+    arrived = [swapped(other, 2 * k) for k, other in enumerate(others, 1)]
+    keep, send, arrived = layer_part(own, partner, weights, tok, arrived)
+    first = sum([rows.astype(jnp.float32) for rows in arrived], first_sum).astype(jnp.bfloat16)
+    second = completed(*summed(state, keep, send))
     return jnp.stack([first, second])[:, None, None]
 
 

time: 44.5 us -> 44.2 us (level)
  starting transfers between devices: 15.7 us -> 14 us
  waiting for transfers between devices: 17 us -> 18.5 us
    ppermute x4, waiting for transfers between devices: 2.47 us -> 4.07 us  [climbed(): return lax.ppermute(value, ('section', 'lane'), pairs)]
    ppermute x4, starting transfers between devices: 4.6 us -> 3.59 us  [climbed(): return lax.ppermute(value, ('section', 'lane'), pairs)]
    ppermute x14, starting transfers between devices: 11.1 us -> 10.4 us  [swapped(): return lax.ppermute(value, BOTH, [(i, i ^ mask) for i in range(count)])]
where the time goes in v9:
time: 44.2 us; the launch traced here: 44 us
  waiting for transfers between devices  18.5 us (42%)
  starting transfers between devices  14 us (32%)
  Pallas kernels  9.76 us (22%)
  between operations  0.89 us (2%)
  other arithmetic  0.79 us (2%)
    ppermute x14, waiting for transfers between devices, swapped(): return lax.ppermute(value, BOTH, [(i, i ^ mask) for i in range(count)])  14.4 us
    ppermute x14, starting transfers between devices, swapped(): return lax.ppermute(value, BOTH, [(i, i ^ mask) for i in range(count)])  10.4 us
    pallas_call x6, Pallas kernels, on_chip(): pl.pallas_call(kernel, out_shape=tuple((jax.ShapeDtypeStruct(shape, dtype...  5.75 us
    ppermute x4, waiting for transfers between devices, climbed(): return lax.ppermute(value, ('section', 'lane'), pairs)  4.07 us
    ppermute x4, starting transfers between devices, climbed(): return lax.ppermute(value, ('section', 'lane'), pairs)  3.59 us
    pallas_call x1, Pallas kernels, load(): pl.pallas_call(load_kernel, out_shape=tuple((pltpu.VMEM(a.shape, a.dtype)...  2.87 us
    pallas_call x1, Pallas kernels, entry(): pl.pallas_call(entry_kernel, out_shape=(pltpu.VMEM(state.shape, jnp.bfloa...  0.98 us
  transfers between devices with their start and end apart: 18, of which 12 were waited for; matrix products, arithmetic and copies ran while one was open for 0% of the time, Pallas kernels for 12%

profile of v9, /device:TPU:0, one launch (start us, length us, event | category | flops | bytes accessed | tf_op | source)
XLA Modules:
  0.0 44.0 jit_solution(11129583191943582972)
XLA Ops:
  0.0 1.0 %shard_map.73 = (bf16[16,3072]{1,0:T(8,128)(2,1)S(1)}, bf16[16,3072]{1,0:T(8,128)(2,1)S(1)}, f32[1,3072]{1,0:T(1,128)S(1)}) custom-call(bf16[16,3072]{1,0:T(8,128)(2,1)} %bitcast.22, f32[1,3072]{1,0:T(1,128)} %bitcast.23), custom_call_target="tpu_custom_call" | custom-call | tf_op jit(solution)/shard_map/pallas_call | solution.py:154
  1.0 4.0 %collective-permute-start.2 = (bf16[16,3072]{1,0:T(8,128)(2,1)S(1)}, bf16[16,3072]{1,0:T(8,128)(2,1)S(1)}, u32[]{:S(2)}, u32[]{:S(2)}) collective-permute-start(bf16[16,3072]{1,0:T(8,128)(2,1)S(1)} %get-tuple-element.33), channel_id=1, source_target_pairs={{0,6},{1,7},{2,4},{3,5},{4,2},{5,3},{6,0},{7,1},{8,14},{9,15},{10,... | collective-permute-start | bytes 294920 | tf_op jit(solution)/shard_map/ppermute | solution.py:18
  4.9 0.5 %collective-permute-start.3 = (bf16[16,3072]{1,0:T(8,128)(2,1)S(1)}, bf16[16,3072]{1,0:T(8,128)(2,1)S(1)}, u32[]{:S(2)}, u32[]{:S(2)}) collective-permute-start(bf16[16,3072]{1,0:T(8,128)(2,1)S(1)} %get-tuple-element.33), channel_id=1, source_target_pairs={{0,4},{1,5},{2,6},{3,7},{4,0},{5,1},{6,2},{7,3},{8,12},{9,13},{10,... | collective-permute-start | bytes 294920 | tf_op jit(solution)/shard_map/ppermute | solution.py:18
  5.5 0.1 collective-permute-start
  5.6 2.9 %shard_map.74.wkv_ref = bf16[6144,512]{1,0:T(8,128)(2,1)S(1)} custom-call(bf16[6144,512]{1,0:T(8,128)(2,1)} %bitcast.21), custom_call_target="tpu_custom_call" | custom-call | bytes 6291456 | tf_op jit(solution)/shard_map/pallas_call | solution.py:184
  8.5 0.0 copy-start.1
  8.5 0.0 copy-start.2
  8.5 0.0 collective-permute-done.2
  8.5 1.7 %collective-permute-done.3 = bf16[16,3072]{1,0:T(8,128)(2,1)S(1)} collective-permute-done((bf16[16,3072]{1,0:T(8,128)(2,1)S(1)}, bf16[16,3072]{1,0:T(8,128)(2,1)S(1)}, u32[]{:S(2)}, u32[]{:S(2)}) %collective-permute-start.3) | collective-permute-done | bytes 98336 | tf_op jit(solution)/shard_map/ppermute | solution.py:18
  10.2 0.1 collective-permute-start.4
  10.3 0.0 collective-permute-done
  10.3 0.5 %collective-permute-start.1 = (bf16[32,3072]{1,0:T(8,128)(2,1)S(1)}, bf16[32,3072]{1,0:T(8,128)(2,1)S(1)}, u32[]{:S(2)}, u32[]{:S(2)}) collective-permute-start(bf16[32,3072]{1,0:T(8,128)(2,1)S(1)} %constant_dynamic-update-slice_fusion.mine_ref), channel_id=1, source_target_pairs={{0,1},{1,0},{2,3},{3,2},{4,5},{5,4},{6,7},{7,6},{8,9},{9,8},{10,11... | collective-permute-start | bytes 589832 | tf_op jit(solution)/shard_map/ppermute | solution.py:18
  10.9 0.8 %collective-permute-done.4.theirs_ref = bf16[32,3072]{1,0:T(8,128)(2,1)S(1)} collective-permute-done((bf16[32,3072]{1,0:T(8,128)(2,1)S(1)}, bf16[32,3072]{1,0:T(8,128)(2,1)S(1)}, u32[]{:S(2)}, u32[]{:S(2)}) %collective-permute-start.4) | collective-permute-done | bytes 196640 | tf_op jit(solution)/shard_map/ppermute | solution.py:18
  11.7 1.2 %shard_map.75 = (bf16[64,512]{1,0:T(8,128)(2,1)S(1)}, bf16[64,512]{1,0:T(8,128)(2,1)S(1)}) custom-call(bf16[32,3072]{1,0:T(8,128)(2,1)S(1)} %pad_maximum_fusion.1.mine_ref, bf16[32,3072]{1,0:T(8,128)(2,1)S(1)} %collective-permute-done.4.theirs_ref, bf16[6144,512]{1,0:T(8,128)(2,1)S(1)} %shard_map.74.wkv_ref), custom_call_target="tpu_custom_call" | custom-call | flops 1610612736 | bytes 6684672 | tf_op jit(solution)/shard_map/pallas_call | solution.py:98
  12.9 0.0 copy-start
  12.9 0.0 collective-permute-done.1.theirs_ref
  12.9 0.0 copy-done.1
  12.9 0.0 copy-done.2
  12.9 1.6 %shard_map.76 = (f32[32,3072]{1,0:T(8,128)S(1)}, bf16[32,3072]{1,0:T(8,128)(2,1)S(1)}) custom-call(bf16[32,3072]{1,0:T(8,128)(2,1)S(1)} %constant_dynamic-update-slice_fusion.mine_ref, bf16[32,3072]{1,0:T(8,128)(2,1)S(1)} %collective-permute-done.1.theirs_ref, bf16[64,512]{1,0:T(8,128)(2,1)S(1)} %get-tuple-element.36.keys_ref, ...), custom_call_target="tpu_custom_call" | custom-call | flops 2415919104 | bytes 6815744 | tf_op jit(solution)/shard_map/pallas_call | solution.py:98
  14.6 0.2 collective-permute-start.5
  14.8 1.3 %collective-permute-done.5.sent_ref = bf16[32,3072]{1,0:T(8,128)(2,1)S(1)} collective-permute-done((bf16[32,3072]{1,0:T(8,128)(2,1)S(1)}, bf16[32,3072]{1,0:T(8,128)(2,1)S(1)}, u32[]{:S(2)}, u32[]{:S(2)}) %collective-permute-start.5) | collective-permute-done | bytes 196640 | tf_op jit(solution)/shard_map/ppermute | solution.py:18
  16.2 1.6 %collective-permute-start.6 = (bf16[16,3072]{1,0:T(8,128)(2,1)S(1)}, bf16[16,3072]{1,0:T(8,128)(2,1)S(1)}, u32[]{:S(2)}, u32[]{:S(2)}) collective-permute-start(bf16[16,3072]{1,0:T(8,128)(2,1)S(1)} %convert_element_type.15), channel_id=1, source_target_pairs={{0,8},{1,0},{2,10},{3,2},{8,16},{9,1},{10,18},{11,3},{16,24},{17,9... | collective-permute-start | bytes 294920 | tf_op jit(solution)/shard_map/ppermute | solution.py:30
  17.8 0.0 collective-permute-start.7
  17.8 0.0 collective-permute-start.8
  17.8 2.0 %collective-permute-start.9 = (bf16[16,3072]{1,0:T(8,128)(2,1)S(1)}, bf16[16,3072]{1,0:T(8,128)(2,1)S(1)}, u32[]{:S(2)}, u32[]{:S(2)}) collective-permute-start(bf16[16,3072]{1,0:T(8,128)(2,1)S(1)} %get-tuple-element.47), channel_id=1, source_target_pairs={{0,10},{1,0},{2,8},{3,2},{8,18},{9,1},{10,16},{11,3},{16,26},{17,9... | collective-permute-start | bytes 294920 | tf_op jit(solution)/shard_map/ppermute | solution.py:30
  20.4 0.5 %collective-permute-done.6 = bf16[16,3072]{1,0:T(8,128)(2,1)S(1)} collective-permute-done((bf16[16,3072]{1,0:T(8,128)(2,1)S(1)}, bf16[16,3072]{1,0:T(8,128)(2,1)S(1)}, u32[]{:S(2)}, u32[]{:S(2)}) %collective-permute-start.6) | collective-permute-done | bytes 98336 | tf_op jit(solution)/shard_map/ppermute | solution.py:30
  20.9 2.2 %collective-permute-done.7 = bf16[16,3072]{1,0:T(8,128)(2,1)S(1)} collective-permute-done((bf16[16,3072]{1,0:T(8,128)(2,1)S(1)}, bf16[16,3072]{1,0:T(8,128)(2,1)S(1)}, u32[]{:S(2)}, u32[]{:S(2)}) %collective-permute-start.7) | collective-permute-done | bytes 98336 | tf_op jit(solution)/shard_map/ppermute | solution.py:30
  23.1 1.3 %collective-permute-done.8 = bf16[16,3072]{1,0:T(8,128)(2,1)S(1)} collective-permute-done((bf16[16,3072]{1,0:T(8,128)(2,1)S(1)}, bf16[16,3072]{1,0:T(8,128)(2,1)S(1)}, u32[]{:S(2)}, u32[]{:S(2)}) %collective-permute-start.8) | collective-permute-done | bytes 98336 | tf_op jit(solution)/shard_map/ppermute | solution.py:30
  24.5 0.0 collective-permute-done.9
  24.5 0.0 copy-done
  24.5 0.2 shard_map.78
  24.7 1.1 %collective-permute-start.10 = (bf16[16,3072]{1,0:T(8,128)(2,1)S(1)}, bf16[16,3072]{1,0:T(8,128)(2,1)S(1)}, u32[]{:S(2)}, u32[]{:S(2)}) collective-permute-start(bf16[16,3072]{1,0:T(8,128)(2,1)S(1)} %get-tuple-element.46), channel_id=1, source_target_pairs={{0,6},{1,7},{2,4},{3,5},{4,2},{5,3},{6,0},{7,1},{8,14},{9,15},{10,... | collective-permute-start | bytes 294920 | tf_op jit(solution)/shard_map/ppermute | solution.py:18
  25.8 0.6 %collective-permute-start.11 = (bf16[16,3072]{1,0:T(8,128)(2,1)S(1)}, bf16[16,3072]{1,0:T(8,128)(2,1)S(1)}, u32[]{:S(2)}, u32[]{:S(2)}) collective-permute-start(bf16[16,3072]{1,0:T(8,128)(2,1)S(1)} %get-tuple-element.46), channel_id=1, source_target_pairs={{0,4},{1,5},{2,6},{3,7},{4,0},{5,1},{6,2},{7,3},{8,12},{9,13},{10,... | collective-permute-start | bytes 294920 | tf_op jit(solution)/shard_map/ppermute | solution.py:18
  26.4 1.8 %collective-permute-start.14 = (bf16[16,3072]{1,0:T(8,128)(2,1)S(1)}, bf16[16,3072]{1,0:T(8,128)(2,1)S(1)}, u32[]{:S(2)}, u32[]{:S(2)}) collective-permute-start(bf16[16,3072]{1,0:T(8,128)(2,1)S(1)} %get-tuple-element.46), channel_id=1, source_target_pairs={{0,2},{1,3},{2,0},{3,1},{4,6},{5,7},{6,4},{7,5},{8,10},{9,11},{10,... | collective-permute-start | bytes 294920 | tf_op jit(solution)/shard_map/ppermute | solution.py:18
  28.3 0.2 collective-permute-start.13
  28.5 2.4 %collective-permute-done.10 = bf16[16,3072]{1,0:T(8,128)(2,1)S(1)} collective-permute-done((bf16[16,3072]{1,0:T(8,128)(2,1)S(1)}, bf16[16,3072]{1,0:T(8,128)(2,1)S(1)}, u32[]{:S(2)}, u32[]{:S(2)}) %collective-permute-start.10) | collective-permute-done | bytes 98336 | tf_op jit(solution)/shard_map/ppermute | solution.py:18
  30.9 0.4 collective-permute-done.11
  31.3 0.1 collective-permute-start.12
  31.4 1.4 %collective-permute-done.14 = bf16[16,3072]{1,0:T(8,128)(2,1)S(1)} collective-permute-done((bf16[16,3072]{1,0:T(8,128)(2,1)S(1)}, bf16[16,3072]{1,0:T(8,128)(2,1)S(1)}, u32[]{:S(2)}, u32[]{:S(2)}) %collective-permute-start.14) | collective-permute-done | bytes 98336 | tf_op jit(solution)/shard_map/ppermute | solution.py:18
  32.8 0.1 collective-permute-start.15
  32.9 1.0 %collective-permute-done.13 = bf16[16,3072]{1,0:T(8,128)(2,1)S(1)} collective-permute-done((bf16[16,3072]{1,0:T(8,128)(2,1)S(1)}, bf16[16,3072]{1,0:T(8,128)(2,1)S(1)}, u32[]{:S(2)}, u32[]{:S(2)}) %collective-permute-start.13) | collective-permute-done | bytes 98336 | tf_op jit(solution)/shard_map/ppermute | solution.py:18
  33.9 0.0 collective-permute-done.12.theirs_ref
  33.9 1.2 %shard_map.79 = (bf16[64,512]{1,0:T(8,128)(2,1)S(1)}, bf16[64,512]{1,0:T(8,128)(2,1)S(1)}) custom-call(bf16[32,3072]{1,0:T(8,128)(2,1)S(1)} %constant_dynamic-update-slice_fusion.2.mine_ref, bf16[32,3072]{1,0:T(8,128)(2,1)S(1)} %collective-permute-done.12.theirs_ref, bf16[6144,512]{1,0:T(8,128)(2,1)S(1)} %shard_map.74.wkv_ref), custom_call_target="tpu_custom_call" | custom-call | flops 1610612736 | bytes 6684672 | tf_op jit(solution)/shard_map/pallas_call | solution.py:98
  35.1 0.0 collective-permute-done.15.theirs_ref
  35.1 1.6 %shard_map.80 = (f32[32,3072]{1,0:T(8,128)S(1)}, bf16[32,3072]{1,0:T(8,128)(2,1)S(1)}) custom-call(bf16[32,3072]{1,0:T(8,128)(2,1)S(1)} %constant_dynamic-update-slice_fusion.4.mine_ref, bf16[32,3072]{1,0:T(8,128)(2,1)S(1)} %collective-permute-done.15.theirs_ref, bf16[64,512]{1,0:T(8,128)(2,1)S(1)} %get-tuple-element.51.keys_ref, ...), custom_call_target="tpu_custom_call" | custom-call | flops 2415919104 | bytes 6815744 | tf_op jit(solution)/shard_map/pallas_call | solution.py:98
  36.8 0.1 collective-permute-start.16
  36.9 1.4 %collective-permute-done.16.sent_ref = bf16[32,3072]{1,0:T(8,128)(2,1)S(1)} collective-permute-done((bf16[32,3072]{1,0:T(8,128)(2,1)S(1)}, bf16[32,3072]{1,0:T(8,128)(2,1)S(1)}, u32[]{:S(2)}, u32[]{:S(2)}) %collective-permute-start.16) | collective-permute-done | bytes 196640 | tf_op jit(solution)/shard_map/ppermute | solution.py:18
  38.4 1.0 %collective-permute-start.17 = (bf16[16,3072]{1,0:T(8,128)(2,1)S(1)}, bf16[16,3072]{1,0:T(8,128)(2,1)S(1)}, u32[]{:S(2)}, u32[]{:S(2)}) collective-permute-start(bf16[16,3072]{1,0:T(8,128)(2,1)S(1)} %get-tuple-element.56), channel_id=1, source_target_pairs={{0,2},{1,3},{2,0},{3,1},{4,6},{5,7},{6,4},{7,5},{8,10},{9,11},{10,... | collective-permute-start | bytes 294920 | tf_op jit(solution)/shard_map/ppermute | solution.py:18
  39.4 3.8 %collective-permute-done.17 = bf16[16,3072]{1,0:T(8,128)(2,1)S(1)} collective-permute-done((bf16[16,3072]{1,0:T(8,128)(2,1)S(1)}, bf16[16,3072]{1,0:T(8,128)(2,1)S(1)}, u32[]{:S(2)}, u32[]{:S(2)}) %collective-permute-start.17) | collective-permute-done | bytes 98336 | tf_op jit(solution)/shard_map/ppermute | solution.py:18
  43.3 0.7 %maximum_bitcast_fusion = bf16[2,1,1,16,3072]{4,3,2,1,0:T(8,128)(2,1)} fusion(bf16[1,16,3072]{2,1,0:T(8,128)(2,1)S(1)} %fusion.1, bf16[1,16,3072]{2,1,0:T(8,128)(2,1)S(1)} %fusion), kind=kLoop, calls=%fused_computation.2 | loop fusion | flops 98304 | bytes 393216 | tf_op jit(solution)/shard_map/broadcast_in_dim | solution.py:267
  (13 shorter events, 0.2 us)
Async XLA Ops:
  1.0 7.5 %collective-permute-start.2 = (bf16[16,3072]{1,0:T(8,128)(2,1)S(1)}, bf16[16,3072]{1,0:T(8,128)(2,1)S(1)}, u32[]{:S(2)}, u32[]{:S(2)}) collective-permute-start(bf16[16,3072]{1,0:T(8,128)(2,1)S(1)} %get-tuple-element.33), channel_id=1, source_target_pairs={{0,6},{1,7},{2,4},{3,5},{4,2},{5,3},{6,0},{7,1},{8,14},{9,15},{10,... | collective-permute-start | bytes 294920 | tf_op jit(solution)/shard_map/ppermute | solution.py:18
  4.9 5.2 %collective-permute-start.3 = (bf16[16,3072]{1,0:T(8,128)(2,1)S(1)}, bf16[16,3072]{1,0:T(8,128)(2,1)S(1)}, u32[]{:S(2)}, u32[]{:S(2)}) collective-permute-start(bf16[16,3072]{1,0:T(8,128)(2,1)S(1)} %get-tuple-element.33), channel_id=1, source_target_pairs={{0,4},{1,5},{2,6},{3,7},{4,0},{5,1},{6,2},{7,3},{8,12},{9,13},{10,... | collective-permute-start | bytes 294920 | tf_op jit(solution)/shard_map/ppermute | solution.py:18
  5.5 4.8 %collective-permute-start = (bf16[16,3072]{1,0:T(8,128)(2,1)S(1)}, bf16[16,3072]{1,0:T(8,128)(2,1)S(1)}, u32[]{:S(2)}, u32[]{:S(2)}) collective-permute-start(bf16[16,3072]{1,0:T(8,128)(2,1)S(1)} %get-tuple-element.33), channel_id=1, source_target_pairs={{0,2},{1,3},{2,0},{3,1},{4,6},{5,7},{6,4},{7,5},{8,10},{9,11},{10,... | collective-permute-start | bytes 294920 | tf_op jit(solution)/shard_map/ppermute | solution.py:18
  8.5 4.5 %copy-start.1 = (bf16[1,1,3072,512]{3,2,1,0:T(8,128)(2,1)S(1)}, bf16[1,1,3072,512]{3,2,1,0:T(8,128)(2,1)}, u32[]{:S(2)}) copy-start(bf16[1,1,3072,512]{3,2,1,0:T(8,128)(2,1)} %param.11) | copy-start | bytes 9437188
  8.5 4.5 %copy-start.2 = (bf16[1,1,512,3072]{3,2,1,0:T(8,128)(2,1)S(1)}, bf16[1,1,512,3072]{3,2,1,0:T(8,128)(2,1)}, u32[]{:S(2)}) copy-start(bf16[1,1,512,3072]{3,2,1,0:T(8,128)(2,1)} %param.13) | copy-start | bytes 9437188
  10.2 1.5 %collective-permute-start.4 = (bf16[32,3072]{1,0:T(8,128)(2,1)S(1)}, bf16[32,3072]{1,0:T(8,128)(2,1)S(1)}, u32[]{:S(2)}, u32[]{:S(2)}) collective-permute-start(bf16[32,3072]{1,0:T(8,128)(2,1)S(1)} %pad_maximum_fusion.1.mine_ref), channel_id=1, source_target_pairs={{0,1},{1,0},{2,3},{3,2},{4,5},{5,4},{6,7},{7,6},{8,9},{9,8},{10,11... | collective-permute-start | bytes 589832 | tf_op jit(solution)/shard_map/ppermute | solution.py:18
  10.3 2.6 %collective-permute-start.1 = (bf16[32,3072]{1,0:T(8,128)(2,1)S(1)}, bf16[32,3072]{1,0:T(8,128)(2,1)S(1)}, u32[]{:S(2)}, u32[]{:S(2)}) collective-permute-start(bf16[32,3072]{1,0:T(8,128)(2,1)S(1)} %constant_dynamic-update-slice_fusion.mine_ref), channel_id=1, source_target_pairs={{0,1},{1,0},{2,3},{3,2},{4,5},{5,4},{6,7},{7,6},{8,9},{9,8},{10,11... | collective-permute-start | bytes 589832 | tf_op jit(solution)/shard_map/ppermute | solution.py:18
  12.9 11.6 %copy-start = (bf16[4,1,16,3072]{3,2,1,0:T(8,128)(2,1)S(1)}, bf16[4,1,16,3072]{3,2,1,0:T(8,128)(2,1)}, u32[]{:S(2)}) copy-start(bf16[4,1,16,3072]{3,2,1,0:T(8,128)(2,1)} %param.8) | copy-start | bytes 1179652
  14.6 1.5 %collective-permute-start.5 = (bf16[32,3072]{1,0:T(8,128)(2,1)S(1)}, bf16[32,3072]{1,0:T(8,128)(2,1)S(1)}, u32[]{:S(2)}, u32[]{:S(2)}) collective-permute-start(bf16[32,3072]{1,0:T(8,128)(2,1)S(1)} %get-tuple-element.39), channel_id=1, source_target_pairs={{0,1},{1,0},{2,3},{3,2},{4,5},{5,4},{6,7},{7,6},{8,9},{9,8},{10,11... | collective-permute-start | bytes 589832 | tf_op jit(solution)/shard_map/ppermute | solution.py:18
  16.2 4.7 %collective-permute-start.6 = (bf16[16,3072]{1,0:T(8,128)(2,1)S(1)}, bf16[16,3072]{1,0:T(8,128)(2,1)S(1)}, u32[]{:S(2)}, u32[]{:S(2)}) collective-permute-start(bf16[16,3072]{1,0:T(8,128)(2,1)S(1)} %convert_element_type.15), channel_id=1, source_target_pairs={{0,8},{1,0},{2,10},{3,2},{8,16},{9,1},{10,18},{11,3},{16,24},{17,9... | collective-permute-start | bytes 294920 | tf_op jit(solution)/shard_map/ppermute | solution.py:30
  17.8 5.4 %collective-permute-start.7 = (bf16[16,3072]{1,0:T(8,128)(2,1)S(1)}, bf16[16,3072]{1,0:T(8,128)(2,1)S(1)}, u32[]{:S(2)}, u32[]{:S(2)}) collective-permute-start(bf16[16,3072]{1,0:T(8,128)(2,1)S(1)} %convert_element_type.15), channel_id=1, source_target_pairs={{0,1},{1,9},{2,3},{3,11},{8,0},{9,17},{10,2},{11,19},{16,8},{17,25... | collective-permute-start | bytes 294920 | tf_op jit(solution)/shard_map/ppermute | solution.py:30
  17.8 6.7 %collective-permute-start.8 = (bf16[16,3072]{1,0:T(8,128)(2,1)S(1)}, bf16[16,3072]{1,0:T(8,128)(2,1)S(1)}, u32[]{:S(2)}, u32[]{:S(2)}) collective-permute-start(bf16[16,3072]{1,0:T(8,128)(2,1)S(1)} %get-tuple-element.47), channel_id=1, source_target_pairs={{0,1},{1,11},{2,3},{3,9},{8,0},{9,19},{10,2},{11,17},{16,8},{17,27... | collective-permute-start | bytes 294920 | tf_op jit(solution)/shard_map/ppermute | solution.py:30
  17.8 6.7 %collective-permute-start.9 = (bf16[16,3072]{1,0:T(8,128)(2,1)S(1)}, bf16[16,3072]{1,0:T(8,128)(2,1)S(1)}, u32[]{:S(2)}, u32[]{:S(2)}) collective-permute-start(bf16[16,3072]{1,0:T(8,128)(2,1)S(1)} %get-tuple-element.47), channel_id=1, source_target_pairs={{0,10},{1,0},{2,8},{3,2},{8,18},{9,1},{10,16},{11,3},{16,26},{17,9... | collective-permute-start | bytes 294920 | tf_op jit(solution)/shard_map/ppermute | solution.py:30
  24.7 6.2 %collective-permute-start.10 = (bf16[16,3072]{1,0:T(8,128)(2,1)S(1)}, bf16[16,3072]{1,0:T(8,128)(2,1)S(1)}, u32[]{:S(2)}, u32[]{:S(2)}) collective-permute-start(bf16[16,3072]{1,0:T(8,128)(2,1)S(1)} %get-tuple-element.46), channel_id=1, source_target_pairs={{0,6},{1,7},{2,4},{3,5},{4,2},{5,3},{6,0},{7,1},{8,14},{9,15},{10,... | collective-permute-start | bytes 294920 | tf_op jit(solution)/shard_map/ppermute | solution.py:18
  25.8 5.5 %collective-permute-start.11 = (bf16[16,3072]{1,0:T(8,128)(2,1)S(1)}, bf16[16,3072]{1,0:T(8,128)(2,1)S(1)}, u32[]{:S(2)}, u32[]{:S(2)}) collective-permute-start(bf16[16,3072]{1,0:T(8,128)(2,1)S(1)} %get-tuple-element.46), channel_id=1, source_target_pairs={{0,4},{1,5},{2,6},{3,7},{4,0},{5,1},{6,2},{7,3},{8,12},{9,13},{10,... | collective-permute-start | bytes 294920 | tf_op jit(solution)/shard_map/ppermute | solution.py:18
  26.4 6.4 %collective-permute-start.14 = (bf16[16,3072]{1,0:T(8,128)(2,1)S(1)}, bf16[16,3072]{1,0:T(8,128)(2,1)S(1)}, u32[]{:S(2)}, u32[]{:S(2)}) collective-permute-start(bf16[16,3072]{1,0:T(8,128)(2,1)S(1)} %get-tuple-element.46), channel_id=1, source_target_pairs={{0,2},{1,3},{2,0},{3,1},{4,6},{5,7},{6,4},{7,5},{8,10},{9,11},{10,... | collective-permute-start | bytes 294920 | tf_op jit(solution)/shard_map/ppermute | solution.py:18
  28.3 5.7 %collective-permute-start.13 = (bf16[16,3072]{1,0:T(8,128)(2,1)S(1)}, bf16[16,3072]{1,0:T(8,128)(2,1)S(1)}, u32[]{:S(2)}, u32[]{:S(2)}) collective-permute-start(bf16[16,3072]{1,0:T(8,128)(2,1)S(1)} %get-tuple-element.47), channel_id=1, source_target_pairs={{0,2},{1,3},{2,0},{3,1},{4,6},{5,7},{6,4},{7,5},{8,10},{9,11},{10,... | collective-permute-start | bytes 294920 | tf_op jit(solution)/shard_map/ppermute | solution.py:18
  31.3 2.6 %collective-permute-start.12 = (bf16[32,3072]{1,0:T(8,128)(2,1)S(1)}, bf16[32,3072]{1,0:T(8,128)(2,1)S(1)}, u32[]{:S(2)}, u32[]{:S(2)}) collective-permute-start(bf16[32,3072]{1,0:T(8,128)(2,1)S(1)} %constant_dynamic-update-slice_fusion.2.mine_ref), channel_id=1, source_target_pairs={{0,1},{1,0},{2,3},{3,2},{4,5},{5,4},{6,7},{7,6},{8,9},{9,8},{10,11... | collective-permute-start | bytes 589832 | tf_op jit(solution)/shard_map/ppermute | solution.py:18
  32.8 2.3 %collective-permute-start.15 = (bf16[32,3072]{1,0:T(8,128)(2,1)S(1)}, bf16[32,3072]{1,0:T(8,128)(2,1)S(1)}, u32[]{:S(2)}, u32[]{:S(2)}) collective-permute-start(bf16[32,3072]{1,0:T(8,128)(2,1)S(1)} %constant_dynamic-update-slice_fusion.4.mine_ref), channel_id=1, source_target_pairs={{0,1},{1,0},{2,3},{3,2},{4,5},{5,4},{6,7},{7,6},{8,9},{9,8},{10,11... | collective-permute-start | bytes 589832 | tf_op jit(solution)/shard_map/ppermute | solution.py:18
  36.8 1.5 %collective-permute-start.16 = (bf16[32,3072]{1,0:T(8,128)(2,1)S(1)}, bf16[32,3072]{1,0:T(8,128)(2,1)S(1)}, u32[]{:S(2)}, u32[]{:S(2)}) collective-permute-start(bf16[32,3072]{1,0:T(8,128)(2,1)S(1)} %get-tuple-element.54), channel_id=1, source_target_pairs={{0,1},{1,0},{2,3},{3,2},{4,5},{5,4},{6,7},{7,6},{8,9},{9,8},{10,11... | collective-permute-start | bytes 589832 | tf_op jit(solution)/shard_map/ppermute | solution.py:18
  38.4 4.9 %collective-permute-start.17 = (bf16[16,3072]{1,0:T(8,128)(2,1)S(1)}, bf16[16,3072]{1,0:T(8,128)(2,1)S(1)}, u32[]{:S(2)}, u32[]{:S(2)}) collective-permute-start(bf16[16,3072]{1,0:T(8,128)(2,1)S(1)} %get-tuple-element.56), channel_id=1, source_target_pairs={{0,2},{1,3},{2,0},{3,1},{4,6},{5,7},{6,4},{7,5},{8,10},{9,11},{10,... | collective-permute-start | bytes 294920 | tf_op jit(solution)/shard_map/ppermute | solution.py:18

commit v10 on v9

--- a/solution.py
+++ b/solution.py
@@ -31,10 +31,9 @@
 
 
 def handed_on(own, others):
-    blocks = [climbed(own, 0, 0), climbed(own, 0, 1)]
-    for k, other in enumerate(others, 1):
-        blocks += [climbed(other, 2 * k, 1), climbed(other, 2 * k, 0)]
-    return jnp.concatenate(blocks, 0)
+    sums = [own, *others]
+    turns = [(k, (k + turn) % 2) for turn in range(2) for k in range(len(sums))]
+    return jnp.concatenate([climbed(sums[k], 2 * k, climbs) for k, climbs in turns], 0)
 
 
 def in_hbm(*arrays):
@@ -201,9 +200,10 @@
         return handed_ref[pl.ds(pl.multiple_of(index * tok, tok), tok)].astype(jnp.float32)
 
     odd = lane_ref[0] % 2
-    handed = block(odd)
-    for index in range(2, handed_ref.shape[0] // tok, 2):
-        handed = handed + block(index + 1 - odd)
+    count = handed_ref.shape[0] // (2 * tok)
+    handed = 0.0
+    for k in range(count):
+        handed = handed + block((k + odd) % 2 * count + k)
     picked = fresh_ref[pl.ds(pl.multiple_of(offset_ref[0] * tok, tok), tok)]
     state = jnp.where(section_ref[0] == 0, picked, handed.astype(jnp.bfloat16))
     state_ref[...] = state

time: 44.2 us -> 44.2 us (level)
  no operation moved by 1% of the time
where the time goes in v10:
time: 44.2 us; the launch traced here: 44 us
  waiting for transfers between devices  18.5 us (42%)
  starting transfers between devices  14 us (32%)
  Pallas kernels  9.77 us (22%)
  between operations  0.89 us (2%)
  other arithmetic  0.79 us (2%)
    ppermute x14, waiting for transfers between devices, swapped(): return lax.ppermute(value, BOTH, [(i, i ^ mask) for i in range(count)])  14.4 us
    ppermute x14, starting transfers between devices, swapped(): return lax.ppermute(value, BOTH, [(i, i ^ mask) for i in range(count)])  10.4 us
    pallas_call x6, Pallas kernels, on_chip(): pl.pallas_call(kernel, out_shape=tuple((jax.ShapeDtypeStruct(shape, dtype...  5.75 us
    ppermute x4, waiting for transfers between devices, climbed(): return lax.ppermute(value, ('section', 'lane'), pairs)  4.07 us
    ppermute x4, starting transfers between devices, climbed(): return lax.ppermute(value, ('section', 'lane'), pairs)  3.59 us
    pallas_call x1, Pallas kernels, load(): pl.pallas_call(load_kernel, out_shape=tuple((pltpu.VMEM(a.shape, a.dtype)...  2.87 us
    pallas_call x1, Pallas kernels, entry(): pl.pallas_call(entry_kernel, out_shape=(pltpu.VMEM(state.shape, jnp.bfloa...  0.98 us
  transfers between devices with their start and end apart: 18, of which 12 were waited for; matrix products, arithmetic and copies ran while one was open for 0% of the time, Pallas kernels for 12%

profile of v10, /device:TPU:0, one launch (start us, length us, event | category | flops | bytes accessed | tf_op | source)
XLA Modules:
  0.0 44.0 jit_solution(17075968050746324002)
XLA Ops:
  0.0 1.0 %shard_map.73 = (bf16[16,3072]{1,0:T(8,128)(2,1)S(1)}, bf16[16,3072]{1,0:T(8,128)(2,1)S(1)}, f32[1,3072]{1,0:T(1,128)S(1)}) custom-call(bf16[16,3072]{1,0:T(8,128)(2,1)} %bitcast.22, f32[1,3072]{1,0:T(1,128)} %bitcast.23), custom_call_target="tpu_custom_call" | custom-call | tf_op jit(solution)/shard_map/pallas_call | solution.py:153
  1.0 4.0 %collective-permute-start.2 = (bf16[16,3072]{1,0:T(8,128)(2,1)S(1)}, bf16[16,3072]{1,0:T(8,128)(2,1)S(1)}, u32[]{:S(2)}, u32[]{:S(2)}) collective-permute-start(bf16[16,3072]{1,0:T(8,128)(2,1)S(1)} %get-tuple-element.33), channel_id=1, source_target_pairs={{0,6},{1,7},{2,4},{3,5},{4,2},{5,3},{6,0},{7,1},{8,14},{9,15},{10,... | collective-permute-start | bytes 294920 | tf_op jit(solution)/shard_map/ppermute | solution.py:18
  4.9 0.5 %collective-permute-start.3 = (bf16[16,3072]{1,0:T(8,128)(2,1)S(1)}, bf16[16,3072]{1,0:T(8,128)(2,1)S(1)}, u32[]{:S(2)}, u32[]{:S(2)}) collective-permute-start(bf16[16,3072]{1,0:T(8,128)(2,1)S(1)} %get-tuple-element.33), channel_id=1, source_target_pairs={{0,4},{1,5},{2,6},{3,7},{4,0},{5,1},{6,2},{7,3},{8,12},{9,13},{10,... | collective-permute-start | bytes 294920 | tf_op jit(solution)/shard_map/ppermute | solution.py:18
  5.5 0.1 collective-permute-start
  5.6 2.9 %shard_map.74.wkv_ref = bf16[6144,512]{1,0:T(8,128)(2,1)S(1)} custom-call(bf16[6144,512]{1,0:T(8,128)(2,1)} %bitcast.21), custom_call_target="tpu_custom_call" | custom-call | bytes 6291456 | tf_op jit(solution)/shard_map/pallas_call | solution.py:183
  8.5 0.0 copy-start.1
  8.5 0.0 copy-start.2
  8.5 0.0 collective-permute-done.2
  8.5 1.7 %collective-permute-done.3 = bf16[16,3072]{1,0:T(8,128)(2,1)S(1)} collective-permute-done((bf16[16,3072]{1,0:T(8,128)(2,1)S(1)}, bf16[16,3072]{1,0:T(8,128)(2,1)S(1)}, u32[]{:S(2)}, u32[]{:S(2)}) %collective-permute-start.3) | collective-permute-done | bytes 98336 | tf_op jit(solution)/shard_map/ppermute | solution.py:18
  10.2 0.1 collective-permute-start.4
  10.3 0.0 collective-permute-done
  10.3 0.5 %collective-permute-start.1 = (bf16[32,3072]{1,0:T(8,128)(2,1)S(1)}, bf16[32,3072]{1,0:T(8,128)(2,1)S(1)}, u32[]{:S(2)}, u32[]{:S(2)}) collective-permute-start(bf16[32,3072]{1,0:T(8,128)(2,1)S(1)} %constant_dynamic-update-slice_fusion.mine_ref), channel_id=1, source_target_pairs={{0,1},{1,0},{2,3},{3,2},{4,5},{5,4},{6,7},{7,6},{8,9},{9,8},{10,11... | collective-permute-start | bytes 589832 | tf_op jit(solution)/shard_map/ppermute | solution.py:18
  10.9 0.8 %collective-permute-done.4.theirs_ref = bf16[32,3072]{1,0:T(8,128)(2,1)S(1)} collective-permute-done((bf16[32,3072]{1,0:T(8,128)(2,1)S(1)}, bf16[32,3072]{1,0:T(8,128)(2,1)S(1)}, u32[]{:S(2)}, u32[]{:S(2)}) %collective-permute-start.4) | collective-permute-done | bytes 196640 | tf_op jit(solution)/shard_map/ppermute | solution.py:18
  11.7 1.2 %shard_map.75 = (bf16[64,512]{1,0:T(8,128)(2,1)S(1)}, bf16[64,512]{1,0:T(8,128)(2,1)S(1)}) custom-call(bf16[32,3072]{1,0:T(8,128)(2,1)S(1)} %pad_maximum_fusion.1.mine_ref, bf16[32,3072]{1,0:T(8,128)(2,1)S(1)} %collective-permute-done.4.theirs_ref, bf16[6144,512]{1,0:T(8,128)(2,1)S(1)} %shard_map.74.wkv_ref), custom_call_target="tpu_custom_call" | custom-call | flops 1610612736 | bytes 6684672 | tf_op jit(solution)/shard_map/pallas_call | solution.py:97
  12.9 0.0 copy-start
  12.9 0.0 collective-permute-done.1.theirs_ref
  12.9 0.0 copy-done.1
  12.9 0.0 copy-done.2
  12.9 1.6 %shard_map.76 = (f32[32,3072]{1,0:T(8,128)S(1)}, bf16[32,3072]{1,0:T(8,128)(2,1)S(1)}) custom-call(bf16[32,3072]{1,0:T(8,128)(2,1)S(1)} %constant_dynamic-update-slice_fusion.mine_ref, bf16[32,3072]{1,0:T(8,128)(2,1)S(1)} %collective-permute-done.1.theirs_ref, bf16[64,512]{1,0:T(8,128)(2,1)S(1)} %get-tuple-element.36.keys_ref, ...), custom_call_target="tpu_custom_call" | custom-call | flops 2415919104 | bytes 6815744 | tf_op jit(solution)/shard_map/pallas_call | solution.py:97
  14.6 0.2 collective-permute-start.5
  14.8 1.3 %collective-permute-done.5.sent_ref = bf16[32,3072]{1,0:T(8,128)(2,1)S(1)} collective-permute-done((bf16[32,3072]{1,0:T(8,128)(2,1)S(1)}, bf16[32,3072]{1,0:T(8,128)(2,1)S(1)}, u32[]{:S(2)}, u32[]{:S(2)}) %collective-permute-start.5) | collective-permute-done | bytes 196640 | tf_op jit(solution)/shard_map/ppermute | solution.py:18
  16.2 1.6 %collective-permute-start.6 = (bf16[16,3072]{1,0:T(8,128)(2,1)S(1)}, bf16[16,3072]{1,0:T(8,128)(2,1)S(1)}, u32[]{:S(2)}, u32[]{:S(2)}) collective-permute-start(bf16[16,3072]{1,0:T(8,128)(2,1)S(1)} %convert_element_type.15), channel_id=1, source_target_pairs={{0,8},{1,0},{2,10},{3,2},{8,16},{9,1},{10,18},{11,3},{16,24},{17,9... | collective-permute-start | bytes 294920 | tf_op jit(solution)/shard_map/ppermute | solution.py:30
  17.8 0.0 collective-permute-start.8
  17.8 0.0 collective-permute-start.7
  17.8 2.0 %collective-permute-start.9 = (bf16[16,3072]{1,0:T(8,128)(2,1)S(1)}, bf16[16,3072]{1,0:T(8,128)(2,1)S(1)}, u32[]{:S(2)}, u32[]{:S(2)}) collective-permute-start(bf16[16,3072]{1,0:T(8,128)(2,1)S(1)} %get-tuple-element.47), channel_id=1, source_target_pairs={{0,10},{1,0},{2,8},{3,2},{8,18},{9,1},{10,16},{11,3},{16,26},{17,9... | collective-permute-start | bytes 294920 | tf_op jit(solution)/shard_map/ppermute | solution.py:30
  20.4 0.5 %collective-permute-done.6 = bf16[16,3072]{1,0:T(8,128)(2,1)S(1)} collective-permute-done((bf16[16,3072]{1,0:T(8,128)(2,1)S(1)}, bf16[16,3072]{1,0:T(8,128)(2,1)S(1)}, u32[]{:S(2)}, u32[]{:S(2)}) %collective-permute-start.6) | collective-permute-done | bytes 98336 | tf_op jit(solution)/shard_map/ppermute | solution.py:30
  20.9 2.2 %collective-permute-done.8 = bf16[16,3072]{1,0:T(8,128)(2,1)S(1)} collective-permute-done((bf16[16,3072]{1,0:T(8,128)(2,1)S(1)}, bf16[16,3072]{1,0:T(8,128)(2,1)S(1)}, u32[]{:S(2)}, u32[]{:S(2)}) %collective-permute-start.8) | collective-permute-done | bytes 98336 | tf_op jit(solution)/shard_map/ppermute | solution.py:30
  23.1 1.3 %collective-permute-done.7 = bf16[16,3072]{1,0:T(8,128)(2,1)S(1)} collective-permute-done((bf16[16,3072]{1,0:T(8,128)(2,1)S(1)}, bf16[16,3072]{1,0:T(8,128)(2,1)S(1)}, u32[]{:S(2)}, u32[]{:S(2)}) %collective-permute-start.7) | collective-permute-done | bytes 98336 | tf_op jit(solution)/shard_map/ppermute | solution.py:30
  24.5 0.0 collective-permute-done.9
  24.5 0.0 copy-done
  24.5 0.2 shard_map.78
  24.7 1.1 %collective-permute-start.10 = (bf16[16,3072]{1,0:T(8,128)(2,1)S(1)}, bf16[16,3072]{1,0:T(8,128)(2,1)S(1)}, u32[]{:S(2)}, u32[]{:S(2)}) collective-permute-start(bf16[16,3072]{1,0:T(8,128)(2,1)S(1)} %get-tuple-element.46), channel_id=1, source_target_pairs={{0,6},{1,7},{2,4},{3,5},{4,2},{5,3},{6,0},{7,1},{8,14},{9,15},{10,... | collective-permute-start | bytes 294920 | tf_op jit(solution)/shard_map/ppermute | solution.py:18
  25.8 0.6 %collective-permute-start.11 = (bf16[16,3072]{1,0:T(8,128)(2,1)S(1)}, bf16[16,3072]{1,0:T(8,128)(2,1)S(1)}, u32[]{:S(2)}, u32[]{:S(2)}) collective-permute-start(bf16[16,3072]{1,0:T(8,128)(2,1)S(1)} %get-tuple-element.46), channel_id=1, source_target_pairs={{0,4},{1,5},{2,6},{3,7},{4,0},{5,1},{6,2},{7,3},{8,12},{9,13},{10,... | collective-permute-start | bytes 294920 | tf_op jit(solution)/shard_map/ppermute | solution.py:18
  26.4 1.8 %collective-permute-start.14 = (bf16[16,3072]{1,0:T(8,128)(2,1)S(1)}, bf16[16,3072]{1,0:T(8,128)(2,1)S(1)}, u32[]{:S(2)}, u32[]{:S(2)}) collective-permute-start(bf16[16,3072]{1,0:T(8,128)(2,1)S(1)} %get-tuple-element.46), channel_id=1, source_target_pairs={{0,2},{1,3},{2,0},{3,1},{4,6},{5,7},{6,4},{7,5},{8,10},{9,11},{10,... | collective-permute-start | bytes 294920 | tf_op jit(solution)/shard_map/ppermute | solution.py:18
  28.3 0.2 collective-permute-start.13
  28.5 2.4 %collective-permute-done.10 = bf16[16,3072]{1,0:T(8,128)(2,1)S(1)} collective-permute-done((bf16[16,3072]{1,0:T(8,128)(2,1)S(1)}, bf16[16,3072]{1,0:T(8,128)(2,1)S(1)}, u32[]{:S(2)}, u32[]{:S(2)}) %collective-permute-start.10) | collective-permute-done | bytes 98336 | tf_op jit(solution)/shard_map/ppermute | solution.py:18
  30.9 0.4 collective-permute-done.11
  31.4 0.1 collective-permute-start.12
  31.4 1.4 %collective-permute-done.14 = bf16[16,3072]{1,0:T(8,128)(2,1)S(1)} collective-permute-done((bf16[16,3072]{1,0:T(8,128)(2,1)S(1)}, bf16[16,3072]{1,0:T(8,128)(2,1)S(1)}, u32[]{:S(2)}, u32[]{:S(2)}) %collective-permute-start.14) | collective-permute-done | bytes 98336 | tf_op jit(solution)/shard_map/ppermute | solution.py:18
  32.8 0.1 collective-permute-start.15
  32.9 1.0 %collective-permute-done.13 = bf16[16,3072]{1,0:T(8,128)(2,1)S(1)} collective-permute-done((bf16[16,3072]{1,0:T(8,128)(2,1)S(1)}, bf16[16,3072]{1,0:T(8,128)(2,1)S(1)}, u32[]{:S(2)}, u32[]{:S(2)}) %collective-permute-start.13) | collective-permute-done | bytes 98336 | tf_op jit(solution)/shard_map/ppermute | solution.py:18
  33.9 0.0 collective-permute-done.12.theirs_ref
  33.9 1.2 %shard_map.79 = (bf16[64,512]{1,0:T(8,128)(2,1)S(1)}, bf16[64,512]{1,0:T(8,128)(2,1)S(1)}) custom-call(bf16[32,3072]{1,0:T(8,128)(2,1)S(1)} %constant_dynamic-update-slice_fusion.2.mine_ref, bf16[32,3072]{1,0:T(8,128)(2,1)S(1)} %collective-permute-done.12.theirs_ref, bf16[6144,512]{1,0:T(8,128)(2,1)S(1)} %shard_map.74.wkv_ref), custom_call_target="tpu_custom_call" | custom-call | flops 1610612736 | bytes 6684672 | tf_op jit(solution)/shard_map/pallas_call | solution.py:97
  35.1 0.0 collective-permute-done.15.theirs_ref
  35.2 1.6 %shard_map.80 = (f32[32,3072]{1,0:T(8,128)S(1)}, bf16[32,3072]{1,0:T(8,128)(2,1)S(1)}) custom-call(bf16[32,3072]{1,0:T(8,128)(2,1)S(1)} %constant_dynamic-update-slice_fusion.4.mine_ref, bf16[32,3072]{1,0:T(8,128)(2,1)S(1)} %collective-permute-done.15.theirs_ref, bf16[64,512]{1,0:T(8,128)(2,1)S(1)} %get-tuple-element.51.keys_ref, ...), custom_call_target="tpu_custom_call" | custom-call | flops 2415919104 | bytes 6815744 | tf_op jit(solution)/shard_map/pallas_call | solution.py:97
  36.8 0.1 collective-permute-start.16
  36.9 1.4 %collective-permute-done.16.sent_ref = bf16[32,3072]{1,0:T(8,128)(2,1)S(1)} collective-permute-done((bf16[32,3072]{1,0:T(8,128)(2,1)S(1)}, bf16[32,3072]{1,0:T(8,128)(2,1)S(1)}, u32[]{:S(2)}, u32[]{:S(2)}) %collective-permute-start.16) | collective-permute-done | bytes 196640 | tf_op jit(solution)/shard_map/ppermute | solution.py:18
  38.4 1.0 %collective-permute-start.17 = (bf16[16,3072]{1,0:T(8,128)(2,1)S(1)}, bf16[16,3072]{1,0:T(8,128)(2,1)S(1)}, u32[]{:S(2)}, u32[]{:S(2)}) collective-permute-start(bf16[16,3072]{1,0:T(8,128)(2,1)S(1)} %get-tuple-element.56), channel_id=1, source_target_pairs={{0,2},{1,3},{2,0},{3,1},{4,6},{5,7},{6,4},{7,5},{8,10},{9,11},{10,... | collective-permute-start | bytes 294920 | tf_op jit(solution)/shard_map/ppermute | solution.py:18
  39.4 3.8 %collective-permute-done.17 = bf16[16,3072]{1,0:T(8,128)(2,1)S(1)} collective-permute-done((bf16[16,3072]{1,0:T(8,128)(2,1)S(1)}, bf16[16,3072]{1,0:T(8,128)(2,1)S(1)}, u32[]{:S(2)}, u32[]{:S(2)}) %collective-permute-start.17) | collective-permute-done | bytes 98336 | tf_op jit(solution)/shard_map/ppermute | solution.py:18
  43.3 0.7 %maximum_bitcast_fusion = bf16[2,1,1,16,3072]{4,3,2,1,0:T(8,128)(2,1)} fusion(bf16[1,16,3072]{2,1,0:T(8,128)(2,1)S(1)} %fusion.1, bf16[1,16,3072]{2,1,0:T(8,128)(2,1)S(1)} %fusion), kind=kLoop, calls=%fused_computation.2 | loop fusion | flops 98304 | bytes 393216 | tf_op jit(solution)/shard_map/broadcast_in_dim | solution.py:267
  (13 shorter events, 0.2 us)
Async XLA Ops:
  1.0 7.5 %collective-permute-start.2 = (bf16[16,3072]{1,0:T(8,128)(2,1)S(1)}, bf16[16,3072]{1,0:T(8,128)(2,1)S(1)}, u32[]{:S(2)}, u32[]{:S(2)}) collective-permute-start(bf16[16,3072]{1,0:T(8,128)(2,1)S(1)} %get-tuple-element.33), channel_id=1, source_target_pairs={{0,6},{1,7},{2,4},{3,5},{4,2},{5,3},{6,0},{7,1},{8,14},{9,15},{10,... | collective-permute-start | bytes 294920 | tf_op jit(solution)/shard_map/ppermute | solution.py:18
  4.9 5.2 %collective-permute-start.3 = (bf16[16,3072]{1,0:T(8,128)(2,1)S(1)}, bf16[16,3072]{1,0:T(8,128)(2,1)S(1)}, u32[]{:S(2)}, u32[]{:S(2)}) collective-permute-start(bf16[16,3072]{1,0:T(8,128)(2,1)S(1)} %get-tuple-element.33), channel_id=1, source_target_pairs={{0,4},{1,5},{2,6},{3,7},{4,0},{5,1},{6,2},{7,3},{8,12},{9,13},{10,... | collective-permute-start | bytes 294920 | tf_op jit(solution)/shard_map/ppermute | solution.py:18
  5.5 4.8 %collective-permute-start = (bf16[16,3072]{1,0:T(8,128)(2,1)S(1)}, bf16[16,3072]{1,0:T(8,128)(2,1)S(1)}, u32[]{:S(2)}, u32[]{:S(2)}) collective-permute-start(bf16[16,3072]{1,0:T(8,128)(2,1)S(1)} %get-tuple-element.33), channel_id=1, source_target_pairs={{0,2},{1,3},{2,0},{3,1},{4,6},{5,7},{6,4},{7,5},{8,10},{9,11},{10,... | collective-permute-start | bytes 294920 | tf_op jit(solution)/shard_map/ppermute | solution.py:18
  8.5 4.5 %copy-start.1 = (bf16[1,1,3072,512]{3,2,1,0:T(8,128)(2,1)S(1)}, bf16[1,1,3072,512]{3,2,1,0:T(8,128)(2,1)}, u32[]{:S(2)}) copy-start(bf16[1,1,3072,512]{3,2,1,0:T(8,128)(2,1)} %param.11) | copy-start | bytes 9437188
  8.5 4.5 %copy-start.2 = (bf16[1,1,512,3072]{3,2,1,0:T(8,128)(2,1)S(1)}, bf16[1,1,512,3072]{3,2,1,0:T(8,128)(2,1)}, u32[]{:S(2)}) copy-start(bf16[1,1,512,3072]{3,2,1,0:T(8,128)(2,1)} %param.13) | copy-start | bytes 9437188
  10.2 1.5 %collective-permute-start.4 = (bf16[32,3072]{1,0:T(8,128)(2,1)S(1)}, bf16[32,3072]{1,0:T(8,128)(2,1)S(1)}, u32[]{:S(2)}, u32[]{:S(2)}) collective-permute-start(bf16[32,3072]{1,0:T(8,128)(2,1)S(1)} %pad_maximum_fusion.1.mine_ref), channel_id=1, source_target_pairs={{0,1},{1,0},{2,3},{3,2},{4,5},{5,4},{6,7},{7,6},{8,9},{9,8},{10,11... | collective-permute-start | bytes 589832 | tf_op jit(solution)/shard_map/ppermute | solution.py:18
  10.3 2.6 %collective-permute-start.1 = (bf16[32,3072]{1,0:T(8,128)(2,1)S(1)}, bf16[32,3072]{1,0:T(8,128)(2,1)S(1)}, u32[]{:S(2)}, u32[]{:S(2)}) collective-permute-start(bf16[32,3072]{1,0:T(8,128)(2,1)S(1)} %constant_dynamic-update-slice_fusion.mine_ref), channel_id=1, source_target_pairs={{0,1},{1,0},{2,3},{3,2},{4,5},{5,4},{6,7},{7,6},{8,9},{9,8},{10,11... | collective-permute-start | bytes 589832 | tf_op jit(solution)/shard_map/ppermute | solution.py:18
  12.9 11.6 %copy-start = (bf16[4,1,16,3072]{3,2,1,0:T(8,128)(2,1)S(1)}, bf16[4,1,16,3072]{3,2,1,0:T(8,128)(2,1)}, u32[]{:S(2)}) copy-start(bf16[4,1,16,3072]{3,2,1,0:T(8,128)(2,1)} %param.8) | copy-start | bytes 1179652
  14.6 1.5 %collective-permute-start.5 = (bf16[32,3072]{1,0:T(8,128)(2,1)S(1)}, bf16[32,3072]{1,0:T(8,128)(2,1)S(1)}, u32[]{:S(2)}, u32[]{:S(2)}) collective-permute-start(bf16[32,3072]{1,0:T(8,128)(2,1)S(1)} %get-tuple-element.39), channel_id=1, source_target_pairs={{0,1},{1,0},{2,3},{3,2},{4,5},{5,4},{6,7},{7,6},{8,9},{9,8},{10,11... | collective-permute-start | bytes 589832 | tf_op jit(solution)/shard_map/ppermute | solution.py:18
  16.2 4.7 %collective-permute-start.6 = (bf16[16,3072]{1,0:T(8,128)(2,1)S(1)}, bf16[16,3072]{1,0:T(8,128)(2,1)S(1)}, u32[]{:S(2)}, u32[]{:S(2)}) collective-permute-start(bf16[16,3072]{1,0:T(8,128)(2,1)S(1)} %convert_element_type.15), channel_id=1, source_target_pairs={{0,8},{1,0},{2,10},{3,2},{8,16},{9,1},{10,18},{11,3},{16,24},{17,9... | collective-permute-start | bytes 294920 | tf_op jit(solution)/shard_map/ppermute | solution.py:30
  17.8 5.4 %collective-permute-start.8 = (bf16[16,3072]{1,0:T(8,128)(2,1)S(1)}, bf16[16,3072]{1,0:T(8,128)(2,1)S(1)}, u32[]{:S(2)}, u32[]{:S(2)}) collective-permute-start(bf16[16,3072]{1,0:T(8,128)(2,1)S(1)} %convert_element_type.15), channel_id=1, source_target_pairs={{0,1},{1,9},{2,3},{3,11},{8,0},{9,17},{10,2},{11,19},{16,8},{17,25... | collective-permute-start | bytes 294920 | tf_op jit(solution)/shard_map/ppermute | solution.py:30
  17.8 6.7 %collective-permute-start.7 = (bf16[16,3072]{1,0:T(8,128)(2,1)S(1)}, bf16[16,3072]{1,0:T(8,128)(2,1)S(1)}, u32[]{:S(2)}, u32[]{:S(2)}) collective-permute-start(bf16[16,3072]{1,0:T(8,128)(2,1)S(1)} %get-tuple-element.47), channel_id=1, source_target_pairs={{0,1},{1,11},{2,3},{3,9},{8,0},{9,19},{10,2},{11,17},{16,8},{17,27... | collective-permute-start | bytes 294920 | tf_op jit(solution)/shard_map/ppermute | solution.py:30
  17.8 6.7 %collective-permute-start.9 = (bf16[16,3072]{1,0:T(8,128)(2,1)S(1)}, bf16[16,3072]{1,0:T(8,128)(2,1)S(1)}, u32[]{:S(2)}, u32[]{:S(2)}) collective-permute-start(bf16[16,3072]{1,0:T(8,128)(2,1)S(1)} %get-tuple-element.47), channel_id=1, source_target_pairs={{0,10},{1,0},{2,8},{3,2},{8,18},{9,1},{10,16},{11,3},{16,26},{17,9... | collective-permute-start | bytes 294920 | tf_op jit(solution)/shard_map/ppermute | solution.py:30
  24.7 6.2 %collective-permute-start.10 = (bf16[16,3072]{1,0:T(8,128)(2,1)S(1)}, bf16[16,3072]{1,0:T(8,128)(2,1)S(1)}, u32[]{:S(2)}, u32[]{:S(2)}) collective-permute-start(bf16[16,3072]{1,0:T(8,128)(2,1)S(1)} %get-tuple-element.46), channel_id=1, source_target_pairs={{0,6},{1,7},{2,4},{3,5},{4,2},{5,3},{6,0},{7,1},{8,14},{9,15},{10,... | collective-permute-start | bytes 294920 | tf_op jit(solution)/shard_map/ppermute | solution.py:18
  25.8 5.5 %collective-permute-start.11 = (bf16[16,3072]{1,0:T(8,128)(2,1)S(1)}, bf16[16,3072]{1,0:T(8,128)(2,1)S(1)}, u32[]{:S(2)}, u32[]{:S(2)}) collective-permute-start(bf16[16,3072]{1,0:T(8,128)(2,1)S(1)} %get-tuple-element.46), channel_id=1, source_target_pairs={{0,4},{1,5},{2,6},{3,7},{4,0},{5,1},{6,2},{7,3},{8,12},{9,13},{10,... | collective-permute-start | bytes 294920 | tf_op jit(solution)/shard_map/ppermute | solution.py:18
  26.4 6.4 %collective-permute-start.14 = (bf16[16,3072]{1,0:T(8,128)(2,1)S(1)}, bf16[16,3072]{1,0:T(8,128)(2,1)S(1)}, u32[]{:S(2)}, u32[]{:S(2)}) collective-permute-start(bf16[16,3072]{1,0:T(8,128)(2,1)S(1)} %get-tuple-element.46), channel_id=1, source_target_pairs={{0,2},{1,3},{2,0},{3,1},{4,6},{5,7},{6,4},{7,5},{8,10},{9,11},{10,... | collective-permute-start | bytes 294920 | tf_op jit(solution)/shard_map/ppermute | solution.py:18
  28.3 5.7 %collective-permute-start.13 = (bf16[16,3072]{1,0:T(8,128)(2,1)S(1)}, bf16[16,3072]{1,0:T(8,128)(2,1)S(1)}, u32[]{:S(2)}, u32[]{:S(2)}) collective-permute-start(bf16[16,3072]{1,0:T(8,128)(2,1)S(1)} %get-tuple-element.47), channel_id=1, source_target_pairs={{0,2},{1,3},{2,0},{3,1},{4,6},{5,7},{6,4},{7,5},{8,10},{9,11},{10,... | collective-permute-start | bytes 294920 | tf_op jit(solution)/shard_map/ppermute | solution.py:18
  31.4 2.6 %collective-permute-start.12 = (bf16[32,3072]{1,0:T(8,128)(2,1)S(1)}, bf16[32,3072]{1,0:T(8,128)(2,1)S(1)}, u32[]{:S(2)}, u32[]{:S(2)}) collective-permute-start(bf16[32,3072]{1,0:T(8,128)(2,1)S(1)} %constant_dynamic-update-slice_fusion.2.mine_ref), channel_id=1, source_target_pairs={{0,1},{1,0},{2,3},{3,2},{4,5},{5,4},{6,7},{7,6},{8,9},{9,8},{10,11... | collective-permute-start | bytes 589832 | tf_op jit(solution)/shard_map/ppermute | solution.py:18
  32.8 2.3 %collective-permute-start.15 = (bf16[32,3072]{1,0:T(8,128)(2,1)S(1)}, bf16[32,3072]{1,0:T(8,128)(2,1)S(1)}, u32[]{:S(2)}, u32[]{:S(2)}) collective-permute-start(bf16[32,3072]{1,0:T(8,128)(2,1)S(1)} %constant_dynamic-update-slice_fusion.4.mine_ref), channel_id=1, source_target_pairs={{0,1},{1,0},{2,3},{3,2},{4,5},{5,4},{6,7},{7,6},{8,9},{9,8},{10,11... | collective-permute-start | bytes 589832 | tf_op jit(solution)/shard_map/ppermute | solution.py:18
  36.8 1.5 %collective-permute-start.16 = (bf16[32,3072]{1,0:T(8,128)(2,1)S(1)}, bf16[32,3072]{1,0:T(8,128)(2,1)S(1)}, u32[]{:S(2)}, u32[]{:S(2)}) collective-permute-start(bf16[32,3072]{1,0:T(8,128)(2,1)S(1)} %get-tuple-element.54), channel_id=1, source_target_pairs={{0,1},{1,0},{2,3},{3,2},{4,5},{5,4},{6,7},{7,6},{8,9},{9,8},{10,11... | collective-permute-start | bytes 589832 | tf_op jit(solution)/shard_map/ppermute | solution.py:18
  38.4 4.9 %collective-permute-start.17 = (bf16[16,3072]{1,0:T(8,128)(2,1)S(1)}, bf16[16,3072]{1,0:T(8,128)(2,1)S(1)}, u32[]{:S(2)}, u32[]{:S(2)}) collective-permute-start(bf16[16,3072]{1,0:T(8,128)(2,1)S(1)} %get-tuple-element.56), channel_id=1, source_target_pairs={{0,2},{1,3},{2,0},{3,1},{4,6},{5,7},{6,4},{7,5},{8,10},{9,11},{10,... | collective-permute-start | bytes 294920 | tf_op jit(solution)/shard_map/ppermute | solution.py:18

commit v11 on v10

--- a/solution.py
+++ b/solution.py
@@ -81,8 +81,8 @@
         for weight, head in zip(weights, heads)
     ]
     mixed = jnp.concatenate([(mix / total).astype(jnp.bfloat16) for mix, total in zip(mixed, sums)], 1)
-    for start in range(0, width, width // 4):
-        columns = slice(start, start + width // 4)
+    for start in range(0, width, width // 2):
+        columns = slice(start, start + width // 2)
         part = jnp.dot(mixed, wo_ref[:, columns], preferred_element_type=jnp.float32)
         keep_ref[:, columns] = part[:half]
         send_ref[:, columns] = part[half:].astype(jnp.bfloat16)

time: 44.2 us -> 44.2 us (level)
  no operation moved by 1% of the time
where the time goes in v11:
time: 44.2 us; the launch traced here: 44 us
  waiting for transfers between devices  18.5 us (42%)
  starting transfers between devices  14 us (32%)
  Pallas kernels  9.77 us (22%)
  between operations  0.89 us (2%)
  other arithmetic  0.79 us (2%)
    ppermute x14, waiting for transfers between devices, swapped(): return lax.ppermute(value, BOTH, [(i, i ^ mask) for i in range(count)])  14.4 us
    ppermute x14, starting transfers between devices, swapped(): return lax.ppermute(value, BOTH, [(i, i ^ mask) for i in range(count)])  10.4 us
    pallas_call x6, Pallas kernels, on_chip(): pl.pallas_call(kernel, out_shape=tuple((jax.ShapeDtypeStruct(shape, dtype...  5.75 us
    ppermute x4, waiting for transfers between devices, climbed(): return lax.ppermute(value, ('section', 'lane'), pairs)  4.07 us
    ppermute x4, starting transfers between devices, climbed(): return lax.ppermute(value, ('section', 'lane'), pairs)  3.59 us
    pallas_call x1, Pallas kernels, load(): pl.pallas_call(load_kernel, out_shape=tuple((pltpu.VMEM(a.shape, a.dtype)...  2.87 us
    pallas_call x1, Pallas kernels, entry(): pl.pallas_call(entry_kernel, out_shape=(pltpu.VMEM(state.shape, jnp.bfloa...  0.98 us
  transfers between devices with their start and end apart: 18, of which 12 were waited for; matrix products, arithmetic and copies ran while one was open for 0% of the time, Pallas kernels for 12%

profile of v11, /device:TPU:0, one launch (start us, length us, event | category | flops | bytes accessed | tf_op | source)
XLA Modules:
  0.0 44.0 jit_solution(17075968050746324002)
XLA Ops:
  0.0 1.0 %shard_map.73 = (bf16[16,3072]{1,0:T(8,128)(2,1)S(1)}, bf16[16,3072]{1,0:T(8,128)(2,1)S(1)}, f32[1,3072]{1,0:T(1,128)S(1)}) custom-call(bf16[16,3072]{1,0:T(8,128)(2,1)} %bitcast.22, f32[1,3072]{1,0:T(1,128)} %bitcast.23), custom_call_target="tpu_custom_call" | custom-call | tf_op jit(solution)/shard_map/pallas_call | solution.py:153
  1.0 4.0 %collective-permute-start.2 = (bf16[16,3072]{1,0:T(8,128)(2,1)S(1)}, bf16[16,3072]{1,0:T(8,128)(2,1)S(1)}, u32[]{:S(2)}, u32[]{:S(2)}) collective-permute-start(bf16[16,3072]{1,0:T(8,128)(2,1)S(1)} %get-tuple-element.33), channel_id=1, source_target_pairs={{0,6},{1,7},{2,4},{3,5},{4,2},{5,3},{6,0},{7,1},{8,14},{9,15},{10,... | collective-permute-start | bytes 294920 | tf_op jit(solution)/shard_map/ppermute | solution.py:18
  4.9 0.5 %collective-permute-start.3 = (bf16[16,3072]{1,0:T(8,128)(2,1)S(1)}, bf16[16,3072]{1,0:T(8,128)(2,1)S(1)}, u32[]{:S(2)}, u32[]{:S(2)}) collective-permute-start(bf16[16,3072]{1,0:T(8,128)(2,1)S(1)} %get-tuple-element.33), channel_id=1, source_target_pairs={{0,4},{1,5},{2,6},{3,7},{4,0},{5,1},{6,2},{7,3},{8,12},{9,13},{10,... | collective-permute-start | bytes 294920 | tf_op jit(solution)/shard_map/ppermute | solution.py:18
  5.5 0.1 collective-permute-start
  5.6 2.9 %shard_map.74.wkv_ref = bf16[6144,512]{1,0:T(8,128)(2,1)S(1)} custom-call(bf16[6144,512]{1,0:T(8,128)(2,1)} %bitcast.21), custom_call_target="tpu_custom_call" | custom-call | bytes 6291456 | tf_op jit(solution)/shard_map/pallas_call | solution.py:183
  8.5 0.0 copy-start.1
  8.5 0.0 copy-start.2
  8.5 0.0 collective-permute-done.2
  8.5 1.7 %collective-permute-done.3 = bf16[16,3072]{1,0:T(8,128)(2,1)S(1)} collective-permute-done((bf16[16,3072]{1,0:T(8,128)(2,1)S(1)}, bf16[16,3072]{1,0:T(8,128)(2,1)S(1)}, u32[]{:S(2)}, u32[]{:S(2)}) %collective-permute-start.3) | collective-permute-done | bytes 98336 | tf_op jit(solution)/shard_map/ppermute | solution.py:18
  10.2 0.1 collective-permute-start.4
  10.3 0.0 collective-permute-done
  10.3 0.5 %collective-permute-start.1 = (bf16[32,3072]{1,0:T(8,128)(2,1)S(1)}, bf16[32,3072]{1,0:T(8,128)(2,1)S(1)}, u32[]{:S(2)}, u32[]{:S(2)}) collective-permute-start(bf16[32,3072]{1,0:T(8,128)(2,1)S(1)} %constant_dynamic-update-slice_fusion.mine_ref), channel_id=1, source_target_pairs={{0,1},{1,0},{2,3},{3,2},{4,5},{5,4},{6,7},{7,6},{8,9},{9,8},{10,11... | collective-permute-start | bytes 589832 | tf_op jit(solution)/shard_map/ppermute | solution.py:18
  10.9 0.8 %collective-permute-done.4.theirs_ref = bf16[32,3072]{1,0:T(8,128)(2,1)S(1)} collective-permute-done((bf16[32,3072]{1,0:T(8,128)(2,1)S(1)}, bf16[32,3072]{1,0:T(8,128)(2,1)S(1)}, u32[]{:S(2)}, u32[]{:S(2)}) %collective-permute-start.4) | collective-permute-done | bytes 196640 | tf_op jit(solution)/shard_map/ppermute | solution.py:18
  11.7 1.2 %shard_map.75 = (bf16[64,512]{1,0:T(8,128)(2,1)S(1)}, bf16[64,512]{1,0:T(8,128)(2,1)S(1)}) custom-call(bf16[32,3072]{1,0:T(8,128)(2,1)S(1)} %pad_maximum_fusion.1.mine_ref, bf16[32,3072]{1,0:T(8,128)(2,1)S(1)} %collective-permute-done.4.theirs_ref, bf16[6144,512]{1,0:T(8,128)(2,1)S(1)} %shard_map.74.wkv_ref), custom_call_target="tpu_custom_call" | custom-call | flops 1610612736 | bytes 6684672 | tf_op jit(solution)/shard_map/pallas_call | solution.py:97
  12.9 0.0 copy-start
  12.9 0.0 collective-permute-done.1.theirs_ref
  12.9 0.0 copy-done.1
  12.9 0.0 copy-done.2
  12.9 1.6 %shard_map.76 = (f32[32,3072]{1,0:T(8,128)S(1)}, bf16[32,3072]{1,0:T(8,128)(2,1)S(1)}) custom-call(bf16[32,3072]{1,0:T(8,128)(2,1)S(1)} %constant_dynamic-update-slice_fusion.mine_ref, bf16[32,3072]{1,0:T(8,128)(2,1)S(1)} %collective-permute-done.1.theirs_ref, bf16[64,512]{1,0:T(8,128)(2,1)S(1)} %get-tuple-element.36.keys_ref, ...), custom_call_target="tpu_custom_call" | custom-call | flops 2415919104 | bytes 6815744 | tf_op jit(solution)/shard_map/pallas_call | solution.py:97
  14.6 0.2 collective-permute-start.5
  14.8 1.3 %collective-permute-done.5.sent_ref = bf16[32,3072]{1,0:T(8,128)(2,1)S(1)} collective-permute-done((bf16[32,3072]{1,0:T(8,128)(2,1)S(1)}, bf16[32,3072]{1,0:T(8,128)(2,1)S(1)}, u32[]{:S(2)}, u32[]{:S(2)}) %collective-permute-start.5) | collective-permute-done | bytes 196640 | tf_op jit(solution)/shard_map/ppermute | solution.py:18
  16.2 1.6 %collective-permute-start.6 = (bf16[16,3072]{1,0:T(8,128)(2,1)S(1)}, bf16[16,3072]{1,0:T(8,128)(2,1)S(1)}, u32[]{:S(2)}, u32[]{:S(2)}) collective-permute-start(bf16[16,3072]{1,0:T(8,128)(2,1)S(1)} %convert_element_type.15), channel_id=1, source_target_pairs={{0,8},{1,0},{2,10},{3,2},{8,16},{9,1},{10,18},{11,3},{16,24},{17,9... | collective-permute-start | bytes 294920 | tf_op jit(solution)/shard_map/ppermute | solution.py:30
  17.8 0.0 collective-permute-start.8
  17.8 0.0 collective-permute-start.7
  17.8 2.0 %collective-permute-start.9 = (bf16[16,3072]{1,0:T(8,128)(2,1)S(1)}, bf16[16,3072]{1,0:T(8,128)(2,1)S(1)}, u32[]{:S(2)}, u32[]{:S(2)}) collective-permute-start(bf16[16,3072]{1,0:T(8,128)(2,1)S(1)} %get-tuple-element.47), channel_id=1, source_target_pairs={{0,10},{1,0},{2,8},{3,2},{8,18},{9,1},{10,16},{11,3},{16,26},{17,9... | collective-permute-start | bytes 294920 | tf_op jit(solution)/shard_map/ppermute | solution.py:30
  20.4 0.5 %collective-permute-done.6 = bf16[16,3072]{1,0:T(8,128)(2,1)S(1)} collective-permute-done((bf16[16,3072]{1,0:T(8,128)(2,1)S(1)}, bf16[16,3072]{1,0:T(8,128)(2,1)S(1)}, u32[]{:S(2)}, u32[]{:S(2)}) %collective-permute-start.6) | collective-permute-done | bytes 98336 | tf_op jit(solution)/shard_map/ppermute | solution.py:30
  20.9 2.2 %collective-permute-done.8 = bf16[16,3072]{1,0:T(8,128)(2,1)S(1)} collective-permute-done((bf16[16,3072]{1,0:T(8,128)(2,1)S(1)}, bf16[16,3072]{1,0:T(8,128)(2,1)S(1)}, u32[]{:S(2)}, u32[]{:S(2)}) %collective-permute-start.8) | collective-permute-done | bytes 98336 | tf_op jit(solution)/shard_map/ppermute | solution.py:30
  23.1 1.3 %collective-permute-done.7 = bf16[16,3072]{1,0:T(8,128)(2,1)S(1)} collective-permute-done((bf16[16,3072]{1,0:T(8,128)(2,1)S(1)}, bf16[16,3072]{1,0:T(8,128)(2,1)S(1)}, u32[]{:S(2)}, u32[]{:S(2)}) %collective-permute-start.7) | collective-permute-done | bytes 98336 | tf_op jit(solution)/shard_map/ppermute | solution.py:30
  24.5 0.0 collective-permute-done.9
  24.5 0.0 copy-done
  24.5 0.2 shard_map.78
  24.7 1.1 %collective-permute-start.10 = (bf16[16,3072]{1,0:T(8,128)(2,1)S(1)}, bf16[16,3072]{1,0:T(8,128)(2,1)S(1)}, u32[]{:S(2)}, u32[]{:S(2)}) collective-permute-start(bf16[16,3072]{1,0:T(8,128)(2,1)S(1)} %get-tuple-element.46), channel_id=1, source_target_pairs={{0,6},{1,7},{2,4},{3,5},{4,2},{5,3},{6,0},{7,1},{8,14},{9,15},{10,... | collective-permute-start | bytes 294920 | tf_op jit(solution)/shard_map/ppermute | solution.py:18
  25.8 0.6 %collective-permute-start.11 = (bf16[16,3072]{1,0:T(8,128)(2,1)S(1)}, bf16[16,3072]{1,0:T(8,128)(2,1)S(1)}, u32[]{:S(2)}, u32[]{:S(2)}) collective-permute-start(bf16[16,3072]{1,0:T(8,128)(2,1)S(1)} %get-tuple-element.46), channel_id=1, source_target_pairs={{0,4},{1,5},{2,6},{3,7},{4,0},{5,1},{6,2},{7,3},{8,12},{9,13},{10,... | collective-permute-start | bytes 294920 | tf_op jit(solution)/shard_map/ppermute | solution.py:18
  26.4 1.8 %collective-permute-start.14 = (bf16[16,3072]{1,0:T(8,128)(2,1)S(1)}, bf16[16,3072]{1,0:T(8,128)(2,1)S(1)}, u32[]{:S(2)}, u32[]{:S(2)}) collective-permute-start(bf16[16,3072]{1,0:T(8,128)(2,1)S(1)} %get-tuple-element.46), channel_id=1, source_target_pairs={{0,2},{1,3},{2,0},{3,1},{4,6},{5,7},{6,4},{7,5},{8,10},{9,11},{10,... | collective-permute-start | bytes 294920 | tf_op jit(solution)/shard_map/ppermute | solution.py:18
  28.3 0.2 collective-permute-start.13
  28.5 2.4 %collective-permute-done.10 = bf16[16,3072]{1,0:T(8,128)(2,1)S(1)} collective-permute-done((bf16[16,3072]{1,0:T(8,128)(2,1)S(1)}, bf16[16,3072]{1,0:T(8,128)(2,1)S(1)}, u32[]{:S(2)}, u32[]{:S(2)}) %collective-permute-start.10) | collective-permute-done | bytes 98336 | tf_op jit(solution)/shard_map/ppermute | solution.py:18
  30.9 0.4 collective-permute-done.11
  31.4 0.1 collective-permute-start.12
  31.4 1.4 %collective-permute-done.14 = bf16[16,3072]{1,0:T(8,128)(2,1)S(1)} collective-permute-done((bf16[16,3072]{1,0:T(8,128)(2,1)S(1)}, bf16[16,3072]{1,0:T(8,128)(2,1)S(1)}, u32[]{:S(2)}, u32[]{:S(2)}) %collective-permute-start.14) | collective-permute-done | bytes 98336 | tf_op jit(solution)/shard_map/ppermute | solution.py:18
  32.8 0.1 collective-permute-start.15
  32.9 1.0 %collective-permute-done.13 = bf16[16,3072]{1,0:T(8,128)(2,1)S(1)} collective-permute-done((bf16[16,3072]{1,0:T(8,128)(2,1)S(1)}, bf16[16,3072]{1,0:T(8,128)(2,1)S(1)}, u32[]{:S(2)}, u32[]{:S(2)}) %collective-permute-start.13) | collective-permute-done | bytes 98336 | tf_op jit(solution)/shard_map/ppermute | solution.py:18
  33.9 0.0 collective-permute-done.12.theirs_ref
  33.9 1.2 %shard_map.79 = (bf16[64,512]{1,0:T(8,128)(2,1)S(1)}, bf16[64,512]{1,0:T(8,128)(2,1)S(1)}) custom-call(bf16[32,3072]{1,0:T(8,128)(2,1)S(1)} %constant_dynamic-update-slice_fusion.2.mine_ref, bf16[32,3072]{1,0:T(8,128)(2,1)S(1)} %collective-permute-done.12.theirs_ref, bf16[6144,512]{1,0:T(8,128)(2,1)S(1)} %shard_map.74.wkv_ref), custom_call_target="tpu_custom_call" | custom-call | flops 1610612736 | bytes 6684672 | tf_op jit(solution)/shard_map/pallas_call | solution.py:97
  35.1 0.0 collective-permute-done.15.theirs_ref
  35.2 1.6 %shard_map.80 = (f32[32,3072]{1,0:T(8,128)S(1)}, bf16[32,3072]{1,0:T(8,128)(2,1)S(1)}) custom-call(bf16[32,3072]{1,0:T(8,128)(2,1)S(1)} %constant_dynamic-update-slice_fusion.4.mine_ref, bf16[32,3072]{1,0:T(8,128)(2,1)S(1)} %collective-permute-done.15.theirs_ref, bf16[64,512]{1,0:T(8,128)(2,1)S(1)} %get-tuple-element.51.keys_ref, ...), custom_call_target="tpu_custom_call" | custom-call | flops 2415919104 | bytes 6815744 | tf_op jit(solution)/shard_map/pallas_call | solution.py:97
  36.8 0.1 collective-permute-start.16
  36.9 1.4 %collective-permute-done.16.sent_ref = bf16[32,3072]{1,0:T(8,128)(2,1)S(1)} collective-permute-done((bf16[32,3072]{1,0:T(8,128)(2,1)S(1)}, bf16[32,3072]{1,0:T(8,128)(2,1)S(1)}, u32[]{:S(2)}, u32[]{:S(2)}) %collective-permute-start.16) | collective-permute-done | bytes 196640 | tf_op jit(solution)/shard_map/ppermute | solution.py:18
  38.4 1.0 %collective-permute-start.17 = (bf16[16,3072]{1,0:T(8,128)(2,1)S(1)}, bf16[16,3072]{1,0:T(8,128)(2,1)S(1)}, u32[]{:S(2)}, u32[]{:S(2)}) collective-permute-start(bf16[16,3072]{1,0:T(8,128)(2,1)S(1)} %get-tuple-element.56), channel_id=1, source_target_pairs={{0,2},{1,3},{2,0},{3,1},{4,6},{5,7},{6,4},{7,5},{8,10},{9,11},{10,... | collective-permute-start | bytes 294920 | tf_op jit(solution)/shard_map/ppermute | solution.py:18
  39.4 3.8 %collective-permute-done.17 = bf16[16,3072]{1,0:T(8,128)(2,1)S(1)} collective-permute-done((bf16[16,3072]{1,0:T(8,128)(2,1)S(1)}, bf16[16,3072]{1,0:T(8,128)(2,1)S(1)}, u32[]{:S(2)}, u32[]{:S(2)}) %collective-permute-start.17) | collective-permute-done | bytes 98336 | tf_op jit(solution)/shard_map/ppermute | solution.py:18
  43.3 0.7 %maximum_bitcast_fusion = bf16[2,1,1,16,3072]{4,3,2,1,0:T(8,128)(2,1)} fusion(bf16[1,16,3072]{2,1,0:T(8,128)(2,1)S(1)} %fusion.1, bf16[1,16,3072]{2,1,0:T(8,128)(2,1)S(1)} %fusion), kind=kLoop, calls=%fused_computation.2 | loop fusion | flops 98304 | bytes 393216 | tf_op jit(solution)/shard_map/broadcast_in_dim | solution.py:267
  (13 shorter events, 0.2 us)
Async XLA Ops:
  1.0 7.5 %collective-permute-start.2 = (bf16[16,3072]{1,0:T(8,128)(2,1)S(1)}, bf16[16,3072]{1,0:T(8,128)(2,1)S(1)}, u32[]{:S(2)}, u32[]{:S(2)}) collective-permute-start(bf16[16,3072]{1,0:T(8,128)(2,1)S(1)} %get-tuple-element.33), channel_id=1, source_target_pairs={{0,6},{1,7},{2,4},{3,5},{4,2},{5,3},{6,0},{7,1},{8,14},{9,15},{10,... | collective-permute-start | bytes 294920 | tf_op jit(solution)/shard_map/ppermute | solution.py:18
  4.9 5.2 %collective-permute-start.3 = (bf16[16,3072]{1,0:T(8,128)(2,1)S(1)}, bf16[16,3072]{1,0:T(8,128)(2,1)S(1)}, u32[]{:S(2)}, u32[]{:S(2)}) collective-permute-start(bf16[16,3072]{1,0:T(8,128)(2,1)S(1)} %get-tuple-element.33), channel_id=1, source_target_pairs={{0,4},{1,5},{2,6},{3,7},{4,0},{5,1},{6,2},{7,3},{8,12},{9,13},{10,... | collective-permute-start | bytes 294920 | tf_op jit(solution)/shard_map/ppermute | solution.py:18
  5.5 4.8 %collective-permute-start = (bf16[16,3072]{1,0:T(8,128)(2,1)S(1)}, bf16[16,3072]{1,0:T(8,128)(2,1)S(1)}, u32[]{:S(2)}, u32[]{:S(2)}) collective-permute-start(bf16[16,3072]{1,0:T(8,128)(2,1)S(1)} %get-tuple-element.33), channel_id=1, source_target_pairs={{0,2},{1,3},{2,0},{3,1},{4,6},{5,7},{6,4},{7,5},{8,10},{9,11},{10,... | collective-permute-start | bytes 294920 | tf_op jit(solution)/shard_map/ppermute | solution.py:18
  8.5 4.5 %copy-start.1 = (bf16[1,1,3072,512]{3,2,1,0:T(8,128)(2,1)S(1)}, bf16[1,1,3072,512]{3,2,1,0:T(8,128)(2,1)}, u32[]{:S(2)}) copy-start(bf16[1,1,3072,512]{3,2,1,0:T(8,128)(2,1)} %param.11) | copy-start | bytes 9437188
  8.5 4.5 %copy-start.2 = (bf16[1,1,512,3072]{3,2,1,0:T(8,128)(2,1)S(1)}, bf16[1,1,512,3072]{3,2,1,0:T(8,128)(2,1)}, u32[]{:S(2)}) copy-start(bf16[1,1,512,3072]{3,2,1,0:T(8,128)(2,1)} %param.13) | copy-start | bytes 9437188
  10.2 1.5 %collective-permute-start.4 = (bf16[32,3072]{1,0:T(8,128)(2,1)S(1)}, bf16[32,3072]{1,0:T(8,128)(2,1)S(1)}, u32[]{:S(2)}, u32[]{:S(2)}) collective-permute-start(bf16[32,3072]{1,0:T(8,128)(2,1)S(1)} %pad_maximum_fusion.1.mine_ref), channel_id=1, source_target_pairs={{0,1},{1,0},{2,3},{3,2},{4,5},{5,4},{6,7},{7,6},{8,9},{9,8},{10,11... | collective-permute-start | bytes 589832 | tf_op jit(solution)/shard_map/ppermute | solution.py:18
  10.3 2.6 %collective-permute-start.1 = (bf16[32,3072]{1,0:T(8,128)(2,1)S(1)}, bf16[32,3072]{1,0:T(8,128)(2,1)S(1)}, u32[]{:S(2)}, u32[]{:S(2)}) collective-permute-start(bf16[32,3072]{1,0:T(8,128)(2,1)S(1)} %constant_dynamic-update-slice_fusion.mine_ref), channel_id=1, source_target_pairs={{0,1},{1,0},{2,3},{3,2},{4,5},{5,4},{6,7},{7,6},{8,9},{9,8},{10,11... | collective-permute-start | bytes 589832 | tf_op jit(solution)/shard_map/ppermute | solution.py:18
  12.9 11.6 %copy-start = (bf16[4,1,16,3072]{3,2,1,0:T(8,128)(2,1)S(1)}, bf16[4,1,16,3072]{3,2,1,0:T(8,128)(2,1)}, u32[]{:S(2)}) copy-start(bf16[4,1,16,3072]{3,2,1,0:T(8,128)(2,1)} %param.8) | copy-start | bytes 1179652
  14.6 1.5 %collective-permute-start.5 = (bf16[32,3072]{1,0:T(8,128)(2,1)S(1)}, bf16[32,3072]{1,0:T(8,128)(2,1)S(1)}, u32[]{:S(2)}, u32[]{:S(2)}) collective-permute-start(bf16[32,3072]{1,0:T(8,128)(2,1)S(1)} %get-tuple-element.39), channel_id=1, source_target_pairs={{0,1},{1,0},{2,3},{3,2},{4,5},{5,4},{6,7},{7,6},{8,9},{9,8},{10,11... | collective-permute-start | bytes 589832 | tf_op jit(solution)/shard_map/ppermute | solution.py:18
  16.2 4.7 %collective-permute-start.6 = (bf16[16,3072]{1,0:T(8,128)(2,1)S(1)}, bf16[16,3072]{1,0:T(8,128)(2,1)S(1)}, u32[]{:S(2)}, u32[]{:S(2)}) collective-permute-start(bf16[16,3072]{1,0:T(8,128)(2,1)S(1)} %convert_element_type.15), channel_id=1, source_target_pairs={{0,8},{1,0},{2,10},{3,2},{8,16},{9,1},{10,18},{11,3},{16,24},{17,9... | collective-permute-start | bytes 294920 | tf_op jit(solution)/shard_map/ppermute | solution.py:30
  17.8 5.4 %collective-permute-start.8 = (bf16[16,3072]{1,0:T(8,128)(2,1)S(1)}, bf16[16,3072]{1,0:T(8,128)(2,1)S(1)}, u32[]{:S(2)}, u32[]{:S(2)}) collective-permute-start(bf16[16,3072]{1,0:T(8,128)(2,1)S(1)} %convert_element_type.15), channel_id=1, source_target_pairs={{0,1},{1,9},{2,3},{3,11},{8,0},{9,17},{10,2},{11,19},{16,8},{17,25... | collective-permute-start | bytes 294920 | tf_op jit(solution)/shard_map/ppermute | solution.py:30
  17.8 6.7 %collective-permute-start.7 = (bf16[16,3072]{1,0:T(8,128)(2,1)S(1)}, bf16[16,3072]{1,0:T(8,128)(2,1)S(1)}, u32[]{:S(2)}, u32[]{:S(2)}) collective-permute-start(bf16[16,3072]{1,0:T(8,128)(2,1)S(1)} %get-tuple-element.47), channel_id=1, source_target_pairs={{0,1},{1,11},{2,3},{3,9},{8,0},{9,19},{10,2},{11,17},{16,8},{17,27... | collective-permute-start | bytes 294920 | tf_op jit(solution)/shard_map/ppermute | solution.py:30
  17.8 6.7 %collective-permute-start.9 = (bf16[16,3072]{1,0:T(8,128)(2,1)S(1)}, bf16[16,3072]{1,0:T(8,128)(2,1)S(1)}, u32[]{:S(2)}, u32[]{:S(2)}) collective-permute-start(bf16[16,3072]{1,0:T(8,128)(2,1)S(1)} %get-tuple-element.47), channel_id=1, source_target_pairs={{0,10},{1,0},{2,8},{3,2},{8,18},{9,1},{10,16},{11,3},{16,26},{17,9... | collective-permute-start | bytes 294920 | tf_op jit(solution)/shard_map/ppermute | solution.py:30
  24.7 6.2 %collective-permute-start.10 = (bf16[16,3072]{1,0:T(8,128)(2,1)S(1)}, bf16[16,3072]{1,0:T(8,128)(2,1)S(1)}, u32[]{:S(2)}, u32[]{:S(2)}) collective-permute-start(bf16[16,3072]{1,0:T(8,128)(2,1)S(1)} %get-tuple-element.46), channel_id=1, source_target_pairs={{0,6},{1,7},{2,4},{3,5},{4,2},{5,3},{6,0},{7,1},{8,14},{9,15},{10,... | collective-permute-start | bytes 294920 | tf_op jit(solution)/shard_map/ppermute | solution.py:18
  25.8 5.5 %collective-permute-start.11 = (bf16[16,3072]{1,0:T(8,128)(2,1)S(1)}, bf16[16,3072]{1,0:T(8,128)(2,1)S(1)}, u32[]{:S(2)}, u32[]{:S(2)}) collective-permute-start(bf16[16,3072]{1,0:T(8,128)(2,1)S(1)} %get-tuple-element.46), channel_id=1, source_target_pairs={{0,4},{1,5},{2,6},{3,7},{4,0},{5,1},{6,2},{7,3},{8,12},{9,13},{10,... | collective-permute-start | bytes 294920 | tf_op jit(solution)/shard_map/ppermute | solution.py:18
  26.4 6.4 %collective-permute-start.14 = (bf16[16,3072]{1,0:T(8,128)(2,1)S(1)}, bf16[16,3072]{1,0:T(8,128)(2,1)S(1)}, u32[]{:S(2)}, u32[]{:S(2)}) collective-permute-start(bf16[16,3072]{1,0:T(8,128)(2,1)S(1)} %get-tuple-element.46), channel_id=1, source_target_pairs={{0,2},{1,3},{2,0},{3,1},{4,6},{5,7},{6,4},{7,5},{8,10},{9,11},{10,... | collective-permute-start | bytes 294920 | tf_op jit(solution)/shard_map/ppermute | solution.py:18
  28.3 5.7 %collective-permute-start.13 = (bf16[16,3072]{1,0:T(8,128)(2,1)S(1)}, bf16[16,3072]{1,0:T(8,128)(2,1)S(1)}, u32[]{:S(2)}, u32[]{:S(2)}) collective-permute-start(bf16[16,3072]{1,0:T(8,128)(2,1)S(1)} %get-tuple-element.47), channel_id=1, source_target_pairs={{0,2},{1,3},{2,0},{3,1},{4,6},{5,7},{6,4},{7,5},{8,10},{9,11},{10,... | collective-permute-start | bytes 294920 | tf_op jit(solution)/shard_map/ppermute | solution.py:18
  31.4 2.6 %collective-permute-start.12 = (bf16[32,3072]{1,0:T(8,128)(2,1)S(1)}, bf16[32,3072]{1,0:T(8,128)(2,1)S(1)}, u32[]{:S(2)}, u32[]{:S(2)}) collective-permute-start(bf16[32,3072]{1,0:T(8,128)(2,1)S(1)} %constant_dynamic-update-slice_fusion.2.mine_ref), channel_id=1, source_target_pairs={{0,1},{1,0},{2,3},{3,2},{4,5},{5,4},{6,7},{7,6},{8,9},{9,8},{10,11... | collective-permute-start | bytes 589832 | tf_op jit(solution)/shard_map/ppermute | solution.py:18
  32.8 2.3 %collective-permute-start.15 = (bf16[32,3072]{1,0:T(8,128)(2,1)S(1)}, bf16[32,3072]{1,0:T(8,128)(2,1)S(1)}, u32[]{:S(2)}, u32[]{:S(2)}) collective-permute-start(bf16[32,3072]{1,0:T(8,128)(2,1)S(1)} %constant_dynamic-update-slice_fusion.4.mine_ref), channel_id=1, source_target_pairs={{0,1},{1,0},{2,3},{3,2},{4,5},{5,4},{6,7},{7,6},{8,9},{9,8},{10,11... | collective-permute-start | bytes 589832 | tf_op jit(solution)/shard_map/ppermute | solution.py:18
  36.8 1.5 %collective-permute-start.16 = (bf16[32,3072]{1,0:T(8,128)(2,1)S(1)}, bf16[32,3072]{1,0:T(8,128)(2,1)S(1)}, u32[]{:S(2)}, u32[]{:S(2)}) collective-permute-start(bf16[32,3072]{1,0:T(8,128)(2,1)S(1)} %get-tuple-element.54), channel_id=1, source_target_pairs={{0,1},{1,0},{2,3},{3,2},{4,5},{5,4},{6,7},{7,6},{8,9},{9,8},{10,11... | collective-permute-start | bytes 589832 | tf_op jit(solution)/shard_map/ppermute | solution.py:18
  38.4 4.9 %collective-permute-start.17 = (bf16[16,3072]{1,0:T(8,128)(2,1)S(1)}, bf16[16,3072]{1,0:T(8,128)(2,1)S(1)}, u32[]{:S(2)}, u32[]{:S(2)}) collective-permute-start(bf16[16,3072]{1,0:T(8,128)(2,1)S(1)} %get-tuple-element.56), channel_id=1, source_target_pairs={{0,2},{1,3},{2,0},{3,1},{4,6},{5,7},{6,4},{7,5},{8,10},{9,11},{10,... | collective-permute-start | bytes 294920 | tf_op jit(solution)/shard_map/ppermute | solution.py:18

commit v12 on v11

--- a/solution.py
+++ b/solution.py
@@ -81,11 +81,9 @@
         for weight, head in zip(weights, heads)
     ]
     mixed = jnp.concatenate([(mix / total).astype(jnp.bfloat16) for mix, total in zip(mixed, sums)], 1)
-    for start in range(0, width, width // 2):
-        columns = slice(start, start + width // 2)
-        part = jnp.dot(mixed, wo_ref[:, columns], preferred_element_type=jnp.float32)
-        keep_ref[:, columns] = part[:half]
-        send_ref[:, columns] = part[half:].astype(jnp.bfloat16)
+    part = jnp.dot(mixed, wo_ref[...], preferred_element_type=jnp.float32)
+    keep_ref[...] = part[:half]
+    send_ref[...] = part[half:].astype(jnp.bfloat16)
 
 
 def in_vmem(*arrays):

time: 44.2 us -> 44.2 us (level)
  no operation moved by 1% of the time
where the time goes in v12:
time: 44.2 us; the launch traced here: 44 us
  waiting for transfers between devices  18.5 us (42%)
  starting transfers between devices  14 us (32%)
  Pallas kernels  9.77 us (22%)
  between operations  0.89 us (2%)
  other arithmetic  0.79 us (2%)
    ppermute x14, waiting for transfers between devices, swapped(): return lax.ppermute(value, BOTH, [(i, i ^ mask) for i in range(count)])  14.4 us
    ppermute x14, starting transfers between devices, swapped(): return lax.ppermute(value, BOTH, [(i, i ^ mask) for i in range(count)])  10.4 us
    pallas_call x6, Pallas kernels, on_chip(): pl.pallas_call(kernel, out_shape=tuple((jax.ShapeDtypeStruct(shape, dtype...  5.75 us
    ppermute x4, waiting for transfers between devices, climbed(): return lax.ppermute(value, ('section', 'lane'), pairs)  4.07 us
    ppermute x4, starting transfers between devices, climbed(): return lax.ppermute(value, ('section', 'lane'), pairs)  3.59 us
    pallas_call x1, Pallas kernels, load(): pl.pallas_call(load_kernel, out_shape=tuple((pltpu.VMEM(a.shape, a.dtype)...  2.87 us
    pallas_call x1, Pallas kernels, entry(): pl.pallas_call(entry_kernel, out_shape=(pltpu.VMEM(state.shape, jnp.bfloa...  0.98 us
  transfers between devices with their start and end apart: 18, of which 12 were waited for; matrix products, arithmetic and copies ran while one was open for 0% of the time, Pallas kernels for 12%

profile of v12, /device:TPU:0, one launch (start us, length us, event | category | flops | bytes accessed | tf_op | source)
XLA Modules:
  0.0 44.0 jit_solution(17075968050746324002)
XLA Ops:
  0.0 1.0 %shard_map.73 = (bf16[16,3072]{1,0:T(8,128)(2,1)S(1)}, bf16[16,3072]{1,0:T(8,128)(2,1)S(1)}, f32[1,3072]{1,0:T(1,128)S(1)}) custom-call(bf16[16,3072]{1,0:T(8,128)(2,1)} %bitcast.22, f32[1,3072]{1,0:T(1,128)} %bitcast.23), custom_call_target="tpu_custom_call" | custom-call | tf_op jit(solution)/shard_map/pallas_call | solution.py:151
  1.0 4.0 %collective-permute-start.2 = (bf16[16,3072]{1,0:T(8,128)(2,1)S(1)}, bf16[16,3072]{1,0:T(8,128)(2,1)S(1)}, u32[]{:S(2)}, u32[]{:S(2)}) collective-permute-start(bf16[16,3072]{1,0:T(8,128)(2,1)S(1)} %get-tuple-element.33), channel_id=1, source_target_pairs={{0,6},{1,7},{2,4},{3,5},{4,2},{5,3},{6,0},{7,1},{8,14},{9,15},{10,... | collective-permute-start | bytes 294920 | tf_op jit(solution)/shard_map/ppermute | solution.py:18
  4.9 0.5 %collective-permute-start.3 = (bf16[16,3072]{1,0:T(8,128)(2,1)S(1)}, bf16[16,3072]{1,0:T(8,128)(2,1)S(1)}, u32[]{:S(2)}, u32[]{:S(2)}) collective-permute-start(bf16[16,3072]{1,0:T(8,128)(2,1)S(1)} %get-tuple-element.33), channel_id=1, source_target_pairs={{0,4},{1,5},{2,6},{3,7},{4,0},{5,1},{6,2},{7,3},{8,12},{9,13},{10,... | collective-permute-start | bytes 294920 | tf_op jit(solution)/shard_map/ppermute | solution.py:18
  5.5 0.1 collective-permute-start
  5.6 2.9 %shard_map.74.wkv_ref = bf16[6144,512]{1,0:T(8,128)(2,1)S(1)} custom-call(bf16[6144,512]{1,0:T(8,128)(2,1)} %bitcast.21), custom_call_target="tpu_custom_call" | custom-call | bytes 6291456 | tf_op jit(solution)/shard_map/pallas_call | solution.py:181
  8.5 0.0 copy-start.1
  8.5 0.0 copy-start.2
  8.5 0.0 collective-permute-done.2
  8.5 1.7 %collective-permute-done.3 = bf16[16,3072]{1,0:T(8,128)(2,1)S(1)} collective-permute-done((bf16[16,3072]{1,0:T(8,128)(2,1)S(1)}, bf16[16,3072]{1,0:T(8,128)(2,1)S(1)}, u32[]{:S(2)}, u32[]{:S(2)}) %collective-permute-start.3) | collective-permute-done | bytes 98336 | tf_op jit(solution)/shard_map/ppermute | solution.py:18
  10.2 0.1 collective-permute-start.4
  10.3 0.0 collective-permute-done
  10.3 0.5 %collective-permute-start.1 = (bf16[32,3072]{1,0:T(8,128)(2,1)S(1)}, bf16[32,3072]{1,0:T(8,128)(2,1)S(1)}, u32[]{:S(2)}, u32[]{:S(2)}) collective-permute-start(bf16[32,3072]{1,0:T(8,128)(2,1)S(1)} %constant_dynamic-update-slice_fusion.mine_ref), channel_id=1, source_target_pairs={{0,1},{1,0},{2,3},{3,2},{4,5},{5,4},{6,7},{7,6},{8,9},{9,8},{10,11... | collective-permute-start | bytes 589832 | tf_op jit(solution)/shard_map/ppermute | solution.py:18
  10.9 0.8 %collective-permute-done.4.theirs_ref = bf16[32,3072]{1,0:T(8,128)(2,1)S(1)} collective-permute-done((bf16[32,3072]{1,0:T(8,128)(2,1)S(1)}, bf16[32,3072]{1,0:T(8,128)(2,1)S(1)}, u32[]{:S(2)}, u32[]{:S(2)}) %collective-permute-start.4) | collective-permute-done | bytes 196640 | tf_op jit(solution)/shard_map/ppermute | solution.py:18
  11.7 1.2 %shard_map.75 = (bf16[64,512]{1,0:T(8,128)(2,1)S(1)}, bf16[64,512]{1,0:T(8,128)(2,1)S(1)}) custom-call(bf16[32,3072]{1,0:T(8,128)(2,1)S(1)} %pad_maximum_fusion.1.mine_ref, bf16[32,3072]{1,0:T(8,128)(2,1)S(1)} %collective-permute-done.4.theirs_ref, bf16[6144,512]{1,0:T(8,128)(2,1)S(1)} %shard_map.74.wkv_ref), custom_call_target="tpu_custom_call" | custom-call | flops 1610612736 | bytes 6684672 | tf_op jit(solution)/shard_map/pallas_call | solution.py:95
  12.9 0.0 copy-start
  12.9 0.0 collective-permute-done.1.theirs_ref
  12.9 0.0 copy-done.1
  12.9 0.0 copy-done.2
  12.9 1.6 %shard_map.76 = (f32[32,3072]{1,0:T(8,128)S(1)}, bf16[32,3072]{1,0:T(8,128)(2,1)S(1)}) custom-call(bf16[32,3072]{1,0:T(8,128)(2,1)S(1)} %constant_dynamic-update-slice_fusion.mine_ref, bf16[32,3072]{1,0:T(8,128)(2,1)S(1)} %collective-permute-done.1.theirs_ref, bf16[64,512]{1,0:T(8,128)(2,1)S(1)} %get-tuple-element.36.keys_ref, ...), custom_call_target="tpu_custom_call" | custom-call | flops 2415919104 | bytes 6815744 | tf_op jit(solution)/shard_map/pallas_call | solution.py:95
  14.6 0.2 collective-permute-start.5
  14.8 1.3 %collective-permute-done.5.sent_ref = bf16[32,3072]{1,0:T(8,128)(2,1)S(1)} collective-permute-done((bf16[32,3072]{1,0:T(8,128)(2,1)S(1)}, bf16[32,3072]{1,0:T(8,128)(2,1)S(1)}, u32[]{:S(2)}, u32[]{:S(2)}) %collective-permute-start.5) | collective-permute-done | bytes 196640 | tf_op jit(solution)/shard_map/ppermute | solution.py:18
  16.2 1.6 %collective-permute-start.6 = (bf16[16,3072]{1,0:T(8,128)(2,1)S(1)}, bf16[16,3072]{1,0:T(8,128)(2,1)S(1)}, u32[]{:S(2)}, u32[]{:S(2)}) collective-permute-start(bf16[16,3072]{1,0:T(8,128)(2,1)S(1)} %convert_element_type.15), channel_id=1, source_target_pairs={{0,8},{1,0},{2,10},{3,2},{8,16},{9,1},{10,18},{11,3},{16,24},{17,9... | collective-permute-start | bytes 294920 | tf_op jit(solution)/shard_map/ppermute | solution.py:30
  17.8 0.0 collective-permute-start.8
  17.8 0.0 collective-permute-start.7
  17.8 2.0 %collective-permute-start.9 = (bf16[16,3072]{1,0:T(8,128)(2,1)S(1)}, bf16[16,3072]{1,0:T(8,128)(2,1)S(1)}, u32[]{:S(2)}, u32[]{:S(2)}) collective-permute-start(bf16[16,3072]{1,0:T(8,128)(2,1)S(1)} %get-tuple-element.47), channel_id=1, source_target_pairs={{0,10},{1,0},{2,8},{3,2},{8,18},{9,1},{10,16},{11,3},{16,26},{17,9... | collective-permute-start | bytes 294920 | tf_op jit(solution)/shard_map/ppermute | solution.py:30
  20.4 0.5 %collective-permute-done.6 = bf16[16,3072]{1,0:T(8,128)(2,1)S(1)} collective-permute-done((bf16[16,3072]{1,0:T(8,128)(2,1)S(1)}, bf16[16,3072]{1,0:T(8,128)(2,1)S(1)}, u32[]{:S(2)}, u32[]{:S(2)}) %collective-permute-start.6) | collective-permute-done | bytes 98336 | tf_op jit(solution)/shard_map/ppermute | solution.py:30
  20.9 2.2 %collective-permute-done.8 = bf16[16,3072]{1,0:T(8,128)(2,1)S(1)} collective-permute-done((bf16[16,3072]{1,0:T(8,128)(2,1)S(1)}, bf16[16,3072]{1,0:T(8,128)(2,1)S(1)}, u32[]{:S(2)}, u32[]{:S(2)}) %collective-permute-start.8) | collective-permute-done | bytes 98336 | tf_op jit(solution)/shard_map/ppermute | solution.py:30
  23.1 1.3 %collective-permute-done.7 = bf16[16,3072]{1,0:T(8,128)(2,1)S(1)} collective-permute-done((bf16[16,3072]{1,0:T(8,128)(2,1)S(1)}, bf16[16,3072]{1,0:T(8,128)(2,1)S(1)}, u32[]{:S(2)}, u32[]{:S(2)}) %collective-permute-start.7) | collective-permute-done | bytes 98336 | tf_op jit(solution)/shard_map/ppermute | solution.py:30
  24.5 0.0 collective-permute-done.9
  24.5 0.0 copy-done
  24.5 0.2 shard_map.78
  24.7 1.1 %collective-permute-start.10 = (bf16[16,3072]{1,0:T(8,128)(2,1)S(1)}, bf16[16,3072]{1,0:T(8,128)(2,1)S(1)}, u32[]{:S(2)}, u32[]{:S(2)}) collective-permute-start(bf16[16,3072]{1,0:T(8,128)(2,1)S(1)} %get-tuple-element.46), channel_id=1, source_target_pairs={{0,6},{1,7},{2,4},{3,5},{4,2},{5,3},{6,0},{7,1},{8,14},{9,15},{10,... | collective-permute-start | bytes 294920 | tf_op jit(solution)/shard_map/ppermute | solution.py:18
  25.8 0.6 %collective-permute-start.11 = (bf16[16,3072]{1,0:T(8,128)(2,1)S(1)}, bf16[16,3072]{1,0:T(8,128)(2,1)S(1)}, u32[]{:S(2)}, u32[]{:S(2)}) collective-permute-start(bf16[16,3072]{1,0:T(8,128)(2,1)S(1)} %get-tuple-element.46), channel_id=1, source_target_pairs={{0,4},{1,5},{2,6},{3,7},{4,0},{5,1},{6,2},{7,3},{8,12},{9,13},{10,... | collective-permute-start | bytes 294920 | tf_op jit(solution)/shard_map/ppermute | solution.py:18
  26.4 1.8 %collective-permute-start.14 = (bf16[16,3072]{1,0:T(8,128)(2,1)S(1)}, bf16[16,3072]{1,0:T(8,128)(2,1)S(1)}, u32[]{:S(2)}, u32[]{:S(2)}) collective-permute-start(bf16[16,3072]{1,0:T(8,128)(2,1)S(1)} %get-tuple-element.46), channel_id=1, source_target_pairs={{0,2},{1,3},{2,0},{3,1},{4,6},{5,7},{6,4},{7,5},{8,10},{9,11},{10,... | collective-permute-start | bytes 294920 | tf_op jit(solution)/shard_map/ppermute | solution.py:18
  28.3 0.2 collective-permute-start.13
  28.5 2.4 %collective-permute-done.10 = bf16[16,3072]{1,0:T(8,128)(2,1)S(1)} collective-permute-done((bf16[16,3072]{1,0:T(8,128)(2,1)S(1)}, bf16[16,3072]{1,0:T(8,128)(2,1)S(1)}, u32[]{:S(2)}, u32[]{:S(2)}) %collective-permute-start.10) | collective-permute-done | bytes 98336 | tf_op jit(solution)/shard_map/ppermute | solution.py:18
  30.9 0.4 collective-permute-done.11
  31.4 0.1 collective-permute-start.12
  31.4 1.4 %collective-permute-done.14 = bf16[16,3072]{1,0:T(8,128)(2,1)S(1)} collective-permute-done((bf16[16,3072]{1,0:T(8,128)(2,1)S(1)}, bf16[16,3072]{1,0:T(8,128)(2,1)S(1)}, u32[]{:S(2)}, u32[]{:S(2)}) %collective-permute-start.14) | collective-permute-done | bytes 98336 | tf_op jit(solution)/shard_map/ppermute | solution.py:18
  32.8 0.1 collective-permute-start.15
  32.9 1.0 %collective-permute-done.13 = bf16[16,3072]{1,0:T(8,128)(2,1)S(1)} collective-permute-done((bf16[16,3072]{1,0:T(8,128)(2,1)S(1)}, bf16[16,3072]{1,0:T(8,128)(2,1)S(1)}, u32[]{:S(2)}, u32[]{:S(2)}) %collective-permute-start.13) | collective-permute-done | bytes 98336 | tf_op jit(solution)/shard_map/ppermute | solution.py:18
  33.9 0.0 collective-permute-done.12.theirs_ref
  33.9 1.2 %shard_map.79 = (bf16[64,512]{1,0:T(8,128)(2,1)S(1)}, bf16[64,512]{1,0:T(8,128)(2,1)S(1)}) custom-call(bf16[32,3072]{1,0:T(8,128)(2,1)S(1)} %constant_dynamic-update-slice_fusion.2.mine_ref, bf16[32,3072]{1,0:T(8,128)(2,1)S(1)} %collective-permute-done.12.theirs_ref, bf16[6144,512]{1,0:T(8,128)(2,1)S(1)} %shard_map.74.wkv_ref), custom_call_target="tpu_custom_call" | custom-call | flops 1610612736 | bytes 6684672 | tf_op jit(solution)/shard_map/pallas_call | solution.py:95
  35.1 0.0 collective-permute-done.15.theirs_ref
  35.2 1.6 %shard_map.80 = (f32[32,3072]{1,0:T(8,128)S(1)}, bf16[32,3072]{1,0:T(8,128)(2,1)S(1)}) custom-call(bf16[32,3072]{1,0:T(8,128)(2,1)S(1)} %constant_dynamic-update-slice_fusion.4.mine_ref, bf16[32,3072]{1,0:T(8,128)(2,1)S(1)} %collective-permute-done.15.theirs_ref, bf16[64,512]{1,0:T(8,128)(2,1)S(1)} %get-tuple-element.51.keys_ref, ...), custom_call_target="tpu_custom_call" | custom-call | flops 2415919104 | bytes 6815744 | tf_op jit(solution)/shard_map/pallas_call | solution.py:95
  36.8 0.1 collective-permute-start.16
  36.9 1.4 %collective-permute-done.16.sent_ref = bf16[32,3072]{1,0:T(8,128)(2,1)S(1)} collective-permute-done((bf16[32,3072]{1,0:T(8,128)(2,1)S(1)}, bf16[32,3072]{1,0:T(8,128)(2,1)S(1)}, u32[]{:S(2)}, u32[]{:S(2)}) %collective-permute-start.16) | collective-permute-done | bytes 196640 | tf_op jit(solution)/shard_map/ppermute | solution.py:18
  38.4 1.0 %collective-permute-start.17 = (bf16[16,3072]{1,0:T(8,128)(2,1)S(1)}, bf16[16,3072]{1,0:T(8,128)(2,1)S(1)}, u32[]{:S(2)}, u32[]{:S(2)}) collective-permute-start(bf16[16,3072]{1,0:T(8,128)(2,1)S(1)} %get-tuple-element.56), channel_id=1, source_target_pairs={{0,2},{1,3},{2,0},{3,1},{4,6},{5,7},{6,4},{7,5},{8,10},{9,11},{10,... | collective-permute-start | bytes 294920 | tf_op jit(solution)/shard_map/ppermute | solution.py:18
  39.4 3.8 %collective-permute-done.17 = bf16[16,3072]{1,0:T(8,128)(2,1)S(1)} collective-permute-done((bf16[16,3072]{1,0:T(8,128)(2,1)S(1)}, bf16[16,3072]{1,0:T(8,128)(2,1)S(1)}, u32[]{:S(2)}, u32[]{:S(2)}) %collective-permute-start.17) | collective-permute-done | bytes 98336 | tf_op jit(solution)/shard_map/ppermute | solution.py:18
  43.3 0.7 %maximum_bitcast_fusion = bf16[2,1,1,16,3072]{4,3,2,1,0:T(8,128)(2,1)} fusion(bf16[1,16,3072]{2,1,0:T(8,128)(2,1)S(1)} %fusion.1, bf16[1,16,3072]{2,1,0:T(8,128)(2,1)S(1)} %fusion), kind=kLoop, calls=%fused_computation.2 | loop fusion | flops 98304 | bytes 393216 | tf_op jit(solution)/shard_map/broadcast_in_dim | solution.py:265
  (13 shorter events, 0.2 us)
Async XLA Ops:
  1.0 7.5 %collective-permute-start.2 = (bf16[16,3072]{1,0:T(8,128)(2,1)S(1)}, bf16[16,3072]{1,0:T(8,128)(2,1)S(1)}, u32[]{:S(2)}, u32[]{:S(2)}) collective-permute-start(bf16[16,3072]{1,0:T(8,128)(2,1)S(1)} %get-tuple-element.33), channel_id=1, source_target_pairs={{0,6},{1,7},{2,4},{3,5},{4,2},{5,3},{6,0},{7,1},{8,14},{9,15},{10,... | collective-permute-start | bytes 294920 | tf_op jit(solution)/shard_map/ppermute | solution.py:18
  4.9 5.2 %collective-permute-start.3 = (bf16[16,3072]{1,0:T(8,128)(2,1)S(1)}, bf16[16,3072]{1,0:T(8,128)(2,1)S(1)}, u32[]{:S(2)}, u32[]{:S(2)}) collective-permute-start(bf16[16,3072]{1,0:T(8,128)(2,1)S(1)} %get-tuple-element.33), channel_id=1, source_target_pairs={{0,4},{1,5},{2,6},{3,7},{4,0},{5,1},{6,2},{7,3},{8,12},{9,13},{10,... | collective-permute-start | bytes 294920 | tf_op jit(solution)/shard_map/ppermute | solution.py:18
  5.5 4.8 %collective-permute-start = (bf16[16,3072]{1,0:T(8,128)(2,1)S(1)}, bf16[16,3072]{1,0:T(8,128)(2,1)S(1)}, u32[]{:S(2)}, u32[]{:S(2)}) collective-permute-start(bf16[16,3072]{1,0:T(8,128)(2,1)S(1)} %get-tuple-element.33), channel_id=1, source_target_pairs={{0,2},{1,3},{2,0},{3,1},{4,6},{5,7},{6,4},{7,5},{8,10},{9,11},{10,... | collective-permute-start | bytes 294920 | tf_op jit(solution)/shard_map/ppermute | solution.py:18
  8.5 4.5 %copy-start.1 = (bf16[1,1,3072,512]{3,2,1,0:T(8,128)(2,1)S(1)}, bf16[1,1,3072,512]{3,2,1,0:T(8,128)(2,1)}, u32[]{:S(2)}) copy-start(bf16[1,1,3072,512]{3,2,1,0:T(8,128)(2,1)} %param.11) | copy-start | bytes 9437188
  8.5 4.5 %copy-start.2 = (bf16[1,1,512,3072]{3,2,1,0:T(8,128)(2,1)S(1)}, bf16[1,1,512,3072]{3,2,1,0:T(8,128)(2,1)}, u32[]{:S(2)}) copy-start(bf16[1,1,512,3072]{3,2,1,0:T(8,128)(2,1)} %param.13) | copy-start | bytes 9437188
  10.2 1.5 %collective-permute-start.4 = (bf16[32,3072]{1,0:T(8,128)(2,1)S(1)}, bf16[32,3072]{1,0:T(8,128)(2,1)S(1)}, u32[]{:S(2)}, u32[]{:S(2)}) collective-permute-start(bf16[32,3072]{1,0:T(8,128)(2,1)S(1)} %pad_maximum_fusion.1.mine_ref), channel_id=1, source_target_pairs={{0,1},{1,0},{2,3},{3,2},{4,5},{5,4},{6,7},{7,6},{8,9},{9,8},{10,11... | collective-permute-start | bytes 589832 | tf_op jit(solution)/shard_map/ppermute | solution.py:18
  10.3 2.6 %collective-permute-start.1 = (bf16[32,3072]{1,0:T(8,128)(2,1)S(1)}, bf16[32,3072]{1,0:T(8,128)(2,1)S(1)}, u32[]{:S(2)}, u32[]{:S(2)}) collective-permute-start(bf16[32,3072]{1,0:T(8,128)(2,1)S(1)} %constant_dynamic-update-slice_fusion.mine_ref), channel_id=1, source_target_pairs={{0,1},{1,0},{2,3},{3,2},{4,5},{5,4},{6,7},{7,6},{8,9},{9,8},{10,11... | collective-permute-start | bytes 589832 | tf_op jit(solution)/shard_map/ppermute | solution.py:18
  12.9 11.6 %copy-start = (bf16[4,1,16,3072]{3,2,1,0:T(8,128)(2,1)S(1)}, bf16[4,1,16,3072]{3,2,1,0:T(8,128)(2,1)}, u32[]{:S(2)}) copy-start(bf16[4,1,16,3072]{3,2,1,0:T(8,128)(2,1)} %param.8) | copy-start | bytes 1179652
  14.6 1.5 %collective-permute-start.5 = (bf16[32,3072]{1,0:T(8,128)(2,1)S(1)}, bf16[32,3072]{1,0:T(8,128)(2,1)S(1)}, u32[]{:S(2)}, u32[]{:S(2)}) collective-permute-start(bf16[32,3072]{1,0:T(8,128)(2,1)S(1)} %get-tuple-element.39), channel_id=1, source_target_pairs={{0,1},{1,0},{2,3},{3,2},{4,5},{5,4},{6,7},{7,6},{8,9},{9,8},{10,11... | collective-permute-start | bytes 589832 | tf_op jit(solution)/shard_map/ppermute | solution.py:18
  16.2 4.7 %collective-permute-start.6 = (bf16[16,3072]{1,0:T(8,128)(2,1)S(1)}, bf16[16,3072]{1,0:T(8,128)(2,1)S(1)}, u32[]{:S(2)}, u32[]{:S(2)}) collective-permute-start(bf16[16,3072]{1,0:T(8,128)(2,1)S(1)} %convert_element_type.15), channel_id=1, source_target_pairs={{0,8},{1,0},{2,10},{3,2},{8,16},{9,1},{10,18},{11,3},{16,24},{17,9... | collective-permute-start | bytes 294920 | tf_op jit(solution)/shard_map/ppermute | solution.py:30
  17.8 5.4 %collective-permute-start.8 = (bf16[16,3072]{1,0:T(8,128)(2,1)S(1)}, bf16[16,3072]{1,0:T(8,128)(2,1)S(1)}, u32[]{:S(2)}, u32[]{:S(2)}) collective-permute-start(bf16[16,3072]{1,0:T(8,128)(2,1)S(1)} %convert_element_type.15), channel_id=1, source_target_pairs={{0,1},{1,9},{2,3},{3,11},{8,0},{9,17},{10,2},{11,19},{16,8},{17,25... | collective-permute-start | bytes 294920 | tf_op jit(solution)/shard_map/ppermute | solution.py:30
  17.8 6.7 %collective-permute-start.7 = (bf16[16,3072]{1,0:T(8,128)(2,1)S(1)}, bf16[16,3072]{1,0:T(8,128)(2,1)S(1)}, u32[]{:S(2)}, u32[]{:S(2)}) collective-permute-start(bf16[16,3072]{1,0:T(8,128)(2,1)S(1)} %get-tuple-element.47), channel_id=1, source_target_pairs={{0,1},{1,11},{2,3},{3,9},{8,0},{9,19},{10,2},{11,17},{16,8},{17,27... | collective-permute-start | bytes 294920 | tf_op jit(solution)/shard_map/ppermute | solution.py:30
  17.8 6.7 %collective-permute-start.9 = (bf16[16,3072]{1,0:T(8,128)(2,1)S(1)}, bf16[16,3072]{1,0:T(8,128)(2,1)S(1)}, u32[]{:S(2)}, u32[]{:S(2)}) collective-permute-start(bf16[16,3072]{1,0:T(8,128)(2,1)S(1)} %get-tuple-element.47), channel_id=1, source_target_pairs={{0,10},{1,0},{2,8},{3,2},{8,18},{9,1},{10,16},{11,3},{16,26},{17,9... | collective-permute-start | bytes 294920 | tf_op jit(solution)/shard_map/ppermute | solution.py:30
  24.7 6.2 %collective-permute-start.10 = (bf16[16,3072]{1,0:T(8,128)(2,1)S(1)}, bf16[16,3072]{1,0:T(8,128)(2,1)S(1)}, u32[]{:S(2)}, u32[]{:S(2)}) collective-permute-start(bf16[16,3072]{1,0:T(8,128)(2,1)S(1)} %get-tuple-element.46), channel_id=1, source_target_pairs={{0,6},{1,7},{2,4},{3,5},{4,2},{5,3},{6,0},{7,1},{8,14},{9,15},{10,... | collective-permute-start | bytes 294920 | tf_op jit(solution)/shard_map/ppermute | solution.py:18
  25.8 5.5 %collective-permute-start.11 = (bf16[16,3072]{1,0:T(8,128)(2,1)S(1)}, bf16[16,3072]{1,0:T(8,128)(2,1)S(1)}, u32[]{:S(2)}, u32[]{:S(2)}) collective-permute-start(bf16[16,3072]{1,0:T(8,128)(2,1)S(1)} %get-tuple-element.46), channel_id=1, source_target_pairs={{0,4},{1,5},{2,6},{3,7},{4,0},{5,1},{6,2},{7,3},{8,12},{9,13},{10,... | collective-permute-start | bytes 294920 | tf_op jit(solution)/shard_map/ppermute | solution.py:18
  26.4 6.4 %collective-permute-start.14 = (bf16[16,3072]{1,0:T(8,128)(2,1)S(1)}, bf16[16,3072]{1,0:T(8,128)(2,1)S(1)}, u32[]{:S(2)}, u32[]{:S(2)}) collective-permute-start(bf16[16,3072]{1,0:T(8,128)(2,1)S(1)} %get-tuple-element.46), channel_id=1, source_target_pairs={{0,2},{1,3},{2,0},{3,1},{4,6},{5,7},{6,4},{7,5},{8,10},{9,11},{10,... | collective-permute-start | bytes 294920 | tf_op jit(solution)/shard_map/ppermute | solution.py:18
  28.3 5.7 %collective-permute-start.13 = (bf16[16,3072]{1,0:T(8,128)(2,1)S(1)}, bf16[16,3072]{1,0:T(8,128)(2,1)S(1)}, u32[]{:S(2)}, u32[]{:S(2)}) collective-permute-start(bf16[16,3072]{1,0:T(8,128)(2,1)S(1)} %get-tuple-element.47), channel_id=1, source_target_pairs={{0,2},{1,3},{2,0},{3,1},{4,6},{5,7},{6,4},{7,5},{8,10},{9,11},{10,... | collective-permute-start | bytes 294920 | tf_op jit(solution)/shard_map/ppermute | solution.py:18
  31.4 2.6 %collective-permute-start.12 = (bf16[32,3072]{1,0:T(8,128)(2,1)S(1)}, bf16[32,3072]{1,0:T(8,128)(2,1)S(1)}, u32[]{:S(2)}, u32[]{:S(2)}) collective-permute-start(bf16[32,3072]{1,0:T(8,128)(2,1)S(1)} %constant_dynamic-update-slice_fusion.2.mine_ref), channel_id=1, source_target_pairs={{0,1},{1,0},{2,3},{3,2},{4,5},{5,4},{6,7},{7,6},{8,9},{9,8},{10,11... | collective-permute-start | bytes 589832 | tf_op jit(solution)/shard_map/ppermute | solution.py:18
  32.8 2.3 %collective-permute-start.15 = (bf16[32,3072]{1,0:T(8,128)(2,1)S(1)}, bf16[32,3072]{1,0:T(8,128)(2,1)S(1)}, u32[]{:S(2)}, u32[]{:S(2)}) collective-permute-start(bf16[32,3072]{1,0:T(8,128)(2,1)S(1)} %constant_dynamic-update-slice_fusion.4.mine_ref), channel_id=1, source_target_pairs={{0,1},{1,0},{2,3},{3,2},{4,5},{5,4},{6,7},{7,6},{8,9},{9,8},{10,11... | collective-permute-start | bytes 589832 | tf_op jit(solution)/shard_map/ppermute | solution.py:18
  36.8 1.5 %collective-permute-start.16 = (bf16[32,3072]{1,0:T(8,128)(2,1)S(1)}, bf16[32,3072]{1,0:T(8,128)(2,1)S(1)}, u32[]{:S(2)}, u32[]{:S(2)}) collective-permute-start(bf16[32,3072]{1,0:T(8,128)(2,1)S(1)} %get-tuple-element.54), channel_id=1, source_target_pairs={{0,1},{1,0},{2,3},{3,2},{4,5},{5,4},{6,7},{7,6},{8,9},{9,8},{10,11... | collective-permute-start | bytes 589832 | tf_op jit(solution)/shard_map/ppermute | solution.py:18
  38.4 4.9 %collective-permute-start.17 = (bf16[16,3072]{1,0:T(8,128)(2,1)S(1)}, bf16[16,3072]{1,0:T(8,128)(2,1)S(1)}, u32[]{:S(2)}, u32[]{:S(2)}) collective-permute-start(bf16[16,3072]{1,0:T(8,128)(2,1)S(1)} %get-tuple-element.56), channel_id=1, source_target_pairs={{0,2},{1,3},{2,0},{3,1},{4,6},{5,7},{6,4},{7,5},{8,10},{9,11},{10,... | collective-permute-start | bytes 294920 | tf_op jit(solution)/shard_map/ppermute | solution.py:18
